TPU v7x, 256 devices: a whole 4x4x8 slice. The times are simulated.
256 devices in a mesh: sample: 4 (over y), space: 64 (over z, x, core).
Axes of the slice: x: 4, y: 4, z: 8, core: 2. Of those that a mesh axis runs over, the one named last changes fastest.
Arguments:
- field: bfloat16 [4, 256, 512, 128], P('sample', 'space'), may hold values from -6 to 6
- send_rows: int32 [64, 5, 512], P('space'), may hold values from 0 to 2047, as said below
- send_count: int32 [64, 5], P('space'), may hold values from 0 to 512, as said below
- dep_slot: int32 [4, 256, 512], P(None, 'space'), may hold values from 0 to 2559, as said below
- dep_weight: float32 [4, 256, 512], P(None, 'space'), may hold values from 0 to 1, as said below
- helm_coef: float32 [128], replicated, may hold values from 0.5 to 4
- w_first: bfloat16 [128, 256], replicated, may hold values from -0.5 to 0.5
- b_first: float32 [256], replicated, may hold values from -3 to 3
- w_second: bfloat16 [256, 256], replicated, may hold values from -0.375 to 0.375
- b_second: float32 [256], replicated, may hold values from -3 to 3
- w_third: bfloat16 [256, 128], replicated, may hold values from -0.375 to 0.375
- cotangent: bfloat16 [4, 256, 512, 128], P('sample', 'space'), may hold values from -6 to 6
Outputs:
- next_state: bfloat16 [4, 256, 512, 128], P('sample', 'space')
- field_grad: float32 [4, 256, 512, 128], P('sample', 'space')
- grad_first: float32 [128, 256], replicated
- grad_bfirst: float32 [256], replicated
- grad_second: float32 [256, 256], replicated
- grad_bsecond: float32 [256], replicated
- grad_third: float32 [256, 128], replicated
Inputs may be any that keep to these rules, and one draw needn't show every extreme that they name: `send_rows`: slots come in quads 4 q to 4 q + 3, the corners (row, lon), (row, lon + 1), (row + 1, lon), (row + 1, lon + 1) of one grid box of band s, longitude periodic. `send_count`: A multiple of 4; 0 where the target band s + e - 2 lies off the grid or farther from s than its reach (1 band, or 2 for the polar and jet bands); 512 for every live pair whose target is among the first or last max(1, 64 // 8) bands. `dep_slot`: tap k of a cell of band t reads slot e * 512 + 4 q + k of one live quad (4 q + 4 <= send_count[t - e + 2, e]), the same quad for all four taps; |e - 2| is at most the reach of band t. `dep_weight`: the four weights of a cell are bilinear and sum to 1.
All inputs are finite; a program needn't handle non-finite values.
Results may differ from a plain program's by a relative error of at most 0.017.
Values may be sent and summed in bfloat16 or wider, within the bound.
No kernel may reach another device: no remote copies, remote signals or barrier semaphores. Data moves between devices by JAX's collectives and lax.ppermute only.
A program may use at most 64 MiB of HBM per device.

v0:
```python
import jax
import jax.numpy as jnp
from jax import lax
from jax.sharding import PartitionSpec as P

SWEEPS = 2


def extended(cells, sides, width):
    for axis, dim in sides:
        count = lax.axis_size(axis)
        ends = count - 1
        head = lax.slice_in_dim(cells, 0, width, axis=dim)
        tail = lax.slice_in_dim(cells, cells.shape[dim] - width, cells.shape[dim], axis=dim)
        cells = jnp.concatenate(
            [
                lax.ppermute(tail, axis, [(i, (i + 1) % count) for i in range(ends)]),
                cells,
                lax.ppermute(head, axis, [((i + 1) % count, i) for i in range(ends)]),
            ],
            axis=dim,
        )
    return cells


def passed_along(shard, axis, by):
    devices = lax.axis_size(axis)
    pairs = [(i, i + by) for i in range(devices) if 0 <= i + by < devices]
    return lax.ppermute(shard, axis, pairs)


def lon_sum(state):
    return jnp.roll(state, 1, axis=2) + jnp.roll(state, -1, axis=2)


def split_parts(values):
    upper = values.astype(jnp.bfloat16)
    lower = (values - upper.astype(jnp.float32)).astype(jnp.bfloat16)
    return (upper, lower)


def smoother(departure, helm_coef):
    denom = 1.0 + 4.0 * helm_coef
    smooth = departure
    for sweep in range(SWEEPS):
        padded = extended(smooth.astype(jnp.bfloat16), (("space", 1),), 1).astype(smooth.dtype)
        beside_all = padded[:, :-2] + padded[:, 2:] + lon_sum(smooth)
        smooth = (departure + helm_coef * beside_all) / denom
    return smooth


def smoother_adjoint(gsmooth, helm_coef):
    denom = 1.0 + 4.0 * helm_coef
    gdeparture = jnp.zeros_like(gsmooth)
    current = gsmooth
    for sweep in range(SWEEPS):
        scaled = current / denom
        gdeparture = gdeparture + scaled
        padded = extended(scaled.astype(jnp.bfloat16), (("space", 1),), 1).astype(scaled.dtype)
        current = helm_coef * (padded[:, :-2] + padded[:, 2:] + lon_sum(scaled))
    return gdeparture + current


def body(
    field,
    send_rows,
    send_count,
    dep_slot,
    dep_weight,
    helm_coef,
    w_first,
    b_first,
    w_second,
    b_second,
    w_third,
    cotangent,
):
    batch_here, band_rows, lon_cells, channels = field.shape
    offsets = send_rows.shape[1]
    span_bands = (offsets - 1) // 2
    slots_each = send_rows.shape[2]
    cell_count = band_rows * lon_cells
    slot_total = offsets * slots_each
    cell_field = field.reshape(batch_here, cell_count, channels)
    row_table = send_rows[0]
    cell_iota = jnp.arange(cell_count, dtype=jnp.int32)
    slot_iota = jnp.arange(slots_each, dtype=jnp.int32)
    selectors = []
    blocks = []
    for offset in range(offsets):
        live_slots = slot_iota < send_count[0, offset]
        select = ((row_table[offset][:, None] == cell_iota[None, :]) & live_slots[:, None]).astype(
            jnp.bfloat16
        )
        selectors.append(select)
        picked = jnp.einsum(
            "sc,bch->bsh", select, cell_field, preferred_element_type=jnp.float32
        ).astype(jnp.bfloat16)
        if offset == span_bands:
            blocks.append(picked)
        else:
            blocks.append(passed_along(picked, "space", offset - span_bands))
    received = jnp.stack(blocks, axis=1).reshape(batch_here, slot_total, channels)
    slot_cells = dep_slot.reshape(4, cell_count)
    weight_cells = dep_weight.reshape(4, cell_count)
    all_slots = jnp.arange(slot_total, dtype=jnp.int32)
    block_rows = min(512, cell_count)
    interp_parts = []
    dep_blocks = []
    for start in range(0, cell_count, block_rows):
        interp = jnp.zeros((block_rows, slot_total), jnp.float32)
        for tap in range(4):
            hit = slot_cells[tap, start : start + block_rows][:, None] == all_slots[None, :]
            interp = interp + jnp.where(
                hit, weight_cells[tap, start : start + block_rows][:, None], 0.0
            )
        upper, lower = split_parts(interp)
        interp_parts.append((upper, lower))
        dep_blocks.append(
            jnp.einsum("cs,bsh->bch", upper, received, preferred_element_type=jnp.float32)
            + jnp.einsum("cs,bsh->bch", lower, received, preferred_element_type=jnp.float32)
        )
    departure = jnp.concatenate(dep_blocks, axis=1).reshape(field.shape)
    smoothed = smoother(departure, helm_coef).astype(jnp.bfloat16)
    smooth_rows = smoothed.reshape(-1, channels)
    pre_first = jnp.dot(smooth_rows, w_first, preferred_element_type=jnp.float32) + b_first
    act_value, first_back = jax.vjp(jax.nn.gelu, pre_first)
    act_first = act_value.astype(jnp.bfloat16)
    pre_second = jnp.dot(act_first, w_second, preferred_element_type=jnp.float32) + b_second
    act_value, second_back = jax.vjp(jax.nn.gelu, pre_second)
    act_second = act_value.astype(jnp.bfloat16)
    next_rows = smooth_rows.astype(jnp.float32) + jnp.dot(
        act_second, w_third, preferred_element_type=jnp.float32
    )
    next_state = next_rows.astype(jnp.bfloat16).reshape(field.shape)
    cot_rows = cotangent.reshape(-1, channels)
    grad_third = jnp.dot(act_second.T, cot_rows, preferred_element_type=jnp.float32)
    gact_second = jnp.dot(cot_rows, w_third.T, preferred_element_type=jnp.float32)
    gpre_second = second_back(gact_second)[0].astype(jnp.bfloat16)
    grad_second = jnp.dot(act_first.T, gpre_second, preferred_element_type=jnp.float32)
    grad_bsecond = jnp.sum(gpre_second.astype(jnp.float32), axis=0)
    gact_first = jnp.dot(gpre_second, w_second.T, preferred_element_type=jnp.float32)
    gpre_first = first_back(gact_first)[0].astype(jnp.bfloat16)
    grad_first = jnp.dot(smooth_rows.T, gpre_first, preferred_element_type=jnp.float32)
    grad_bfirst = jnp.sum(gpre_first.astype(jnp.float32), axis=0)
    gsmooth = cot_rows.astype(jnp.float32) + jnp.dot(
        gpre_first, w_first.T, preferred_element_type=jnp.float32
    )
    local_grads = (grad_first, grad_bfirst, grad_second, grad_bsecond, grad_third)
    summed = lax.psum(
        (local_grads[0], local_grads[1], local_grads[2], local_grads[3], local_grads[4]),
        ("sample", "space"),
    )
    gdeparture = smoother_adjoint(gsmooth.reshape(field.shape), helm_coef).reshape(
        batch_here, cell_count, channels
    )
    slot_grads = jnp.zeros((batch_here, slot_total, channels), jnp.float32)
    for index, start in enumerate(range(0, cell_count, block_rows)):
        upper, lower = interp_parts[index]
        grad_upper, grad_lower = split_parts(gdeparture[:, start : start + block_rows])
        slot_grads = slot_grads + jnp.einsum(
            "cs,bch->bsh", upper, grad_upper, preferred_element_type=jnp.float32
        )
        slot_grads = slot_grads + jnp.einsum(
            "cs,bch->bsh", upper, grad_lower, preferred_element_type=jnp.float32
        )
        slot_grads = slot_grads + jnp.einsum(
            "cs,bch->bsh", lower, grad_upper, preferred_element_type=jnp.float32
        )
    slot_blocks = slot_grads.reshape(batch_here, offsets, slots_each, channels)
    field_grad = jnp.zeros((batch_here, cell_count, channels), jnp.float32)
    for offset in range(offsets):
        if offset == span_bands:
            back = slot_blocks[:, offset]
        else:
            back = passed_along(
                slot_blocks[:, offset].astype(jnp.bfloat16), "space", span_bands - offset
            ).astype(jnp.float32)
        back_upper, back_lower = split_parts(back)
        field_grad = field_grad + jnp.einsum(
            "sc,bsh->bch", selectors[offset], back_upper, preferred_element_type=jnp.float32
        )
        field_grad = field_grad + jnp.einsum(
            "sc,bsh->bch", selectors[offset], back_lower, preferred_element_type=jnp.float32
        )
    return (
        next_state,
        field_grad.reshape(field.shape),
        summed[0],
        summed[1],
        summed[2],
        summed[3],
        summed[4],
    )


def solution(mesh):
    placed = (
        P("sample", "space", None, None),
        P("space", None, None),
        P("space", None),
        P(None, "space", None),
        P(None, "space", None),
        P(),
        P(),
        P(),
        P(),
        P(),
        P(),
        P("sample", "space", None, None),
    )
    return jax.shard_map(
        body,
        mesh=mesh,
        in_specs=placed,
        out_specs=(
            P("sample", "space", None, None),
            P("sample", "space", None, None),
            P(),
            P(),
            P(),
            P(),
            P(),
        ),
        check_vma=False,
    )
```

profile of v0, /device:TPU:1, one launch (start us, length us, event | category | flops | bytes accessed | tf_op | source)
XLA Modules:
  0.0 467.3 jit_solution(14566426679829260820)
XLA Ops:
  7.2 1.4 fusion.239
  11.6 4.5 collective-permute-start.2
  17.8 1.3 collective-permute-start
  20.8 2.1 collective-permute-start.1
  25.1 4.3 collective-permute-start.3
  32.3 3.8 fusion.205
  36.1 3.2 fusion.115
  39.3 3.3 fusion.209
  42.7 3.2 fusion.116
  45.9 3.3 fusion.213
  49.3 3.2 fusion.117
  52.5 3.3 fusion.217
  55.9 3.4 fusion.118
  62.5 2.2 concatenate.142
  64.7 1.7 fusion.235
  66.5 4.8 %collective-permute-start.4 = (bf16[1,1,512,128]{2,1,3,0:T(2,128)(2,1)S(1)}, bf16[1,1,512,128]{2,1,3,0:T(2,128)(2,1)S(1)}, u32[]{:S(2)}, u32[]{:S(2)}) collective-permute-start(bf16[1,1,512,128]{2,1,3,0:T(2,128)(2,1)S(1)} %get-tuple-element.60), channel_id=1, source_target_pairs={{0,1},{1,2},{2,3},{3,4},{4,5},{5,6},{6,7},{7,8},{8,9},{9,10},{10,1... | collective-permute-start | bytes 393224 | tf_op jit(solution)/shard_map/ppermute | solution.py:17
  71.2 1.9 collective-permute-start.5
  74.5 4.4 collective-permute-done.5
  79.7 1.7 fusion.222
  81.8 1.9 collective-permute-start.6
  83.7 2.4 collective-permute-start.7
  87.0 4.4 collective-permute-done.7
  92.3 1.9 fusion.166
  95.1 1.4 multiply_convert_fusion
  98.9 1.6 convert_reduce_fusion
  100.5 1.6 fusion.201
  102.1 1.6 convert_reduce_fusion.1
  107.2 1.9 collective-permute-start.8
  109.1 2.4 collective-permute-start.9
  113.7 93.0 %all-reduce = (f32[256]{0:T(256)}, f32[256]{0:T(256)}) all-reduce(f32[256]{0:T(256)S(1)} %get-tuple-element.26, f32[256]{0:T(256)S(1)} %get-tuple-element.106), channel_id=1, replica_groups=mesh['sample'=4,'space'=64] {'sample','space'}, use_global_device_ids=true, to_apply=%region_2.3 | all-reduce | flops 512 | bytes 4096 | tf_op jit(solution)/shard_map/psum | solution.py:150
  206.9 1.9 maximum_convert_fusion.2
  208.8 1.6 fusion.219
  210.8 1.9 collective-permute-start.10
  212.8 2.9 collective-permute-start.11
  216.5 4.4 collective-permute-done.11
  221.7 1.5 fusion.154
  223.9 3.1 fusion.196
  227.0 3.2 convolution_add_fusion.10
  230.2 3.5 convolution_add_fusion.9
  233.7 3.2 convolution_add_fusion.8
  236.9 3.2 convolution_add_fusion.7
  240.1 3.3 convolution_add_fusion.6
  243.3 3.6 convolution_add_fusion.5
  246.9 3.2 convolution_add_fusion.4
  250.1 3.3 convolution_add_fusion.3
  253.4 3.2 convolution_add_fusion.2
  256.6 3.4 convolution_add_fusion.1
  260.0 3.3 fusion.39
  263.8 3.3 collective-permute-start.12
  267.2 1.3 collective-permute-start.15
  268.5 1.9 collective-permute-start.14
  270.4 3.6 collective-permute-start.13
  278.5 1.2 fusion.5
  279.7 1.3 fusion.67
  281.0 1.3 fusion.58
  282.3 1.2 fusion.26
  283.6 1.3 fusion.52
  284.9 1.2 fusion.33
  286.2 1.3 fusion.46
  287.4 1.3 copy.28
  288.7 166.8 %all-reduce.4.cloned.1.call-done = (f32[128,256]{1,0:T(8,128)}, f32[256,256]{1,0:T(8,128)}, f32[256,128]{1,0:T(8,128)}) async-done(((f32[128,256]{1,0:T(8,128)}, f32[256,256]{1,0:T(8,128)}, f32[256,128]{1,0:T(8,128)}), (f32[128,256]{1,0:T(8,128)}, f32[256,256]{1,0:T(8,128)}, f32[256,128]{1,0:T(8,128)})) %all-reduce.4.cloned.1.call-update) | async-done | bytes 524304 | tf_op jit(solution)/shard_map/psum | solution.py:150
  455.5 1.6 copy.38
  457.1 1.7 copy.39
  458.7 1.6 copy.40
  (134 shorter events, 35.3 us)
Async XLA Ops:
  7.2 2.9 copy-start
  7.2 448.3 %all-reduce.4.cloned.1.call-start = ((), (), s32[]{:S(2)}) async-start(), calls=%async_computation | async-start | bytes 1048576 | tf_op jit(solution)/shard_map/psum | solution.py:150
  9.3 0.8 copy-start.20
  10.1 0.6 copy-start.10
  10.1 7.7 %copy-start.14 = (s32[1,1,512]{2,0,1:T(1,128)}, s32[1,1,512]{2,0,1:T(1,128)S(1)}, u32[]{:S(2)}) copy-start(s32[1,1,512]{2,0,1:T(1,128)S(1)} %get-tuple-element.97) | copy-start | bytes 6148
  10.1 9.7 %copy-start.17 = (s32[1,1,512]{2,0,1:T(1,128)}, s32[1,1,512]{2,0,1:T(1,128)S(1)}, u32[]{:S(2)}) copy-start(s32[1,1,512]{2,0,1:T(1,128)S(1)} %get-tuple-element.96) | copy-start | bytes 6148
  10.1 13.5 %copy-start.8 = (s32[1,1,512]{2,0,1:T(1,128)}, s32[1,1,512]{2,0,1:T(1,128)S(1)}, u32[]{:S(2)}) copy-start(s32[1,1,512]{2,0,1:T(1,128)S(1)} %get-tuple-element.94) | copy-start | bytes 6148
  10.1 20.1 %copy-start.12 = (s32[1,1,512]{2,0,1:T(1,128)}, s32[1,1,512]{2,0,1:T(1,128)S(1)}, u32[]{:S(2)}) copy-start(s32[1,1,512]{2,0,1:T(1,128)S(1)} %get-tuple-element.95) | copy-start | bytes 6148
  11.6 19.6 %collective-permute-start.2 = (bf16[1,512,128]{2,1,0:T(8,128)(2,1)S(1)}, bf16[1,512,128]{2,1,0:T(8,128)(2,1)S(1)}, u32[]{:S(2)}, u32[]{:S(2)}) collective-permute-start(bf16[1,512,128]{2,1,0:T(8,128)(2,1)S(1)} %fusion.146), channel_id=1, source_target_pairs={{0,1},{1,2},{2,3},{3,4},{4,5},{5,6},{6,7},{7,8},{8,9},{9,10},{10,1... | collective-permute-start | bytes 393224 | tf_op jit(solution)/shard_map/ppermute | solution.py:29
  16.8 3.9 copy-start.24
  17.8 12.4 %collective-permute-start = (bf16[1,512,128]{2,1,0:T(8,128)(2,1)S(1)}, bf16[1,512,128]{2,1,0:T(8,128)(2,1)S(1)}, u32[]{:S(2)}, u32[]{:S(2)}) collective-permute-start(bf16[1,512,128]{2,1,0:T(8,128)(2,1)S(1)} %fusion.134), channel_id=1, source_target_pairs={{2,0},{3,1},{4,2},{5,3},{6,4},{7,5},{8,6},{9,7},{10,8},{11,9},{12,... | collective-permute-start | bytes 393224 | tf_op jit(solution)/shard_map/ppermute | solution.py:29
  19.8 3.1 copy-start.30
  20.8 8.6 %copy-start.6 = (s32[4,4,512]{2,1,0:T(4,128)S(1)}, s32[4,4,512]{2,1,0:T(4,128)}, u32[]{:S(2)}) copy-start(s32[4,4,512]{2,1,0:T(4,128)} %param.15) | copy-start | bytes 98308
  20.8 8.6 %copy-start.7 = (f32[4,4,512]{2,1,0:T(4,128)S(1)}, f32[4,4,512]{2,1,0:T(4,128)}, u32[]{:S(2)}) copy-start(f32[4,4,512]{2,1,0:T(4,128)} %param.16) | copy-start | bytes 98308
  20.8 8.7 %copy-start.16 = (f32[128]{0:T(128)S(1)}, f32[128]{0:T(128)}, u32[]{:S(2)}) copy-start(f32[128]{0:T(128)} %param.17) | copy-start | bytes 1540
  20.8 9.4 %collective-permute-start.1 = (bf16[1,512,128]{2,1,0:T(8,128)(2,1)S(1)}, bf16[1,512,128]{2,1,0:T(8,128)(2,1)S(1)}, u32[]{:S(2)}, u32[]{:S(2)}) collective-permute-start(bf16[1,512,128]{2,1,0:T(8,128)(2,1)S(1)} %fusion.137), channel_id=1, source_target_pairs={{1,0},{2,1},{3,2},{4,3},{5,4},{6,5},{7,6},{8,7},{9,8},{10,9},{11,1... | collective-permute-start | bytes 393224 | tf_op jit(solution)/shard_map/ppermute | solution.py:29
  23.5 0.6 copy-start.22
  25.1 7.2 %collective-permute-start.3 = (bf16[1,512,128]{2,1,0:T(8,128)(2,1)S(1)}, bf16[1,512,128]{2,1,0:T(8,128)(2,1)S(1)}, u32[]{:S(2)}, u32[]{:S(2)}) collective-permute-start(bf16[1,512,128]{2,1,0:T(8,128)(2,1)S(1)} %fusion.149), channel_id=1, source_target_pairs={{0,2},{1,3},{2,4},{3,5},{4,6},{5,7},{6,8},{7,9},{8,10},{9,11},{10,... | collective-permute-start | bytes 393224 | tf_op jit(solution)/shard_map/ppermute | solution.py:29
  30.2 2.1 copy-start.26
  64.7 14.2 %copy-start.3 = (bf16[1,4,512,128]{2,1,3,0:T(4,128)(2,1)S(1)}, bf16[1,4,512,128]{2,1,3,0:T(4,128)(2,1)}, u32[]{:S(2)}) copy-start(bf16[1,4,512,128]{2,1,3,0:T(4,128)(2,1)} %concatenate.142) | copy-start | bytes 1572868
  66.5 8.1 %collective-permute-start.4 = (bf16[1,1,512,128]{2,1,3,0:T(2,128)(2,1)S(1)}, bf16[1,1,512,128]{2,1,3,0:T(2,128)(2,1)S(1)}, u32[]{:S(2)}, u32[]{:S(2)}) collective-permute-start(bf16[1,1,512,128]{2,1,3,0:T(2,128)(2,1)S(1)} %get-tuple-element.60), channel_id=1, source_target_pairs={{0,1},{1,2},{2,3},{3,4},{4,5},{5,6},{6,7},{7,8},{8,9},{9,10},{10,1... | collective-permute-start | bytes 393224 | tf_op jit(solution)/shard_map/ppermute | solution.py:17
  71.2 7.7 %collective-permute-start.5 = (bf16[1,1,512,128]{2,1,3,0:T(2,128)(2,1)S(1)}, bf16[1,1,512,128]{2,1,3,0:T(2,128)(2,1)S(1)}, u32[]{:S(2)}, u32[]{:S(2)}) collective-permute-start(bf16[1,1,512,128]{2,1,3,0:T(2,128)(2,1)S(1)} %get-tuple-element.61), channel_id=1, source_target_pairs={{1,0},{2,1},{3,2},{4,3},{5,4},{6,5},{7,6},{8,7},{9,8},{10,9},{11,1... | collective-permute-start | bytes 393224 | tf_op jit(solution)/shard_map/ppermute | solution.py:19
  81.8 5.2 %collective-permute-start.6 = (bf16[1,1,512,128]{2,1,3,0:T(2,128)(2,1)S(1)}, bf16[1,1,512,128]{2,1,3,0:T(2,128)(2,1)S(1)}, u32[]{:S(2)}, u32[]{:S(2)}) collective-permute-start(bf16[1,1,512,128]{2,1,3,0:T(2,128)(2,1)S(1)} %get-tuple-element.58), channel_id=1, source_target_pairs={{0,1},{1,2},{2,3},{3,4},{4,5},{5,6},{6,7},{7,8},{8,9},{9,10},{10,1... | collective-permute-start | bytes 393224 | tf_op jit(solution)/shard_map/ppermute | solution.py:17
  83.7 7.7 %collective-permute-start.7 = (bf16[1,1,512,128]{2,1,3,0:T(2,128)(2,1)S(1)}, bf16[1,1,512,128]{2,1,3,0:T(2,128)(2,1)S(1)}, u32[]{:S(2)}, u32[]{:S(2)}) collective-permute-start(bf16[1,1,512,128]{2,1,3,0:T(2,128)(2,1)S(1)} %get-tuple-element.59), channel_id=1, source_target_pairs={{1,0},{2,1},{3,2},{4,3},{5,4},{6,5},{7,6},{8,7},{9,8},{10,9},{11,1... | collective-permute-start | bytes 393224 | tf_op jit(solution)/shard_map/ppermute | solution.py:19
  92.2 2.4 copy-start.4
  92.3 2.4 copy-start.19
  94.2 0.9 copy-start.28
  94.2 0.9 copy-start.29
  95.1 1.4 copy-start.2
  95.1 2.6 copy-start.5
  107.2 99.7 %collective-permute-start.8 = (bf16[1,1,512,128]{2,1,3,0:T(2,128)(2,1)}, bf16[1,1,512,128]{2,1,3,0:T(2,128)(2,1)S(1)}, u32[]{:S(2)}, u32[]{:S(2)}) collective-permute-start(bf16[1,1,512,128]{2,1,3,0:T(2,128)(2,1)} %get-tuple-element.56), channel_id=1, source_target_pairs={{0,1},{1,2},{2,3},{3,4},{4,5},{5,6},{6,7},{7,8},{8,9},{9,10},{10,1... | collective-permute-start | bytes 393224 | tf_op jit(solution)/shard_map/ppermute | solution.py:17
  109.1 97.8 %collective-permute-start.9 = (bf16[1,1,512,128]{2,1,3,0:T(2,128)(2,1)}, bf16[1,1,512,128]{2,1,3,0:T(2,128)(2,1)}, u32[]{:S(2)}, u32[]{:S(2)}) collective-permute-start(bf16[1,1,512,128]{2,1,3,0:T(2,128)(2,1)} %get-tuple-element.57), channel_id=1, source_target_pairs={{1,0},{2,1},{3,2},{4,3},{5,4},{6,5},{7,6},{8,7},{9,8},{10,9},{11,1... | collective-permute-start | bytes 393224 | tf_op jit(solution)/shard_map/ppermute | solution.py:19
  210.8 5.6 %collective-permute-start.10 = (bf16[1,1,512,128]{2,1,3,0:T(2,128)(2,1)S(1)}, bf16[1,1,512,128]{2,1,3,0:T(2,128)(2,1)S(1)}, u32[]{:S(2)}, u32[]{:S(2)}) collective-permute-start(bf16[1,1,512,128]{2,1,3,0:T(2,128)(2,1)S(1)} %get-tuple-element.54), channel_id=1, source_target_pairs={{0,1},{1,2},{2,3},{3,4},{4,5},{5,6},{6,7},{7,8},{8,9},{9,10},{10,1... | collective-permute-start | bytes 393224 | tf_op jit(solution)/shard_map/ppermute | solution.py:17
  212.8 8.1 %collective-permute-start.11 = (bf16[1,1,512,128]{2,1,3,0:T(2,128)(2,1)S(1)}, bf16[1,1,512,128]{2,1,3,0:T(2,128)(2,1)S(1)}, u32[]{:S(2)}, u32[]{:S(2)}) collective-permute-start(bf16[1,1,512,128]{2,1,3,0:T(2,128)(2,1)S(1)} %get-tuple-element.55), channel_id=1, source_target_pairs={{1,0},{2,1},{3,2},{4,3},{5,4},{6,5},{7,6},{8,7},{9,8},{10,9},{11,1... | collective-permute-start | bytes 393224 | tf_op jit(solution)/shard_map/ppermute | solution.py:19
  263.7 10.4 %copy-start.13 = (s32[1,1,512]{2,0,1:T(1,128)S(1)}, s32[1,1,512]{2,0,1:T(1,128)}, u32[]{:S(2)}) copy-start(s32[1,1,512]{2,0,1:T(1,128)} %copy-done.12) | copy-start | bytes 6148
  263.7 10.4 %copy-start.27 = (pred[512]{0:T(512)(128)(4,1)S(1)}, pred[512]{0:T(512)(128)(4,1)}, u32[]{:S(2)}) copy-start(pred[512]{0:T(512)(128)(4,1)} %copy-done.26) | copy-start | bytes 1540
  263.8 12.2 %copy-start.18 = (s32[1,1,512]{2,0,1:T(1,128)S(1)}, s32[1,1,512]{2,0,1:T(1,128)}, u32[]{:S(2)}) copy-start(s32[1,1,512]{2,0,1:T(1,128)} %copy-done.17) | copy-start | bytes 6148
  263.8 12.2 %copy-start.31 = (pred[512]{0:T(512)(128)(4,1)S(1)}, pred[512]{0:T(512)(128)(4,1)}, u32[]{:S(2)}) copy-start(pred[512]{0:T(512)(128)(4,1)} %copy-done.30) | copy-start | bytes 1540
  263.8 14.6 %collective-permute-start.12 = (bf16[1,512,128]{2,1,0:T(8,128)(2,1)S(1)}, bf16[1,512,128]{2,1,0:T(8,128)(2,1)S(1)}, u32[]{:S(2)}, u32[]{:S(2)}) collective-permute-start(bf16[1,512,128]{2,1,0:T(8,128)(2,1)S(1)} %get-tuple-element.50), channel_id=1, source_target_pairs={{0,2},{1,3},{2,4},{3,5},{4,6},{5,7},{6,8},{7,9},{8,10},{9,11},{10,... | collective-permute-start | bytes 393224 | tf_op jit(solution)/shard_map/ppermute | solution.py:29
  267.2 17.7 %collective-permute-start.15 = (bf16[1,512,128]{2,1,0:T(8,128)(2,1)S(1)}, bf16[1,512,128]{2,1,0:T(8,128)(2,1)S(1)}, u32[]{:S(2)}, u32[]{:S(2)}) collective-permute-start(bf16[1,512,128]{2,1,0:T(8,128)(2,1)S(1)} %get-tuple-element.51), channel_id=1, source_target_pairs={{2,0},{3,1},{4,2},{5,3},{6,4},{7,5},{8,6},{9,7},{10,8},{11,9},{12,... | collective-permute-start | bytes 393224 | tf_op jit(solution)/shard_map/ppermute | solution.py:29
  268.5 13.8 %collective-permute-start.14 = (bf16[1,512,128]{2,1,0:T(8,128)(2,1)S(1)}, bf16[1,512,128]{2,1,0:T(8,128)(2,1)S(1)}, u32[]{:S(2)}, u32[]{:S(2)}) collective-permute-start(bf16[1,512,128]{2,1,0:T(8,128)(2,1)S(1)} %get-tuple-element.52), channel_id=1, source_target_pairs={{1,0},{2,1},{3,2},{4,3},{5,4},{6,5},{7,6},{8,7},{9,8},{10,9},{11,1... | collective-permute-start | bytes 393224 | tf_op jit(solution)/shard_map/ppermute | solution.py:29
  270.4 5.6 %collective-permute-start.13 = (bf16[1,512,128]{2,1,0:T(8,128)(2,1)S(1)}, bf16[1,512,128]{2,1,0:T(8,128)(2,1)S(1)}, u32[]{:S(2)}, u32[]{:S(2)}) collective-permute-start(bf16[1,512,128]{2,1,0:T(8,128)(2,1)S(1)} %get-tuple-element.53), channel_id=1, source_target_pairs={{0,1},{1,2},{2,3},{3,4},{4,5},{5,6},{6,7},{7,8},{8,9},{9,10},{10,1... | collective-permute-start | bytes 393224 | tf_op jit(solution)/shard_map/ppermute | solution.py:29
  275.3 3.2 copy-start.15
  275.3 3.2 copy-start.25
  281.0 1.3 copy-start.11
  281.0 1.3 copy-start.21
  283.6 1.3 copy-start.9
  283.6 1.3 copy-start.23
  286.1 174.2 %copy-start.1 = (bf16[1,4,512,128]{3,2,1,0:T(8,128)(2,1)S(1)}, bf16[1,4,512,128]{3,2,1,0:T(8,128)(2,1)}, u32[]{:S(2)}) copy-start(bf16[1,4,512,128]{3,2,1,0:T(8,128)(2,1)} %param.12) | copy-start | bytes 1572868
Sparse Core Ops, SparseCore 0:
  206.8 248.6 all-reduce.3
where the time goes:
time: 473 us; the launch traced here: 467 us
  waiting for transfers between devices  183 us (39%)
  matrix products  94 us (20%)
  blocking collectives  93 us (20%)
  starting transfers between devices  42.5 us (9%)
  local copies, waits for them, and re-layouts  22.1 us (5%)
  other arithmetic  17.8 us (4%)
  between operations  15.2 us (3%)
    psum x1, waiting for transfers between devices, body(): lax.psum((local_grads[0], local_grads[1], local_grads[2], local_grads[3],...  167 us
    psum x1, blocking collectives, body(): lax.psum((local_grads[0], local_grads[1], local_grads[2], local_grads[3],...  93 us
    ppermute x8, starting transfers between devices, passed_along(): return lax.ppermute(shard, axis, pairs)  22.3 us
    dot_general x4, matrix products, body(): jnp.einsum('cs,bsh->bch', lower, received, preferred_element_type=jnp.flo...  13.8 us
    dot_general x4, matrix products, body(): jnp.einsum('cs,bch->bsh', lower, grad_upper, preferred_element_type=jnp.f...  13.3 us
    ppermute x4, waiting for transfers between devices, extended(): lax.ppermute(head, axis, [((i + 1) % count, i) for i in range(ends)])  13.2 us
    dot_general x4, matrix products, body(): jnp.einsum('cs,bsh->bch', upper, received, preferred_element_type=jnp.flo...  13.1 us
    dot_general x4, matrix products, body(): jnp.einsum('cs,bch->bsh', upper, grad_upper, preferred_element_type=jnp.f...  13 us
  transfers between devices with their start and end apart: 17, of which 7 were waited for; matrix products, arithmetic and copies ran while one was open for 15% of the time, Pallas kernels for 0%

commit v1 on v0

v1 whole, which is shorter than its diff:
```python
import functools
import math

import jax
import jax.numpy as jnp
from jax import lax
from jax.experimental import pallas as pl
from jax.experimental.pallas import tpu as pltpu
from jax.sharding import Mesh
from jax.sharding import PartitionSpec as P

F32 = jnp.float32
BF16 = jnp.bfloat16
SPACE = ("z", "x", "core")
GELU_SCALE = math.sqrt(2.0 / math.pi)
GELU_CUBE = 0.044715
PART_ROWS = 40

VMEM = pl.BlockSpec(memory_space=pltpu.VMEM)
SMEM = pl.BlockSpec(memory_space=pltpu.SMEM)


def dot(left, right, left_dim=1, right_dim=0):
    return lax.dot_general(
        left,
        right,
        (((left_dim,), (right_dim,)), ((), ())),
        preferred_element_type=F32,
    )


def call(kernel, outs, ins, scratch=(), flops=0, name=None):
    nbytes = sum(math.prod(o.shape) * o.dtype.itemsize for o in outs)
    return pl.pallas_call(
        kernel,
        out_shape=outs,
        in_specs=ins,
        out_specs=[VMEM] * len(outs),
        scratch_shapes=list(scratch),
        compiler_params=pltpu.CompilerParams(vmem_limit_bytes=40 * 1024 * 1024),
        cost_estimate=pl.CostEstimate(
            flops=flops, bytes_accessed=2 * nbytes, transcendentals=0
        ),
        name=name,
    )


def quad_boxes(rows_ref, count_ref, offsets, slots):
    quads = slots // 4
    rows = rows_ref[...]
    pick = (
        lax.broadcasted_iota(jnp.int32, (slots, quads), 0)
        == 4 * lax.broadcasted_iota(jnp.int32, (slots, quads), 1)
    ).astype(F32).astype(BF16)
    high = (rows >> 3).astype(F32).astype(BF16)
    low = (rows & 7).astype(F32).astype(BF16)
    cells = (dot(high, pick) * 8.0 + dot(low, pick)).astype(jnp.int32)
    offset_at = lax.broadcasted_iota(jnp.int32, cells.shape, 0)
    live = jnp.zeros(cells.shape, jnp.int32)
    for offset in range(offsets):
        live = jnp.where(offset_at == offset, count_ref[0, offset], live)
    slot_at = 4 * lax.broadcasted_iota(jnp.int32, cells.shape, 1)
    return jnp.where(slot_at < live, cells, -1)


def pack_kernel(offsets, field_ref, rows_ref, count_ref, *refs):
    outs, (pair, select) = refs[:offsets], refs[offsets:]
    band_rows, lon, ch = field_ref.shape
    slots = rows_ref.shape[1]
    quads = slots // 4
    boxes = (band_rows - 1) * lon
    cells = quad_boxes(rows_ref, count_ref, offsets, slots)
    columns = cells.astype(F32).T.astype(jnp.int32)
    box_at = lax.broadcasted_iota(jnp.int32, (quads, boxes), 1)
    for offset in range(offsets):
        select[offset * quads : (offset + 1) * quads] = (
            (box_at == columns[:, offset : offset + 1]).astype(F32).astype(BF16)
        )
    for row in range(band_rows):
        line = field_ref[row]
        pair[row * lon : (row + 1) * lon, :ch] = line
        pair[row * lon : (row + 1) * lon, ch:] = pltpu.roll(
            line.astype(F32), lon - 1, 0
        ).astype(BF16)
    for part in range(2):
        picked = dot(select[...], pair[part * lon : part * lon + boxes]).astype(BF16)
        for offset in range(offsets):
            outs[offset][:, part * 2 * ch : (part + 1) * 2 * ch] = picked[
                offset * quads : (offset + 1) * quads
            ]


def tap_columns(weight_ref, stack):
    taps, band_rows, _ = weight_ref.shape
    for tap in range(taps):
        stack[tap * band_rows : (tap + 1) * band_rows] = weight_ref[tap]
    return stack[...].T


def interp_kernel(offsets, *refs):
    blocks = refs[:offsets]
    slot_ref, weight_ref, dep_ref, up_ref, down_ref, table, stack, slot_stack = refs[offsets:]
    taps, band_rows, lon = weight_ref.shape
    quads, wide = blocks[0].shape
    ch = wide // taps
    weights = tap_columns(weight_ref, stack)
    slot_stack[...] = jnp.zeros_like(slot_stack)
    slot_stack[:band_rows] = (slot_ref[0] >> 2).astype(F32)
    quad_columns = slot_stack[...].T.astype(jnp.int32)
    for offset in range(offsets):
        table[offset * quads : (offset + 1) * quads] = blocks[offset][...]
    quad_at = lax.broadcasted_iota(jnp.int32, (lon, offsets * quads), 1)
    for row in range(band_rows):
        hit = (quad_at == quad_columns[:, row : row + 1]).astype(F32).astype(BF16)
        tapped = dot(hit, table[...])
        line = jnp.zeros((lon, ch), F32)
        for tap in range(taps):
            at = tap * band_rows + row
            line = line + weights[:, at : at + 1] * tapped[:, tap * ch : (tap + 1) * ch]
        dep_ref[row] = line
        if row < 2:
            up_ref[row] = line.astype(BF16)
        if row >= band_rows - 2:
            down_ref[row - band_rows + 2] = line.astype(BF16)


def lon_sum(line):
    lon = line.shape[0]
    return pltpu.roll(line, 1, 0) + pltpu.roll(line, lon - 1, 0)


def gelu_parts(pre):
    square = pre * pre
    curve = jnp.tanh(pre * (GELU_SCALE + (GELU_SCALE * GELU_CUBE) * square))
    half = 0.5 + 0.5 * curve
    slope = half + (0.5 * pre) * (1.0 - curve * curve) * (
        GELU_SCALE + (3.0 * GELU_SCALE * GELU_CUBE) * square
    )
    return pre * half, slope


def mlp_kernel(
    dep_ref,
    before_ref,
    after_ref,
    cot_ref,
    place_ref,
    helm_ref,
    w1_ref,
    b1_ref,
    w2_ref,
    b2_ref,
    w3_ref,
    next_ref,
    scaled_ref,
    up_ref,
    down_ref,
    keep_ref,
    give_ref,
    once,
    smooth,
    g1,
    gb1,
    g2,
    gb2,
    g3,
):
    band_rows, lon, ch = dep_ref.shape
    helm = helm_ref[...]
    inverse = 1.0 / (1.0 + 4.0 * helm)

    def departure(row):
        if row < 0:
            return before_ref[row + 2].astype(F32)
        if row >= band_rows:
            return after_ref[row - band_rows].astype(F32)
        return dep_ref[row]

    first = jnp.where(place_ref[0] == 0, 0.0, 1.0)
    last = jnp.where(place_ref[0] == place_ref[1] - 1, 0.0, 1.0)
    ahead = departure(-2), departure(-1)
    if True:
        ahead = ahead[0] * first, ahead[1] * first
    behind = departure(band_rows) * last, departure(band_rows + 1) * last
    lines = {-2: ahead[0], -1: ahead[1], band_rows: behind[0], band_rows + 1: behind[1]}
    for row in range(-1, band_rows + 1):
        mid, above, below = (
            lines[r] if r in lines else departure(r) for r in (row, row - 1, row + 1)
        )
        value = (mid + helm * (above + below + lon_sum(mid))) * inverse
        if row < 0:
            value = value * first
        if row >= band_rows:
            value = value * last
        once[row + 1] = value
    for row in range(band_rows):
        value = (
            dep_ref[row] + helm * (once[row] + once[row + 2] + lon_sum(once[row + 1]))
        ) * inverse
        smooth[row] = value.astype(BF16)
    for total in (g1, gb1, g2, gb2, g3):
        total[...] = jnp.zeros_like(total)

    def one_row(row, carry):
        rows = smooth[row]
        cot = cot_ref[row]
        act, slope_first = gelu_parts(dot(rows, w1_ref[...]) + b1_ref[...])
        act_first = act.astype(BF16)
        act, slope_second = gelu_parts(dot(act_first, w2_ref[...]) + b2_ref[...])
        act_second = act.astype(BF16)
        next_ref[row] = (rows.astype(F32) + dot(act_second, w3_ref[...])).astype(BF16)
        g3[...] += dot(act_second, cot, 0, 0)
        gpre = dot(cot, w3_ref[...], 1, 1) * slope_second
        gpre_second = gpre.astype(BF16)
        gb2[...] += jnp.sum(gpre_second.astype(F32), axis=0, keepdims=True)
        g2[...] += dot(act_first, gpre_second, 0, 0)
        gpre = dot(gpre_second, w2_ref[...], 1, 1) * slope_first
        gpre_first = gpre.astype(BF16)
        gb1[...] += jnp.sum(gpre_first.astype(F32), axis=0, keepdims=True)
        g1[...] += dot(rows, gpre_first, 0, 0)
        gsmooth = cot.astype(F32) + dot(gpre_first, w1_ref[...], 1, 1)
        scaled_ref[row] = gsmooth * inverse
        return carry

    lax.fori_loop(0, band_rows, one_row, 0)
    for row in range(2):
        up_ref[row] = scaled_ref[row].astype(BF16)
        down_ref[row] = scaled_ref[band_rows - 2 + row].astype(BF16)
    half = keep_ref.shape[0]
    low = place_ref[2] == 0
    hid = g1.shape[1]

    def place(at, zero, one):
        rows = zero.shape[0]
        keep_ref[at : at + rows] = jnp.where(low, zero, one).astype(BF16)
        give_ref[at : at + rows] = jnp.where(low, one, zero).astype(BF16)

    place(0, g1[:, :ch], g2[:ch, :ch])
    place(ch, g1[:, ch:], g2[ch:, :ch])
    place(2 * ch, g3[:ch], g2[:ch, ch:])
    place(3 * ch, g3[ch:], g2[ch:, ch:])
    row_at = lax.broadcasted_iota(jnp.int32, (half - 4 * ch, ch), 0)

    def bias(ref):
        return jnp.where(
            row_at == 0, ref[:, :ch], jnp.where(row_at == 1, ref[:, ch:], 0.0)
        )

    place(4 * ch, bias(gb1), bias(gb2))


def adjoint_kernel(
    offsets,
    scaled_ref,
    before_ref,
    after_ref,
    place_ref,
    helm_ref,
    slot_ref,
    weight_ref,
    *refs,
):
    outs, (once, spread, hit, stack) = refs[:offsets], refs[offsets:]
    band_rows, lon, ch = scaled_ref.shape
    taps = weight_ref.shape[0]
    quads = outs[0].shape[0]
    helm = helm_ref[...]
    inverse = 1.0 / (1.0 + 4.0 * helm)
    first = jnp.where(place_ref[0] == 0, 0.0, 1.0)
    last = jnp.where(place_ref[0] == place_ref[1] - 1, 0.0, 1.0)
    weights = tap_columns(weight_ref, stack)
    quad_lanes = slot_ref[0] >> 2
    quad_at = lax.broadcasted_iota(jnp.int32, (offsets * quads, lon), 0)
    for row in range(band_rows):
        hit[:, row * lon : (row + 1) * lon] = (
            (quad_at == quad_lanes[row : row + 1]).astype(F32).astype(BF16)
        )

    def scaled(row):
        if row < 0:
            return before_ref[row + 2].astype(F32) * first
        if row >= band_rows:
            return after_ref[row - band_rows].astype(F32) * last
        return scaled_ref[row]

    for row in range(-1, band_rows + 1):
        value = (helm * inverse) * (scaled(row - 1) + scaled(row + 1) + lon_sum(scaled(row)))
        if row < 0:
            value = value * first
        if row >= band_rows:
            value = value * last
        once[row + 1] = value
    for row in range(band_rows):
        value = (
            scaled_ref[row]
            + once[row + 1]
            + helm * (once[row] + once[row + 2] + lon_sum(once[row + 1]))
        )
        for tap in range(taps):
            at = tap * band_rows + row
            spread[row * lon : (row + 1) * lon, tap * ch : (tap + 1) * ch] = (
                weights[:, at : at + 1] * value
            ).astype(BF16)
    slot_grads = dot(hit[...], spread[...]).astype(BF16)
    for offset in range(offsets):
        outs[offset][...] = slot_grads[offset * quads : (offset + 1) * quads]


def scatter_kernel(offsets, rows_ref, count_ref, *refs):
    blocks = refs[:offsets]
    out_ref, table, hit = refs[offsets:]
    band_rows, lon, ch = out_ref.shape
    slots = rows_ref.shape[1]
    quads = slots // 4
    boxes = (band_rows - 1) * lon
    cells = quad_boxes(rows_ref, count_ref, offsets, slots)
    box_at = lax.broadcasted_iota(jnp.int32, (boxes, quads), 0)
    for offset in range(offsets):
        table[offset * quads : (offset + 1) * quads] = blocks[offset][...]
        hit[:, offset * quads : (offset + 1) * quads] = (
            (box_at == cells[offset : offset + 1]).astype(F32).astype(BF16)
        )
    for row in range(band_rows):
        here = jnp.zeros((lon, ch), F32)
        right = jnp.zeros((lon, ch), F32)
        if row < band_rows - 1:
            both = dot(hit[row * lon : (row + 1) * lon], table[:, : 2 * ch])
            here = here + both[:, :ch]
            right = right + both[:, ch:]
        if row > 0:
            both = dot(hit[(row - 1) * lon : row * lon], table[:, 2 * ch :])
            here = here + both[:, :ch]
            right = right + both[:, ch:]
        out_ref[row] = here + pltpu.roll(right, 1, 0)


def add_kernel(left_ref, right_ref, out_ref):
    out_ref[...] = (left_ref[...].astype(F32) + right_ref[...].astype(F32)).astype(BF16)


def sum_kernel(copies, parts_ref, out_ref):
    total = parts_ref[0].astype(F32)
    for part in range(1, parts_ref.shape[0]):
        total = total + parts_ref[part].astype(F32)
    total = total.astype(BF16)
    for copy in range(copies):
        out_ref[copy] = total


def unpack_kernel(mine_ref, other_ref, place_ref, g1, gb1, g2, gb2, g3):
    ch, hid = g1.shape
    low = place_ref[2] == 0

    def halves(at, rows):
        mine = mine_ref[at : at + rows].astype(F32)
        other = other_ref[at : at + rows].astype(F32)
        return jnp.where(low, mine, other), jnp.where(low, other, mine)

    zero, one = halves(0, ch)
    g1[:, :ch], g2[:ch, :ch] = zero, one
    zero, one = halves(ch, ch)
    g1[:, ch:], g2[ch:, :ch] = zero, one
    zero, one = halves(2 * ch, ch)
    g3[:ch], g2[:ch, ch:] = zero, one
    zero, one = halves(3 * ch, ch)
    g3[ch:], g2[ch:, ch:] = zero, one
    zero, one = halves(4 * ch, 8)
    gb1[:, :ch], gb1[:, ch:] = zero[:1], zero[1:2]
    gb2[:, :ch], gb2[:, ch:] = one[:1], one[1:2]


def shifted(block, by, count):
    return lax.ppermute(block, SPACE, [(i, (i + by) % count) for i in range(count)])


def body(
    field,
    send_rows,
    send_count,
    dep_slot,
    dep_weight,
    helm_coef,
    w_first,
    b_first,
    w_second,
    b_second,
    w_third,
    cotangent,
):
    _, band_rows, lon, ch = field.shape
    hid = w_first.shape[1]
    offsets, slots = send_rows.shape[1:]
    taps = dep_slot.shape[0]
    reach = (offsets - 1) // 2
    quads = slots // 4
    bands = lax.axis_size(SPACE)
    shape = jax.ShapeDtypeStruct
    core = lax.axis_index("core").astype(jnp.int32)
    place = jnp.stack(
        [lax.axis_index(SPACE).astype(jnp.int32), jnp.int32(bands), core]
    )
    rows8 = jnp.pad(send_rows[0], ((0, 8 - offsets), (0, 0)))
    helm = helm_coef.reshape(1, ch)
    block = shape((quads, taps * ch), BF16)
    edge = shape((2, lon, ch), BF16)

    packed = call(
        functools.partial(pack_kernel, offsets),
        [block] * offsets,
        [VMEM, VMEM, SMEM],
        [
            pltpu.VMEM((band_rows * lon, 2 * ch), BF16),
            pltpu.VMEM((offsets * quads, (band_rows - 1) * lon), BF16),
        ],
        name="pack",
    )(field[0], rows8, send_count)
    received = [
        packed[e] if e == reach else shifted(packed[e], e - reach, bands)
        for e in range(offsets)
    ]
    departure, up, down = call(
        functools.partial(interp_kernel, offsets),
        [shape((band_rows, lon, ch), F32), edge, edge],
        [VMEM] * (offsets + 2),
        [
            pltpu.VMEM((offsets * quads, taps * ch), BF16),
            pltpu.VMEM((taps * band_rows, lon), F32),
            pltpu.VMEM((8, lon), F32),
        ],
        name="interp",
    )(*received, dep_slot, dep_weight)
    before = shifted(down, 1, bands)
    after = shifted(up, -1, bands)
    half = shape((16 * PART_ROWS, ch), BF16)
    next_state, scaled, up, down, keep, give = call(
        mlp_kernel,
        [
            shape((band_rows, lon, ch), BF16),
            shape((band_rows, lon, ch), F32),
            edge,
            edge,
            half,
            half,
        ],
        [VMEM] * 4 + [SMEM] + [VMEM] * 6,
        [
            pltpu.VMEM((band_rows + 2, lon, ch), F32),
            pltpu.VMEM((band_rows, lon, ch), BF16),
            pltpu.VMEM((ch, hid), F32),
            pltpu.VMEM((1, hid), F32),
            pltpu.VMEM((hid, hid), F32),
            pltpu.VMEM((1, hid), F32),
            pltpu.VMEM((hid, ch), F32),
        ],
        name="smooth_mlp",
    )(
        departure,
        before,
        after,
        cotangent[0],
        place,
        helm,
        w_first,
        b_first.reshape(1, hid),
        w_second,
        b_second.reshape(1, hid),
        w_third,
    )
    before = shifted(down, 1, bands)
    after = shifted(up, -1, bands)

    swap = [(0, 1), (1, 0)]
    groups = ("y", "x")
    group = lax.axis_size(groups)
    depth = lax.axis_size("z")
    gained = lax.ppermute(give, "core", swap)
    (half_sum,) = call(add_kernel, [half], [VMEM] * 2, name="half_sum")(keep, gained)
    parts = lax.all_to_all(half_sum.reshape(group, PART_ROWS, ch), groups, 0, 0)
    (part_sum,) = call(
        functools.partial(sum_kernel, depth),
        [shape((depth, PART_ROWS, ch), BF16)],
        [VMEM],
        name="part_sum",
    )(parts)
    parts = lax.all_to_all(part_sum, "z", 0, 0)
    (part_sum,) = call(
        functools.partial(sum_kernel, group),
        [shape((group, PART_ROWS, ch), BF16)],
        [VMEM],
        name="whole_sum",
    )(parts)
    mine = lax.all_to_all(part_sum, groups, 0, 0).reshape(16 * PART_ROWS, ch)
    other = lax.ppermute(mine, "core", swap)

    slot_grads = call(
        functools.partial(adjoint_kernel, offsets),
        [block] * offsets,
        [VMEM] * 3 + [SMEM] + [VMEM] * 3,
        [
            pltpu.VMEM((band_rows + 2, lon, ch), F32),
            pltpu.VMEM((band_rows * lon, taps * ch), BF16),
            pltpu.VMEM((offsets * quads, band_rows * lon), BF16),
            pltpu.VMEM((taps * band_rows, lon), F32),
        ],
        name="adjoint",
    )(scaled, before, after, place, helm, dep_slot, dep_weight)
    back = [
        slot_grads[e] if e == reach else shifted(slot_grads[e], reach - e, bands)
        for e in range(offsets)
    ]
    (field_grad,) = call(
        functools.partial(scatter_kernel, offsets),
        [shape((band_rows, lon, ch), F32)],
        [VMEM, SMEM] + [VMEM] * offsets,
        [
            pltpu.VMEM((offsets * quads, taps * ch), BF16),
            pltpu.VMEM(((band_rows - 1) * lon, offsets * quads), BF16),
        ],
        name="scatter",
    )(rows8, send_count, *back)
    grads = call(
        unpack_kernel,
        [
            shape((ch, hid), F32),
            shape((1, hid), F32),
            shape((hid, hid), F32),
            shape((1, hid), F32),
            shape((hid, ch), F32),
        ],
        [VMEM, VMEM, SMEM],
        name="unpack",
    )(mine, other, place)
    return (
        next_state[None],
        field_grad[None],
        grads[0],
        grads[1].reshape(hid),
        grads[2],
        grads[3].reshape(hid),
        grads[4],
    )


def solution(mesh):
    fine = Mesh(mesh.devices.reshape(4, 8, 4, 2), ("y",) + SPACE)
    state = P("y", SPACE, None, None)
    return jax.shard_map(
        body,
        mesh=fine,
        in_specs=(
            state,
            P(SPACE, None, None),
            P(SPACE, None),
            P(None, SPACE, None),
            P(None, SPACE, None),
            P(),
            P(),
            P(),
            P(),
            P(),
            P(),
            state,
        ),
        out_specs=(state, state, P(), P(), P(), P(), P()),
        check_vma=False,
    )
```

time: 473 us -> 104 us (0.22); the launches traced: 467 us -> 104 us
  waiting for transfers between devices: 183 us -> 24 us
  matrix products: 94 us -> 0 us
  blocking collectives: 93 us -> 21 us
  Pallas kernels: 0 us -> 19.9 us
  other arithmetic: 17.8 us -> 0.08 us
  local copies, waits for them, and re-layouts: 22.1 us -> 5.26 us
  between operations: 15.2 us -> 0.76 us
  starting transfers between devices: 42.5 us -> 32.7 us
    psum x1 -> x0, waiting for transfers between devices: 167 us -> none  [body(): lax.psum((local_grads[0], local_grads[1], local_grads[2], local_grads[3],...]
    dot_general x44 -> x0, matrix products: 94 us -> none  [the longest x4 13.8 us: body(): jnp.einsum('cs,bsh->bch', lower, received, preferred_element_type=jnp.flo...]
    psum x1 -> x0, blocking collectives: 93 us -> none  [body(): lax.psum((local_grads[0], local_grads[1], local_grads[2], local_grads[3],...]
    all_to_all x0 -> x2, blocking collectives: none -> 21 us  [the longest x1 11.2 us: body(): parts = lax.all_to_all(half_sum.reshape(group, PART_ROWS, ch), groups, 0, 0)]
    pallas_call x0 -> x9, Pallas kernels: none -> 19.9 us  [the longest x1 7.22 us: body(): call(mlp_kernel, [shape((band_rows, lon, ch), BF16), shape((band_rows, lo...]
    ppermute x16 -> x14, starting transfers between devices: 42.5 us -> 26.1 us  [the longest x12 18.3 us: shifted(): lax.ppermute(block, SPACE, [(i, (i + by) % count) for i in range(count)])]
    convert_element_type x10 -> x0, other arithmetic: 11.8 us -> none  [the longest x3 3.51 us: smoother(): smooth.astype(jnp.bfloat16)]
    slice x16 -> x0, local copies, waits for them, and re-layouts: 9.12 us -> none  [the longest x4 3.6 us: extended(): lax.slice_in_dim(cells, cells.shape[dim] - width, cells.shape[dim], axis=...]
  transfers between devices with their start and end apart: 17 -> 15, of which waited for: 7 -> 9; matrix products, arithmetic and copies ran while one was open for 15% -> 0% of each run, Pallas kernels for 0% -> 6%
where the time goes in v1:
time: 104 us
  starting transfers between devices  32.7 us (31%)
  waiting for transfers between devices  24 us (23%)
  blocking collectives  21 us (20%)
  Pallas kernels  19.9 us (19%)
  local copies, waits for them, and re-layouts  5.26 us (5%)
    ppermute x12, starting transfers between devices, shifted(): lax.ppermute(block, SPACE, [(i, (i + by) % count) for i in range(count)])  18.3 us
    ppermute x12, waiting for transfers between devices, shifted(): lax.ppermute(block, SPACE, [(i, (i + by) % count) for i in range(count)])  17.5 us
    all_to_all x1, blocking collectives, body(): parts = lax.all_to_all(half_sum.reshape(group, PART_ROWS, ch), groups, 0, 0)  11.2 us
    all_to_all x1, blocking collectives, body(): mine = lax.all_to_all(part_sum, groups, 0, 0).reshape(16 * PART_ROWS, ch)  9.77 us
    pallas_call x1, Pallas kernels, body(): call(mlp_kernel, [shape((band_rows, lon, ch), BF16), shape((band_rows, lo...  7.22 us
    all_to_all x1, starting transfers between devices, body(): parts = lax.all_to_all(part_sum, 'z', 0, 0)  6.61 us
    all_to_all x1, waiting for transfers between devices, body(): parts = lax.all_to_all(part_sum, 'z', 0, 0)  5.47 us
    unnamed x33, local copies, waits for them, and re-layouts  5.26 us
  transfers between devices with their start and end apart: 15, of which 9 were waited for; matrix products, arithmetic and copies ran while one was open for 0% of the time, Pallas kernels for 6%

profile of v1, /device:TPU:1, one launch (start us, length us, event | category | flops | bytes accessed | tf_op | source)
XLA Modules:
  0.0 103.7 jit_solution(12776466816917107093)
XLA Ops:
  0.6 0.7 copy.21
  1.3 0.0 copy-start.3
  1.3 0.0 copy-start.8
  1.4 0.6 copy-done.8
  2.0 0.0 copy-start.1
  2.0 1.0 %copy-done.1 = bf16[1,4,512,128]{3,2,1,0:T(8,128)(2,1)S(1)} copy-done((bf16[1,4,512,128]{3,2,1,0:T(8,128)(2,1)S(1)}, bf16[1,4,512,128]{3,2,1,0:T(8,128)(2,1)}, u32[]{:S(2)}) %copy-start.1) | copy-done | bytes 524312
  3.1 0.0 copy-start
  3.1 2.1 %pack.1 = (bf16[128,512]{1,0:T(8,128)(2,1)S(1)}, bf16[128,512]{1,0:T(8,128)(2,1)S(1)}, bf16[128,512]{1,0:T(8,128)(2,1)S(1)}, bf16[128,512]{1,0:T(8,128)(2,1)S(1)}, bf16[128,512]{1,0:T(8,128)(2,1)S(1)}) custom-call(bf16[4,512,128]{2,1,0:T(8,128)(2,1)S(1)} %bitcast.20, s32[8,512]{1,0:T(8,128)S(1)} %pad.4.rows_ref, s32[1,5]{1,0:T(1,128)S(1)} %copy-done.8), custom_call_target="tpu_custom_call" | custom-call | bytes 1310720 | tf_op jit(solution)/shard_map/pack/pallas_call | solution.py:407
  5.2 8.7 %collective-permute-start = (bf16[128,512]{1,0:T(8,128)(2,1)S(1)}, bf16[128,512]{1,0:T(8,128)(2,1)S(1)}, u32[]{:S(2)}, u32[]{:S(2)}) collective-permute-start(bf16[128,512]{1,0:T(8,128)(2,1)S(1)} %get-tuple-element.31), channel_id=1, source_target_pairs={{0,62},{1,63},{2,0},{3,1},{4,2},{5,3},{6,4},{7,5},{8,6},{9,7},{10,... | collective-permute-start | bytes 393224 | tf_op jit(solution)/shard_map/ppermute | solution.py:373
  13.9 1.0 collective-permute-start.1
  14.8 0.8 collective-permute-start.2
  15.6 0.0 collective-permute-start.3
  15.6 0.4 collective-permute-done.refs_0_
  16.0 2.3 %collective-permute-done.1.refs_1_ = bf16[128,512]{1,0:T(8,128)(2,1)S(1)} collective-permute-done((bf16[128,512]{1,0:T(8,128)(2,1)S(1)}, bf16[128,512]{1,0:T(8,128)(2,1)S(1)}, u32[]{:S(2)}, u32[]{:S(2)}) %collective-permute-start.1) | collective-permute-done | bytes 131104 | tf_op jit(solution)/shard_map/ppermute | solution.py:373
  18.2 0.1 collective-permute-done.2.refs_3_
  18.4 6.3 %collective-permute-done.3.refs_4_ = bf16[128,512]{1,0:T(8,128)(2,1)S(1)} collective-permute-done((bf16[128,512]{1,0:T(8,128)(2,1)S(1)}, bf16[128,512]{1,0:T(8,128)(2,1)S(1)}, u32[]{:S(2)}, u32[]{:S(2)}) %collective-permute-start.3) | collective-permute-done | bytes 131104 | tf_op jit(solution)/shard_map/ppermute | solution.py:373
  24.7 0.0 copy-done.3
  24.7 0.0 copy-start.4
  24.7 0.8 copy-done.4
  25.4 2.1 %interp.1 = (f32[4,512,128]{2,1,0:T(8,128)S(1)}, bf16[2,512,128]{2,1,0:T(8,128)(2,1)S(1)}, bf16[2,512,128]{2,1,0:T(8,128)(2,1)S(1)}) custom-call(bf16[128,512]{1,0:T(8,128)(2,1)S(1)} %collective-permute-done.refs_0_, bf16[128,512]{1,0:T(8,128)(2,1)S(1)} %collective-permute-done.1.refs_1_, bf16[128,512]{1,0:T(8,128)(2,1)S(1)} %get-tuple-element.33.refs_2_, ...), custom_call_target="tpu_custom_call" | custom-call | bytes 3145728 | tf_op jit(solution)/shard_map/interp/pallas_call | solution.py:421
  27.5 0.1 collective-permute-start.4
  27.6 0.5 collective-permute-start.5
  28.1 0.1 pad_add_fusion.place_ref
  28.2 2.7 %collective-permute-done.4.before_ref = bf16[2,512,128]{2,1,0:T(8,128)(2,1)S(1)} collective-permute-done((bf16[2,512,128]{2,1,0:T(8,128)(2,1)S(1)}, bf16[2,512,128]{2,1,0:T(8,128)(2,1)S(1)}, u32[]{:S(2)}, u32[]{:S(2)}) %collective-permute-start.4) | collective-permute-done | bytes 262176 | tf_op jit(solution)/shard_map/ppermute | solution.py:373
  30.9 2.6 %collective-permute-done.5.after_ref = bf16[2,512,128]{2,1,0:T(8,128)(2,1)S(1)} collective-permute-done((bf16[2,512,128]{2,1,0:T(8,128)(2,1)S(1)}, bf16[2,512,128]{2,1,0:T(8,128)(2,1)S(1)}, u32[]{:S(2)}, u32[]{:S(2)}) %collective-permute-start.5) | collective-permute-done | bytes 262176 | tf_op jit(solution)/shard_map/ppermute | solution.py:373
  33.5 0.0 copy-done
  33.5 0.0 copy-done.2
  33.5 0.0 copy-done.6
  33.5 0.0 copy-done.7
  33.5 0.0 copy-done.11
  33.5 0.6 copy-done.9
  34.1 0.0 copy-done.10
  34.2 7.2 %smooth_mlp.1 = (bf16[4,512,128]{2,1,0:T(8,128)(2,1)}, f32[4,512,128]{2,1,0:T(8,128)S(1)}, bf16[2,512,128]{2,1,0:T(8,128)(2,1)S(1)}, bf16[2,512,128]{2,1,0:T(8,1...) custom-call(f32[4,512,128]{2,1,0:T(8,128)S(1)} %get-tuple-element.36.dep_ref, ...), custom_call_target="tpu_custom_call" | custom-call | bytes 4849664 | tf_op jit(solution)/shard_map/smooth_mlp/pallas_call | solution.py:435
  41.4 0.7 copy-done.12
  42.1 0.7 copy-done.14
  42.8 3.6 %collective-permute-start.12 = (bf16[640,128]{1,0:T(8,128)(2,1)S(1)}, bf16[640,128]{1,0:T(8,128)(2,1)S(1)}, u32[]{:S(2)}, u32[]{:S(2)}) collective-permute-start(bf16[640,128]{1,0:T(8,128)(2,1)S(1)} %get-tuple-element.49), channel_id=1, source_target_pairs={{0,1},{1,0},{2,3},{3,2},{4,5},{5,4},{6,7},{7,6},{8,9},{9,8},{10,11... | collective-permute-start | bytes 491528 | tf_op jit(solution)/shard_map/ppermute | solution.py:476
  46.4 1.0 collective-permute-done.12.right_ref
  47.5 0.0 copy-start.15
  47.5 11.2 %all_to_all.15.parts_ref = bf16[16,40,128]{2,1,0:T(8,128)(2,1)S(1)} all-to-all(bf16[16,40,128]{2,1,0:T(8,128)(2,1)S(1)} %bitcast.18), channel_id=1, replica_groups=mesh['y'=4,'z'=8,'x'=4,'core'=2] {'y','x'}, dimensions={0} | all-to-all | bytes 327680 | tf_op jit(solution)/shard_map/all_to_all | solution.py:478
  58.7 0.7 part_sum.1
  59.4 6.6 %all-to-all-start.1 = ((bf16[8,40,128]{2,1,0:T(8,128)(2,1)}), bf16[8,40,128]{2,1,0:T(8,128)(2,1)S(1)}, u32[]{:S(2)}, u32[]{:S(2)}) async-start(bf16[8,40,128]{2,1,0:T(8,128)(2,1)} %part_sum.1), calls=%async_computation.1 | async-start | bytes 163840 | tf_op jit(solution)/shard_map/all_to_all | solution.py:485
  66.0 0.0 copy-done.15
  66.0 1.8 %collective-permute-start.6 = (bf16[2,512,128]{2,1,0:T(8,128)(2,1)S(1)}, bf16[2,512,128]{2,1,0:T(8,128)(2,1)S(1)}, u32[]{:S(2)}, u32[]{:S(2)}) collective-permute-start(bf16[2,512,128]{2,1,0:T(8,128)(2,1)S(1)} %copy-done.15), channel_id=1, source_target_pairs={{0,1},{1,2},{2,3},{3,4},{4,5},{5,6},{6,7},{7,8},{8,9},{9,10},{10,1... | collective-permute-start | bytes 786440 | tf_op jit(solution)/shard_map/ppermute | solution.py:373
  67.8 0.0 copy-done.13
  67.8 0.1 collective-permute-start.7
  68.0 5.5 %all-to-all-done.1.parts_ref = bf16[8,40,128]{2,1,0:T(8,128)(2,1)S(1)} async-done(((bf16[8,40,128]{2,1,0:T(8,128)(2,1)}), bf16[8,40,128]{2,1,0:T(8,128)(2,1)S(1)}, u32[]{:S(2)}, u32[]{:S(2)}) %all-to-all-start.1) | async-done | bytes 81952 | tf_op jit(solution)/shard_map/all_to_all | solution.py:485
  73.4 0.0 copy-start.5
  73.5 9.8 %all_to_all.16 = bf16[16,40,128]{2,1,0:T(8,128)(2,1)S(1)} all-to-all(bf16[16,40,128]{2,1,0:T(8,128)(2,1)S(1)} %whole_sum.1), channel_id=1, replica_groups=mesh['y'=4,'z'=8,'x'=4,'core'=2] {'y','x'}, dimensions={0} | all-to-all | bytes 327680 | tf_op jit(solution)/shard_map/all_to_all | solution.py:492
  83.2 4.2 %collective-permute-start.13 = (bf16[640,128]{1,0:T(8,128)(2,1)S(1)}, bf16[640,128]{1,0:T(8,128)(2,1)S(1)}, u32[]{:S(2)}, u32[]{:S(2)}) collective-permute-start(bf16[640,128]{1,0:T(8,128)(2,1)S(1)} %bitcast.16), channel_id=1, source_target_pairs={{0,1},{1,0},{2,3},{3,2},{4,5},{5,4},{6,7},{7,6},{8,9},{9,8},{10,11... | collective-permute-start | bytes 491528 | tf_op jit(solution)/shard_map/ppermute | solution.py:493
  87.4 0.0 collective-permute-done.6.before_ref
  87.4 0.0 collective-permute-done.7.after_ref
  87.4 0.0 copy-done.5
  87.4 3.3 %adjoint.1 = (bf16[128,512]{1,0:T(8,128)(2,1)S(1)}, bf16[128,512]{1,0:T(8,128)(2,1)S(1)}, bf16[128,512]{1,0:T(8,128)(2,1)S(1)}, bf16[128,512]{1,0:T(8,128)(2,1)S(1)}, bf16[128,512]{1,0:T(8,128)(2,1)S(1)}) custom-call(f32[4,512,128]{2,1,0:T(8,128)S(1)} %get-tuple-element.40.scaled_ref, bf16[2,512,128]{2,1,0:T(8,128)(2,1)S(1)} %collective-permute-done.6.before_ref, ...), custom_call_target="tpu_custom_call" | custom-call | bytes 1310720 | tf_op jit(solution)/shard_map/adjoint/pallas_call | solution.py:495
  90.7 0.4 collective-permute-start.8
  91.1 0.4 collective-permute-start.9
  91.5 0.1 collective-permute-start.10
  91.6 4.5 %collective-permute-start.11 = (bf16[128,512]{1,0:T(8,128)(2,1)S(1)}, bf16[128,512]{1,0:T(8,128)(2,1)S(1)}, u32[]{:S(2)}, u32[]{:S(2)}) collective-permute-start(bf16[128,512]{1,0:T(8,128)(2,1)S(1)} %get-tuple-element.47), channel_id=1, source_target_pairs={{0,62},{1,63},{2,0},{3,1},{4,2},{5,3},{6,4},{7,5},{8,6},{9,7},{10,... | collective-permute-start | bytes 393224 | tf_op jit(solution)/shard_map/ppermute | solution.py:373
  96.1 3.1 %collective-permute-done.8.refs_0_ = bf16[128,512]{1,0:T(8,128)(2,1)S(1)} collective-permute-done((bf16[128,512]{1,0:T(8,128)(2,1)S(1)}, bf16[128,512]{1,0:T(8,128)(2,1)S(1)}, u32[]{:S(2)}, u32[]{:S(2)}) %collective-permute-start.8) | collective-permute-done | bytes 131104 | tf_op jit(solution)/shard_map/ppermute | solution.py:373
  99.2 0.0 collective-permute-done.9.refs_1_
  99.2 0.0 collective-permute-done.10.refs_3_
  99.2 0.0 collective-permute-done.11.refs_4_
  99.2 3.1 %scatter.1 = f32[4,512,128]{2,1,0:T(8,128)} custom-call(s32[8,512]{1,0:T(8,128)S(1)} %pad.4.rows_ref, s32[1,5]{1,0:T(1,128)S(1)} %copy-done.8, bf16[128,512]{1,0:T(8,128)(2,1)S(1)} %collective-permute-done.8.refs_0_, bf16[128,512]{1,0:T(8,128)(2,1)S(1)} %collective-permute-done.9.refs_1_, bf16[128,512]{1,0:T(8,128)(2,1)S(1)} %get-tuple-element.45.refs_2_, ...), custom_call_target="tpu_custom_call" | custom-call | bytes 2097152 | tf_op jit(solution)/shard_map/scatter/pallas_call | solution.py:511
  102.4 0.0 collective-permute-done.13.other_ref
  102.4 1.4 %unpack.1 = (f32[128,256]{1,0:T(8,128)}, f32[1,256]{1,0:T(1,128)}, f32[256,256]{1,0:T(8,128)}, f32[1,256]{1,0:T(1,128)}, f32[256,128]{1,0:T(8,128)}) custom-call(bf16[640,128]{1,0:T(8,128)(2,1)S(1)} %bitcast.17, bf16[640,128]{1,0:T(8,128)(2,1)S(1)} %collective-permute-done.13.other_ref, s32[3]{0:T(128)S(1)} %pad_add_fusion.place_ref), custom_call_target="tpu_custom_call" | custom-call | bytes 1052672 | tf_op jit(solution)/shard_map/unpack/pallas_call | solution.py:521
  (12 shorter events, 0.1 us)
Async XLA Ops:
  1.3 23.3 %copy-start.3 = (s32[4,4,512]{2,1,0:T(4,128)S(1)}, s32[4,4,512]{2,1,0:T(4,128)}, u32[]{:S(2)}) copy-start(s32[4,4,512]{2,1,0:T(4,128)} %slot_ref.1) | copy-start | bytes 98308
  1.3 0.7 copy-start.8
  2.0 1.0 %copy-start.1 = (bf16[1,4,512,128]{3,2,1,0:T(8,128)(2,1)S(1)}, bf16[1,4,512,128]{3,2,1,0:T(8,128)(2,1)}, u32[]{:S(2)}) copy-start(bf16[1,4,512,128]{3,2,1,0:T(8,128)(2,1)} %param.12) | copy-start | bytes 1572868
  3.1 30.4 %copy-start = (bf16[1,4,512,128]{3,2,1,0:T(8,128)(2,1)S(1)}, bf16[1,4,512,128]{3,2,1,0:T(8,128)(2,1)}, u32[]{:S(2)}) copy-start(bf16[1,4,512,128]{3,2,1,0:T(8,128)(2,1)} %param.23) | copy-start | bytes 1572868
  5.2 10.8 %collective-permute-start = (bf16[128,512]{1,0:T(8,128)(2,1)S(1)}, bf16[128,512]{1,0:T(8,128)(2,1)S(1)}, u32[]{:S(2)}, u32[]{:S(2)}) collective-permute-start(bf16[128,512]{1,0:T(8,128)(2,1)S(1)} %get-tuple-element.31), channel_id=1, source_target_pairs={{0,62},{1,63},{2,0},{3,1},{4,2},{5,3},{6,4},{7,5},{8,6},{9,7},{10,... | collective-permute-start | bytes 393224 | tf_op jit(solution)/shard_map/ppermute | solution.py:373
  13.9 4.4 %collective-permute-start.1 = (bf16[128,512]{1,0:T(8,128)(2,1)S(1)}, bf16[128,512]{1,0:T(8,128)(2,1)S(1)}, u32[]{:S(2)}, u32[]{:S(2)}) collective-permute-start(bf16[128,512]{1,0:T(8,128)(2,1)S(1)} %get-tuple-element.32), channel_id=1, source_target_pairs={{0,63},{1,0},{2,1},{3,2},{4,3},{5,4},{6,5},{7,6},{8,7},{9,8},{10,9... | collective-permute-start | bytes 393224 | tf_op jit(solution)/shard_map/ppermute | solution.py:373
  14.8 3.5 %collective-permute-start.2 = (bf16[128,512]{1,0:T(8,128)(2,1)S(1)}, bf16[128,512]{1,0:T(8,128)(2,1)S(1)}, u32[]{:S(2)}, u32[]{:S(2)}) collective-permute-start(bf16[128,512]{1,0:T(8,128)(2,1)S(1)} %get-tuple-element.34), channel_id=1, source_target_pairs={{0,1},{1,2},{2,3},{3,4},{4,5},{5,6},{6,7},{7,8},{8,9},{9,10},{10,1... | collective-permute-start | bytes 393224 | tf_op jit(solution)/shard_map/ppermute | solution.py:373
  15.6 9.1 %collective-permute-start.3 = (bf16[128,512]{1,0:T(8,128)(2,1)S(1)}, bf16[128,512]{1,0:T(8,128)(2,1)S(1)}, u32[]{:S(2)}, u32[]{:S(2)}) collective-permute-start(bf16[128,512]{1,0:T(8,128)(2,1)S(1)} %get-tuple-element.35), channel_id=1, source_target_pairs={{0,2},{1,3},{2,4},{3,5},{4,6},{5,7},{6,8},{7,9},{8,10},{9,11},{10,... | collective-permute-start | bytes 393224 | tf_op jit(solution)/shard_map/ppermute | solution.py:373
  24.7 0.8 copy-start.4
  25.4 8.1 %copy-start.2 = (bf16[256,256]{1,0:T(8,128)(2,1)S(1)}, bf16[256,256]{1,0:T(8,128)(2,1)}, u32[]{:S(2)}) copy-start(bf16[256,256]{1,0:T(8,128)(2,1)} %w2_ref.1) | copy-start | bytes 393220
  25.4 8.1 %copy-start.6 = (bf16[128,256]{1,0:T(8,128)(2,1)S(1)}, bf16[128,256]{1,0:T(8,128)(2,1)}, u32[]{:S(2)}) copy-start(bf16[128,256]{1,0:T(8,128)(2,1)} %w1_ref.1) | copy-start | bytes 196612
  25.4 8.1 %copy-start.7 = (bf16[256,128]{1,0:T(8,128)(2,1)S(1)}, bf16[256,128]{1,0:T(8,128)(2,1)}, u32[]{:S(2)}) copy-start(bf16[256,128]{1,0:T(8,128)(2,1)} %w3_ref.1) | copy-start | bytes 196612
  27.5 3.4 %collective-permute-start.4 = (bf16[2,512,128]{2,1,0:T(8,128)(2,1)S(1)}, bf16[2,512,128]{2,1,0:T(8,128)(2,1)S(1)}, u32[]{:S(2)}, u32[]{:S(2)}) collective-permute-start(bf16[2,512,128]{2,1,0:T(8,128)(2,1)S(1)} %get-tuple-element.37), channel_id=1, source_target_pairs={{0,1},{1,2},{2,3},{3,4},{4,5},{5,6},{6,7},{7,8},{8,9},{9,10},{10,1... | collective-permute-start | bytes 786440 | tf_op jit(solution)/shard_map/ppermute | solution.py:373
  27.6 5.9 %collective-permute-start.5 = (bf16[2,512,128]{2,1,0:T(8,128)(2,1)S(1)}, bf16[2,512,128]{2,1,0:T(8,128)(2,1)S(1)}, u32[]{:S(2)}, u32[]{:S(2)}) collective-permute-start(bf16[2,512,128]{2,1,0:T(8,128)(2,1)S(1)} %get-tuple-element.38), channel_id=1, source_target_pairs={{0,63},{1,0},{2,1},{3,2},{4,3},{5,4},{6,5},{7,6},{8,7},{9,8},{10,9... | collective-permute-start | bytes 786440 | tf_op jit(solution)/shard_map/ppermute | solution.py:373
  28.1 5.4 %copy-start.11 = (f32[256]{0:T(256)S(1)}, f32[256]{0:T(256)}, u32[]{:S(2)}) copy-start(f32[256]{0:T(256)} %param.21) | copy-start | bytes 3076
  33.5 0.7 copy-start.9
  33.5 0.7 copy-start.10
  41.4 0.7 copy-start.12
  42.1 0.7 copy-start.14
  42.8 4.6 %collective-permute-start.12 = (bf16[640,128]{1,0:T(8,128)(2,1)S(1)}, bf16[640,128]{1,0:T(8,128)(2,1)S(1)}, u32[]{:S(2)}, u32[]{:S(2)}) collective-permute-start(bf16[640,128]{1,0:T(8,128)(2,1)S(1)} %get-tuple-element.49), channel_id=1, source_target_pairs={{0,1},{1,0},{2,3},{3,2},{4,5},{5,4},{6,7},{7,6},{8,9},{9,8},{10,11... | collective-permute-start | bytes 491528 | tf_op jit(solution)/shard_map/ppermute | solution.py:476
  47.5 18.5 %copy-start.15 = (bf16[2,512,128]{2,1,0:T(8,128)(2,1)S(1)}, bf16[2,512,128]{2,1,0:T(8,128)(2,1)}, u32[]{:S(2)}) copy-start(bf16[2,512,128]{2,1,0:T(8,128)(2,1)} %copy-done.14) | copy-start | bytes 786436
  58.7 9.1 %copy-start.13 = (bf16[2,512,128]{2,1,0:T(8,128)(2,1)S(1)}, bf16[2,512,128]{2,1,0:T(8,128)(2,1)}, u32[]{:S(2)}) copy-start(bf16[2,512,128]{2,1,0:T(8,128)(2,1)} %copy-done.12) | copy-start | bytes 786436
  59.4 14.0 %all-to-all-start.1 = ((bf16[8,40,128]{2,1,0:T(8,128)(2,1)}), bf16[8,40,128]{2,1,0:T(8,128)(2,1)S(1)}, u32[]{:S(2)}, u32[]{:S(2)}) async-start(bf16[8,40,128]{2,1,0:T(8,128)(2,1)} %part_sum.1), calls=%async_computation.1 | async-start | bytes 163840 | tf_op jit(solution)/shard_map/all_to_all | solution.py:485
  66.0 21.4 %collective-permute-start.6 = (bf16[2,512,128]{2,1,0:T(8,128)(2,1)S(1)}, bf16[2,512,128]{2,1,0:T(8,128)(2,1)S(1)}, u32[]{:S(2)}, u32[]{:S(2)}) collective-permute-start(bf16[2,512,128]{2,1,0:T(8,128)(2,1)S(1)} %copy-done.15), channel_id=1, source_target_pairs={{0,1},{1,2},{2,3},{3,4},{4,5},{5,6},{6,7},{7,8},{8,9},{9,10},{10,1... | collective-permute-start | bytes 786440 | tf_op jit(solution)/shard_map/ppermute | solution.py:373
  67.8 19.5 %collective-permute-start.7 = (bf16[2,512,128]{2,1,0:T(8,128)(2,1)S(1)}, bf16[2,512,128]{2,1,0:T(8,128)(2,1)S(1)}, u32[]{:S(2)}, u32[]{:S(2)}) collective-permute-start(bf16[2,512,128]{2,1,0:T(8,128)(2,1)S(1)} %copy-done.13), channel_id=1, source_target_pairs={{0,63},{1,0},{2,1},{3,2},{4,3},{5,4},{6,5},{7,6},{8,7},{9,8},{10,9... | collective-permute-start | bytes 786440 | tf_op jit(solution)/shard_map/ppermute | solution.py:373
  73.4 13.9 %copy-start.5 = (f32[4,4,512]{2,1,0:T(4,128)S(1)}, f32[4,4,512]{2,1,0:T(4,128)}, u32[]{:S(2)}) copy-start(f32[4,4,512]{2,1,0:T(4,128)} %weight_ref.1) | copy-start | bytes 98308
  83.2 19.1 %collective-permute-start.13 = (bf16[640,128]{1,0:T(8,128)(2,1)S(1)}, bf16[640,128]{1,0:T(8,128)(2,1)S(1)}, u32[]{:S(2)}, u32[]{:S(2)}) collective-permute-start(bf16[640,128]{1,0:T(8,128)(2,1)S(1)} %bitcast.16), channel_id=1, source_target_pairs={{0,1},{1,0},{2,3},{3,2},{4,5},{5,4},{6,7},{7,6},{8,9},{9,8},{10,11... | collective-permute-start | bytes 491528 | tf_op jit(solution)/shard_map/ppermute | solution.py:493
  90.7 8.5 %collective-permute-start.8 = (bf16[128,512]{1,0:T(8,128)(2,1)S(1)}, bf16[128,512]{1,0:T(8,128)(2,1)S(1)}, u32[]{:S(2)}, u32[]{:S(2)}) collective-permute-start(bf16[128,512]{1,0:T(8,128)(2,1)S(1)} %get-tuple-element.43), channel_id=1, source_target_pairs={{0,2},{1,3},{2,4},{3,5},{4,6},{5,7},{6,8},{7,9},{8,10},{9,11},{10,... | collective-permute-start | bytes 393224 | tf_op jit(solution)/shard_map/ppermute | solution.py:373
  91.1 8.2 %collective-permute-start.9 = (bf16[128,512]{1,0:T(8,128)(2,1)S(1)}, bf16[128,512]{1,0:T(8,128)(2,1)S(1)}, u32[]{:S(2)}, u32[]{:S(2)}) collective-permute-start(bf16[128,512]{1,0:T(8,128)(2,1)S(1)} %get-tuple-element.44), channel_id=1, source_target_pairs={{0,1},{1,2},{2,3},{3,4},{4,5},{5,6},{6,7},{7,8},{8,9},{9,10},{10,1... | collective-permute-start | bytes 393224 | tf_op jit(solution)/shard_map/ppermute | solution.py:373
  91.5 7.7 %collective-permute-start.10 = (bf16[128,512]{1,0:T(8,128)(2,1)S(1)}, bf16[128,512]{1,0:T(8,128)(2,1)S(1)}, u32[]{:S(2)}, u32[]{:S(2)}) collective-permute-start(bf16[128,512]{1,0:T(8,128)(2,1)S(1)} %get-tuple-element.46), channel_id=1, source_target_pairs={{0,63},{1,0},{2,1},{3,2},{4,3},{5,4},{6,5},{7,6},{8,7},{9,8},{10,9... | collective-permute-start | bytes 393224 | tf_op jit(solution)/shard_map/ppermute | solution.py:373
  91.6 7.7 %collective-permute-start.11 = (bf16[128,512]{1,0:T(8,128)(2,1)S(1)}, bf16[128,512]{1,0:T(8,128)(2,1)S(1)}, u32[]{:S(2)}, u32[]{:S(2)}) collective-permute-start(bf16[128,512]{1,0:T(8,128)(2,1)S(1)} %get-tuple-element.47), channel_id=1, source_target_pairs={{0,62},{1,63},{2,0},{3,1},{4,2},{5,3},{6,4},{7,5},{8,6},{9,7},{10,... | collective-permute-start | bytes 393224 | tf_op jit(solution)/shard_map/ppermute | solution.py:373

commit v2 on v1

--- a/solution.py
+++ b/solution.py
@@ -17,6 +17,7 @@
 PART_ROWS = 40
 
 VMEM = pl.BlockSpec(memory_space=pltpu.VMEM)
+ANY = pl.BlockSpec(memory_space=pl.ANY)
 SMEM = pl.BlockSpec(memory_space=pltpu.SMEM)
 
 
@@ -308,7 +309,8 @@
 
 def scatter_kernel(offsets, rows_ref, count_ref, *refs):
     blocks = refs[:offsets]
-    out_ref, table, hit = refs[offsets:]
+    out_ref, done_ref, table, hit = refs[offsets:]
+    done_ref[...] = jnp.zeros_like(done_ref)
     band_rows, lon, ch = out_ref.shape
     slots = rows_ref.shape[1]
     quads = slots // 4
@@ -338,7 +340,7 @@
     out_ref[...] = (left_ref[...].astype(F32) + right_ref[...].astype(F32)).astype(BF16)
 
 
-def sum_kernel(copies, parts_ref, out_ref):
+def sum_kernel(copies, parts_ref, ahead_ref, out_ref):
     total = parts_ref[0].astype(F32)
     for part in range(1, parts_ref.shape[0]):
         total = total + parts_ref[part].astype(F32)
@@ -476,22 +478,6 @@
     gained = lax.ppermute(give, "core", swap)
     (half_sum,) = call(add_kernel, [half], [VMEM] * 2, name="half_sum")(keep, gained)
     parts = lax.all_to_all(half_sum.reshape(group, PART_ROWS, ch), groups, 0, 0)
-    (part_sum,) = call(
-        functools.partial(sum_kernel, depth),
-        [shape((depth, PART_ROWS, ch), BF16)],
-        [VMEM],
-        name="part_sum",
-    )(parts)
-    parts = lax.all_to_all(part_sum, "z", 0, 0)
-    (part_sum,) = call(
-        functools.partial(sum_kernel, group),
-        [shape((group, PART_ROWS, ch), BF16)],
-        [VMEM],
-        name="whole_sum",
-    )(parts)
-    mine = lax.all_to_all(part_sum, groups, 0, 0).reshape(16 * PART_ROWS, ch)
-    other = lax.ppermute(mine, "core", swap)
-
     slot_grads = call(
         functools.partial(adjoint_kernel, offsets),
         [block] * offsets,
@@ -504,13 +490,20 @@
         ],
         name="adjoint",
     )(scaled, before, after, place, helm, dep_slot, dep_weight)
+    (part_sum,) = call(
+        functools.partial(sum_kernel, depth),
+        [shape((depth, PART_ROWS, ch), BF16)],
+        [VMEM, ANY],
+        name="part_sum",
+    )(parts, slot_grads[reach])
+    parts = lax.all_to_all(part_sum, "z", 0, 0)
     back = [
         slot_grads[e] if e == reach else shifted(slot_grads[e], reach - e, bands)
         for e in range(offsets)
     ]
-    (field_grad,) = call(
+    field_grad, done = call(
         functools.partial(scatter_kernel, offsets),
-        [shape((band_rows, lon, ch), F32)],
+        [shape((band_rows, lon, ch), F32), shape((8, ch), F32)],
         [VMEM, SMEM] + [VMEM] * offsets,
         [
             pltpu.VMEM((offsets * quads, taps * ch), BF16),
@@ -518,6 +511,15 @@
         ],
         name="scatter",
     )(rows8, send_count, *back)
+    (part_sum,) = call(
+        functools.partial(sum_kernel, group),
+        [shape((group, PART_ROWS, ch), BF16)],
+        [VMEM, ANY],
+        name="whole_sum",
+    )(parts, done)
+    mine = lax.all_to_all(part_sum, groups, 0, 0).reshape(16 * PART_ROWS, ch)
+    other = lax.ppermute(mine, "core", swap)
+
     grads = call(
         unpack_kernel,
         [

time: 104 us -> 98.3 us (0.945)
  blocking collectives: 21 us -> 12.3 us
  starting transfers between devices: 32.7 us -> 37.4 us
  waiting for transfers between devices: 24 us -> 22.4 us
  local copies, waits for them, and re-layouts: 5.26 us -> 3.84 us
    all_to_all x1 -> x0, blocking collectives: 11.2 us -> none  [body(): parts = lax.all_to_all(half_sum.reshape(group, PART_ROWS, ch), groups, 0, 0)]
    all_to_all x1, waiting for transfers between devices: 5.47 us -> 0.01 us  [body(): parts = lax.all_to_all(part_sum, 'z', 0, 0)]
    all_to_all x0 -> x1, starting transfers between devices: none -> 4.61 us  [body(): parts = lax.all_to_all(half_sum.reshape(group, PART_ROWS, ch), groups, 0, 0)]
    all_to_all x0 -> x1, waiting for transfers between devices: none -> 3.67 us  [body(): parts = lax.all_to_all(half_sum.reshape(group, PART_ROWS, ch), groups, 0, 0)]
    all_to_all x1, blocking collectives: 9.77 us -> 12.3 us  [body(): mine = lax.all_to_all(part_sum, groups, 0, 0).reshape(16 * PART_ROWS, ch)]
    unnamed x33 -> x25, local copies, waits for them, and re-layouts: 5.26 us -> 3.84 us
  transfers between devices with their start and end apart: 15 -> 16, of which waited for: 9 -> 11; matrix products, arithmetic and copies ran while one was open for 0% -> 0% of each run, Pallas kernels for 6% -> 7%
where the time goes in v2:
time: 98.3 us; the launch traced here: 97.5 us
  starting transfers between devices  37.4 us (38%)
  waiting for transfers between devices  22.4 us (23%)
  Pallas kernels  20.7 us (21%)
  blocking collectives  12.3 us (13%)
  local copies, waits for them, and re-layouts  3.84 us (4%)
    ppermute x12, starting transfers between devices, shifted(): lax.ppermute(block, SPACE, [(i, (i + by) % count) for i in range(count)])  19.2 us
    ppermute x12, waiting for transfers between devices, shifted(): lax.ppermute(block, SPACE, [(i, (i + by) % count) for i in range(count)])  17.2 us
    all_to_all x1, blocking collectives, body(): mine = lax.all_to_all(part_sum, groups, 0, 0).reshape(16 * PART_ROWS, ch)  12.3 us
    pallas_call x1, Pallas kernels, body(): call(mlp_kernel, [shape((band_rows, lon, ch), BF16), shape((band_rows, lo...  7.3 us
    all_to_all x1, starting transfers between devices, body(): parts = lax.all_to_all(part_sum, 'z', 0, 0)  6.51 us
    all_to_all x1, starting transfers between devices, body(): parts = lax.all_to_all(half_sum.reshape(group, PART_ROWS, ch), groups, 0, 0)  4.61 us
    unnamed x25, local copies, waits for them, and re-layouts  3.84 us
    all_to_all x1, waiting for transfers between devices, body(): parts = lax.all_to_all(half_sum.reshape(group, PART_ROWS, ch), groups, 0, 0)  3.67 us
  transfers between devices with their start and end apart: 16, of which 11 were waited for; matrix products, arithmetic and copies ran while one was open for 0% of the time, Pallas kernels for 7%

profile of v2, /device:TPU:1, one launch (start us, length us, event | category | flops | bytes accessed | tf_op | source)
XLA Modules:
  0.0 97.5 jit_solution(2863112197917149997)
XLA Ops:
  0.6 0.7 copy.21
  1.3 0.0 copy-start.3
  1.3 0.0 copy-start.9
  1.4 0.6 copy-done.9
  2.0 0.0 copy-start.1
  2.0 1.0 %copy-done.1 = bf16[1,4,512,128]{3,2,1,0:T(8,128)(2,1)S(1)} copy-done((bf16[1,4,512,128]{3,2,1,0:T(8,128)(2,1)S(1)}, bf16[1,4,512,128]{3,2,1,0:T(8,128)(2,1)}, u32[]{:S(2)}) %copy-start.1) | copy-done | bytes 524312
  3.1 2.1 %pack.1 = (bf16[128,512]{1,0:T(8,128)(2,1)S(1)}, bf16[128,512]{1,0:T(8,128)(2,1)S(1)}, bf16[128,512]{1,0:T(8,128)(2,1)S(1)}, bf16[128,512]{1,0:T(8,128)(2,1)S(1)}, bf16[128,512]{1,0:T(8,128)(2,1)S(1)}) custom-call(bf16[4,512,128]{2,1,0:T(8,128)(2,1)S(1)} %bitcast.19, s32[8,512]{1,0:T(8,128)S(1)} %pad.4.rows_ref, s32[1,5]{1,0:T(1,128)S(1)} %copy-done.9), custom_call_target="tpu_custom_call" | custom-call | bytes 1310720 | tf_op jit(solution)/shard_map/pack/pallas_call | solution.py:409
  5.2 8.7 %collective-permute-start = (bf16[128,512]{1,0:T(8,128)(2,1)S(1)}, bf16[128,512]{1,0:T(8,128)(2,1)S(1)}, u32[]{:S(2)}, u32[]{:S(2)}) collective-permute-start(bf16[128,512]{1,0:T(8,128)(2,1)S(1)} %get-tuple-element.33), channel_id=1, source_target_pairs={{0,62},{1,63},{2,0},{3,1},{4,2},{5,3},{6,4},{7,5},{8,6},{9,7},{10,... | collective-permute-start | bytes 393224 | tf_op jit(solution)/shard_map/ppermute | solution.py:375
  13.9 1.0 %collective-permute-start.1 = (bf16[128,512]{1,0:T(8,128)(2,1)S(1)}, bf16[128,512]{1,0:T(8,128)(2,1)S(1)}, u32[]{:S(2)}, u32[]{:S(2)}) collective-permute-start(bf16[128,512]{1,0:T(8,128)(2,1)S(1)} %get-tuple-element.34), channel_id=1, source_target_pairs={{0,63},{1,0},{2,1},{3,2},{4,3},{5,4},{6,5},{7,6},{8,7},{9,8},{10,9... | collective-permute-start | bytes 393224 | tf_op jit(solution)/shard_map/ppermute | solution.py:375
  14.8 0.8 collective-permute-start.2
  15.6 0.0 collective-permute-start.3
  15.6 0.4 collective-permute-done.refs_0_
  16.0 2.3 %collective-permute-done.1.refs_1_ = bf16[128,512]{1,0:T(8,128)(2,1)S(1)} collective-permute-done((bf16[128,512]{1,0:T(8,128)(2,1)S(1)}, bf16[128,512]{1,0:T(8,128)(2,1)S(1)}, u32[]{:S(2)}, u32[]{:S(2)}) %collective-permute-start.1) | collective-permute-done | bytes 131104 | tf_op jit(solution)/shard_map/ppermute | solution.py:375
  18.2 0.1 collective-permute-done.2.refs_3_
  18.4 6.3 %collective-permute-done.3.refs_4_ = bf16[128,512]{1,0:T(8,128)(2,1)S(1)} collective-permute-done((bf16[128,512]{1,0:T(8,128)(2,1)S(1)}, bf16[128,512]{1,0:T(8,128)(2,1)S(1)}, u32[]{:S(2)}, u32[]{:S(2)}) %collective-permute-start.3) | collective-permute-done | bytes 131104 | tf_op jit(solution)/shard_map/ppermute | solution.py:375
  24.7 0.0 copy-done.3
  24.7 0.0 copy-start.4
  24.7 0.8 copy-done.4
  25.4 0.0 copy-start.2
  25.4 0.0 copy-start.6
  25.4 0.0 copy-start.7
  25.4 2.1 %interp.1 = (f32[4,512,128]{2,1,0:T(8,128)S(1)}, bf16[2,512,128]{2,1,0:T(8,128)(2,1)S(1)}, bf16[2,512,128]{2,1,0:T(8,128)(2,1)S(1)}) custom-call(bf16[128,512]{1,0:T(8,128)(2,1)S(1)} %collective-permute-done.refs_0_, bf16[128,512]{1,0:T(8,128)(2,1)S(1)} %collective-permute-done.1.refs_1_, bf16[128,512]{1,0:T(8,128)(2,1)S(1)} %get-tuple-element.35.refs_2_, ...), custom_call_target="tpu_custom_call" | custom-call | bytes 3145728 | tf_op jit(solution)/shard_map/interp/pallas_call | solution.py:423
  27.5 0.1 collective-permute-start.4
  27.6 0.5 collective-permute-start.5
  28.1 0.0 copy-start.11
  28.1 0.1 pad_add_fusion.place_ref
  28.2 2.7 %collective-permute-done.4.before_ref = bf16[2,512,128]{2,1,0:T(8,128)(2,1)S(1)} collective-permute-done((bf16[2,512,128]{2,1,0:T(8,128)(2,1)S(1)}, bf16[2,512,128]{2,1,0:T(8,128)(2,1)S(1)}, u32[]{:S(2)}, u32[]{:S(2)}) %collective-permute-start.4) | collective-permute-done | bytes 262176 | tf_op jit(solution)/shard_map/ppermute | solution.py:375
  30.9 2.6 %collective-permute-done.5.after_ref = bf16[2,512,128]{2,1,0:T(8,128)(2,1)S(1)} collective-permute-done((bf16[2,512,128]{2,1,0:T(8,128)(2,1)S(1)}, bf16[2,512,128]{2,1,0:T(8,128)(2,1)S(1)}, u32[]{:S(2)}, u32[]{:S(2)}) %collective-permute-start.5) | collective-permute-done | bytes 262176 | tf_op jit(solution)/shard_map/ppermute | solution.py:375
  33.5 0.0 copy-start.8
  33.5 0.0 copy-done
  33.5 0.0 copy-done.2
  33.5 0.0 copy-done.6
  33.5 0.0 copy-done.7
  33.5 0.0 copy-done.11
  33.5 0.6 copy-done.8
  34.1 0.0 copy-done.10
  34.2 7.3 %smooth_mlp.1 = (bf16[4,512,128]{2,1,0:T(8,128)(2,1)}, f32[4,512,128]{2,1,0:T(8,128)S(1)}, bf16[2,512,128]{2,1,0:T(8,128)(2,1)}, bf16[2,512,128]{2,1,0:T(8,128)(...) custom-call(f32[4,512,128]{2,1,0:T(8,128)S(1)} %get-tuple-element.38.dep_ref, ...), custom_call_target="tpu_custom_call" | custom-call | bytes 4849664 | tf_op jit(solution)/shard_map/smooth_mlp/pallas_call | solution.py:437
  41.5 3.6 %collective-permute-start.12 = (bf16[640,128]{1,0:T(8,128)(2,1)S(1)}, bf16[640,128]{1,0:T(8,128)(2,1)S(1)}, u32[]{:S(2)}, u32[]{:S(2)}) collective-permute-start(bf16[640,128]{1,0:T(8,128)(2,1)S(1)} %get-tuple-element.52), channel_id=1, source_target_pairs={{0,1},{1,0},{2,3},{3,2},{4,5},{5,4},{6,7},{7,6},{8,9},{9,8},{10,11... | collective-permute-start | bytes 491528 | tf_op jit(solution)/shard_map/ppermute | solution.py:478
  45.1 0.0 collective-permute-start.6
  45.1 0.5 collective-permute-start.7
  45.6 0.5 collective-permute-done.12.right_ref
  46.1 0.7 half_sum.1
  46.8 4.6 %all-to-all-start = ((bf16[16,40,128]{2,1,0:T(8,128)(2,1)}), bf16[16,40,128]{2,1,0:T(8,128)(2,1)S(1)}, u32[]{:S(2)}, u32[]{:S(2)}) async-start(bf16[16,40,128]{2,1,0:T(8,128)(2,1)} %bitcast.9), calls=%async_computation | async-start | bytes 327680 | tf_op jit(solution)/shard_map/all_to_all | solution.py:480
  51.4 0.0 collective-permute-done.6.before_ref
  51.4 0.0 collective-permute-done.7.after_ref
  51.4 0.0 copy-done.5
  51.5 3.3 %adjoint.1 = (bf16[128,512]{1,0:T(8,128)(2,1)S(1)}, bf16[128,512]{1,0:T(8,128)(2,1)S(1)}, bf16[128,512]{1,0:T(8,128)(2,1)S(1)}, bf16[128,512]{1,0:T(8,128)(2,1)S(1)}, bf16[128,512]{1,0:T(8,128)(2,1)S(1)}) custom-call(f32[4,512,128]{2,1,0:T(8,128)S(1)} %get-tuple-element.42.scaled_ref, bf16[2,512,128]{2,1,0:T(8,128)(2,1)S(1)} %collective-permute-done.6.before_ref, ...), custom_call_target="tpu_custom_call" | custom-call | bytes 1310720 | tf_op jit(solution)/shard_map/adjoint/pallas_call | solution.py:481
  54.8 3.7 %all-to-all-done.parts_ref = bf16[16,40,128]{2,1,0:T(8,128)(2,1)S(1)} async-done(((bf16[16,40,128]{2,1,0:T(8,128)(2,1)}), bf16[16,40,128]{2,1,0:T(8,128)(2,1)S(1)}, u32[]{:S(2)}, u32[]{:S(2)}) %all-to-all-start) | async-done | bytes 163872 | tf_op jit(solution)/shard_map/all_to_all | solution.py:480
  58.4 0.7 part_sum.1
  59.1 6.5 %all-to-all-start.1 = ((bf16[8,40,128]{2,1,0:T(8,128)(2,1)}), bf16[8,40,128]{2,1,0:T(8,128)(2,1)S(1)}, u32[]{:S(2)}, u32[]{:S(2)}) async-start(bf16[8,40,128]{2,1,0:T(8,128)(2,1)} %part_sum.1), calls=%async_computation.1 | async-start | bytes 163840 | tf_op jit(solution)/shard_map/all_to_all | solution.py:499
  65.6 0.5 collective-permute-start.8
  66.2 2.6 %collective-permute-start.9 = (bf16[128,512]{1,0:T(8,128)(2,1)S(1)}, bf16[128,512]{1,0:T(8,128)(2,1)S(1)}, u32[]{:S(2)}, u32[]{:S(2)}) collective-permute-start(bf16[128,512]{1,0:T(8,128)(2,1)S(1)} %get-tuple-element.46), channel_id=1, source_target_pairs={{0,1},{1,2},{2,3},{3,4},{4,5},{5,6},{6,7},{7,8},{8,9},{9,10},{10,1... | collective-permute-start | bytes 393224 | tf_op jit(solution)/shard_map/ppermute | solution.py:375
  68.7 0.0 collective-permute-start.10
  68.7 4.6 %collective-permute-start.11 = (bf16[128,512]{1,0:T(8,128)(2,1)S(1)}, bf16[128,512]{1,0:T(8,128)(2,1)S(1)}, u32[]{:S(2)}, u32[]{:S(2)}) collective-permute-start(bf16[128,512]{1,0:T(8,128)(2,1)S(1)} %get-tuple-element.49), channel_id=1, source_target_pairs={{0,62},{1,63},{2,0},{3,1},{4,2},{5,3},{6,4},{7,5},{8,6},{9,7},{10,... | collective-permute-start | bytes 393224 | tf_op jit(solution)/shard_map/ppermute | solution.py:375
  73.3 0.0 collective-permute-done.8.refs_0_
  73.3 0.0 collective-permute-done.9.refs_1_
  73.3 1.0 collective-permute-done.10.refs_3_
  74.3 1.9 %collective-permute-done.11.refs_4_ = bf16[128,512]{1,0:T(8,128)(2,1)S(1)} collective-permute-done((bf16[128,512]{1,0:T(8,128)(2,1)S(1)}, bf16[128,512]{1,0:T(8,128)(2,1)S(1)}, u32[]{:S(2)}, u32[]{:S(2)}) %collective-permute-start.11) | collective-permute-done | bytes 131104 | tf_op jit(solution)/shard_map/ppermute | solution.py:375
  76.2 3.1 %scatter.1 = (f32[4,512,128]{2,1,0:T(8,128)}, f32[8,128]{1,0:T(8,128)S(1)}) custom-call(s32[8,512]{1,0:T(8,128)S(1)} %pad.4.rows_ref, s32[1,5]{1,0:T(1,128)S(1)} %copy-done.9, bf16[128,512]{1,0:T(8,128)(2,1)S(1)} %collective-permute-done.8.refs_0_, bf16[128,512]{1,0:T(8,128)(2,1)S(1)} %collective-permute-done.9.refs_1_, ...), custom_call_target="tpu_custom_call" | custom-call | bytes 2105344 | tf_op jit(solution)/shard_map/scatter/pallas_call | solution.py:504
  79.3 0.0 all-to-all-done.1.parts_ref
  79.3 12.3 %all_to_all.15 = bf16[16,40,128]{2,1,0:T(8,128)(2,1)S(1)} all-to-all(bf16[16,40,128]{2,1,0:T(8,128)(2,1)S(1)} %whole_sum.1), channel_id=1, replica_groups=mesh['y'=4,'z'=8,'x'=4,'core'=2] {'y','x'}, dimensions={0} | all-to-all | bytes 327680 | tf_op jit(solution)/shard_map/all_to_all | solution.py:520
  91.6 3.5 %collective-permute-start.13 = (bf16[640,128]{1,0:T(8,128)(2,1)S(1)}, bf16[640,128]{1,0:T(8,128)(2,1)S(1)}, u32[]{:S(2)}, u32[]{:S(2)}) collective-permute-start(bf16[640,128]{1,0:T(8,128)(2,1)S(1)} %bitcast.16), channel_id=1, source_target_pairs={{0,1},{1,0},{2,3},{3,2},{4,5},{5,4},{6,7},{7,6},{8,9},{9,8},{10,11... | collective-permute-start | bytes 491528 | tf_op jit(solution)/shard_map/ppermute | solution.py:521
  95.1 1.0 %collective-permute-done.13.other_ref = bf16[640,128]{1,0:T(8,128)(2,1)S(1)} collective-permute-done((bf16[640,128]{1,0:T(8,128)(2,1)S(1)}, bf16[640,128]{1,0:T(8,128)(2,1)S(1)}, u32[]{:S(2)}, u32[]{:S(2)}) %collective-permute-start.13) | collective-permute-done | bytes 163872 | tf_op jit(solution)/shard_map/ppermute | solution.py:521
  96.1 1.4 %unpack.1 = (f32[128,256]{1,0:T(8,128)}, f32[1,256]{1,0:T(1,128)}, f32[256,256]{1,0:T(8,128)}, f32[1,256]{1,0:T(1,128)}, f32[256,128]{1,0:T(8,128)}) custom-call(bf16[640,128]{1,0:T(8,128)(2,1)S(1)} %bitcast.17, bf16[640,128]{1,0:T(8,128)(2,1)S(1)} %collective-permute-done.13.other_ref, s32[3]{0:T(128)S(1)} %pad_add_fusion.place_ref), custom_call_target="tpu_custom_call" | custom-call | bytes 1052672 | tf_op jit(solution)/shard_map/unpack/pallas_call | solution.py:523
  (5 shorter events, 0.0 us)
Async XLA Ops:
  1.3 23.3 %copy-start.3 = (s32[4,4,512]{2,1,0:T(4,128)S(1)}, s32[4,4,512]{2,1,0:T(4,128)}, u32[]{:S(2)}) copy-start(s32[4,4,512]{2,1,0:T(4,128)} %slot_ref.1) | copy-start | bytes 98308
  1.3 0.7 copy-start.9
  2.0 1.0 %copy-start.1 = (bf16[1,4,512,128]{3,2,1,0:T(8,128)(2,1)S(1)}, bf16[1,4,512,128]{3,2,1,0:T(8,128)(2,1)}, u32[]{:S(2)}) copy-start(bf16[1,4,512,128]{3,2,1,0:T(8,128)(2,1)} %param.12) | copy-start | bytes 1572868
  3.1 30.4 %copy-start = (bf16[1,4,512,128]{3,2,1,0:T(8,128)(2,1)S(1)}, bf16[1,4,512,128]{3,2,1,0:T(8,128)(2,1)}, u32[]{:S(2)}) copy-start(bf16[1,4,512,128]{3,2,1,0:T(8,128)(2,1)} %param.23) | copy-start | bytes 1572868
  5.2 10.8 %collective-permute-start = (bf16[128,512]{1,0:T(8,128)(2,1)S(1)}, bf16[128,512]{1,0:T(8,128)(2,1)S(1)}, u32[]{:S(2)}, u32[]{:S(2)}) collective-permute-start(bf16[128,512]{1,0:T(8,128)(2,1)S(1)} %get-tuple-element.33), channel_id=1, source_target_pairs={{0,62},{1,63},{2,0},{3,1},{4,2},{5,3},{6,4},{7,5},{8,6},{9,7},{10,... | collective-permute-start | bytes 393224 | tf_op jit(solution)/shard_map/ppermute | solution.py:375
  13.9 4.4 %collective-permute-start.1 = (bf16[128,512]{1,0:T(8,128)(2,1)S(1)}, bf16[128,512]{1,0:T(8,128)(2,1)S(1)}, u32[]{:S(2)}, u32[]{:S(2)}) collective-permute-start(bf16[128,512]{1,0:T(8,128)(2,1)S(1)} %get-tuple-element.34), channel_id=1, source_target_pairs={{0,63},{1,0},{2,1},{3,2},{4,3},{5,4},{6,5},{7,6},{8,7},{9,8},{10,9... | collective-permute-start | bytes 393224 | tf_op jit(solution)/shard_map/ppermute | solution.py:375
  14.8 3.5 %collective-permute-start.2 = (bf16[128,512]{1,0:T(8,128)(2,1)S(1)}, bf16[128,512]{1,0:T(8,128)(2,1)S(1)}, u32[]{:S(2)}, u32[]{:S(2)}) collective-permute-start(bf16[128,512]{1,0:T(8,128)(2,1)S(1)} %get-tuple-element.36), channel_id=1, source_target_pairs={{0,1},{1,2},{2,3},{3,4},{4,5},{5,6},{6,7},{7,8},{8,9},{9,10},{10,1... | collective-permute-start | bytes 393224 | tf_op jit(solution)/shard_map/ppermute | solution.py:375
  15.6 9.1 %collective-permute-start.3 = (bf16[128,512]{1,0:T(8,128)(2,1)S(1)}, bf16[128,512]{1,0:T(8,128)(2,1)S(1)}, u32[]{:S(2)}, u32[]{:S(2)}) collective-permute-start(bf16[128,512]{1,0:T(8,128)(2,1)S(1)} %get-tuple-element.37), channel_id=1, source_target_pairs={{0,2},{1,3},{2,4},{3,5},{4,6},{5,7},{6,8},{7,9},{8,10},{9,11},{10,... | collective-permute-start | bytes 393224 | tf_op jit(solution)/shard_map/ppermute | solution.py:375
  24.7 0.8 copy-start.4
  25.4 8.1 %copy-start.2 = (bf16[256,256]{1,0:T(8,128)(2,1)S(1)}, bf16[256,256]{1,0:T(8,128)(2,1)}, u32[]{:S(2)}) copy-start(bf16[256,256]{1,0:T(8,128)(2,1)} %w2_ref.1) | copy-start | bytes 393220
  25.4 8.1 %copy-start.6 = (bf16[128,256]{1,0:T(8,128)(2,1)S(1)}, bf16[128,256]{1,0:T(8,128)(2,1)}, u32[]{:S(2)}) copy-start(bf16[128,256]{1,0:T(8,128)(2,1)} %w1_ref.1) | copy-start | bytes 196612
  25.4 8.1 %copy-start.7 = (bf16[256,128]{1,0:T(8,128)(2,1)S(1)}, bf16[256,128]{1,0:T(8,128)(2,1)}, u32[]{:S(2)}) copy-start(bf16[256,128]{1,0:T(8,128)(2,1)} %w3_ref.1) | copy-start | bytes 196612
  27.5 3.4 %collective-permute-start.4 = (bf16[2,512,128]{2,1,0:T(8,128)(2,1)S(1)}, bf16[2,512,128]{2,1,0:T(8,128)(2,1)S(1)}, u32[]{:S(2)}, u32[]{:S(2)}) collective-permute-start(bf16[2,512,128]{2,1,0:T(8,128)(2,1)S(1)} %get-tuple-element.39), channel_id=1, source_target_pairs={{0,1},{1,2},{2,3},{3,4},{4,5},{5,6},{6,7},{7,8},{8,9},{9,10},{10,1... | collective-permute-start | bytes 786440 | tf_op jit(solution)/shard_map/ppermute | solution.py:375
  27.6 5.9 %collective-permute-start.5 = (bf16[2,512,128]{2,1,0:T(8,128)(2,1)S(1)}, bf16[2,512,128]{2,1,0:T(8,128)(2,1)S(1)}, u32[]{:S(2)}, u32[]{:S(2)}) collective-permute-start(bf16[2,512,128]{2,1,0:T(8,128)(2,1)S(1)} %get-tuple-element.40), channel_id=1, source_target_pairs={{0,63},{1,0},{2,1},{3,2},{4,3},{5,4},{6,5},{7,6},{8,7},{9,8},{10,9... | collective-permute-start | bytes 786440 | tf_op jit(solution)/shard_map/ppermute | solution.py:375
  28.1 5.4 %copy-start.11 = (f32[256]{0:T(256)S(1)}, f32[256]{0:T(256)}, u32[]{:S(2)}) copy-start(f32[256]{0:T(256)} %param.21) | copy-start | bytes 3076
  33.5 0.7 copy-start.8
  33.5 0.7 copy-start.10
  41.5 4.6 %collective-permute-start.12 = (bf16[640,128]{1,0:T(8,128)(2,1)S(1)}, bf16[640,128]{1,0:T(8,128)(2,1)S(1)}, u32[]{:S(2)}, u32[]{:S(2)}) collective-permute-start(bf16[640,128]{1,0:T(8,128)(2,1)S(1)} %get-tuple-element.52), channel_id=1, source_target_pairs={{0,1},{1,0},{2,3},{3,2},{4,5},{5,4},{6,7},{7,6},{8,9},{9,8},{10,11... | collective-permute-start | bytes 491528 | tf_op jit(solution)/shard_map/ppermute | solution.py:478
  45.1 6.3 %collective-permute-start.6 = (bf16[2,512,128]{2,1,0:T(8,128)(2,1)}, bf16[2,512,128]{2,1,0:T(8,128)(2,1)S(1)}, u32[]{:S(2)}, u32[]{:S(2)}) collective-permute-start(bf16[2,512,128]{2,1,0:T(8,128)(2,1)} %get-tuple-element.43), channel_id=1, source_target_pairs={{0,1},{1,2},{2,3},{3,4},{4,5},{5,6},{6,7},{7,8},{8,9},{9,10},{10,1... | collective-permute-start | bytes 786440 | tf_op jit(solution)/shard_map/ppermute | solution.py:375
  45.1 6.4 %collective-permute-start.7 = (bf16[2,512,128]{2,1,0:T(8,128)(2,1)}, bf16[2,512,128]{2,1,0:T(8,128)(2,1)S(1)}, u32[]{:S(2)}, u32[]{:S(2)}) collective-permute-start(bf16[2,512,128]{2,1,0:T(8,128)(2,1)} %get-tuple-element.44), channel_id=1, source_target_pairs={{0,63},{1,0},{2,1},{3,2},{4,3},{5,4},{6,5},{7,6},{8,7},{9,8},{10,9... | collective-permute-start | bytes 786440 | tf_op jit(solution)/shard_map/ppermute | solution.py:375
  46.8 4.6 %copy-start.5 = (f32[4,4,512]{2,1,0:T(4,128)S(1)}, f32[4,4,512]{2,1,0:T(4,128)}, u32[]{:S(2)}) copy-start(f32[4,4,512]{2,1,0:T(4,128)} %weight_ref.1) | copy-start | bytes 98308
  46.8 11.6 %all-to-all-start = ((bf16[16,40,128]{2,1,0:T(8,128)(2,1)}), bf16[16,40,128]{2,1,0:T(8,128)(2,1)S(1)}, u32[]{:S(2)}, u32[]{:S(2)}) async-start(bf16[16,40,128]{2,1,0:T(8,128)(2,1)} %bitcast.9), calls=%async_computation | async-start | bytes 327680 | tf_op jit(solution)/shard_map/all_to_all | solution.py:480
  59.1 20.2 %all-to-all-start.1 = ((bf16[8,40,128]{2,1,0:T(8,128)(2,1)}), bf16[8,40,128]{2,1,0:T(8,128)(2,1)S(1)}, u32[]{:S(2)}, u32[]{:S(2)}) async-start(bf16[8,40,128]{2,1,0:T(8,128)(2,1)} %part_sum.1), calls=%async_computation.1 | async-start | bytes 163840 | tf_op jit(solution)/shard_map/all_to_all | solution.py:499
  65.6 7.7 %collective-permute-start.8 = (bf16[128,512]{1,0:T(8,128)(2,1)S(1)}, bf16[128,512]{1,0:T(8,128)(2,1)S(1)}, u32[]{:S(2)}, u32[]{:S(2)}) collective-permute-start(bf16[128,512]{1,0:T(8,128)(2,1)S(1)} %get-tuple-element.45), channel_id=1, source_target_pairs={{0,2},{1,3},{2,4},{3,5},{4,6},{5,7},{6,8},{7,9},{8,10},{9,11},{10,... | collective-permute-start | bytes 393224 | tf_op jit(solution)/shard_map/ppermute | solution.py:375
  66.2 7.2 %collective-permute-start.9 = (bf16[128,512]{1,0:T(8,128)(2,1)S(1)}, bf16[128,512]{1,0:T(8,128)(2,1)S(1)}, u32[]{:S(2)}, u32[]{:S(2)}) collective-permute-start(bf16[128,512]{1,0:T(8,128)(2,1)S(1)} %get-tuple-element.46), channel_id=1, source_target_pairs={{0,1},{1,2},{2,3},{3,4},{4,5},{5,6},{6,7},{7,8},{8,9},{9,10},{10,1... | collective-permute-start | bytes 393224 | tf_op jit(solution)/shard_map/ppermute | solution.py:375
  68.7 5.6 %collective-permute-start.10 = (bf16[128,512]{1,0:T(8,128)(2,1)S(1)}, bf16[128,512]{1,0:T(8,128)(2,1)S(1)}, u32[]{:S(2)}, u32[]{:S(2)}) collective-permute-start(bf16[128,512]{1,0:T(8,128)(2,1)S(1)} %get-tuple-element.48), channel_id=1, source_target_pairs={{0,63},{1,0},{2,1},{3,2},{4,3},{5,4},{6,5},{7,6},{8,7},{9,8},{10,9... | collective-permute-start | bytes 393224 | tf_op jit(solution)/shard_map/ppermute | solution.py:375
  68.7 7.4 %collective-permute-start.11 = (bf16[128,512]{1,0:T(8,128)(2,1)S(1)}, bf16[128,512]{1,0:T(8,128)(2,1)S(1)}, u32[]{:S(2)}, u32[]{:S(2)}) collective-permute-start(bf16[128,512]{1,0:T(8,128)(2,1)S(1)} %get-tuple-element.49), channel_id=1, source_target_pairs={{0,62},{1,63},{2,0},{3,1},{4,2},{5,3},{6,4},{7,5},{8,6},{9,7},{10,... | collective-permute-start | bytes 393224 | tf_op jit(solution)/shard_map/ppermute | solution.py:375
  91.6 4.5 %collective-permute-start.13 = (bf16[640,128]{1,0:T(8,128)(2,1)S(1)}, bf16[640,128]{1,0:T(8,128)(2,1)S(1)}, u32[]{:S(2)}, u32[]{:S(2)}) collective-permute-start(bf16[640,128]{1,0:T(8,128)(2,1)S(1)} %bitcast.16), channel_id=1, source_target_pairs={{0,1},{1,0},{2,3},{3,2},{4,5},{5,4},{6,7},{7,6},{8,9},{9,8},{10,11... | collective-permute-start | bytes 491528 | tf_op jit(solution)/shard_map/ppermute | solution.py:521

commit v3 on v2

v3 whole, which is shorter than its diff:
```python
import functools
import math

import jax
import jax.numpy as jnp
from jax import lax
from jax.experimental import pallas as pl
from jax.experimental.pallas import tpu as pltpu
from jax.sharding import Mesh
from jax.sharding import PartitionSpec as P

F32 = jnp.float32
BF16 = jnp.bfloat16
SPACE = ("z", "x", "core")
GELU_SCALE = math.sqrt(2.0 / math.pi)
GELU_CUBE = 0.044715
PART_ROWS = 40
TABLE_AT = 16
PREPARE_COST = 10**9
GATHER_COST = 10**10
PART_COST = 10**10
ADJOINT_COST = 10**11
SCATTER_COST = 10**11
CHOOSE_COST = 2 * 10**9

VMEM = pl.BlockSpec(memory_space=pltpu.VMEM)
ANY = pl.BlockSpec(memory_space=pl.ANY)
SMEM = pl.BlockSpec(memory_space=pltpu.SMEM)


def dot(left, right, left_dim=1, right_dim=0):
    return lax.dot_general(
        left,
        right,
        (((left_dim,), (right_dim,)), ((), ())),
        preferred_element_type=F32,
    )


def call(kernel, outs, ins, scratch=(), flops=0, name=None):
    nbytes = sum(math.prod(o.shape) * o.dtype.itemsize for o in outs)
    return pl.pallas_call(
        kernel,
        out_shape=outs,
        in_specs=ins,
        out_specs=[VMEM] * len(outs),
        scratch_shapes=list(scratch),
        compiler_params=pltpu.CompilerParams(vmem_limit_bytes=32 * 1024 * 1024),
        cost_estimate=pl.CostEstimate(
            flops=flops, bytes_accessed=2 * nbytes, transcendentals=0
        ),
        name=name,
    )


def quad_boxes(rows, counts, offsets, quads):
    lines = rows.shape[0]
    parts = lines // offsets
    share = quads // parts
    line_at = lax.broadcasted_iota(jnp.int32, rows.shape, 0)
    from_lane = lax.broadcasted_iota(jnp.int32, (quads, quads), 0)
    to_lane = lax.broadcasted_iota(jnp.int32, (quads, quads), 1)
    high = jnp.zeros(rows.shape, F32)
    low = jnp.zeros(rows.shape, F32)
    for part in range(parts):
        pick = (from_lane == 4 * (to_lane - part * share)).astype(F32).astype(BF16)
        here = jnp.where(line_at % parts == part, rows, 0)
        high = high + dot((here >> 3).astype(F32).astype(BF16), pick)
        low = low + dot((here & 7).astype(F32).astype(BF16), pick)
    gather = (
        lax.broadcasted_iota(jnp.int32, (8, lines), 1) // parts
        == lax.broadcasted_iota(jnp.int32, (8, lines), 0)
    ).astype(F32).astype(BF16)
    cells = dot(gather, high.astype(BF16)) * 8.0 + dot(gather, low.astype(BF16))
    cells = cells.astype(jnp.int32)
    offset_at = lax.broadcasted_iota(jnp.int32, cells.shape, 0)
    live = jnp.zeros(cells.shape, jnp.int32)
    for offset in range(offsets):
        live = jnp.where(offset_at == offset, counts[:, offset : offset + 1], live)
    slot_at = 4 * lax.broadcasted_iota(jnp.int32, cells.shape, 1)
    return jnp.where(slot_at < live, cells, -1)


def one_hot(mask):
    return mask.astype(F32).astype(BF16)


def choose_kernel(offsets, rows_ref, count_ref, cells_ref, select_ref):
    quads = cells_ref.shape[1]
    cells = quad_boxes(rows_ref[...], count_ref[...], offsets, quads)
    cells_ref[...] = cells
    columns = cells.astype(F32).T.astype(jnp.int32)
    box_at = lax.broadcasted_iota(jnp.int32, (quads, select_ref.shape[1]), 1)
    for offset in range(offsets):
        select_ref[offset * quads : (offset + 1) * quads] = one_hot(
            box_at == columns[:, offset : offset + 1]
        )


def pack_kernel(offsets, field_ref, select_ref, *refs):
    outs, pair = refs[:offsets], refs[offsets]
    band_rows, lon, ch = field_ref.shape
    quads = outs[0].shape[0]
    boxes = (band_rows - 1) * lon
    for row in range(band_rows):
        line = field_ref[row]
        pair[row * lon : (row + 1) * lon, :ch] = line
        pair[row * lon : (row + 1) * lon, ch:] = pltpu.roll(
            line.astype(F32), lon - 1, 0
        ).astype(BF16)
    for part in range(2):
        picked = dot(select_ref[...], pair[part * lon : part * lon + boxes]).astype(BF16)
        for offset in range(offsets):
            outs[offset][:, part * 2 * ch : (part + 1) * 2 * ch] = picked[
                offset * quads : (offset + 1) * quads
            ]


def prepare_kernel(slot_ref, weight_ref, helm_ref, b1_ref, b2_ref, table_ref):
    taps, band_rows, lon = weight_ref.shape
    ch = helm_ref.shape[1]
    hid = b1_ref.shape[1]
    table_ref[...] = jnp.zeros_like(table_ref)
    for tap in range(taps):
        table_ref[tap * band_rows : (tap + 1) * band_rows] = weight_ref[tap]
    at = taps * band_rows
    table_ref[at : at + band_rows] = (slot_ref[0] >> 2).astype(F32)
    helm = helm_ref[...]
    table_ref[at + 8 : at + 9, :ch] = helm
    table_ref[at + 8 : at + 9, ch : 2 * ch] = 1.0 / (1.0 + 4.0 * helm)
    table_ref[at + 9 : at + 10, :hid] = b1_ref[...]
    table_ref[at + 10 : at + 11, :hid] = b2_ref[...]


def coefficients(table_ref, at, ch):
    return table_ref[at + 8 : at + 9, :ch], table_ref[at + 8 : at + 9, ch : 2 * ch]


def interp_kernel(offsets, *refs):
    blocks = refs[:offsets]
    table_ref, dep_ref, up_ref, down_ref, table = refs[offsets:]
    band_rows, lon, ch = dep_ref.shape
    quads, wide = blocks[0].shape
    taps = wide // ch
    weights = table_ref[: taps * band_rows + 8].T
    columns = weights[:, taps * band_rows :].astype(jnp.int32)
    quad_at = lax.broadcasted_iota(jnp.int32, (lon, offsets * quads), 1)
    for offset in range(offsets):
        table[offset * quads : (offset + 1) * quads] = blocks[offset][...]
    for row in range(band_rows):
        tapped = dot(one_hot(quad_at == columns[:, row : row + 1]), table[...])
        line = jnp.zeros((lon, ch), F32)
        for tap in range(taps):
            at = tap * band_rows + row
            line = line + weights[:, at : at + 1] * tapped[:, tap * ch : (tap + 1) * ch]
        dep_ref[row] = line
        if row < 2:
            up_ref[row] = line.astype(BF16)
        if row >= band_rows - 2:
            down_ref[row - band_rows + 2] = line.astype(BF16)


def lon_sum(line):
    lon = line.shape[0]
    return pltpu.roll(line, 1, 0) + pltpu.roll(line, lon - 1, 0)


def gelu_parts(pre):
    square = pre * pre
    curve = jnp.tanh(pre * (GELU_SCALE + (GELU_SCALE * GELU_CUBE) * square))
    share = 0.5 + 0.5 * curve
    act = pre * share
    slope = share + (act - act * share) * (
        2.0 * GELU_SCALE + (6.0 * GELU_SCALE * GELU_CUBE) * square
    )
    return act, slope


def mlp_kernel(
    dep_ref,
    before_ref,
    after_ref,
    cot_ref,
    place_ref,
    table_ref,
    w1_ref,
    w2_ref,
    w3_ref,
    next_ref,
    scaled_ref,
    up_ref,
    down_ref,
    g1,
    gb1,
    g2,
    gb2,
    g3,
    once,
    smooth,
):
    band_rows, lon, ch = dep_ref.shape
    hid = w1_ref.shape[1]
    helm, inverse = coefficients(table_ref, TABLE_AT, ch)
    b1 = table_ref[TABLE_AT + 9 : TABLE_AT + 10, :hid]
    b2 = table_ref[TABLE_AT + 10 : TABLE_AT + 11, :hid]

    def departure(row):
        if row < 0:
            return before_ref[row + 2].astype(F32)
        if row >= band_rows:
            return after_ref[row - band_rows].astype(F32)
        return dep_ref[row]

    first = jnp.where(place_ref[0] == 0, 0.0, 1.0)
    last = jnp.where(place_ref[0] == place_ref[1] - 1, 0.0, 1.0)
    ahead = departure(-2) * first, departure(-1) * first
    behind = departure(band_rows) * last, departure(band_rows + 1) * last
    lines = {-2: ahead[0], -1: ahead[1], band_rows: behind[0], band_rows + 1: behind[1]}
    for row in range(-1, band_rows + 1):
        mid, above, below = (
            lines[r] if r in lines else departure(r) for r in (row, row - 1, row + 1)
        )
        value = (mid + helm * (above + below + lon_sum(mid))) * inverse
        if row < 0:
            value = value * first
        if row >= band_rows:
            value = value * last
        once[row + 1] = value
    for row in range(band_rows):
        value = (
            dep_ref[row] + helm * (once[row] + once[row + 2] + lon_sum(once[row + 1]))
        ) * inverse
        smooth[row] = value.astype(BF16)
    for total in (g1, gb1, g2, gb2, g3):
        total[...] = jnp.zeros_like(total)

    def one_row(row, carry):
        rows = smooth[row]
        cot = cot_ref[row]
        act, slope_first = gelu_parts(dot(rows, w1_ref[...]) + b1)
        act_first = act.astype(BF16)
        act, slope_second = gelu_parts(dot(act_first, w2_ref[...]) + b2)
        act_second = act.astype(BF16)
        next_ref[row] = (rows.astype(F32) + dot(act_second, w3_ref[...])).astype(BF16)
        g3[...] += dot(act_second, cot, 0, 0)
        gpre = dot(cot, w3_ref[...], 1, 1) * slope_second
        gpre_second = gpre.astype(BF16)
        gb2[...] += jnp.sum(gpre_second.astype(F32), axis=0, keepdims=True)
        g2[...] += dot(act_first, gpre_second, 0, 0)
        gpre = dot(gpre_second, w2_ref[...], 1, 1) * slope_first
        gpre_first = gpre.astype(BF16)
        gb1[...] += jnp.sum(gpre_first.astype(F32), axis=0, keepdims=True)
        g1[...] += dot(rows, gpre_first, 0, 0)
        gsmooth = cot.astype(F32) + dot(gpre_first, w1_ref[...], 1, 1)
        scaled_ref[row] = gsmooth * inverse
        return carry

    lax.fori_loop(0, band_rows, one_row, 0)
    for row in range(2):
        up_ref[row] = scaled_ref[row].astype(BF16)
        down_ref[row] = scaled_ref[band_rows - 2 + row].astype(BF16)


def gather_kernel(g1, gb1, g2, gb2, g3, grads_ref):
    ch = g1.shape[0]
    grads_ref[:ch] = g1[:, :ch].astype(BF16)
    grads_ref[ch : 2 * ch] = g1[:, ch:].astype(BF16)
    grads_ref[2 * ch : 4 * ch] = g2[:, :ch].astype(BF16)
    grads_ref[4 * ch : 6 * ch] = g2[:, ch:].astype(BF16)
    grads_ref[6 * ch : 8 * ch] = g3[...].astype(BF16)
    rest = grads_ref.shape[0] - 8 * ch
    row_at = lax.broadcasted_iota(jnp.int32, (rest, ch), 0)
    tail = jnp.zeros((rest, ch), F32)
    for index, line in enumerate((gb1[:, :ch], gb1[:, ch:], gb2[:, :ch], gb2[:, ch:])):
        tail = jnp.where(row_at == index, line, tail)
    grads_ref[8 * ch :] = tail.astype(BF16)


def adjoint_kernel(
    offsets,
    scaled_ref,
    before_ref,
    after_ref,
    place_ref,
    table_ref,
    *refs,
):
    outs, (once, spread, hit) = refs[:offsets], refs[offsets:]
    band_rows, lon, ch = scaled_ref.shape
    quads, wide = outs[0].shape
    taps = wide // ch
    helm, inverse = coefficients(table_ref, TABLE_AT, ch)
    first = jnp.where(place_ref[0] == 0, 0.0, 1.0)
    last = jnp.where(place_ref[0] == place_ref[1] - 1, 0.0, 1.0)
    weights = table_ref[:TABLE_AT].T
    quad_lanes = table_ref[TABLE_AT : TABLE_AT + 8].astype(jnp.int32)
    quad_at = lax.broadcasted_iota(jnp.int32, (offsets * quads, lon), 0)
    for row in range(band_rows):
        hit[:, row * lon : (row + 1) * lon] = one_hot(quad_at == quad_lanes[row : row + 1])

    def scaled(row):
        if row < 0:
            return before_ref[row + 2].astype(F32) * first
        if row >= band_rows:
            return after_ref[row - band_rows].astype(F32) * last
        return scaled_ref[row]

    for row in range(-1, band_rows + 1):
        value = (helm * inverse) * (scaled(row - 1) + scaled(row + 1) + lon_sum(scaled(row)))
        if row < 0:
            value = value * first
        if row >= band_rows:
            value = value * last
        once[row + 1] = value
    for row in range(band_rows):
        value = (
            scaled_ref[row]
            + once[row + 1]
            + helm * (once[row] + once[row + 2] + lon_sum(once[row + 1]))
        )
        for tap in range(taps):
            at = tap * band_rows + row
            spread[row * lon : (row + 1) * lon, tap * ch : (tap + 1) * ch] = (
                weights[:, at : at + 1] * value
            ).astype(BF16)
    slot_grads = dot(hit[...], spread[...]).astype(BF16)
    for offset in range(offsets):
        outs[offset][...] = slot_grads[offset * quads : (offset + 1) * quads]


def scatter_kernel(offsets, cells_ref, *refs):
    blocks = refs[:offsets]
    out_ref, done_ref, table, hit = refs[offsets:]
    done_ref[...] = jnp.zeros_like(done_ref)
    band_rows, lon, ch = out_ref.shape
    quads = blocks[0].shape[0]
    box_at = lax.broadcasted_iota(jnp.int32, ((band_rows - 1) * lon, quads), 0)
    for offset in range(offsets):
        table[offset * quads : (offset + 1) * quads] = blocks[offset][...]
        hit[:, offset * quads : (offset + 1) * quads] = one_hot(
            box_at == cells_ref[offset : offset + 1]
        )
    for row in range(band_rows):
        here = jnp.zeros((lon, ch), F32)
        right = jnp.zeros((lon, ch), F32)
        if row < band_rows - 1:
            both = dot(hit[row * lon : (row + 1) * lon], table[:, : 2 * ch])
            here = here + both[:, :ch]
            right = right + both[:, ch:]
        if row > 0:
            both = dot(hit[(row - 1) * lon : row * lon], table[:, 2 * ch :])
            here = here + both[:, :ch]
            right = right + both[:, ch:]
        out_ref[row] = here + pltpu.roll(right, 1, 0)


def sum_kernel(copies, parts_ref, ahead_ref, out_ref):
    total = parts_ref[0].astype(F32)
    for part in range(1, parts_ref.shape[0]):
        total = total + parts_ref[part].astype(F32)
    total = total.astype(BF16)
    for copy in range(copies):
        out_ref[copy] = total


def unpack_kernel(sums_ref, g1, gb1, g2, gb2, g3):
    ch, hid = g1.shape
    g1[:, :ch] = sums_ref[:ch].astype(F32)
    g1[:, ch:] = sums_ref[ch : 2 * ch].astype(F32)
    g2[:, :ch] = sums_ref[2 * ch : 4 * ch].astype(F32)
    g2[:, ch:] = sums_ref[4 * ch : 6 * ch].astype(F32)
    g3[...] = sums_ref[6 * ch : 8 * ch].astype(F32)
    tail = sums_ref[8 * ch : 8 * ch + 8].astype(F32)
    gb1[:, :ch], gb1[:, ch:] = tail[0:1], tail[1:2]
    gb2[:, :ch], gb2[:, ch:] = tail[2:3], tail[3:4]


def shifted(block, by, count):
    return lax.ppermute(block, SPACE, [(i, (i + by) % count) for i in range(count)])


def body(
    field,
    send_rows,
    send_count,
    dep_slot,
    dep_weight,
    helm_coef,
    w_first,
    b_first,
    w_second,
    b_second,
    w_third,
    cotangent,
):
    _, band_rows, lon, ch = field.shape
    hid = w_first.shape[1]
    offsets, slots = send_rows.shape[1:]
    taps = dep_slot.shape[0]
    reach = (offsets - 1) // 2
    quads = slots // 4
    bands = lax.axis_size(SPACE)
    shape = jax.ShapeDtypeStruct
    place = jnp.stack([lax.axis_index(SPACE).astype(jnp.int32), jnp.int32(bands)])
    block = shape((quads, taps * ch), BF16)
    edge = shape((2, lon, ch), BF16)
    lines = send_rows.reshape(offsets * slots // quads, quads)

    cells, select = call(
        functools.partial(choose_kernel, offsets),
        [
            shape((8, quads), jnp.int32),
            shape((offsets * quads, (band_rows - 1) * lon), BF16),
        ],
        [VMEM] * 2,
        flops=CHOOSE_COST,
        name="choose",
    )(lines, send_count)
    packed = call(
        functools.partial(pack_kernel, offsets),
        [block] * offsets,
        [VMEM] * 2,
        [pltpu.VMEM((band_rows * lon, 2 * ch), BF16)],
        name="pack",
    )(field[0], select)
    received = [
        packed[e] if e == reach else shifted(packed[e], e - reach, bands)
        for e in range(offsets)
    ]
    (table,) = call(
        prepare_kernel,
        [shape((TABLE_AT + 16, lon), F32)],
        [VMEM] * 5,
        flops=PREPARE_COST,
        name="prepare",
    )(
        dep_slot,
        dep_weight,
        helm_coef.reshape(1, ch),
        b_first.reshape(1, hid),
        b_second.reshape(1, hid),
    )
    departure, up, down = call(
        functools.partial(interp_kernel, offsets),
        [shape((band_rows, lon, ch), F32), edge, edge],
        [VMEM] * (offsets + 1),
        [pltpu.VMEM((offsets * quads, taps * ch), BF16)],
        name="interp",
    )(*received, table)
    before = shifted(down, 1, bands)
    after = shifted(up, -1, bands)
    groups = ("y", "x", "core")
    group = lax.axis_size(groups)
    depth = lax.axis_size("z")
    grad_shapes = [
        shape((ch, hid), F32),
        shape((1, hid), F32),
        shape((hid, hid), F32),
        shape((1, hid), F32),
        shape((hid, ch), F32),
    ]
    next_state, scaled, up, down, *grads = call(
        mlp_kernel,
        [shape((band_rows, lon, ch), BF16), shape((band_rows, lon, ch), F32), edge, edge]
        + grad_shapes,
        [VMEM] * 4 + [SMEM] + [VMEM] * 4,
        [
            pltpu.VMEM((band_rows + 2, lon, ch), F32),
            pltpu.VMEM((band_rows, lon, ch), BF16),
        ],
        name="smooth_mlp",
    )(departure, before, after, cotangent[0], place, table, w_first, w_second, w_third)
    before = shifted(down, 1, bands)
    after = shifted(up, -1, bands)

    (grads,) = call(
        gather_kernel,
        [shape((group * PART_ROWS, ch), BF16)],
        [VMEM] * 5,
        flops=GATHER_COST,
        name="gather",
    )(*grads)
    parts = lax.all_to_all(grads.reshape(group, PART_ROWS, ch), groups, 0, 0)
    slot_grads = call(
        functools.partial(adjoint_kernel, offsets),
        [block] * offsets,
        [VMEM] * 3 + [SMEM, VMEM],
        [
            pltpu.VMEM((band_rows + 2, lon, ch), F32),
            pltpu.VMEM((band_rows * lon, taps * ch), BF16),
            pltpu.VMEM((offsets * quads, band_rows * lon), BF16),
        ],
        flops=ADJOINT_COST,
        name="adjoint",
    )(scaled, before, after, place, table)
    (part_sum,) = call(
        functools.partial(sum_kernel, depth),
        [shape((depth, PART_ROWS, ch), BF16)],
        [VMEM, ANY],
        flops=PART_COST,
        name="part_sum",
    )(parts, slot_grads[reach])
    parts = lax.all_to_all(part_sum, "z", 0, 0)
    back = [
        slot_grads[e] if e == reach else shifted(slot_grads[e], reach - e, bands)
        for e in range(offsets)
    ]
    field_grad, done = call(
        functools.partial(scatter_kernel, offsets),
        [shape((band_rows, lon, ch), F32), shape((8, ch), F32)],
        [VMEM] * (offsets + 1),
        [
            pltpu.VMEM((offsets * quads, taps * ch), BF16),
            pltpu.VMEM(((band_rows - 1) * lon, offsets * quads), BF16),
        ],
        flops=SCATTER_COST,
        name="scatter",
    )(cells, *back)
    (whole_sum,) = call(
        functools.partial(sum_kernel, group),
        [shape((group, PART_ROWS, ch), BF16)],
        [VMEM, ANY],
        name="whole_sum",
    )(parts, done)
    sums = lax.all_to_all(whole_sum, groups, 0, 0).reshape(group * PART_ROWS, ch)
    grads = call(
        unpack_kernel,
        grad_shapes,
        [VMEM],
        name="unpack",
    )(sums)
    return (
        next_state[None],
        field_grad[None],
        grads[0],
        grads[1].reshape(hid),
        grads[2],
        grads[3].reshape(hid),
        grads[4],
    )


def solution(mesh):
    fine = Mesh(mesh.devices.reshape(4, 8, 4, 2), ("y",) + SPACE)
    state = P("y", SPACE, None, None)
    return jax.shard_map(
        body,
        mesh=fine,
        in_specs=(
            state,
            P(SPACE, None, None),
            P(SPACE, None),
            P(None, SPACE, None),
            P(None, SPACE, None),
            P(),
            P(),
            P(),
            P(),
            P(),
            P(),
            state,
        ),
        out_specs=(state, state, P(), P(), P(), P(), P()),
        check_vma=False,
    )
```

time: 98.3 us -> 92.6 us (0.942)
  blocking collectives: 12.3 us -> 16.7 us
  waiting for transfers between devices: 22.4 us -> 19.2 us
  local copies, waits for them, and re-layouts: 3.84 us -> 0.92 us
  starting transfers between devices: 37.4 us -> 34.5 us
  Pallas kernels: 20.7 us -> 19.3 us
    ppermute x2 -> x0, starting transfers between devices: 7.08 us -> none  [the longest x1 3.61 us: body(): gained = lax.ppermute(give, 'core', swap)]
    all_to_all x1, starting transfers between devices: 4.61 us -> 9.69 us  [body(): parts = lax.all_to_all(grads.reshape(group, PART_ROWS, ch), groups, 0, 0)]
    all_to_all x1, waiting for transfers between devices: 0.01 us -> 4.89 us  [body(): parts = lax.all_to_all(part_sum, 'z', 0, 0)]
    all_to_all x1, blocking collectives: 12.3 us -> 16.7 us  [body(): lax.all_to_all(whole_sum, groups, 0, 0).reshape(group * PART_ROWS, ch)]
    all_to_all x1, waiting for transfers between devices: 3.67 us -> 0.01 us  [body(): parts = lax.all_to_all(grads.reshape(group, PART_ROWS, ch), groups, 0, 0)]
    all_to_all x1, starting transfers between devices: 6.51 us -> 3.36 us  [body(): parts = lax.all_to_all(part_sum, 'z', 0, 0)]
    ppermute x12, waiting for transfers between devices: 17.2 us -> 14.3 us  [shifted(): lax.ppermute(block, SPACE, [(i, (i + by) % count) for i in range(count)])]
    unnamed x25 -> x22, local copies, waits for them, and re-layouts: 3.84 us -> 0.92 us
  transfers between devices with their start and end apart: 16 -> 14, of which waited for: 11 -> 7; matrix products, arithmetic and copies ran while one was open for 0% -> 0% of each run, Pallas kernels for 7% -> 8%
where the time goes in v3:
time: 92.6 us; the launch traced here: 92.2 us
  starting transfers between devices  34.5 us (37%)
  Pallas kernels  19.3 us (21%)
  waiting for transfers between devices  19.2 us (21%)
  blocking collectives  16.7 us (18%)
    ppermute x12, starting transfers between devices, shifted(): lax.ppermute(block, SPACE, [(i, (i + by) % count) for i in range(count)])  21.4 us
    all_to_all x1, blocking collectives, body(): lax.all_to_all(whole_sum, groups, 0, 0).reshape(group * PART_ROWS, ch)  16.7 us
    ppermute x12, waiting for transfers between devices, shifted(): lax.ppermute(block, SPACE, [(i, (i + by) % count) for i in range(count)])  14.3 us
    all_to_all x1, starting transfers between devices, body(): parts = lax.all_to_all(grads.reshape(group, PART_ROWS, ch), groups, 0, 0)  9.69 us
    pallas_call x1, Pallas kernels, body(): call(mlp_kernel, [shape((band_rows, lon, ch), BF16), shape((band_rows, lo...  7.11 us
    all_to_all x1, waiting for transfers between devices, body(): parts = lax.all_to_all(part_sum, 'z', 0, 0)  4.89 us
    all_to_all x1, starting transfers between devices, body(): parts = lax.all_to_all(part_sum, 'z', 0, 0)  3.36 us
    pallas_call x1, Pallas kernels, body(): call(functools.partial(adjoint_kernel, offsets), [block] * offsets, [VMEM...  3.34 us
  transfers between devices with their start and end apart: 14, of which 7 were waited for; matrix products, arithmetic and copies ran while one was open for 0% of the time, Pallas kernels for 8%

profile of v3, /device:TPU:1, one launch (start us, length us, event | category | flops | bytes accessed | tf_op | source)
XLA Modules:
  0.0 92.2 jit_solution(7095805729771580751)
XLA Ops:
  0.6 0.7 reduce
  1.4 0.0 copy-start.9
  1.4 0.6 copy-done.9
  2.0 0.0 copy-start
  2.0 0.8 choose.1
  2.8 0.0 copy-start.5
  2.8 0.0 copy-start.6
  2.8 0.0 copy-start.7
  2.8 0.0 copy-start.8
  2.9 0.0 copy-start.10
  2.9 0.2 copy-done
  3.1 1.3 %pack.1 = (bf16[128,512]{1,0:T(8,128)(2,1)S(1)}, bf16[128,512]{1,0:T(8,128)(2,1)S(1)}, bf16[128,512]{1,0:T(8,128)(2,1)S(1)}, bf16[128,512]{1,0:T(8,128)(2,1)S(1)}, bf16[128,512]{1,0:T(8,128)(2,1)S(1)}) custom-call(bf16[4,512,128]{2,1,0:T(8,128)(2,1)S(1)} %bitcast.13, bf16[640,1536]{1,0:T(8,128)(2,1)S(1)} %get-tuple-element.38.select_ref), custom_call_target="tpu_custom_call" | custom-call | bytes 1310720 | tf_op jit(solution)/shard_map/pack/pallas_call | solution.py:419
  4.4 8.7 %collective-permute-start = (bf16[128,512]{1,0:T(8,128)(2,1)S(1)}, bf16[128,512]{1,0:T(8,128)(2,1)S(1)}, u32[]{:S(2)}, u32[]{:S(2)}) collective-permute-start(bf16[128,512]{1,0:T(8,128)(2,1)S(1)} %get-tuple-element.39), channel_id=1, source_target_pairs={{0,62},{1,63},{2,0},{3,1},{4,2},{5,3},{6,4},{7,5},{8,6},{9,7},{10,... | collective-permute-start | bytes 393224 | tf_op jit(solution)/shard_map/ppermute | solution.py:379
  13.1 1.0 %collective-permute-start.1 = (bf16[128,512]{1,0:T(8,128)(2,1)S(1)}, bf16[128,512]{1,0:T(8,128)(2,1)S(1)}, u32[]{:S(2)}, u32[]{:S(2)}) collective-permute-start(bf16[128,512]{1,0:T(8,128)(2,1)S(1)} %get-tuple-element.40), channel_id=1, source_target_pairs={{0,63},{1,0},{2,1},{3,2},{4,3},{5,4},{6,5},{7,6},{8,7},{9,8},{10,9... | collective-permute-start | bytes 393224 | tf_op jit(solution)/shard_map/ppermute | solution.py:379
  14.1 0.8 collective-permute-start.2
  14.8 0.0 collective-permute-start.3
  14.8 0.0 copy-done.5
  14.9 0.0 copy-done.6
  14.9 0.0 copy-done.7
  14.9 0.0 copy-done.8
  14.9 0.0 copy-done.10
  14.9 0.0 copy-start.1
  14.9 0.0 copy-start.2
  14.9 0.0 copy-start.3
  14.9 0.0 copy-start.4
  15.0 0.3 collective-permute-done.refs_0_
  15.2 2.3 %collective-permute-done.1.refs_1_ = bf16[128,512]{1,0:T(8,128)(2,1)S(1)} collective-permute-done((bf16[128,512]{1,0:T(8,128)(2,1)S(1)}, bf16[128,512]{1,0:T(8,128)(2,1)S(1)}, u32[]{:S(2)}, u32[]{:S(2)}) %collective-permute-start.1) | collective-permute-done | bytes 131104 | tf_op jit(solution)/shard_map/ppermute | solution.py:379
  17.5 0.1 collective-permute-done.2.refs_3_
  17.6 6.3 %collective-permute-done.3.refs_4_ = bf16[128,512]{1,0:T(8,128)(2,1)S(1)} collective-permute-done((bf16[128,512]{1,0:T(8,128)(2,1)S(1)}, bf16[128,512]{1,0:T(8,128)(2,1)S(1)}, u32[]{:S(2)}, u32[]{:S(2)}) %collective-permute-start.3) | collective-permute-done | bytes 131104 | tf_op jit(solution)/shard_map/ppermute | solution.py:379
  23.9 2.0 %interp.1 = (f32[4,512,128]{2,1,0:T(8,128)S(1)}, bf16[2,512,128]{2,1,0:T(8,128)(2,1)S(1)}, bf16[2,512,128]{2,1,0:T(8,128)(2,1)S(1)}) custom-call(bf16[128,512]{1,0:T(8,128)(2,1)S(1)} %collective-permute-done.refs_0_, bf16[128,512]{1,0:T(8,128)(2,1)S(1)} %collective-permute-done.1.refs_1_, bf16[128,512]{1,0:T(8,128)(2,1)S(1)} %get-tuple-element.41.refs_2_, ...), custom_call_target="tpu_custom_call" | custom-call | bytes 3145728 | tf_op jit(solution)/shard_map/interp/pallas_call | solution.py:443
  25.9 0.1 collective-permute-start.4
  26.0 0.5 collective-permute-start.5
  26.5 0.1 pad_add_fusion.place_ref
  26.6 2.7 %collective-permute-done.4.before_ref = bf16[2,512,128]{2,1,0:T(8,128)(2,1)S(1)} collective-permute-done((bf16[2,512,128]{2,1,0:T(8,128)(2,1)S(1)}, bf16[2,512,128]{2,1,0:T(8,128)(2,1)S(1)}, u32[]{:S(2)}, u32[]{:S(2)}) %collective-permute-start.4) | collective-permute-done | bytes 262176 | tf_op jit(solution)/shard_map/ppermute | solution.py:379
  29.3 2.6 %collective-permute-done.5.after_ref = bf16[2,512,128]{2,1,0:T(8,128)(2,1)S(1)} collective-permute-done((bf16[2,512,128]{2,1,0:T(8,128)(2,1)S(1)}, bf16[2,512,128]{2,1,0:T(8,128)(2,1)S(1)}, u32[]{:S(2)}, u32[]{:S(2)}) %collective-permute-start.5) | collective-permute-done | bytes 262176 | tf_op jit(solution)/shard_map/ppermute | solution.py:379
  31.9 0.0 copy-done.1
  31.9 0.0 copy-done.2
  31.9 0.0 copy-done.3
  31.9 0.0 copy-done.4
  31.9 7.1 %smooth_mlp.1 = (bf16[4,512,128]{2,1,0:T(8,128)(2,1)}, f32[4,512,128]{2,1,0:T(8,128)S(1)}, bf16[2,512,128]{2,1,0:T(8,128)(2,1)}, bf16[2,512,128]{2,1,0:T(8,128)(...) custom-call(f32[4,512,128]{2,1,0:T(8,128)S(1)} %get-tuple-element.44, ...), custom_call_target="tpu_custom_call" | custom-call | bytes 5246976 | tf_op jit(solution)/shard_map/smooth_mlp/pallas_call | solution.py:462
  39.0 0.0 collective-permute-start.6
  39.0 3.6 %collective-permute-start.7 = (bf16[2,512,128]{2,1,0:T(8,128)(2,1)}, bf16[2,512,128]{2,1,0:T(8,128)(2,1)S(1)}, u32[]{:S(2)}, u32[]{:S(2)}) collective-permute-start(bf16[2,512,128]{2,1,0:T(8,128)(2,1)} %get-tuple-element.51), channel_id=1, source_target_pairs={{0,63},{1,0},{2,1},{3,2},{4,3},{5,4},{6,5},{7,6},{8,7},{9,8},{10,9... | collective-permute-start | bytes 786440 | tf_op jit(solution)/shard_map/ppermute | solution.py:379
  42.6 0.8 gather.1
  43.4 9.7 %all-to-all-start = ((bf16[32,40,128]{2,1,0:T(8,128)(2,1)}), bf16[32,40,128]{2,1,0:T(8,128)(2,1)S(1)}, u32[]{:S(2)}, u32[]{:S(2)}) async-start(bf16[32,40,128]{2,1,0:T(8,128)(2,1)} %bitcast.8), calls=%async_computation | async-start | bytes 655360 | tf_op jit(solution)/shard_map/all_to_all | solution.py:483
  53.1 0.0 collective-permute-done.6.before_ref
  53.1 0.0 collective-permute-done.7.after_ref
  53.1 3.3 %adjoint.1 = (bf16[128,512]{1,0:T(8,128)(2,1)S(1)}, bf16[128,512]{1,0:T(8,128)(2,1)S(1)}, bf16[128,512]{1,0:T(8,128)(2,1)S(1)}, bf16[128,512]{1,0:T(8,128)(2,1)S(1)}, bf16[128,512]{1,0:T(8,128)(2,1)S(1)}) custom-call(f32[4,512,128]{2,1,0:T(8,128)S(1)} %get-tuple-element.49.scaled_ref, bf16[2,512,128]{2,1,0:T(8,128)(2,1)S(1)} %collective-permute-done.6.before_ref, ...), custom_call_target="tpu_custom_call" | custom-call | flops 99999997952 | bytes 1310720 | tf_op jit(solution)/shard_map/adjoint/pallas_call | solution.py:484
  56.5 1.5 %collective-permute-start.8 = (bf16[128,512]{1,0:T(8,128)(2,1)S(1)}, bf16[128,512]{1,0:T(8,128)(2,1)S(1)}, u32[]{:S(2)}, u32[]{:S(2)}) collective-permute-start(bf16[128,512]{1,0:T(8,128)(2,1)S(1)} %get-tuple-element.52), channel_id=1, source_target_pairs={{0,2},{1,3},{2,4},{3,5},{4,6},{5,7},{6,8},{7,9},{8,10},{9,11},{10,... | collective-permute-start | bytes 393224 | tf_op jit(solution)/shard_map/ppermute | solution.py:379
  57.9 1.7 %collective-permute-start.9 = (bf16[128,512]{1,0:T(8,128)(2,1)S(1)}, bf16[128,512]{1,0:T(8,128)(2,1)S(1)}, u32[]{:S(2)}, u32[]{:S(2)}) collective-permute-start(bf16[128,512]{1,0:T(8,128)(2,1)S(1)} %get-tuple-element.53), channel_id=1, source_target_pairs={{0,1},{1,2},{2,3},{3,4},{4,5},{5,6},{6,7},{7,8},{8,9},{9,10},{10,1... | collective-permute-start | bytes 393224 | tf_op jit(solution)/shard_map/ppermute | solution.py:379
  59.6 0.0 collective-permute-start.10
  59.7 3.6 %collective-permute-start.11 = (bf16[128,512]{1,0:T(8,128)(2,1)S(1)}, bf16[128,512]{1,0:T(8,128)(2,1)S(1)}, u32[]{:S(2)}, u32[]{:S(2)}) collective-permute-start(bf16[128,512]{1,0:T(8,128)(2,1)S(1)} %get-tuple-element.56), channel_id=1, source_target_pairs={{0,62},{1,63},{2,0},{3,1},{4,2},{5,3},{6,4},{7,5},{8,6},{9,7},{10,... | collective-permute-start | bytes 393224 | tf_op jit(solution)/shard_map/ppermute | solution.py:379
  63.3 0.0 all-to-all-done.parts_ref
  63.3 0.7 part_sum.1
  64.0 3.4 %all-to-all-start.1 = ((bf16[8,40,128]{2,1,0:T(8,128)(2,1)}), bf16[8,40,128]{2,1,0:T(8,128)(2,1)S(1)}, u32[]{:S(2)}, u32[]{:S(2)}) async-start(bf16[8,40,128]{2,1,0:T(8,128)(2,1)} %part_sum.1), calls=%async_computation.1 | async-start | bytes 163840 | tf_op jit(solution)/shard_map/all_to_all | solution.py:503
  67.4 0.0 collective-permute-done.8.refs_0_
  67.4 0.0 collective-permute-done.9.refs_1_
  67.4 0.0 collective-permute-done.10.refs_3_
  67.4 0.0 collective-permute-done.11.refs_4_
  67.4 2.4 %scatter.1 = (f32[4,512,128]{2,1,0:T(8,128)}, f32[8,128]{1,0:T(8,128)S(1)}) custom-call(s32[8,128]{1,0:T(8,128)S(1)} %get-tuple-element.48.cells_ref, bf16[128,512]{1,0:T(8,128)(2,1)S(1)} %collective-permute-done.8.refs_0_, bf16[128,512]{1,0:T(8,128)(2,1)S(1)} %collective-permute-done.9.refs_1_, bf16[128,512]{1,0:T(8,128)(2,1)S(1)} %get-tuple-element.54.refs_2_.ahead_ref, ...), custom_call_target="tpu_custom_call" | custom-call | flops 99999997952 | bytes 2105344 | tf_op jit(solution)/shard_map/scatter/pallas_call | solution.py:508
  69.8 4.9 %all-to-all-done.1.parts_ref = bf16[8,40,128]{2,1,0:T(8,128)(2,1)S(1)} async-done(((bf16[8,40,128]{2,1,0:T(8,128)(2,1)}), bf16[8,40,128]{2,1,0:T(8,128)(2,1)S(1)}, u32[]{:S(2)}, u32[]{:S(2)}) %all-to-all-start.1) | async-done | bytes 81952 | tf_op jit(solution)/shard_map/all_to_all | solution.py:503
  74.7 16.7 %all_to_all.15 = bf16[32,40,128]{2,1,0:T(8,128)(2,1)S(1)} all-to-all(bf16[32,40,128]{2,1,0:T(8,128)(2,1)S(1)} %whole_sum.1), channel_id=1, replica_groups=mesh['y'=4,'z'=8,'x'=4,'core'=2] {'y','x','core'}, dimensions={0} | all-to-all | bytes 655360 | tf_op jit(solution)/shard_map/all_to_all | solution.py:525
  91.4 0.8 unpack.1
  (3 shorter events, 0.0 us)
Async XLA Ops:
  1.4 0.7 copy-start.9
  2.0 1.0 %copy-start = (bf16[1,4,512,128]{3,2,1,0:T(8,128)(2,1)S(1)}, bf16[1,4,512,128]{3,2,1,0:T(8,128)(2,1)}, u32[]{:S(2)}) copy-start(bf16[1,4,512,128]{3,2,1,0:T(8,128)(2,1)} %param.12) | copy-start | bytes 1572868
  2.8 12.0 %copy-start.5 = (s32[4,4,512]{2,1,0:T(4,128)S(1)}, s32[4,4,512]{2,1,0:T(4,128)}, u32[]{:S(2)}) copy-start(s32[4,4,512]{2,1,0:T(4,128)} %slot_ref.1) | copy-start | bytes 98308
  2.8 12.0 %copy-start.6 = (f32[4,4,512]{2,1,0:T(4,128)S(1)}, f32[4,4,512]{2,1,0:T(4,128)}, u32[]{:S(2)}) copy-start(f32[4,4,512]{2,1,0:T(4,128)} %weight_ref.1) | copy-start | bytes 98308
  2.8 12.0 %copy-start.7 = (f32[256]{0:T(256)S(1)}, f32[256]{0:T(256)}, u32[]{:S(2)}) copy-start(f32[256]{0:T(256)} %param.19) | copy-start | bytes 3076
  2.8 12.0 %copy-start.8 = (f32[256]{0:T(256)S(1)}, f32[256]{0:T(256)}, u32[]{:S(2)}) copy-start(f32[256]{0:T(256)} %param.21) | copy-start | bytes 3076
  2.9 12.0 %copy-start.10 = (f32[128]{0:T(128)S(1)}, f32[128]{0:T(128)}, u32[]{:S(2)}) copy-start(f32[128]{0:T(128)} %param.17) | copy-start | bytes 1540
  4.4 10.8 %collective-permute-start = (bf16[128,512]{1,0:T(8,128)(2,1)S(1)}, bf16[128,512]{1,0:T(8,128)(2,1)S(1)}, u32[]{:S(2)}, u32[]{:S(2)}) collective-permute-start(bf16[128,512]{1,0:T(8,128)(2,1)S(1)} %get-tuple-element.39), channel_id=1, source_target_pairs={{0,62},{1,63},{2,0},{3,1},{4,2},{5,3},{6,4},{7,5},{8,6},{9,7},{10,... | collective-permute-start | bytes 393224 | tf_op jit(solution)/shard_map/ppermute | solution.py:379
  13.1 4.4 %collective-permute-start.1 = (bf16[128,512]{1,0:T(8,128)(2,1)S(1)}, bf16[128,512]{1,0:T(8,128)(2,1)S(1)}, u32[]{:S(2)}, u32[]{:S(2)}) collective-permute-start(bf16[128,512]{1,0:T(8,128)(2,1)S(1)} %get-tuple-element.40), channel_id=1, source_target_pairs={{0,63},{1,0},{2,1},{3,2},{4,3},{5,4},{6,5},{7,6},{8,7},{9,8},{10,9... | collective-permute-start | bytes 393224 | tf_op jit(solution)/shard_map/ppermute | solution.py:379
  14.1 3.5 %collective-permute-start.2 = (bf16[128,512]{1,0:T(8,128)(2,1)S(1)}, bf16[128,512]{1,0:T(8,128)(2,1)S(1)}, u32[]{:S(2)}, u32[]{:S(2)}) collective-permute-start(bf16[128,512]{1,0:T(8,128)(2,1)S(1)} %get-tuple-element.42), channel_id=1, source_target_pairs={{0,1},{1,2},{2,3},{3,4},{4,5},{5,6},{6,7},{7,8},{8,9},{9,10},{10,1... | collective-permute-start | bytes 393224 | tf_op jit(solution)/shard_map/ppermute | solution.py:379
  14.8 9.1 %collective-permute-start.3 = (bf16[128,512]{1,0:T(8,128)(2,1)S(1)}, bf16[128,512]{1,0:T(8,128)(2,1)S(1)}, u32[]{:S(2)}, u32[]{:S(2)}) collective-permute-start(bf16[128,512]{1,0:T(8,128)(2,1)S(1)} %get-tuple-element.43), channel_id=1, source_target_pairs={{0,2},{1,3},{2,4},{3,5},{4,6},{5,7},{6,8},{7,9},{8,10},{9,11},{10,... | collective-permute-start | bytes 393224 | tf_op jit(solution)/shard_map/ppermute | solution.py:379
  14.9 17.0 %copy-start.1 = (bf16[1,4,512,128]{3,2,1,0:T(8,128)(2,1)S(1)}, bf16[1,4,512,128]{3,2,1,0:T(8,128)(2,1)}, u32[]{:S(2)}) copy-start(bf16[1,4,512,128]{3,2,1,0:T(8,128)(2,1)} %param.23) | copy-start | bytes 1572868
  14.9 17.0 %copy-start.2 = (bf16[256,256]{1,0:T(8,128)(2,1)S(1)}, bf16[256,256]{1,0:T(8,128)(2,1)}, u32[]{:S(2)}) copy-start(bf16[256,256]{1,0:T(8,128)(2,1)} %w2_ref.1) | copy-start | bytes 393220
  14.9 17.0 %copy-start.3 = (bf16[128,256]{1,0:T(8,128)(2,1)S(1)}, bf16[128,256]{1,0:T(8,128)(2,1)}, u32[]{:S(2)}) copy-start(bf16[128,256]{1,0:T(8,128)(2,1)} %w1_ref.1) | copy-start | bytes 196612
  14.9 17.0 %copy-start.4 = (bf16[256,128]{1,0:T(8,128)(2,1)S(1)}, bf16[256,128]{1,0:T(8,128)(2,1)}, u32[]{:S(2)}) copy-start(bf16[256,128]{1,0:T(8,128)(2,1)} %w3_ref.1) | copy-start | bytes 196612
  25.9 3.4 %collective-permute-start.4 = (bf16[2,512,128]{2,1,0:T(8,128)(2,1)S(1)}, bf16[2,512,128]{2,1,0:T(8,128)(2,1)S(1)}, u32[]{:S(2)}, u32[]{:S(2)}) collective-permute-start(bf16[2,512,128]{2,1,0:T(8,128)(2,1)S(1)} %get-tuple-element.45), channel_id=1, source_target_pairs={{0,1},{1,2},{2,3},{3,4},{4,5},{5,6},{6,7},{7,8},{8,9},{9,10},{10,1... | collective-permute-start | bytes 786440 | tf_op jit(solution)/shard_map/ppermute | solution.py:379
  26.0 5.9 %collective-permute-start.5 = (bf16[2,512,128]{2,1,0:T(8,128)(2,1)S(1)}, bf16[2,512,128]{2,1,0:T(8,128)(2,1)S(1)}, u32[]{:S(2)}, u32[]{:S(2)}) collective-permute-start(bf16[2,512,128]{2,1,0:T(8,128)(2,1)S(1)} %get-tuple-element.46), channel_id=1, source_target_pairs={{0,63},{1,0},{2,1},{3,2},{4,3},{5,4},{6,5},{7,6},{8,7},{9,8},{10,9... | collective-permute-start | bytes 786440 | tf_op jit(solution)/shard_map/ppermute | solution.py:379
  39.0 14.1 %collective-permute-start.6 = (bf16[2,512,128]{2,1,0:T(8,128)(2,1)}, bf16[2,512,128]{2,1,0:T(8,128)(2,1)S(1)}, u32[]{:S(2)}, u32[]{:S(2)}) collective-permute-start(bf16[2,512,128]{2,1,0:T(8,128)(2,1)} %get-tuple-element.50), channel_id=1, source_target_pairs={{0,1},{1,2},{2,3},{3,4},{4,5},{5,6},{6,7},{7,8},{8,9},{9,10},{10,1... | collective-permute-start | bytes 786440 | tf_op jit(solution)/shard_map/ppermute | solution.py:379
  39.0 14.1 %collective-permute-start.7 = (bf16[2,512,128]{2,1,0:T(8,128)(2,1)}, bf16[2,512,128]{2,1,0:T(8,128)(2,1)S(1)}, u32[]{:S(2)}, u32[]{:S(2)}) collective-permute-start(bf16[2,512,128]{2,1,0:T(8,128)(2,1)} %get-tuple-element.51), channel_id=1, source_target_pairs={{0,63},{1,0},{2,1},{3,2},{4,3},{5,4},{6,5},{7,6},{8,7},{9,8},{10,9... | collective-permute-start | bytes 786440 | tf_op jit(solution)/shard_map/ppermute | solution.py:379
  43.4 19.9 %all-to-all-start = ((bf16[32,40,128]{2,1,0:T(8,128)(2,1)}), bf16[32,40,128]{2,1,0:T(8,128)(2,1)S(1)}, u32[]{:S(2)}, u32[]{:S(2)}) async-start(bf16[32,40,128]{2,1,0:T(8,128)(2,1)} %bitcast.8), calls=%async_computation | async-start | bytes 655360 | tf_op jit(solution)/shard_map/all_to_all | solution.py:483
  56.5 10.9 %collective-permute-start.8 = (bf16[128,512]{1,0:T(8,128)(2,1)S(1)}, bf16[128,512]{1,0:T(8,128)(2,1)S(1)}, u32[]{:S(2)}, u32[]{:S(2)}) collective-permute-start(bf16[128,512]{1,0:T(8,128)(2,1)S(1)} %get-tuple-element.52), channel_id=1, source_target_pairs={{0,2},{1,3},{2,4},{3,5},{4,6},{5,7},{6,8},{7,9},{8,10},{9,11},{10,... | collective-permute-start | bytes 393224 | tf_op jit(solution)/shard_map/ppermute | solution.py:379
  57.9 9.4 %collective-permute-start.9 = (bf16[128,512]{1,0:T(8,128)(2,1)S(1)}, bf16[128,512]{1,0:T(8,128)(2,1)S(1)}, u32[]{:S(2)}, u32[]{:S(2)}) collective-permute-start(bf16[128,512]{1,0:T(8,128)(2,1)S(1)} %get-tuple-element.53), channel_id=1, source_target_pairs={{0,1},{1,2},{2,3},{3,4},{4,5},{5,6},{6,7},{7,8},{8,9},{9,10},{10,1... | collective-permute-start | bytes 393224 | tf_op jit(solution)/shard_map/ppermute | solution.py:379
  59.6 7.7 %collective-permute-start.10 = (bf16[128,512]{1,0:T(8,128)(2,1)S(1)}, bf16[128,512]{1,0:T(8,128)(2,1)S(1)}, u32[]{:S(2)}, u32[]{:S(2)}) collective-permute-start(bf16[128,512]{1,0:T(8,128)(2,1)S(1)} %get-tuple-element.55), channel_id=1, source_target_pairs={{0,63},{1,0},{2,1},{3,2},{4,3},{5,4},{6,5},{7,6},{8,7},{9,8},{10,9... | collective-permute-start | bytes 393224 | tf_op jit(solution)/shard_map/ppermute | solution.py:379
  59.7 7.7 %collective-permute-start.11 = (bf16[128,512]{1,0:T(8,128)(2,1)S(1)}, bf16[128,512]{1,0:T(8,128)(2,1)S(1)}, u32[]{:S(2)}, u32[]{:S(2)}) collective-permute-start(bf16[128,512]{1,0:T(8,128)(2,1)S(1)} %get-tuple-element.56), channel_id=1, source_target_pairs={{0,62},{1,63},{2,0},{3,1},{4,2},{5,3},{6,4},{7,5},{8,6},{9,7},{10,... | collective-permute-start | bytes 393224 | tf_op jit(solution)/shard_map/ppermute | solution.py:379
  64.0 10.7 %all-to-all-start.1 = ((bf16[8,40,128]{2,1,0:T(8,128)(2,1)}), bf16[8,40,128]{2,1,0:T(8,128)(2,1)S(1)}, u32[]{:S(2)}, u32[]{:S(2)}) async-start(bf16[8,40,128]{2,1,0:T(8,128)(2,1)} %part_sum.1), calls=%async_computation.1 | async-start | bytes 163840 | tf_op jit(solution)/shard_map/all_to_all | solution.py:503

commit v4 on v3

--- a/solution.py
+++ b/solution.py
@@ -18,7 +18,7 @@
 TABLE_AT = 16
 PREPARE_COST = 10**9
 GATHER_COST = 10**10
-PART_COST = 10**10
+PART_COST = 0
 ADJOINT_COST = 10**11
 SCATTER_COST = 10**11
 CHOOSE_COST = 2 * 10**9
@@ -53,30 +53,20 @@
     )
 
 
-def quad_boxes(rows, counts, offsets, quads):
-    lines = rows.shape[0]
-    parts = lines // offsets
-    share = quads // parts
-    line_at = lax.broadcasted_iota(jnp.int32, rows.shape, 0)
-    from_lane = lax.broadcasted_iota(jnp.int32, (quads, quads), 0)
-    to_lane = lax.broadcasted_iota(jnp.int32, (quads, quads), 1)
-    high = jnp.zeros(rows.shape, F32)
-    low = jnp.zeros(rows.shape, F32)
-    for part in range(parts):
-        pick = (from_lane == 4 * (to_lane - part * share)).astype(F32).astype(BF16)
-        here = jnp.where(line_at % parts == part, rows, 0)
-        high = high + dot((here >> 3).astype(F32).astype(BF16), pick)
-        low = low + dot((here & 7).astype(F32).astype(BF16), pick)
-    gather = (
-        lax.broadcasted_iota(jnp.int32, (8, lines), 1) // parts
-        == lax.broadcasted_iota(jnp.int32, (8, lines), 0)
-    ).astype(F32).astype(BF16)
-    cells = dot(gather, high.astype(BF16)) * 8.0 + dot(gather, low.astype(BF16))
-    cells = cells.astype(jnp.int32)
+def quad_boxes(index_ref, offsets, quads):
+    index = index_ref[...]
+    pick = one_hot(
+        lax.broadcasted_iota(jnp.int32, (4 * quads, quads), 0)
+        == 4 * lax.broadcasted_iota(jnp.int32, (4 * quads, quads), 1)
+    )
+    high = (index >> 3).astype(F32).astype(BF16)
+    low = (index & 7).astype(F32).astype(BF16)
+    cells = (dot(high, pick) * 8.0 + dot(low, pick)).astype(jnp.int32)
     offset_at = lax.broadcasted_iota(jnp.int32, cells.shape, 0)
     live = jnp.zeros(cells.shape, jnp.int32)
     for offset in range(offsets):
-        live = jnp.where(offset_at == offset, counts[:, offset : offset + 1], live)
+        count = index[offsets : offsets + 1, offset : offset + 1]
+        live = jnp.where(offset_at == offset, count, live)
     slot_at = 4 * lax.broadcasted_iota(jnp.int32, cells.shape, 1)
     return jnp.where(slot_at < live, cells, -1)
 
@@ -85,9 +75,9 @@
     return mask.astype(F32).astype(BF16)
 
 
-def choose_kernel(offsets, rows_ref, count_ref, cells_ref, select_ref):
+def choose_kernel(offsets, index_ref, cells_ref, select_ref):
     quads = cells_ref.shape[1]
-    cells = quad_boxes(rows_ref[...], count_ref[...], offsets, quads)
+    cells = quad_boxes(index_ref, offsets, quads)
     cells_ref[...] = cells
     columns = cells.astype(F32).T.astype(jnp.int32)
     box_at = lax.broadcasted_iota(jnp.int32, (quads, select_ref.shape[1]), 1)
@@ -197,6 +187,10 @@
     g3,
     once,
     smooth,
+    a1,
+    a2,
+    p1,
+    p2,
 ):
     band_rows, lon, ch = dep_ref.shape
     hid = w1_ref.shape[1]
@@ -231,10 +225,10 @@
             dep_ref[row] + helm * (once[row] + once[row + 2] + lon_sum(once[row + 1]))
         ) * inverse
         smooth[row] = value.astype(BF16)
-    for total in (g1, gb1, g2, gb2, g3):
-        total[...] = jnp.zeros_like(total)
-
-    def one_row(row, carry):
+    gb1[...] = jnp.zeros_like(gb1)
+    gb2[...] = jnp.zeros_like(gb2)
+
+    for row in range(band_rows):
         rows = smooth[row]
         cot = cot_ref[row]
         act, slope_first = gelu_parts(dot(rows, w1_ref[...]) + b1)
@@ -242,20 +236,23 @@
         act, slope_second = gelu_parts(dot(act_first, w2_ref[...]) + b2)
         act_second = act.astype(BF16)
         next_ref[row] = (rows.astype(F32) + dot(act_second, w3_ref[...])).astype(BF16)
-        g3[...] += dot(act_second, cot, 0, 0)
         gpre = dot(cot, w3_ref[...], 1, 1) * slope_second
         gpre_second = gpre.astype(BF16)
         gb2[...] += jnp.sum(gpre_second.astype(F32), axis=0, keepdims=True)
-        g2[...] += dot(act_first, gpre_second, 0, 0)
         gpre = dot(gpre_second, w2_ref[...], 1, 1) * slope_first
         gpre_first = gpre.astype(BF16)
         gb1[...] += jnp.sum(gpre_first.astype(F32), axis=0, keepdims=True)
-        g1[...] += dot(rows, gpre_first, 0, 0)
+        a1[row], a2[row], p1[row], p2[row] = act_first, act_second, gpre_first, gpre_second
         gsmooth = cot.astype(F32) + dot(gpre_first, w1_ref[...], 1, 1)
         scaled_ref[row] = gsmooth * inverse
-        return carry
-
-    lax.fori_loop(0, band_rows, one_row, 0)
+    flat = band_rows * lon
+
+    def whole(ref):
+        return ref[...].reshape(flat, ref.shape[2])
+
+    g3[...] = dot(whole(a2), whole(cot_ref), 0, 0)
+    g2[...] = dot(whole(a1), whole(p2), 0, 0)
+    g1[...] = dot(whole(smooth), whole(p1), 0, 0)
     for row in range(2):
         up_ref[row] = scaled_ref[row].astype(BF16)
         down_ref[row] = scaled_ref[band_rows - 2 + row].astype(BF16)
@@ -363,7 +360,7 @@
         out_ref[copy] = total
 
 
-def unpack_kernel(sums_ref, g1, gb1, g2, gb2, g3):
+def unpack_kernel(sums_ref, ahead_ref, g1, gb1, g2, gb2, g3):
     ch, hid = g1.shape
     g1[:, :ch] = sums_ref[:ch].astype(F32)
     g1[:, ch:] = sums_ref[ch : 2 * ch].astype(F32)
@@ -404,7 +401,9 @@
     place = jnp.stack([lax.axis_index(SPACE).astype(jnp.int32), jnp.int32(bands)])
     block = shape((quads, taps * ch), BF16)
     edge = shape((2, lon, ch), BF16)
-    lines = send_rows.reshape(offsets * slots // quads, quads)
+    index = jnp.pad(send_rows[0], ((0, 8 - offsets), (0, 0))) + jnp.pad(
+        send_count, ((offsets, 7 - offsets), (0, slots - offsets))
+    )
 
     cells, select = call(
         functools.partial(choose_kernel, offsets),
@@ -412,10 +411,10 @@
             shape((8, quads), jnp.int32),
             shape((offsets * quads, (band_rows - 1) * lon), BF16),
         ],
-        [VMEM] * 2,
+        [VMEM],
         flops=CHOOSE_COST,
         name="choose",
-    )(lines, send_count)
+    )(index)
     packed = call(
         functools.partial(pack_kernel, offsets),
         [block] * offsets,
@@ -467,7 +466,8 @@
         [
             pltpu.VMEM((band_rows + 2, lon, ch), F32),
             pltpu.VMEM((band_rows, lon, ch), BF16),
-        ],
+        ]
+        + [pltpu.VMEM((band_rows, lon, hid), BF16)] * 4,
         name="smooth_mlp",
     )(departure, before, after, cotangent[0], place, table, w_first, w_second, w_third)
     before = shifted(down, 1, bands)
@@ -521,14 +521,14 @@
         [shape((group, PART_ROWS, ch), BF16)],
         [VMEM, ANY],
         name="whole_sum",
-    )(parts, done)
+    )(parts, slot_grads[reach])
     sums = lax.all_to_all(whole_sum, groups, 0, 0).reshape(group * PART_ROWS, ch)
     grads = call(
         unpack_kernel,
         grad_shapes,
-        [VMEM],
+        [VMEM, ANY],
         name="unpack",
-    )(sums)
+    )(sums, done)
     return (
         next_state[None],
         field_grad[None],

time: 92.6 us -> 89.3 us (0.964)
  blocking collectives: 16.7 us -> 0 us
  waiting for transfers between devices: 19.2 us -> 29.4 us
  starting transfers between devices: 34.5 us -> 38.3 us
    all_to_all x1 -> x0, blocking collectives: 16.7 us -> none  [body(): lax.all_to_all(whole_sum, groups, 0, 0).reshape(group * PART_ROWS, ch)]
    all_to_all x0 -> x1, waiting for transfers between devices: none -> 7.11 us  [body(): lax.all_to_all(whole_sum, groups, 0, 0).reshape(group * PART_ROWS, ch)]
    all_to_all x1, waiting for transfers between devices: 0.01 us -> 6.17 us  [body(): parts = lax.all_to_all(grads.reshape(group, PART_ROWS, ch), groups, 0, 0)]
    all_to_all x0 -> x1, starting transfers between devices: none -> 5.29 us  [body(): lax.all_to_all(whole_sum, groups, 0, 0).reshape(group * PART_ROWS, ch)]
    all_to_all x1, waiting for transfers between devices: 4.89 us -> 1.55 us  [body(): parts = lax.all_to_all(part_sum, 'z', 0, 0)]
    pallas_call x1, Pallas kernels: 7.11 us -> 5.62 us  [body(): call(mlp_kernel, [shape((band_rows, lon, ch), BF16), shape((band_rows, lo...]
    ppermute x12, starting transfers between devices: 21.4 us -> 20 us  [shifted(): lax.ppermute(block, SPACE, [(i, (i + by) % count) for i in range(count)])]
  transfers between devices with their start and end apart: 14 -> 15, of which waited for: 7 -> 9; matrix products, arithmetic and copies ran while one was open for 0% -> 0% of each run, Pallas kernels for 8% -> 8%
where the time goes in v4:
time: 89.3 us; the launch traced here: 88.8 us
  starting transfers between devices  38.3 us (43%)
  waiting for transfers between devices  29.4 us (33%)
  Pallas kernels  18.4 us (21%)
  local copies, waits for them, and re-layouts  1.1 us (1%)
    ppermute x12, starting transfers between devices, shifted(): lax.ppermute(block, SPACE, [(i, (i + by) % count) for i in range(count)])  20 us
    ppermute x12, waiting for transfers between devices, shifted(): lax.ppermute(block, SPACE, [(i, (i + by) % count) for i in range(count)])  14.6 us
    all_to_all x1, starting transfers between devices, body(): parts = lax.all_to_all(grads.reshape(group, PART_ROWS, ch), groups, 0, 0)  9.68 us
    all_to_all x1, waiting for transfers between devices, body(): lax.all_to_all(whole_sum, groups, 0, 0).reshape(group * PART_ROWS, ch)  7.11 us
    all_to_all x1, waiting for transfers between devices, body(): parts = lax.all_to_all(grads.reshape(group, PART_ROWS, ch), groups, 0, 0)  6.17 us
    pallas_call x1, Pallas kernels, body(): call(mlp_kernel, [shape((band_rows, lon, ch), BF16), shape((band_rows, lo...  5.62 us
    all_to_all x1, starting transfers between devices, body(): lax.all_to_all(whole_sum, groups, 0, 0).reshape(group * PART_ROWS, ch)  5.29 us
    all_to_all x1, starting transfers between devices, body(): parts = lax.all_to_all(part_sum, 'z', 0, 0)  3.36 us
  transfers between devices with their start and end apart: 15, of which 9 were waited for; matrix products, arithmetic and copies ran while one was open for 0% of the time, Pallas kernels for 8%

profile of v4, /device:TPU:1, one launch (start us, length us, event | category | flops | bytes accessed | tf_op | source)
XLA Modules:
  0.0 88.8 jit_solution(16797575897552819265)
XLA Ops:
  0.6 0.7 copy.21
  1.3 0.7 pad_add_fusion.index_ref
  2.0 0.0 copy-start
  2.0 0.6 choose.1
  2.6 0.0 copy-start.5
  2.7 0.0 copy-start.6
  2.7 0.0 copy-start.7
  2.7 0.0 copy-start.8
  2.7 0.0 copy-start.9
  2.7 0.3 copy-done
  3.0 1.3 %pack.1 = (bf16[128,512]{1,0:T(8,128)(2,1)S(1)}, bf16[128,512]{1,0:T(8,128)(2,1)S(1)}, bf16[128,512]{1,0:T(8,128)(2,1)S(1)}, bf16[128,512]{1,0:T(8,128)(2,1)S(1)}, bf16[128,512]{1,0:T(8,128)(2,1)S(1)}) custom-call(bf16[4,512,128]{2,1,0:T(8,128)(2,1)S(1)} %bitcast.16, bf16[640,1536]{1,0:T(8,128)(2,1)S(1)} %get-tuple-element.38.select_ref), custom_call_target="tpu_custom_call" | custom-call | bytes 1310720 | tf_op jit(solution)/shard_map/pack/pallas_call | solution.py:418
  4.4 8.7 %collective-permute-start = (bf16[128,512]{1,0:T(8,128)(2,1)S(1)}, bf16[128,512]{1,0:T(8,128)(2,1)S(1)}, u32[]{:S(2)}, u32[]{:S(2)}) collective-permute-start(bf16[128,512]{1,0:T(8,128)(2,1)S(1)} %get-tuple-element.39), channel_id=1, source_target_pairs={{0,62},{1,63},{2,0},{3,1},{4,2},{5,3},{6,4},{7,5},{8,6},{9,7},{10,... | collective-permute-start | bytes 393224 | tf_op jit(solution)/shard_map/ppermute | solution.py:376
  13.1 1.0 %collective-permute-start.1 = (bf16[128,512]{1,0:T(8,128)(2,1)S(1)}, bf16[128,512]{1,0:T(8,128)(2,1)S(1)}, u32[]{:S(2)}, u32[]{:S(2)}) collective-permute-start(bf16[128,512]{1,0:T(8,128)(2,1)S(1)} %get-tuple-element.40), channel_id=1, source_target_pairs={{0,63},{1,0},{2,1},{3,2},{4,3},{5,4},{6,5},{7,6},{8,7},{9,8},{10,9... | collective-permute-start | bytes 393224 | tf_op jit(solution)/shard_map/ppermute | solution.py:376
  14.0 0.8 collective-permute-start.2
  14.8 0.0 collective-permute-start.3
  14.8 0.0 copy-done.5
  14.8 0.0 copy-done.6
  14.8 0.0 copy-done.7
  14.8 0.0 copy-done.8
  14.8 0.0 copy-done.9
  14.8 0.0 copy-start.1
  14.9 0.0 copy-start.2
  14.9 0.0 copy-start.3
  14.9 0.0 copy-start.4
  14.9 0.3 collective-permute-done.refs_0_
  15.2 2.3 %collective-permute-done.1.refs_1_ = bf16[128,512]{1,0:T(8,128)(2,1)S(1)} collective-permute-done((bf16[128,512]{1,0:T(8,128)(2,1)S(1)}, bf16[128,512]{1,0:T(8,128)(2,1)S(1)}, u32[]{:S(2)}, u32[]{:S(2)}) %collective-permute-start.1) | collective-permute-done | bytes 131104 | tf_op jit(solution)/shard_map/ppermute | solution.py:376
  17.5 0.1 collective-permute-done.2.refs_3_
  17.6 6.3 %collective-permute-done.3.refs_4_ = bf16[128,512]{1,0:T(8,128)(2,1)S(1)} collective-permute-done((bf16[128,512]{1,0:T(8,128)(2,1)S(1)}, bf16[128,512]{1,0:T(8,128)(2,1)S(1)}, u32[]{:S(2)}, u32[]{:S(2)}) %collective-permute-start.3) | collective-permute-done | bytes 131104 | tf_op jit(solution)/shard_map/ppermute | solution.py:376
  23.9 2.0 %interp.1 = (f32[4,512,128]{2,1,0:T(8,128)S(1)}, bf16[2,512,128]{2,1,0:T(8,128)(2,1)S(1)}, bf16[2,512,128]{2,1,0:T(8,128)(2,1)S(1)}) custom-call(bf16[128,512]{1,0:T(8,128)(2,1)S(1)} %collective-permute-done.refs_0_, bf16[128,512]{1,0:T(8,128)(2,1)S(1)} %collective-permute-done.1.refs_1_, bf16[128,512]{1,0:T(8,128)(2,1)S(1)} %get-tuple-element.41.refs_2_, ...), custom_call_target="tpu_custom_call" | custom-call | bytes 3145728 | tf_op jit(solution)/shard_map/interp/pallas_call | solution.py:442
  25.9 0.1 collective-permute-start.4
  26.0 0.6 collective-permute-start.5
  26.6 0.1 pad_add_fusion.1.place_ref
  26.7 2.6 %collective-permute-done.4.before_ref = bf16[2,512,128]{2,1,0:T(8,128)(2,1)S(1)} collective-permute-done((bf16[2,512,128]{2,1,0:T(8,128)(2,1)S(1)}, bf16[2,512,128]{2,1,0:T(8,128)(2,1)S(1)}, u32[]{:S(2)}, u32[]{:S(2)}) %collective-permute-start.4) | collective-permute-done | bytes 262176 | tf_op jit(solution)/shard_map/ppermute | solution.py:376
  29.3 3.0 %collective-permute-done.5.after_ref = bf16[2,512,128]{2,1,0:T(8,128)(2,1)S(1)} collective-permute-done((bf16[2,512,128]{2,1,0:T(8,128)(2,1)S(1)}, bf16[2,512,128]{2,1,0:T(8,128)(2,1)S(1)}, u32[]{:S(2)}, u32[]{:S(2)}) %collective-permute-start.5) | collective-permute-done | bytes 262176 | tf_op jit(solution)/shard_map/ppermute | solution.py:376
  32.3 0.0 copy-done.1
  32.3 0.0 copy-done.2
  32.3 0.0 copy-done.3
  32.3 0.0 copy-done.4
  32.4 5.6 %smooth_mlp.1 = (bf16[4,512,128]{2,1,0:T(8,128)(2,1)}, f32[4,512,128]{2,1,0:T(8,128)S(1)}, bf16[2,512,128]{2,1,0:T(8,128)(2,1)}, bf16[2,512,128]{2,1,0:T(8,128)(...) custom-call(f32[4,512,128]{2,1,0:T(8,128)S(1)} %get-tuple-element.44, ...), custom_call_target="tpu_custom_call" | custom-call | bytes 5246976 | tf_op jit(solution)/shard_map/smooth_mlp/pallas_call | solution.py:461
  38.0 0.0 collective-permute-start.6
  38.0 3.2 %collective-permute-start.7 = (bf16[2,512,128]{2,1,0:T(8,128)(2,1)}, bf16[2,512,128]{2,1,0:T(8,128)(2,1)S(1)}, u32[]{:S(2)}, u32[]{:S(2)}) collective-permute-start(bf16[2,512,128]{2,1,0:T(8,128)(2,1)} %get-tuple-element.51), channel_id=1, source_target_pairs={{0,63},{1,0},{2,1},{3,2},{4,3},{5,4},{6,5},{7,6},{8,7},{9,8},{10,9... | collective-permute-start | bytes 786440 | tf_op jit(solution)/shard_map/ppermute | solution.py:376
  41.1 0.8 gather.1
  41.9 9.7 %all-to-all-start = ((bf16[32,40,128]{2,1,0:T(8,128)(2,1)}), bf16[32,40,128]{2,1,0:T(8,128)(2,1)S(1)}, u32[]{:S(2)}, u32[]{:S(2)}) async-start(bf16[32,40,128]{2,1,0:T(8,128)(2,1)} %bitcast.8), calls=%async_computation | async-start | bytes 655360 | tf_op jit(solution)/shard_map/all_to_all | solution.py:483
  51.6 0.0 collective-permute-done.6.before_ref
  51.6 0.0 collective-permute-done.7.after_ref
  51.6 3.3 %adjoint.1 = (bf16[128,512]{1,0:T(8,128)(2,1)S(1)}, bf16[128,512]{1,0:T(8,128)(2,1)S(1)}, bf16[128,512]{1,0:T(8,128)(2,1)S(1)}, bf16[128,512]{1,0:T(8,128)(2,1)S(1)}, bf16[128,512]{1,0:T(8,128)(2,1)S(1)}) custom-call(f32[4,512,128]{2,1,0:T(8,128)S(1)} %get-tuple-element.49.scaled_ref, bf16[2,512,128]{2,1,0:T(8,128)(2,1)S(1)} %collective-permute-done.6.before_ref, ...), custom_call_target="tpu_custom_call" | custom-call | flops 99999997952 | bytes 1310720 | tf_op jit(solution)/shard_map/adjoint/pallas_call | solution.py:484
  55.0 6.2 %all-to-all-done.parts_ref = bf16[32,40,128]{2,1,0:T(8,128)(2,1)S(1)} async-done(((bf16[32,40,128]{2,1,0:T(8,128)(2,1)}), bf16[32,40,128]{2,1,0:T(8,128)(2,1)S(1)}, u32[]{:S(2)}, u32[]{:S(2)}) %all-to-all-start) | async-done | bytes 327712 | tf_op jit(solution)/shard_map/all_to_all | solution.py:483
  61.1 0.7 part_sum.1
  61.8 3.4 %all-to-all-start.1 = ((bf16[8,40,128]{2,1,0:T(8,128)(2,1)}), bf16[8,40,128]{2,1,0:T(8,128)(2,1)S(1)}, u32[]{:S(2)}, u32[]{:S(2)}) async-start(bf16[8,40,128]{2,1,0:T(8,128)(2,1)} %part_sum.1), calls=%async_computation.1 | async-start | bytes 163840 | tf_op jit(solution)/shard_map/all_to_all | solution.py:503
  65.2 0.6 collective-permute-start.8
  65.8 0.6 collective-permute-start.9
  66.4 0.0 collective-permute-start.10
  66.4 4.4 %collective-permute-start.11 = (bf16[128,512]{1,0:T(8,128)(2,1)S(1)}, bf16[128,512]{1,0:T(8,128)(2,1)S(1)}, u32[]{:S(2)}, u32[]{:S(2)}) collective-permute-start(bf16[128,512]{1,0:T(8,128)(2,1)S(1)} %get-tuple-element.56), channel_id=1, source_target_pairs={{0,62},{1,63},{2,0},{3,1},{4,2},{5,3},{6,4},{7,5},{8,6},{9,7},{10,... | collective-permute-start | bytes 393224 | tf_op jit(solution)/shard_map/ppermute | solution.py:376
  70.8 1.5 %all-to-all-done.1.parts_ref = bf16[8,40,128]{2,1,0:T(8,128)(2,1)S(1)} async-done(((bf16[8,40,128]{2,1,0:T(8,128)(2,1)}), bf16[8,40,128]{2,1,0:T(8,128)(2,1)S(1)}, u32[]{:S(2)}, u32[]{:S(2)}) %all-to-all-start.1) | async-done | bytes 81952 | tf_op jit(solution)/shard_map/all_to_all | solution.py:503
  72.4 0.8 whole_sum.1
  73.2 5.3 %all-to-all-start.2 = ((bf16[32,40,128]{2,1,0:T(8,128)(2,1)}), bf16[32,40,128]{2,1,0:T(8,128)(2,1)S(1)}, u32[]{:S(2)}, u32[]{:S(2)}) async-start(bf16[32,40,128]{2,1,0:T(8,128)(2,1)} %whole_sum.1), calls=%async_computation.2 | async-start | bytes 655360 | tf_op jit(solution)/shard_map/all_to_all | solution.py:525
  78.5 0.0 collective-permute-done.8.refs_0_
  78.5 0.0 collective-permute-done.9.refs_1_
  78.5 0.0 collective-permute-done.10.refs_3_
  78.5 0.0 collective-permute-done.11.refs_4_
  78.5 2.4 %scatter.1 = (f32[4,512,128]{2,1,0:T(8,128)}, f32[8,128]{1,0:T(8,128)S(1)}) custom-call(s32[8,128]{1,0:T(8,128)S(1)} %get-tuple-element.48.cells_ref, bf16[128,512]{1,0:T(8,128)(2,1)S(1)} %collective-permute-done.8.refs_0_, bf16[128,512]{1,0:T(8,128)(2,1)S(1)} %collective-permute-done.9.refs_1_, bf16[128,512]{1,0:T(8,128)(2,1)S(1)} %get-tuple-element.54.refs_2_.ahead_ref, ...), custom_call_target="tpu_custom_call" | custom-call | flops 99999997952 | bytes 2105344 | tf_op jit(solution)/shard_map/scatter/pallas_call | solution.py:508
  80.9 7.1 %all-to-all-done.2 = bf16[32,40,128]{2,1,0:T(8,128)(2,1)S(1)} async-done(((bf16[32,40,128]{2,1,0:T(8,128)(2,1)}), bf16[32,40,128]{2,1,0:T(8,128)(2,1)S(1)}, u32[]{:S(2)}, u32[]{:S(2)}) %all-to-all-start.2) | async-done | bytes 327712 | tf_op jit(solution)/shard_map/all_to_all | solution.py:525
  88.0 0.8 unpack.1
  (1 shorter events, 0.0 us)
Async XLA Ops:
  2.0 1.0 %copy-start = (bf16[1,4,512,128]{3,2,1,0:T(8,128)(2,1)S(1)}, bf16[1,4,512,128]{3,2,1,0:T(8,128)(2,1)}, u32[]{:S(2)}) copy-start(bf16[1,4,512,128]{3,2,1,0:T(8,128)(2,1)} %param.12) | copy-start | bytes 1572868
  2.6 12.2 %copy-start.5 = (s32[4,4,512]{2,1,0:T(4,128)S(1)}, s32[4,4,512]{2,1,0:T(4,128)}, u32[]{:S(2)}) copy-start(s32[4,4,512]{2,1,0:T(4,128)} %slot_ref.1) | copy-start | bytes 98308
  2.7 12.2 %copy-start.6 = (f32[4,4,512]{2,1,0:T(4,128)S(1)}, f32[4,4,512]{2,1,0:T(4,128)}, u32[]{:S(2)}) copy-start(f32[4,4,512]{2,1,0:T(4,128)} %weight_ref.1) | copy-start | bytes 98308
  2.7 12.2 %copy-start.7 = (f32[256]{0:T(256)S(1)}, f32[256]{0:T(256)}, u32[]{:S(2)}) copy-start(f32[256]{0:T(256)} %param.19) | copy-start | bytes 3076
  2.7 12.1 %copy-start.8 = (f32[256]{0:T(256)S(1)}, f32[256]{0:T(256)}, u32[]{:S(2)}) copy-start(f32[256]{0:T(256)} %param.21) | copy-start | bytes 3076
  2.7 12.1 %copy-start.9 = (f32[128]{0:T(128)S(1)}, f32[128]{0:T(128)}, u32[]{:S(2)}) copy-start(f32[128]{0:T(128)} %param.17) | copy-start | bytes 1540
  4.4 10.8 %collective-permute-start = (bf16[128,512]{1,0:T(8,128)(2,1)S(1)}, bf16[128,512]{1,0:T(8,128)(2,1)S(1)}, u32[]{:S(2)}, u32[]{:S(2)}) collective-permute-start(bf16[128,512]{1,0:T(8,128)(2,1)S(1)} %get-tuple-element.39), channel_id=1, source_target_pairs={{0,62},{1,63},{2,0},{3,1},{4,2},{5,3},{6,4},{7,5},{8,6},{9,7},{10,... | collective-permute-start | bytes 393224 | tf_op jit(solution)/shard_map/ppermute | solution.py:376
  13.1 4.4 %collective-permute-start.1 = (bf16[128,512]{1,0:T(8,128)(2,1)S(1)}, bf16[128,512]{1,0:T(8,128)(2,1)S(1)}, u32[]{:S(2)}, u32[]{:S(2)}) collective-permute-start(bf16[128,512]{1,0:T(8,128)(2,1)S(1)} %get-tuple-element.40), channel_id=1, source_target_pairs={{0,63},{1,0},{2,1},{3,2},{4,3},{5,4},{6,5},{7,6},{8,7},{9,8},{10,9... | collective-permute-start | bytes 393224 | tf_op jit(solution)/shard_map/ppermute | solution.py:376
  14.0 3.5 %collective-permute-start.2 = (bf16[128,512]{1,0:T(8,128)(2,1)S(1)}, bf16[128,512]{1,0:T(8,128)(2,1)S(1)}, u32[]{:S(2)}, u32[]{:S(2)}) collective-permute-start(bf16[128,512]{1,0:T(8,128)(2,1)S(1)} %get-tuple-element.42), channel_id=1, source_target_pairs={{0,1},{1,2},{2,3},{3,4},{4,5},{5,6},{6,7},{7,8},{8,9},{9,10},{10,1... | collective-permute-start | bytes 393224 | tf_op jit(solution)/shard_map/ppermute | solution.py:376
  14.8 9.1 %collective-permute-start.3 = (bf16[128,512]{1,0:T(8,128)(2,1)S(1)}, bf16[128,512]{1,0:T(8,128)(2,1)S(1)}, u32[]{:S(2)}, u32[]{:S(2)}) collective-permute-start(bf16[128,512]{1,0:T(8,128)(2,1)S(1)} %get-tuple-element.43), channel_id=1, source_target_pairs={{0,2},{1,3},{2,4},{3,5},{4,6},{5,7},{6,8},{7,9},{8,10},{9,11},{10,... | collective-permute-start | bytes 393224 | tf_op jit(solution)/shard_map/ppermute | solution.py:376
  14.8 17.5 %copy-start.1 = (bf16[1,4,512,128]{3,2,1,0:T(8,128)(2,1)S(1)}, bf16[1,4,512,128]{3,2,1,0:T(8,128)(2,1)}, u32[]{:S(2)}) copy-start(bf16[1,4,512,128]{3,2,1,0:T(8,128)(2,1)} %param.23) | copy-start | bytes 1572868
  14.9 17.5 %copy-start.2 = (bf16[256,256]{1,0:T(8,128)(2,1)S(1)}, bf16[256,256]{1,0:T(8,128)(2,1)}, u32[]{:S(2)}) copy-start(bf16[256,256]{1,0:T(8,128)(2,1)} %w2_ref.1) | copy-start | bytes 393220
  14.9 17.5 %copy-start.3 = (bf16[128,256]{1,0:T(8,128)(2,1)S(1)}, bf16[128,256]{1,0:T(8,128)(2,1)}, u32[]{:S(2)}) copy-start(bf16[128,256]{1,0:T(8,128)(2,1)} %w1_ref.1) | copy-start | bytes 196612
  14.9 17.5 %copy-start.4 = (bf16[256,128]{1,0:T(8,128)(2,1)S(1)}, bf16[256,128]{1,0:T(8,128)(2,1)}, u32[]{:S(2)}) copy-start(bf16[256,128]{1,0:T(8,128)(2,1)} %w3_ref.1) | copy-start | bytes 196612
  25.9 3.4 %collective-permute-start.4 = (bf16[2,512,128]{2,1,0:T(8,128)(2,1)S(1)}, bf16[2,512,128]{2,1,0:T(8,128)(2,1)S(1)}, u32[]{:S(2)}, u32[]{:S(2)}) collective-permute-start(bf16[2,512,128]{2,1,0:T(8,128)(2,1)S(1)} %get-tuple-element.45), channel_id=1, source_target_pairs={{0,1},{1,2},{2,3},{3,4},{4,5},{5,6},{6,7},{7,8},{8,9},{9,10},{10,1... | collective-permute-start | bytes 786440 | tf_op jit(solution)/shard_map/ppermute | solution.py:376
  26.0 6.3 %collective-permute-start.5 = (bf16[2,512,128]{2,1,0:T(8,128)(2,1)S(1)}, bf16[2,512,128]{2,1,0:T(8,128)(2,1)S(1)}, u32[]{:S(2)}, u32[]{:S(2)}) collective-permute-start(bf16[2,512,128]{2,1,0:T(8,128)(2,1)S(1)} %get-tuple-element.46), channel_id=1, source_target_pairs={{0,63},{1,0},{2,1},{3,2},{4,3},{5,4},{6,5},{7,6},{8,7},{9,8},{10,9... | collective-permute-start | bytes 786440 | tf_op jit(solution)/shard_map/ppermute | solution.py:376
  38.0 13.6 %collective-permute-start.6 = (bf16[2,512,128]{2,1,0:T(8,128)(2,1)}, bf16[2,512,128]{2,1,0:T(8,128)(2,1)S(1)}, u32[]{:S(2)}, u32[]{:S(2)}) collective-permute-start(bf16[2,512,128]{2,1,0:T(8,128)(2,1)} %get-tuple-element.50), channel_id=1, source_target_pairs={{0,1},{1,2},{2,3},{3,4},{4,5},{5,6},{6,7},{7,8},{8,9},{9,10},{10,1... | collective-permute-start | bytes 786440 | tf_op jit(solution)/shard_map/ppermute | solution.py:376
  38.0 13.6 %collective-permute-start.7 = (bf16[2,512,128]{2,1,0:T(8,128)(2,1)}, bf16[2,512,128]{2,1,0:T(8,128)(2,1)S(1)}, u32[]{:S(2)}, u32[]{:S(2)}) collective-permute-start(bf16[2,512,128]{2,1,0:T(8,128)(2,1)} %get-tuple-element.51), channel_id=1, source_target_pairs={{0,63},{1,0},{2,1},{3,2},{4,3},{5,4},{6,5},{7,6},{8,7},{9,8},{10,9... | collective-permute-start | bytes 786440 | tf_op jit(solution)/shard_map/ppermute | solution.py:376
  41.9 19.2 %all-to-all-start = ((bf16[32,40,128]{2,1,0:T(8,128)(2,1)}), bf16[32,40,128]{2,1,0:T(8,128)(2,1)S(1)}, u32[]{:S(2)}, u32[]{:S(2)}) async-start(bf16[32,40,128]{2,1,0:T(8,128)(2,1)} %bitcast.8), calls=%async_computation | async-start | bytes 655360 | tf_op jit(solution)/shard_map/all_to_all | solution.py:483
  61.8 10.6 %all-to-all-start.1 = ((bf16[8,40,128]{2,1,0:T(8,128)(2,1)}), bf16[8,40,128]{2,1,0:T(8,128)(2,1)S(1)}, u32[]{:S(2)}, u32[]{:S(2)}) async-start(bf16[8,40,128]{2,1,0:T(8,128)(2,1)} %part_sum.1), calls=%async_computation.1 | async-start | bytes 163840 | tf_op jit(solution)/shard_map/all_to_all | solution.py:503
  65.2 13.3 %collective-permute-start.8 = (bf16[128,512]{1,0:T(8,128)(2,1)S(1)}, bf16[128,512]{1,0:T(8,128)(2,1)S(1)}, u32[]{:S(2)}, u32[]{:S(2)}) collective-permute-start(bf16[128,512]{1,0:T(8,128)(2,1)S(1)} %get-tuple-element.52), channel_id=1, source_target_pairs={{0,2},{1,3},{2,4},{3,5},{4,6},{5,7},{6,8},{7,9},{8,10},{9,11},{10,... | collective-permute-start | bytes 393224 | tf_op jit(solution)/shard_map/ppermute | solution.py:376
  65.8 12.7 %collective-permute-start.9 = (bf16[128,512]{1,0:T(8,128)(2,1)S(1)}, bf16[128,512]{1,0:T(8,128)(2,1)S(1)}, u32[]{:S(2)}, u32[]{:S(2)}) collective-permute-start(bf16[128,512]{1,0:T(8,128)(2,1)S(1)} %get-tuple-element.53), channel_id=1, source_target_pairs={{0,1},{1,2},{2,3},{3,4},{4,5},{5,6},{6,7},{7,8},{8,9},{9,10},{10,1... | collective-permute-start | bytes 393224 | tf_op jit(solution)/shard_map/ppermute | solution.py:376
  66.4 12.1 %collective-permute-start.10 = (bf16[128,512]{1,0:T(8,128)(2,1)S(1)}, bf16[128,512]{1,0:T(8,128)(2,1)S(1)}, u32[]{:S(2)}, u32[]{:S(2)}) collective-permute-start(bf16[128,512]{1,0:T(8,128)(2,1)S(1)} %get-tuple-element.55), channel_id=1, source_target_pairs={{0,63},{1,0},{2,1},{3,2},{4,3},{5,4},{6,5},{7,6},{8,7},{9,8},{10,9... | collective-permute-start | bytes 393224 | tf_op jit(solution)/shard_map/ppermute | solution.py:376
  66.4 12.1 %collective-permute-start.11 = (bf16[128,512]{1,0:T(8,128)(2,1)S(1)}, bf16[128,512]{1,0:T(8,128)(2,1)S(1)}, u32[]{:S(2)}, u32[]{:S(2)}) collective-permute-start(bf16[128,512]{1,0:T(8,128)(2,1)S(1)} %get-tuple-element.56), channel_id=1, source_target_pairs={{0,62},{1,63},{2,0},{3,1},{4,2},{5,3},{6,4},{7,5},{8,6},{9,7},{10,... | collective-permute-start | bytes 393224 | tf_op jit(solution)/shard_map/ppermute | solution.py:376
  73.2 14.9 %all-to-all-start.2 = ((bf16[32,40,128]{2,1,0:T(8,128)(2,1)}), bf16[32,40,128]{2,1,0:T(8,128)(2,1)S(1)}, u32[]{:S(2)}, u32[]{:S(2)}) async-start(bf16[32,40,128]{2,1,0:T(8,128)(2,1)} %whole_sum.1), calls=%async_computation.2 | async-start | bytes 655360 | tf_op jit(solution)/shard_map/all_to_all | solution.py:525

commit v5 on v4

--- a/solution.py
+++ b/solution.py
@@ -17,7 +17,6 @@
 PART_ROWS = 40
 TABLE_AT = 16
 PREPARE_COST = 10**9
-GATHER_COST = 10**10
 PART_COST = 0
 ADJOINT_COST = 10**11
 SCATTER_COST = 10**11
@@ -53,31 +52,32 @@
     )
 
 
-def quad_boxes(index_ref, offsets, quads):
-    index = index_ref[...]
+def quad_boxes(index, quads):
     pick = one_hot(
         lax.broadcasted_iota(jnp.int32, (4 * quads, quads), 0)
         == 4 * lax.broadcasted_iota(jnp.int32, (4 * quads, quads), 1)
     )
     high = (index >> 3).astype(F32).astype(BF16)
     low = (index & 7).astype(F32).astype(BF16)
-    cells = (dot(high, pick) * 8.0 + dot(low, pick)).astype(jnp.int32)
-    offset_at = lax.broadcasted_iota(jnp.int32, cells.shape, 0)
-    live = jnp.zeros(cells.shape, jnp.int32)
-    for offset in range(offsets):
-        count = index[offsets : offsets + 1, offset : offset + 1]
-        live = jnp.where(offset_at == offset, count, live)
-    slot_at = 4 * lax.broadcasted_iota(jnp.int32, cells.shape, 1)
-    return jnp.where(slot_at < live, cells, -1)
+    return (dot(high, pick) * 8.0 + dot(low, pick)).astype(jnp.int32)
+
+
+def live_quads(count_ref, offset, quads):
+    slot_at = 4 * lax.broadcasted_iota(jnp.int32, (quads, 1), 0)
+    return slot_at < count_ref[:, offset : offset + 1]
 
 
 def one_hot(mask):
     return mask.astype(F32).astype(BF16)
 
 
-def choose_kernel(offsets, index_ref, cells_ref, select_ref):
+def choose_kernel(rows_ref, cells_ref, select_ref, index):
     quads = cells_ref.shape[1]
-    cells = quad_boxes(index_ref, offsets, quads)
+    offsets = rows_ref.shape[0]
+    index[...] = jnp.zeros_like(index)
+    for offset in range(offsets):
+        index[offset : offset + 1] = rows_ref[offset]
+    cells = quad_boxes(index[...], quads)
     cells_ref[...] = cells
     columns = cells.astype(F32).T.astype(jnp.int32)
     box_at = lax.broadcasted_iota(jnp.int32, (quads, select_ref.shape[1]), 1)
@@ -87,7 +87,7 @@
         )
 
 
-def pack_kernel(offsets, field_ref, select_ref, *refs):
+def pack_kernel(offsets, field_ref, select_ref, count_ref, *refs):
     outs, pair = refs[:offsets], refs[offsets]
     band_rows, lon, ch = field_ref.shape
     quads = outs[0].shape[0]
@@ -99,11 +99,13 @@
             line.astype(F32), lon - 1, 0
         ).astype(BF16)
     for part in range(2):
-        picked = dot(select_ref[...], pair[part * lon : part * lon + boxes]).astype(BF16)
+        picked = dot(select_ref[...], pair[part * lon : part * lon + boxes])
         for offset in range(offsets):
-            outs[offset][:, part * 2 * ch : (part + 1) * 2 * ch] = picked[
-                offset * quads : (offset + 1) * quads
-            ]
+            outs[offset][:, part * 2 * ch : (part + 1) * 2 * ch] = jnp.where(
+                live_quads(count_ref, offset, quads),
+                picked[offset * quads : (offset + 1) * quads],
+                0.0,
+            ).astype(BF16)
 
 
 def prepare_kernel(slot_ref, weight_ref, helm_ref, b1_ref, b2_ref, table_ref):
@@ -126,11 +128,11 @@
     return table_ref[at + 8 : at + 9, :ch], table_ref[at + 8 : at + 9, ch : 2 * ch]
 
 
-def interp_kernel(offsets, *refs):
-    blocks = refs[:offsets]
+def interp_kernel(offsets, order, *refs):
+    blocks = dict(zip(order, refs[:offsets]))
     table_ref, dep_ref, up_ref, down_ref, table = refs[offsets:]
     band_rows, lon, ch = dep_ref.shape
-    quads, wide = blocks[0].shape
+    quads, wide = refs[0].shape
     taps = wide // ch
     weights = table_ref[: taps * band_rows + 8].T
     columns = weights[:, taps * band_rows :].astype(jnp.int32)
@@ -168,8 +170,8 @@
 
 def mlp_kernel(
     dep_ref,
+    after_ref,
     before_ref,
-    after_ref,
     cot_ref,
     place_ref,
     table_ref,
@@ -180,11 +182,9 @@
     scaled_ref,
     up_ref,
     down_ref,
-    g1,
+    grads_ref,
     gb1,
-    g2,
     gb2,
-    g3,
     once,
     smooth,
     a1,
@@ -250,21 +250,17 @@
     def whole(ref):
         return ref[...].reshape(flat, ref.shape[2])
 
-    g3[...] = dot(whole(a2), whole(cot_ref), 0, 0)
-    g2[...] = dot(whole(a1), whole(p2), 0, 0)
-    g1[...] = dot(whole(smooth), whole(p1), 0, 0)
+    g3 = dot(whole(a2), whole(cot_ref), 0, 0).astype(BF16)
+    g2 = dot(whole(a1), whole(p2), 0, 0).astype(BF16)
+    g1 = dot(whole(smooth), whole(p1), 0, 0).astype(BF16)
     for row in range(2):
         up_ref[row] = scaled_ref[row].astype(BF16)
         down_ref[row] = scaled_ref[band_rows - 2 + row].astype(BF16)
-
-
-def gather_kernel(g1, gb1, g2, gb2, g3, grads_ref):
-    ch = g1.shape[0]
-    grads_ref[:ch] = g1[:, :ch].astype(BF16)
-    grads_ref[ch : 2 * ch] = g1[:, ch:].astype(BF16)
-    grads_ref[2 * ch : 4 * ch] = g2[:, :ch].astype(BF16)
-    grads_ref[4 * ch : 6 * ch] = g2[:, ch:].astype(BF16)
-    grads_ref[6 * ch : 8 * ch] = g3[...].astype(BF16)
+    grads_ref[:ch] = g1[:, :ch]
+    grads_ref[ch : 2 * ch] = g1[:, ch:]
+    grads_ref[2 * ch : 4 * ch] = g2[:, :ch]
+    grads_ref[4 * ch : 6 * ch] = g2[:, ch:]
+    grads_ref[6 * ch : 8 * ch] = g3
     rest = grads_ref.shape[0] - 8 * ch
     row_at = lax.broadcasted_iota(jnp.int32, (rest, ch), 0)
     tail = jnp.zeros((rest, ch), F32)
@@ -325,7 +321,7 @@
         outs[offset][...] = slot_grads[offset * quads : (offset + 1) * quads]
 
 
-def scatter_kernel(offsets, cells_ref, *refs):
+def scatter_kernel(offsets, cells_ref, count_ref, *refs):
     blocks = refs[:offsets]
     out_ref, done_ref, table, hit = refs[offsets:]
     done_ref[...] = jnp.zeros_like(done_ref)
@@ -333,7 +329,9 @@
     quads = blocks[0].shape[0]
     box_at = lax.broadcasted_iota(jnp.int32, ((band_rows - 1) * lon, quads), 0)
     for offset in range(offsets):
-        table[offset * quads : (offset + 1) * quads] = blocks[offset][...]
+        table[offset * quads : (offset + 1) * quads] = jnp.where(
+            live_quads(count_ref, offset, quads), blocks[offset][...].astype(F32), 0.0
+        ).astype(BF16)
         hit[:, offset * quads : (offset + 1) * quads] = one_hot(
             box_at == cells_ref[offset : offset + 1]
         )
@@ -401,31 +399,30 @@
     place = jnp.stack([lax.axis_index(SPACE).astype(jnp.int32), jnp.int32(bands)])
     block = shape((quads, taps * ch), BF16)
     edge = shape((2, lon, ch), BF16)
-    index = jnp.pad(send_rows[0], ((0, 8 - offsets), (0, 0))) + jnp.pad(
-        send_count, ((offsets, 7 - offsets), (0, slots - offsets))
-    )
 
     cells, select = call(
-        functools.partial(choose_kernel, offsets),
+        choose_kernel,
         [
             shape((8, quads), jnp.int32),
             shape((offsets * quads, (band_rows - 1) * lon), BF16),
         ],
         [VMEM],
+        [pltpu.VMEM((8, slots), jnp.int32)],
         flops=CHOOSE_COST,
         name="choose",
-    )(index)
+    )(jnp.transpose(send_rows, (1, 0, 2)))
     packed = call(
         functools.partial(pack_kernel, offsets),
         [block] * offsets,
-        [VMEM] * 2,
+        [VMEM] * 3,
         [pltpu.VMEM((band_rows * lon, 2 * ch), BF16)],
         name="pack",
-    )(field[0], select)
+    )(field[0], select, send_count)
     received = [
         packed[e] if e == reach else shifted(packed[e], e - reach, bands)
         for e in range(offsets)
     ]
+    order = sorted(range(offsets), key=lambda e: -abs(e - reach))
     (table,) = call(
         prepare_kernel,
         [shape((TABLE_AT + 16, lon), F32)],
@@ -440,46 +437,39 @@
         b_second.reshape(1, hid),
     )
     departure, up, down = call(
-        functools.partial(interp_kernel, offsets),
+        functools.partial(interp_kernel, offsets, order),
         [shape((band_rows, lon, ch), F32), edge, edge],
         [VMEM] * (offsets + 1),
         [pltpu.VMEM((offsets * quads, taps * ch), BF16)],
         name="interp",
-    )(*received, table)
+    )(*(received[e] for e in order), table)
+    after = shifted(up, -1, bands)
     before = shifted(down, 1, bands)
-    after = shifted(up, -1, bands)
     groups = ("y", "x", "core")
     group = lax.axis_size(groups)
     depth = lax.axis_size("z")
-    grad_shapes = [
-        shape((ch, hid), F32),
-        shape((1, hid), F32),
-        shape((hid, hid), F32),
-        shape((1, hid), F32),
-        shape((hid, ch), F32),
-    ]
-    next_state, scaled, up, down, *grads = call(
+    next_state, scaled, up, down, grads = call(
         mlp_kernel,
-        [shape((band_rows, lon, ch), BF16), shape((band_rows, lon, ch), F32), edge, edge]
-        + grad_shapes,
+        [
+            shape((band_rows, lon, ch), BF16),
+            shape((band_rows, lon, ch), F32),
+            edge,
+            edge,
+            shape((group * PART_ROWS, ch), BF16),
+        ],
         [VMEM] * 4 + [SMEM] + [VMEM] * 4,
         [
+            pltpu.VMEM((1, hid), F32),
+            pltpu.VMEM((1, hid), F32),
             pltpu.VMEM((band_rows + 2, lon, ch), F32),
             pltpu.VMEM((band_rows, lon, ch), BF16),
         ]
         + [pltpu.VMEM((band_rows, lon, hid), BF16)] * 4,
         name="smooth_mlp",
-    )(departure, before, after, cotangent[0], place, table, w_first, w_second, w_third)
+    )(departure, after, before, cotangent[0], place, table, w_first, w_second, w_third)
+    after = shifted(up, -1, bands)
     before = shifted(down, 1, bands)
-    after = shifted(up, -1, bands)
-
-    (grads,) = call(
-        gather_kernel,
-        [shape((group * PART_ROWS, ch), BF16)],
-        [VMEM] * 5,
-        flops=GATHER_COST,
-        name="gather",
-    )(*grads)
+
     parts = lax.all_to_all(grads.reshape(group, PART_ROWS, ch), groups, 0, 0)
     slot_grads = call(
         functools.partial(adjoint_kernel, offsets),
@@ -508,14 +498,14 @@
     field_grad, done = call(
         functools.partial(scatter_kernel, offsets),
         [shape((band_rows, lon, ch), F32), shape((8, ch), F32)],
-        [VMEM] * (offsets + 1),
+        [VMEM] * (offsets + 2),
         [
             pltpu.VMEM((offsets * quads, taps * ch), BF16),
             pltpu.VMEM(((band_rows - 1) * lon, offsets * quads), BF16),
         ],
         flops=SCATTER_COST,
         name="scatter",
-    )(cells, *back)
+    )(cells, send_count, *back)
     (whole_sum,) = call(
         functools.partial(sum_kernel, group),
         [shape((group, PART_ROWS, ch), BF16)],
@@ -523,6 +513,13 @@
         name="whole_sum",
     )(parts, slot_grads[reach])
     sums = lax.all_to_all(whole_sum, groups, 0, 0).reshape(group * PART_ROWS, ch)
+    grad_shapes = [
+        shape((ch, hid), F32),
+        shape((1, hid), F32),
+        shape((hid, hid), F32),
+        shape((1, hid), F32),
+        shape((hid, ch), F32),
+    ]
     grads = call(
         unpack_kernel,
         grad_shapes,

time: 89.3 us -> 90.4 us (1.012)
  starting transfers between devices: 38.3 us -> 46.3 us
  waiting for transfers between devices: 29.4 us -> 23.3 us
    ppermute x12, starting transfers between devices: 20 us -> 28 us  [shifted(): lax.ppermute(block, SPACE, [(i, (i + by) % count) for i in range(count)])]
    ppermute x12, waiting for transfers between devices: 14.6 us -> 8.56 us  [shifted(): lax.ppermute(block, SPACE, [(i, (i + by) % count) for i in range(count)])]
    pallas_call x3 -> x2, Pallas kernels: 3.41 us -> 2.65 us  [the longest x1 2.02 us: body(): call(functools.partial(interp_kernel, offsets, order), [shape((band_rows,...]
  transfers between devices with their start and end apart: 15 -> 15, of which waited for: 9 -> 7; matrix products, arithmetic and copies ran while one was open for 0% -> 0% of each run, Pallas kernels for 8% -> 7%
where the time goes in v5:
time: 90.4 us; the launch traced here: 89.9 us
  starting transfers between devices  46.3 us (51%)
  waiting for transfers between devices  23.3 us (26%)
  Pallas kernels  18.3 us (20%)
  local copies, waits for them, and re-layouts  1.1 us (1%)
    ppermute x12, starting transfers between devices, shifted(): lax.ppermute(block, SPACE, [(i, (i + by) % count) for i in range(count)])  28 us
    all_to_all x1, starting transfers between devices, body(): parts = lax.all_to_all(grads.reshape(group, PART_ROWS, ch), groups, 0, 0)  9.69 us
    ppermute x12, waiting for transfers between devices, shifted(): lax.ppermute(block, SPACE, [(i, (i + by) % count) for i in range(count)])  8.56 us
    all_to_all x1, waiting for transfers between devices, body(): lax.all_to_all(whole_sum, groups, 0, 0).reshape(group * PART_ROWS, ch)  7.03 us
    all_to_all x1, waiting for transfers between devices, body(): parts = lax.all_to_all(grads.reshape(group, PART_ROWS, ch), groups, 0, 0)  6.18 us
    pallas_call x1, Pallas kernels, body(): call(mlp_kernel, [shape((band_rows, lon, ch), BF16), shape((band_rows, lo...  6.18 us
    all_to_all x1, starting transfers between devices, body(): lax.all_to_all(whole_sum, groups, 0, 0).reshape(group * PART_ROWS, ch)  5.29 us
    all_to_all x1, starting transfers between devices, body(): parts = lax.all_to_all(part_sum, 'z', 0, 0)  3.36 us
  transfers between devices with their start and end apart: 15, of which 7 were waited for; matrix products, arithmetic and copies ran while one was open for 0% of the time, Pallas kernels for 7%

profile of v5, /device:TPU:1, one launch (start us, length us, event | category | flops | bytes accessed | tf_op | source)
XLA Modules:
  0.0 89.9 jit_solution(18341705810315743640)
XLA Ops:
  0.6 0.0 copy-start.8
  0.6 0.7 copy-done.8
  1.3 0.0 copy-start
  1.3 0.0 copy-start.5
  1.3 0.6 choose.1
  2.0 0.0 copy-start.6
  2.0 0.0 copy-start.7
  2.0 0.0 copy-start.9
  2.0 0.0 copy-start.10
  2.0 0.0 copy-start.11
  2.0 0.3 copy-done
  2.4 0.0 copy-done.5
  2.4 1.3 %pack.1 = (bf16[128,512]{1,0:T(8,128)(2,1)S(1)}, bf16[128,512]{1,0:T(8,128)(2,1)S(1)}, bf16[128,512]{1,0:T(8,128)(2,1)S(1)}, bf16[128,512]{1,0:T(8,128)(2,1)S(1)}, bf16[128,512]{1,0:T(8,128)(2,1)S(1)}) custom-call(bf16[4,512,128]{2,1,0:T(8,128)(2,1)S(1)} %bitcast.14, bf16[640,1536]{1,0:T(8,128)(2,1)S(1)} %get-tuple-element.34.select_ref, s32[1,5]{1,0:T(1,128)S(1)} %copy-done.5), custom_call_target="tpu_custom_call" | custom-call | bytes 1310720 | tf_op jit(solution)/shard_map/pack/pallas_call | solution.py:414
  3.7 8.7 %collective-permute-start = (bf16[128,512]{1,0:T(8,128)(2,1)S(1)}, bf16[128,512]{1,0:T(8,128)(2,1)S(1)}, u32[]{:S(2)}, u32[]{:S(2)}) collective-permute-start(bf16[128,512]{1,0:T(8,128)(2,1)S(1)} %get-tuple-element.35), channel_id=1, source_target_pairs={{0,62},{1,63},{2,0},{3,1},{4,2},{5,3},{6,4},{7,5},{8,6},{9,7},{10,... | collective-permute-start | bytes 393224 | tf_op jit(solution)/shard_map/ppermute | solution.py:374
  12.4 0.0 collective-permute-start.1
  12.4 1.0 %collective-permute-start.2 = (bf16[128,512]{1,0:T(8,128)(2,1)S(1)}, bf16[128,512]{1,0:T(8,128)(2,1)S(1)}, u32[]{:S(2)}, u32[]{:S(2)}) collective-permute-start(bf16[128,512]{1,0:T(8,128)(2,1)S(1)} %get-tuple-element.37), channel_id=1, source_target_pairs={{0,63},{1,0},{2,1},{3,2},{4,3},{5,4},{6,5},{7,6},{8,7},{9,8},{10,9... | collective-permute-start | bytes 393224 | tf_op jit(solution)/shard_map/ppermute | solution.py:374
  13.4 0.8 collective-permute-start.3
  14.1 0.0 copy-done.6
  14.1 0.0 copy-done.7
  14.1 0.0 copy-done.9
  14.2 0.0 copy-done.10
  14.2 0.0 copy-done.11
  14.2 0.0 copy-start.1
  14.2 0.0 copy-start.2
  14.2 0.0 copy-start.3
  14.2 0.0 copy-start.4
  14.2 0.3 collective-permute-done.refs_0_
  14.6 5.0 %collective-permute-done.1.refs_1_ = bf16[128,512]{1,0:T(8,128)(2,1)S(1)} collective-permute-done((bf16[128,512]{1,0:T(8,128)(2,1)S(1)}, bf16[128,512]{1,0:T(8,128)(2,1)S(1)}, u32[]{:S(2)}, u32[]{:S(2)}) %collective-permute-start.1) | collective-permute-done | bytes 131104 | tf_op jit(solution)/shard_map/ppermute | solution.py:374
  19.5 0.0 collective-permute-done.2.refs_2_
  19.5 0.0 collective-permute-done.3.refs_3_
  19.5 2.0 %interp.1 = (f32[4,512,128]{2,1,0:T(8,128)S(1)}, bf16[2,512,128]{2,1,0:T(8,128)(2,1)S(1)}, bf16[2,512,128]{2,1,0:T(8,128)(2,1)S(1)}) custom-call(bf16[128,512]{1,0:T(8,128)(2,1)S(1)} %collective-permute-done.refs_0_, bf16[128,512]{1,0:T(8,128)(2,1)S(1)} %collective-permute-done.1.refs_1_, bf16[128,512]{1,0:T(8,128)(2,1)S(1)} %collective-permute-done.2.refs_2_, ...), custom_call_target="tpu_custom_call" | custom-call | bytes 3145728 | tf_op jit(solution)/shard_map/interp/pallas_call | solution.py:439
  21.6 5.8 %collective-permute-start.4 = (bf16[2,512,128]{2,1,0:T(8,128)(2,1)S(1)}, bf16[2,512,128]{2,1,0:T(8,128)(2,1)S(1)}, u32[]{:S(2)}, u32[]{:S(2)}) collective-permute-start(bf16[2,512,128]{2,1,0:T(8,128)(2,1)S(1)} %get-tuple-element.41), channel_id=1, source_target_pairs={{0,63},{1,0},{2,1},{3,2},{4,3},{5,4},{6,5},{7,6},{8,7},{9,8},{10,9... | collective-permute-start | bytes 786440 | tf_op jit(solution)/shard_map/ppermute | solution.py:374
  27.4 0.0 collective-permute-start.5
  27.4 0.1 pad_add_fusion.place_ref
  27.5 1.1 %collective-permute-done.4.after_ref = bf16[2,512,128]{2,1,0:T(8,128)(2,1)S(1)} collective-permute-done((bf16[2,512,128]{2,1,0:T(8,128)(2,1)S(1)}, bf16[2,512,128]{2,1,0:T(8,128)(2,1)S(1)}, u32[]{:S(2)}, u32[]{:S(2)}) %collective-permute-start.4) | collective-permute-done | bytes 262176 | tf_op jit(solution)/shard_map/ppermute | solution.py:374
  28.6 2.2 %collective-permute-done.5.before_ref = bf16[2,512,128]{2,1,0:T(8,128)(2,1)S(1)} collective-permute-done((bf16[2,512,128]{2,1,0:T(8,128)(2,1)S(1)}, bf16[2,512,128]{2,1,0:T(8,128)(2,1)S(1)}, u32[]{:S(2)}, u32[]{:S(2)}) %collective-permute-start.5) | collective-permute-done | bytes 262176 | tf_op jit(solution)/shard_map/ppermute | solution.py:374
  30.7 0.0 copy-done.1
  30.7 0.0 copy-done.2
  30.7 0.0 copy-done.3
  30.7 0.0 copy-done.4
  30.7 6.2 %smooth_mlp.1 = (bf16[4,512,128]{2,1,0:T(8,128)(2,1)}, f32[4,512,128]{2,1,0:T(8,128)S(1)}, bf16[2,512,128]{2,1,0:T(8,128)(2,1)}, bf16[2,512,128]{2,1,0:T(8,128)(2,1)}, bf16[1280,128]{1,0:T(8,128)(2,1)}) custom-call(f32[4,512,128]{2,1,0:T(8,128)S(1)} %get-tuple-element.40.dep_ref, bf16[2,512,128]{2,1,0:T(8,128)(2,1)S(1)} %collective-permute-done.4.after_ref, ...), custom_call_target="tpu_custom_call" | custom-call | bytes 4849664 | tf_op jit(solution)/shard_map/smooth_mlp/pallas_call | solution.py:451
  36.9 2.5 %collective-permute-start.6 = (bf16[2,512,128]{2,1,0:T(8,128)(2,1)}, bf16[2,512,128]{2,1,0:T(8,128)(2,1)S(1)}, u32[]{:S(2)}, u32[]{:S(2)}) collective-permute-start(bf16[2,512,128]{2,1,0:T(8,128)(2,1)} %get-tuple-element.46), channel_id=1, source_target_pairs={{0,1},{1,2},{2,3},{3,4},{4,5},{5,6},{6,7},{7,8},{8,9},{9,10},{10,1... | collective-permute-start | bytes 786440 | tf_op jit(solution)/shard_map/ppermute | solution.py:374
  39.4 3.6 %collective-permute-start.7 = (bf16[2,512,128]{2,1,0:T(8,128)(2,1)}, bf16[2,512,128]{2,1,0:T(8,128)(2,1)S(1)}, u32[]{:S(2)}, u32[]{:S(2)}) collective-permute-start(bf16[2,512,128]{2,1,0:T(8,128)(2,1)} %get-tuple-element.47), channel_id=1, source_target_pairs={{0,63},{1,0},{2,1},{3,2},{4,3},{5,4},{6,5},{7,6},{8,7},{9,8},{10,9... | collective-permute-start | bytes 786440 | tf_op jit(solution)/shard_map/ppermute | solution.py:374
  43.0 9.7 %all-to-all-start = ((bf16[32,40,128]{2,1,0:T(8,128)(2,1)}), bf16[32,40,128]{2,1,0:T(8,128)(2,1)S(1)}, u32[]{:S(2)}, u32[]{:S(2)}) async-start(bf16[32,40,128]{2,1,0:T(8,128)(2,1)} %bitcast.9), calls=%async_computation | async-start | bytes 655360 | tf_op jit(solution)/shard_map/all_to_all | solution.py:473
  52.7 0.0 collective-permute-done.6.before_ref
  52.7 0.0 collective-permute-done.7.after_ref
  52.7 3.3 %adjoint.1 = (bf16[128,512]{1,0:T(8,128)(2,1)S(1)}, bf16[128,512]{1,0:T(8,128)(2,1)S(1)}, bf16[128,512]{1,0:T(8,128)(2,1)S(1)}, bf16[128,512]{1,0:T(8,128)(2,1)S(1)}, bf16[128,512]{1,0:T(8,128)(2,1)S(1)}) custom-call(f32[4,512,128]{2,1,0:T(8,128)S(1)} %get-tuple-element.45.scaled_ref, bf16[2,512,128]{2,1,0:T(8,128)(2,1)S(1)} %collective-permute-done.6.before_ref, ...), custom_call_target="tpu_custom_call" | custom-call | flops 99999997952 | bytes 1310720 | tf_op jit(solution)/shard_map/adjoint/pallas_call | solution.py:474
  56.0 6.2 %all-to-all-done.parts_ref = bf16[32,40,128]{2,1,0:T(8,128)(2,1)S(1)} async-done(((bf16[32,40,128]{2,1,0:T(8,128)(2,1)}), bf16[32,40,128]{2,1,0:T(8,128)(2,1)S(1)}, u32[]{:S(2)}, u32[]{:S(2)}) %all-to-all-start) | async-done | bytes 327712 | tf_op jit(solution)/shard_map/all_to_all | solution.py:473
  62.2 0.7 part_sum.1
  62.9 3.4 %all-to-all-start.1 = ((bf16[8,40,128]{2,1,0:T(8,128)(2,1)}), bf16[8,40,128]{2,1,0:T(8,128)(2,1)S(1)}, u32[]{:S(2)}, u32[]{:S(2)}) async-start(bf16[8,40,128]{2,1,0:T(8,128)(2,1)} %part_sum.1), calls=%async_computation.1 | async-start | bytes 163840 | tf_op jit(solution)/shard_map/all_to_all | solution.py:493
  66.3 0.6 collective-permute-start.8
  66.9 0.6 collective-permute-start.9
  67.5 0.0 collective-permute-start.10
  67.5 4.4 %collective-permute-start.11 = (bf16[128,512]{1,0:T(8,128)(2,1)S(1)}, bf16[128,512]{1,0:T(8,128)(2,1)S(1)}, u32[]{:S(2)}, u32[]{:S(2)}) collective-permute-start(bf16[128,512]{1,0:T(8,128)(2,1)S(1)} %get-tuple-element.52), channel_id=1, source_target_pairs={{0,62},{1,63},{2,0},{3,1},{4,2},{5,3},{6,4},{7,5},{8,6},{9,7},{10,... | collective-permute-start | bytes 393224 | tf_op jit(solution)/shard_map/ppermute | solution.py:374
  71.9 1.5 %all-to-all-done.1.parts_ref = bf16[8,40,128]{2,1,0:T(8,128)(2,1)S(1)} async-done(((bf16[8,40,128]{2,1,0:T(8,128)(2,1)}), bf16[8,40,128]{2,1,0:T(8,128)(2,1)S(1)}, u32[]{:S(2)}, u32[]{:S(2)}) %all-to-all-start.1) | async-done | bytes 81952 | tf_op jit(solution)/shard_map/all_to_all | solution.py:493
  73.5 0.8 whole_sum.1
  74.2 5.3 %all-to-all-start.2 = ((bf16[32,40,128]{2,1,0:T(8,128)(2,1)}), bf16[32,40,128]{2,1,0:T(8,128)(2,1)S(1)}, u32[]{:S(2)}, u32[]{:S(2)}) async-start(bf16[32,40,128]{2,1,0:T(8,128)(2,1)} %whole_sum.1), calls=%async_computation.2 | async-start | bytes 655360 | tf_op jit(solution)/shard_map/all_to_all | solution.py:515
  79.5 0.0 collective-permute-done.8.refs_0_
  79.6 0.0 collective-permute-done.9.refs_1_
  79.6 0.0 collective-permute-done.10.refs_3_
  79.6 0.0 collective-permute-done.11.refs_4_
  79.6 2.5 %scatter.1 = (f32[4,512,128]{2,1,0:T(8,128)}, f32[8,128]{1,0:T(8,128)S(1)}) custom-call(s32[8,128]{1,0:T(8,128)S(1)} %get-tuple-element.44.cells_ref, s32[1,5]{1,0:T(1,128)S(1)} %copy-done.5, bf16[128,512]{1,0:T(8,128)(2,1)S(1)} %collective-permute-done.8.refs_0_, bf16[128,512]{1,0:T(8,128)(2,1)S(1)} %collective-permute-done.9.refs_1_, ...), custom_call_target="tpu_custom_call" | custom-call | flops 99999997952 | bytes 2105344 | tf_op jit(solution)/shard_map/scatter/pallas_call | solution.py:498
  82.1 7.0 %all-to-all-done.2 = bf16[32,40,128]{2,1,0:T(8,128)(2,1)S(1)} async-done(((bf16[32,40,128]{2,1,0:T(8,128)(2,1)}), bf16[32,40,128]{2,1,0:T(8,128)(2,1)S(1)}, u32[]{:S(2)}, u32[]{:S(2)}) %all-to-all-start.2) | async-done | bytes 327712 | tf_op jit(solution)/shard_map/all_to_all | solution.py:515
  89.1 0.8 unpack.1
  (1 shorter events, 0.0 us)
Async XLA Ops:
  0.6 0.7 copy-start.8
  1.3 1.0 %copy-start = (bf16[1,4,512,128]{3,2,1,0:T(8,128)(2,1)S(1)}, bf16[1,4,512,128]{3,2,1,0:T(8,128)(2,1)}, u32[]{:S(2)}) copy-start(bf16[1,4,512,128]{3,2,1,0:T(8,128)(2,1)} %param.12) | copy-start | bytes 1572868
  1.3 1.0 %copy-start.5 = (s32[1,5]{1,0:T(1,128)S(1)}, s32[1,5]{1,0:T(1,128)}, u32[]{:S(2)}) copy-start(s32[1,5]{1,0:T(1,128)} %count_ref.3) | copy-start | bytes 64
  2.0 12.2 %copy-start.6 = (s32[4,4,512]{2,1,0:T(4,128)S(1)}, s32[4,4,512]{2,1,0:T(4,128)}, u32[]{:S(2)}) copy-start(s32[4,4,512]{2,1,0:T(4,128)} %slot_ref.1) | copy-start | bytes 98308
  2.0 12.2 %copy-start.7 = (f32[4,4,512]{2,1,0:T(4,128)S(1)}, f32[4,4,512]{2,1,0:T(4,128)}, u32[]{:S(2)}) copy-start(f32[4,4,512]{2,1,0:T(4,128)} %weight_ref.1) | copy-start | bytes 98308
  2.0 12.1 %copy-start.9 = (f32[256]{0:T(256)S(1)}, f32[256]{0:T(256)}, u32[]{:S(2)}) copy-start(f32[256]{0:T(256)} %param.19) | copy-start | bytes 3076
  2.0 12.1 %copy-start.10 = (f32[256]{0:T(256)S(1)}, f32[256]{0:T(256)}, u32[]{:S(2)}) copy-start(f32[256]{0:T(256)} %param.21) | copy-start | bytes 3076
  2.0 12.1 %copy-start.11 = (f32[128]{0:T(128)S(1)}, f32[128]{0:T(128)}, u32[]{:S(2)}) copy-start(f32[128]{0:T(128)} %param.17) | copy-start | bytes 1540
  3.7 10.8 %collective-permute-start = (bf16[128,512]{1,0:T(8,128)(2,1)S(1)}, bf16[128,512]{1,0:T(8,128)(2,1)S(1)}, u32[]{:S(2)}, u32[]{:S(2)}) collective-permute-start(bf16[128,512]{1,0:T(8,128)(2,1)S(1)} %get-tuple-element.35), channel_id=1, source_target_pairs={{0,62},{1,63},{2,0},{3,1},{4,2},{5,3},{6,4},{7,5},{8,6},{9,7},{10,... | collective-permute-start | bytes 393224 | tf_op jit(solution)/shard_map/ppermute | solution.py:374
  12.4 7.1 %collective-permute-start.1 = (bf16[128,512]{1,0:T(8,128)(2,1)S(1)}, bf16[128,512]{1,0:T(8,128)(2,1)S(1)}, u32[]{:S(2)}, u32[]{:S(2)}) collective-permute-start(bf16[128,512]{1,0:T(8,128)(2,1)S(1)} %get-tuple-element.36), channel_id=1, source_target_pairs={{0,2},{1,3},{2,4},{3,5},{4,6},{5,7},{6,8},{7,9},{8,10},{9,11},{10,... | collective-permute-start | bytes 393224 | tf_op jit(solution)/shard_map/ppermute | solution.py:374
  12.4 7.1 %collective-permute-start.2 = (bf16[128,512]{1,0:T(8,128)(2,1)S(1)}, bf16[128,512]{1,0:T(8,128)(2,1)S(1)}, u32[]{:S(2)}, u32[]{:S(2)}) collective-permute-start(bf16[128,512]{1,0:T(8,128)(2,1)S(1)} %get-tuple-element.37), channel_id=1, source_target_pairs={{0,63},{1,0},{2,1},{3,2},{4,3},{5,4},{6,5},{7,6},{8,7},{9,8},{10,9... | collective-permute-start | bytes 393224 | tf_op jit(solution)/shard_map/ppermute | solution.py:374
  13.4 6.2 %collective-permute-start.3 = (bf16[128,512]{1,0:T(8,128)(2,1)S(1)}, bf16[128,512]{1,0:T(8,128)(2,1)S(1)}, u32[]{:S(2)}, u32[]{:S(2)}) collective-permute-start(bf16[128,512]{1,0:T(8,128)(2,1)S(1)} %get-tuple-element.38), channel_id=1, source_target_pairs={{0,1},{1,2},{2,3},{3,4},{4,5},{5,6},{6,7},{7,8},{8,9},{9,10},{10,1... | collective-permute-start | bytes 393224 | tf_op jit(solution)/shard_map/ppermute | solution.py:374
  14.2 16.5 %copy-start.1 = (bf16[1,4,512,128]{3,2,1,0:T(8,128)(2,1)S(1)}, bf16[1,4,512,128]{3,2,1,0:T(8,128)(2,1)}, u32[]{:S(2)}) copy-start(bf16[1,4,512,128]{3,2,1,0:T(8,128)(2,1)} %param.23) | copy-start | bytes 1572868
  14.2 16.5 %copy-start.2 = (bf16[256,256]{1,0:T(8,128)(2,1)S(1)}, bf16[256,256]{1,0:T(8,128)(2,1)}, u32[]{:S(2)}) copy-start(bf16[256,256]{1,0:T(8,128)(2,1)} %w2_ref.1) | copy-start | bytes 393220
  14.2 16.5 %copy-start.3 = (bf16[128,256]{1,0:T(8,128)(2,1)S(1)}, bf16[128,256]{1,0:T(8,128)(2,1)}, u32[]{:S(2)}) copy-start(bf16[128,256]{1,0:T(8,128)(2,1)} %w1_ref.1) | copy-start | bytes 196612
  14.2 16.5 %copy-start.4 = (bf16[256,128]{1,0:T(8,128)(2,1)S(1)}, bf16[256,128]{1,0:T(8,128)(2,1)}, u32[]{:S(2)}) copy-start(bf16[256,128]{1,0:T(8,128)(2,1)} %w3_ref.1) | copy-start | bytes 196612
  21.6 7.0 %collective-permute-start.4 = (bf16[2,512,128]{2,1,0:T(8,128)(2,1)S(1)}, bf16[2,512,128]{2,1,0:T(8,128)(2,1)S(1)}, u32[]{:S(2)}, u32[]{:S(2)}) collective-permute-start(bf16[2,512,128]{2,1,0:T(8,128)(2,1)S(1)} %get-tuple-element.41), channel_id=1, source_target_pairs={{0,63},{1,0},{2,1},{3,2},{4,3},{5,4},{6,5},{7,6},{8,7},{9,8},{10,9... | collective-permute-start | bytes 786440 | tf_op jit(solution)/shard_map/ppermute | solution.py:374
  27.4 3.3 %collective-permute-start.5 = (bf16[2,512,128]{2,1,0:T(8,128)(2,1)S(1)}, bf16[2,512,128]{2,1,0:T(8,128)(2,1)S(1)}, u32[]{:S(2)}, u32[]{:S(2)}) collective-permute-start(bf16[2,512,128]{2,1,0:T(8,128)(2,1)S(1)} %get-tuple-element.42), channel_id=1, source_target_pairs={{0,1},{1,2},{2,3},{3,4},{4,5},{5,6},{6,7},{7,8},{8,9},{9,10},{10,1... | collective-permute-start | bytes 786440 | tf_op jit(solution)/shard_map/ppermute | solution.py:374
  36.9 15.8 %collective-permute-start.6 = (bf16[2,512,128]{2,1,0:T(8,128)(2,1)}, bf16[2,512,128]{2,1,0:T(8,128)(2,1)S(1)}, u32[]{:S(2)}, u32[]{:S(2)}) collective-permute-start(bf16[2,512,128]{2,1,0:T(8,128)(2,1)} %get-tuple-element.46), channel_id=1, source_target_pairs={{0,1},{1,2},{2,3},{3,4},{4,5},{5,6},{6,7},{7,8},{8,9},{9,10},{10,1... | collective-permute-start | bytes 786440 | tf_op jit(solution)/shard_map/ppermute | solution.py:374
  39.4 13.3 %collective-permute-start.7 = (bf16[2,512,128]{2,1,0:T(8,128)(2,1)}, bf16[2,512,128]{2,1,0:T(8,128)(2,1)S(1)}, u32[]{:S(2)}, u32[]{:S(2)}) collective-permute-start(bf16[2,512,128]{2,1,0:T(8,128)(2,1)} %get-tuple-element.47), channel_id=1, source_target_pairs={{0,63},{1,0},{2,1},{3,2},{4,3},{5,4},{6,5},{7,6},{8,7},{9,8},{10,9... | collective-permute-start | bytes 786440 | tf_op jit(solution)/shard_map/ppermute | solution.py:374
  43.0 19.2 %all-to-all-start = ((bf16[32,40,128]{2,1,0:T(8,128)(2,1)}), bf16[32,40,128]{2,1,0:T(8,128)(2,1)S(1)}, u32[]{:S(2)}, u32[]{:S(2)}) async-start(bf16[32,40,128]{2,1,0:T(8,128)(2,1)} %bitcast.9), calls=%async_computation | async-start | bytes 655360 | tf_op jit(solution)/shard_map/all_to_all | solution.py:473
  62.9 10.6 %all-to-all-start.1 = ((bf16[8,40,128]{2,1,0:T(8,128)(2,1)}), bf16[8,40,128]{2,1,0:T(8,128)(2,1)S(1)}, u32[]{:S(2)}, u32[]{:S(2)}) async-start(bf16[8,40,128]{2,1,0:T(8,128)(2,1)} %part_sum.1), calls=%async_computation.1 | async-start | bytes 163840 | tf_op jit(solution)/shard_map/all_to_all | solution.py:493
  66.3 13.3 %collective-permute-start.8 = (bf16[128,512]{1,0:T(8,128)(2,1)S(1)}, bf16[128,512]{1,0:T(8,128)(2,1)S(1)}, u32[]{:S(2)}, u32[]{:S(2)}) collective-permute-start(bf16[128,512]{1,0:T(8,128)(2,1)S(1)} %get-tuple-element.48), channel_id=1, source_target_pairs={{0,2},{1,3},{2,4},{3,5},{4,6},{5,7},{6,8},{7,9},{8,10},{9,11},{10,... | collective-permute-start | bytes 393224 | tf_op jit(solution)/shard_map/ppermute | solution.py:374
  66.9 12.7 %collective-permute-start.9 = (bf16[128,512]{1,0:T(8,128)(2,1)S(1)}, bf16[128,512]{1,0:T(8,128)(2,1)S(1)}, u32[]{:S(2)}, u32[]{:S(2)}) collective-permute-start(bf16[128,512]{1,0:T(8,128)(2,1)S(1)} %get-tuple-element.49), channel_id=1, source_target_pairs={{0,1},{1,2},{2,3},{3,4},{4,5},{5,6},{6,7},{7,8},{8,9},{9,10},{10,1... | collective-permute-start | bytes 393224 | tf_op jit(solution)/shard_map/ppermute | solution.py:374
  67.5 12.1 %collective-permute-start.10 = (bf16[128,512]{1,0:T(8,128)(2,1)S(1)}, bf16[128,512]{1,0:T(8,128)(2,1)S(1)}, u32[]{:S(2)}, u32[]{:S(2)}) collective-permute-start(bf16[128,512]{1,0:T(8,128)(2,1)S(1)} %get-tuple-element.51), channel_id=1, source_target_pairs={{0,63},{1,0},{2,1},{3,2},{4,3},{5,4},{6,5},{7,6},{8,7},{9,8},{10,9... | collective-permute-start | bytes 393224 | tf_op jit(solution)/shard_map/ppermute | solution.py:374
  67.5 12.1 %collective-permute-start.11 = (bf16[128,512]{1,0:T(8,128)(2,1)S(1)}, bf16[128,512]{1,0:T(8,128)(2,1)S(1)}, u32[]{:S(2)}, u32[]{:S(2)}) collective-permute-start(bf16[128,512]{1,0:T(8,128)(2,1)S(1)} %get-tuple-element.52), channel_id=1, source_target_pairs={{0,62},{1,63},{2,0},{3,1},{4,2},{5,3},{6,4},{7,5},{8,6},{9,7},{10,... | collective-permute-start | bytes 393224 | tf_op jit(solution)/shard_map/ppermute | solution.py:374
  74.2 14.9 %all-to-all-start.2 = ((bf16[32,40,128]{2,1,0:T(8,128)(2,1)}), bf16[32,40,128]{2,1,0:T(8,128)(2,1)S(1)}, u32[]{:S(2)}, u32[]{:S(2)}) async-start(bf16[32,40,128]{2,1,0:T(8,128)(2,1)} %whole_sum.1), calls=%async_computation.2 | async-start | bytes 655360 | tf_op jit(solution)/shard_map/all_to_all | solution.py:515

commit v6 on v5

--- a/solution.py
+++ b/solution.py
@@ -180,8 +180,6 @@
     w3_ref,
     next_ref,
     scaled_ref,
-    up_ref,
-    down_ref,
     grads_ref,
     gb1,
     gb2,
@@ -253,9 +251,6 @@
     g3 = dot(whole(a2), whole(cot_ref), 0, 0).astype(BF16)
     g2 = dot(whole(a1), whole(p2), 0, 0).astype(BF16)
     g1 = dot(whole(smooth), whole(p1), 0, 0).astype(BF16)
-    for row in range(2):
-        up_ref[row] = scaled_ref[row].astype(BF16)
-        down_ref[row] = scaled_ref[band_rows - 2 + row].astype(BF16)
     grads_ref[:ch] = g1[:, :ch]
     grads_ref[ch : 2 * ch] = g1[:, ch:]
     grads_ref[2 * ch : 4 * ch] = g2[:, :ch]
@@ -267,6 +262,11 @@
     for index, line in enumerate((gb1[:, :ch], gb1[:, ch:], gb2[:, :ch], gb2[:, ch:])):
         tail = jnp.where(row_at == index, line, tail)
     grads_ref[8 * ch :] = tail.astype(BF16)
+
+
+def edges_kernel(scaled_ref, up_ref, down_ref):
+    up_ref[...] = scaled_ref[:2].astype(BF16)
+    down_ref[...] = scaled_ref[scaled_ref.shape[0] - 2 :].astype(BF16)
 
 
 def adjoint_kernel(
@@ -349,7 +349,8 @@
         out_ref[row] = here + pltpu.roll(right, 1, 0)
 
 
-def sum_kernel(copies, parts_ref, ahead_ref, out_ref):
+def sum_kernel(copies, parts_ref, *refs):
+    out_ref = refs[-1]
     total = parts_ref[0].astype(F32)
     for part in range(1, parts_ref.shape[0]):
         total = total + parts_ref[part].astype(F32)
@@ -448,13 +449,11 @@
     groups = ("y", "x", "core")
     group = lax.axis_size(groups)
     depth = lax.axis_size("z")
-    next_state, scaled, up, down, grads = call(
+    next_state, scaled, grads = call(
         mlp_kernel,
         [
             shape((band_rows, lon, ch), BF16),
             shape((band_rows, lon, ch), F32),
-            edge,
-            edge,
             shape((group * PART_ROWS, ch), BF16),
         ],
         [VMEM] * 4 + [SMEM] + [VMEM] * 4,
@@ -467,6 +466,7 @@
         + [pltpu.VMEM((band_rows, lon, hid), BF16)] * 4,
         name="smooth_mlp",
     )(departure, after, before, cotangent[0], place, table, w_first, w_second, w_third)
+    up, down = call(edges_kernel, [edge, edge], [VMEM], name="edges")(scaled)
     after = shifted(up, -1, bands)
     before = shifted(down, 1, bands)
 
@@ -486,10 +486,10 @@
     (part_sum,) = call(
         functools.partial(sum_kernel, depth),
         [shape((depth, PART_ROWS, ch), BF16)],
-        [VMEM, ANY],
+        [VMEM],
         flops=PART_COST,
         name="part_sum",
-    )(parts, slot_grads[reach])
+    )(parts)
     parts = lax.all_to_all(part_sum, "z", 0, 0)
     back = [
         slot_grads[e] if e == reach else shifted(slot_grads[e], reach - e, bands)

time: 90.4 us -> 90.1 us (level)
  starting transfers between devices: 46.3 us -> 43.1 us
  waiting for transfers between devices: 23.3 us -> 26.2 us
    ppermute x12, starting transfers between devices: 28 us -> 23.5 us  [shifted(): lax.ppermute(block, SPACE, [(i, (i + by) % count) for i in range(count)])]
    all_to_all x1, waiting for transfers between devices: 6.18 us -> 10.6 us  [body(): parts = lax.all_to_all(grads.reshape(group, PART_ROWS, ch), groups, 0, 0)]
    all_to_all x1, waiting for transfers between devices: 1.55 us -> 0.01 us  [body(): parts = lax.all_to_all(part_sum, 'z', 0, 0)]
    all_to_all x1, starting transfers between devices: 9.69 us -> 10.7 us  [body(): parts = lax.all_to_all(grads.reshape(group, PART_ROWS, ch), groups, 0, 0)]
  transfers between devices with their start and end apart: 15 -> 15, of which waited for: 7 -> 6; matrix products, arithmetic and copies ran while one was open for 0% -> 0% of each run, Pallas kernels for 7% -> 8%
where the time goes in v6:
time: 90.1 us; the launch traced here: 89.6 us
  starting transfers between devices  43.1 us (48%)
  waiting for transfers between devices  26.2 us (29%)
  Pallas kernels  18.2 us (20%)
  local copies, waits for them, and re-layouts  1.1 us (1%)
    ppermute x12, starting transfers between devices, shifted(): lax.ppermute(block, SPACE, [(i, (i + by) % count) for i in range(count)])  23.5 us
    all_to_all x1, starting transfers between devices, body(): parts = lax.all_to_all(grads.reshape(group, PART_ROWS, ch), groups, 0, 0)  10.7 us
    all_to_all x1, waiting for transfers between devices, body(): parts = lax.all_to_all(grads.reshape(group, PART_ROWS, ch), groups, 0, 0)  10.6 us
    ppermute x12, waiting for transfers between devices, shifted(): lax.ppermute(block, SPACE, [(i, (i + by) % count) for i in range(count)])  8.56 us
    all_to_all x1, waiting for transfers between devices, body(): lax.all_to_all(whole_sum, groups, 0, 0).reshape(group * PART_ROWS, ch)  7.13 us
    pallas_call x1, Pallas kernels, body(): call(mlp_kernel, [shape((band_rows, lon, ch), BF16), shape((band_rows, lo...  6.16 us
    all_to_all x1, starting transfers between devices, body(): lax.all_to_all(whole_sum, groups, 0, 0).reshape(group * PART_ROWS, ch)  5.55 us
    all_to_all x1, starting transfers between devices, body(): parts = lax.all_to_all(part_sum, 'z', 0, 0)  3.36 us
  transfers between devices with their start and end apart: 15, of which 6 were waited for; matrix products, arithmetic and copies ran while one was open for 0% of the time, Pallas kernels for 8%

profile of v6, /device:TPU:1, one launch (start us, length us, event | category | flops | bytes accessed | tf_op | source)
XLA Modules:
  0.0 89.6 jit_solution(17510645258658909316)
XLA Ops:
  0.6 0.0 copy-start.8
  0.6 0.7 copy-done.8
  1.3 0.0 copy-start
  1.3 0.6 choose.1
  2.0 0.0 copy-start.6
  2.0 0.0 copy-start.7
  2.0 0.0 copy-start.9
  2.0 0.0 copy-start.10
  2.0 0.0 copy-start.11
  2.0 0.3 copy-done
  2.4 0.0 copy-done.5
  2.4 1.3 %pack.1 = (bf16[128,512]{1,0:T(8,128)(2,1)S(1)}, bf16[128,512]{1,0:T(8,128)(2,1)S(1)}, bf16[128,512]{1,0:T(8,128)(2,1)S(1)}, bf16[128,512]{1,0:T(8,128)(2,1)S(1)}, bf16[128,512]{1,0:T(8,128)(2,1)S(1)}) custom-call(bf16[4,512,128]{2,1,0:T(8,128)(2,1)S(1)} %bitcast.14, bf16[640,1536]{1,0:T(8,128)(2,1)S(1)} %get-tuple-element.34.select_ref, s32[1,5]{1,0:T(1,128)S(1)} %copy-done.5), custom_call_target="tpu_custom_call" | custom-call | bytes 1310720 | tf_op jit(solution)/shard_map/pack/pallas_call | solution.py:415
  3.7 8.7 %collective-permute-start = (bf16[128,512]{1,0:T(8,128)(2,1)S(1)}, bf16[128,512]{1,0:T(8,128)(2,1)S(1)}, u32[]{:S(2)}, u32[]{:S(2)}) collective-permute-start(bf16[128,512]{1,0:T(8,128)(2,1)S(1)} %get-tuple-element.35), channel_id=1, source_target_pairs={{0,62},{1,63},{2,0},{3,1},{4,2},{5,3},{6,4},{7,5},{8,6},{9,7},{10,... | collective-permute-start | bytes 393224 | tf_op jit(solution)/shard_map/ppermute | solution.py:375
  12.4 0.0 collective-permute-start.1
  12.4 1.0 %collective-permute-start.2 = (bf16[128,512]{1,0:T(8,128)(2,1)S(1)}, bf16[128,512]{1,0:T(8,128)(2,1)S(1)}, u32[]{:S(2)}, u32[]{:S(2)}) collective-permute-start(bf16[128,512]{1,0:T(8,128)(2,1)S(1)} %get-tuple-element.37), channel_id=1, source_target_pairs={{0,63},{1,0},{2,1},{3,2},{4,3},{5,4},{6,5},{7,6},{8,7},{9,8},{10,9... | collective-permute-start | bytes 393224 | tf_op jit(solution)/shard_map/ppermute | solution.py:375
  13.4 0.8 collective-permute-start.3
  14.1 0.0 copy-done.6
  14.1 0.0 copy-done.7
  14.1 0.0 copy-done.9
  14.2 0.0 copy-done.10
  14.2 0.0 copy-done.11
  14.2 0.0 copy-start.1
  14.2 0.0 copy-start.2
  14.2 0.0 copy-start.3
  14.2 0.0 copy-start.4
  14.2 0.3 collective-permute-done.refs_0_
  14.6 5.0 %collective-permute-done.1.refs_1_ = bf16[128,512]{1,0:T(8,128)(2,1)S(1)} collective-permute-done((bf16[128,512]{1,0:T(8,128)(2,1)S(1)}, bf16[128,512]{1,0:T(8,128)(2,1)S(1)}, u32[]{:S(2)}, u32[]{:S(2)}) %collective-permute-start.1) | collective-permute-done | bytes 131104 | tf_op jit(solution)/shard_map/ppermute | solution.py:375
  19.5 0.0 collective-permute-done.2.refs_2_
  19.5 0.0 collective-permute-done.3.refs_3_
  19.5 2.0 %interp.1 = (f32[4,512,128]{2,1,0:T(8,128)S(1)}, bf16[2,512,128]{2,1,0:T(8,128)(2,1)S(1)}, bf16[2,512,128]{2,1,0:T(8,128)(2,1)S(1)}) custom-call(bf16[128,512]{1,0:T(8,128)(2,1)S(1)} %collective-permute-done.refs_0_, bf16[128,512]{1,0:T(8,128)(2,1)S(1)} %collective-permute-done.1.refs_1_, bf16[128,512]{1,0:T(8,128)(2,1)S(1)} %collective-permute-done.2.refs_2_, ...), custom_call_target="tpu_custom_call" | custom-call | bytes 3145728 | tf_op jit(solution)/shard_map/interp/pallas_call | solution.py:440
  21.6 5.8 %collective-permute-start.4 = (bf16[2,512,128]{2,1,0:T(8,128)(2,1)S(1)}, bf16[2,512,128]{2,1,0:T(8,128)(2,1)S(1)}, u32[]{:S(2)}, u32[]{:S(2)}) collective-permute-start(bf16[2,512,128]{2,1,0:T(8,128)(2,1)S(1)} %get-tuple-element.41), channel_id=1, source_target_pairs={{0,63},{1,0},{2,1},{3,2},{4,3},{5,4},{6,5},{7,6},{8,7},{9,8},{10,9... | collective-permute-start | bytes 786440 | tf_op jit(solution)/shard_map/ppermute | solution.py:375
  27.4 0.0 collective-permute-start.5
  27.4 0.1 pad_add_fusion.place_ref
  27.5 1.1 %collective-permute-done.4.after_ref = bf16[2,512,128]{2,1,0:T(8,128)(2,1)S(1)} collective-permute-done((bf16[2,512,128]{2,1,0:T(8,128)(2,1)S(1)}, bf16[2,512,128]{2,1,0:T(8,128)(2,1)S(1)}, u32[]{:S(2)}, u32[]{:S(2)}) %collective-permute-start.4) | collective-permute-done | bytes 262176 | tf_op jit(solution)/shard_map/ppermute | solution.py:375
  28.5 2.2 %collective-permute-done.5.before_ref = bf16[2,512,128]{2,1,0:T(8,128)(2,1)S(1)} collective-permute-done((bf16[2,512,128]{2,1,0:T(8,128)(2,1)S(1)}, bf16[2,512,128]{2,1,0:T(8,128)(2,1)S(1)}, u32[]{:S(2)}, u32[]{:S(2)}) %collective-permute-start.5) | collective-permute-done | bytes 262176 | tf_op jit(solution)/shard_map/ppermute | solution.py:375
  30.7 0.0 copy-done.1
  30.7 0.0 copy-done.2
  30.7 0.0 copy-done.3
  30.7 0.0 copy-done.4
  30.7 6.2 %smooth_mlp.1 = (bf16[4,512,128]{2,1,0:T(8,128)(2,1)}, f32[4,512,128]{2,1,0:T(8,128)S(1)}, bf16[1280,128]{1,0:T(8,128)(2,1)}) custom-call(f32[4,512,128]{2,1,0:T(8,128)S(1)} %get-tuple-element.40.dep_ref, bf16[2,512,128]{2,1,0:T(8,128)(2,1)S(1)} %collective-permute-done.4.after_ref, bf16[2,512,128]{2,1,0:T(8,128)(2,1)S(1)} %collective-permute-done.5.before_ref, ...), custom_call_target="tpu_custom_call" | custom-call | bytes 3801088 | tf_op jit(solution)/shard_map/smooth_mlp/pallas_call | solution.py:452
  36.9 10.7 %all-to-all-start = ((bf16[32,40,128]{2,1,0:T(8,128)(2,1)}), bf16[32,40,128]{2,1,0:T(8,128)(2,1)S(1)}, u32[]{:S(2)}, u32[]{:S(2)}) async-start(bf16[32,40,128]{2,1,0:T(8,128)(2,1)} %bitcast.9), calls=%async_computation | async-start | bytes 655360 | tf_op jit(solution)/shard_map/all_to_all | solution.py:473
  47.6 0.1 edges.1
  47.6 1.7 %collective-permute-start.6 = (bf16[2,512,128]{2,1,0:T(8,128)(2,1)S(1)}, bf16[2,512,128]{2,1,0:T(8,128)(2,1)S(1)}, u32[]{:S(2)}, u32[]{:S(2)}) collective-permute-start(bf16[2,512,128]{2,1,0:T(8,128)(2,1)S(1)} %get-tuple-element.46), channel_id=1, source_target_pairs={{0,1},{1,2},{2,3},{3,4},{4,5},{5,6},{6,7},{7,8},{8,9},{9,10},{10,1... | collective-permute-start | bytes 786440 | tf_op jit(solution)/shard_map/ppermute | solution.py:375
  49.4 0.0 collective-permute-start.7
  49.4 10.6 %all-to-all-done.parts_ref = bf16[32,40,128]{2,1,0:T(8,128)(2,1)S(1)} async-done(((bf16[32,40,128]{2,1,0:T(8,128)(2,1)}), bf16[32,40,128]{2,1,0:T(8,128)(2,1)S(1)}, u32[]{:S(2)}, u32[]{:S(2)}) %all-to-all-start) | async-done | bytes 327712 | tf_op jit(solution)/shard_map/all_to_all | solution.py:473
  59.9 0.7 part_sum.1
  60.6 3.4 %all-to-all-start.1 = ((bf16[8,40,128]{2,1,0:T(8,128)(2,1)}), bf16[8,40,128]{2,1,0:T(8,128)(2,1)S(1)}, u32[]{:S(2)}, u32[]{:S(2)}) async-start(bf16[8,40,128]{2,1,0:T(8,128)(2,1)} %part_sum.1), calls=%async_computation.1 | async-start | bytes 163840 | tf_op jit(solution)/shard_map/all_to_all | solution.py:493
  64.0 0.0 collective-permute-done.6.before_ref
  64.0 0.0 collective-permute-done.7.after_ref
  64.0 3.3 %adjoint.1 = (bf16[128,512]{1,0:T(8,128)(2,1)S(1)}, bf16[128,512]{1,0:T(8,128)(2,1)S(1)}, bf16[128,512]{1,0:T(8,128)(2,1)S(1)}, bf16[128,512]{1,0:T(8,128)(2,1)S(1)}, bf16[128,512]{1,0:T(8,128)(2,1)S(1)}) custom-call(f32[4,512,128]{2,1,0:T(8,128)S(1)} %get-tuple-element.45.scaled_ref, bf16[2,512,128]{2,1,0:T(8,128)(2,1)S(1)} %collective-permute-done.6.before_ref, ...), custom_call_target="tpu_custom_call" | custom-call | flops 99999997952 | bytes 1310720 | tf_op jit(solution)/shard_map/adjoint/pallas_call | solution.py:474
  67.3 0.1 collective-permute-start.8
  67.4 0.1 collective-permute-start.9
  67.5 0.5 collective-permute-start.10
  68.0 4.9 %collective-permute-start.11 = (bf16[128,512]{1,0:T(8,128)(2,1)S(1)}, bf16[128,512]{1,0:T(8,128)(2,1)S(1)}, u32[]{:S(2)}, u32[]{:S(2)}) collective-permute-start(bf16[128,512]{1,0:T(8,128)(2,1)S(1)} %get-tuple-element.52), channel_id=1, source_target_pairs={{0,62},{1,63},{2,0},{3,1},{4,2},{5,3},{6,4},{7,5},{8,6},{9,7},{10,... | collective-permute-start | bytes 393224 | tf_op jit(solution)/shard_map/ppermute | solution.py:375
  72.9 0.0 all-to-all-done.1.parts_ref
  72.9 0.8 whole_sum.1
  73.6 5.5 %all-to-all-start.2 = ((bf16[32,40,128]{2,1,0:T(8,128)(2,1)}), bf16[32,40,128]{2,1,0:T(8,128)(2,1)S(1)}, u32[]{:S(2)}, u32[]{:S(2)}) async-start(bf16[32,40,128]{2,1,0:T(8,128)(2,1)} %whole_sum.1), calls=%async_computation.2 | async-start | bytes 655360 | tf_op jit(solution)/shard_map/all_to_all | solution.py:515
  79.2 0.0 collective-permute-done.8.refs_0_
  79.2 0.0 collective-permute-done.9.refs_1_
  79.2 0.0 collective-permute-done.10.refs_3_
  79.2 0.0 collective-permute-done.11.refs_4_
  79.2 2.5 %scatter.1 = (f32[4,512,128]{2,1,0:T(8,128)}, f32[8,128]{1,0:T(8,128)S(1)}) custom-call(s32[8,128]{1,0:T(8,128)S(1)} %get-tuple-element.44.cells_ref, s32[1,5]{1,0:T(1,128)S(1)} %copy-done.5, bf16[128,512]{1,0:T(8,128)(2,1)S(1)} %collective-permute-done.8.refs_0_, bf16[128,512]{1,0:T(8,128)(2,1)S(1)} %collective-permute-done.9.refs_1_, ...), custom_call_target="tpu_custom_call" | custom-call | flops 99999997952 | bytes 2105344 | tf_op jit(solution)/shard_map/scatter/pallas_call | solution.py:498
  81.7 7.1 %all-to-all-done.2 = bf16[32,40,128]{2,1,0:T(8,128)(2,1)S(1)} async-done(((bf16[32,40,128]{2,1,0:T(8,128)(2,1)}), bf16[32,40,128]{2,1,0:T(8,128)(2,1)S(1)}, u32[]{:S(2)}, u32[]{:S(2)}) %all-to-all-start.2) | async-done | bytes 327712 | tf_op jit(solution)/shard_map/all_to_all | solution.py:515
  88.8 0.8 unpack.1
  (2 shorter events, 0.0 us)
Async XLA Ops:
  0.6 0.7 copy-start.8
  1.3 1.0 %copy-start = (bf16[1,4,512,128]{3,2,1,0:T(8,128)(2,1)S(1)}, bf16[1,4,512,128]{3,2,1,0:T(8,128)(2,1)}, u32[]{:S(2)}) copy-start(bf16[1,4,512,128]{3,2,1,0:T(8,128)(2,1)} %param.12) | copy-start | bytes 1572868
  1.3 1.0 %copy-start.5 = (s32[1,5]{1,0:T(1,128)S(1)}, s32[1,5]{1,0:T(1,128)}, u32[]{:S(2)}) copy-start(s32[1,5]{1,0:T(1,128)} %count_ref.3) | copy-start | bytes 64
  2.0 12.2 %copy-start.6 = (s32[4,4,512]{2,1,0:T(4,128)S(1)}, s32[4,4,512]{2,1,0:T(4,128)}, u32[]{:S(2)}) copy-start(s32[4,4,512]{2,1,0:T(4,128)} %slot_ref.1) | copy-start | bytes 98308
  2.0 12.2 %copy-start.7 = (f32[4,4,512]{2,1,0:T(4,128)S(1)}, f32[4,4,512]{2,1,0:T(4,128)}, u32[]{:S(2)}) copy-start(f32[4,4,512]{2,1,0:T(4,128)} %weight_ref.1) | copy-start | bytes 98308
  2.0 12.1 %copy-start.9 = (f32[256]{0:T(256)S(1)}, f32[256]{0:T(256)}, u32[]{:S(2)}) copy-start(f32[256]{0:T(256)} %param.19) | copy-start | bytes 3076
  2.0 12.1 %copy-start.10 = (f32[256]{0:T(256)S(1)}, f32[256]{0:T(256)}, u32[]{:S(2)}) copy-start(f32[256]{0:T(256)} %param.21) | copy-start | bytes 3076
  2.0 12.1 %copy-start.11 = (f32[128]{0:T(128)S(1)}, f32[128]{0:T(128)}, u32[]{:S(2)}) copy-start(f32[128]{0:T(128)} %param.17) | copy-start | bytes 1540
  3.7 10.8 %collective-permute-start = (bf16[128,512]{1,0:T(8,128)(2,1)S(1)}, bf16[128,512]{1,0:T(8,128)(2,1)S(1)}, u32[]{:S(2)}, u32[]{:S(2)}) collective-permute-start(bf16[128,512]{1,0:T(8,128)(2,1)S(1)} %get-tuple-element.35), channel_id=1, source_target_pairs={{0,62},{1,63},{2,0},{3,1},{4,2},{5,3},{6,4},{7,5},{8,6},{9,7},{10,... | collective-permute-start | bytes 393224 | tf_op jit(solution)/shard_map/ppermute | solution.py:375
  12.4 7.1 %collective-permute-start.1 = (bf16[128,512]{1,0:T(8,128)(2,1)S(1)}, bf16[128,512]{1,0:T(8,128)(2,1)S(1)}, u32[]{:S(2)}, u32[]{:S(2)}) collective-permute-start(bf16[128,512]{1,0:T(8,128)(2,1)S(1)} %get-tuple-element.36), channel_id=1, source_target_pairs={{0,2},{1,3},{2,4},{3,5},{4,6},{5,7},{6,8},{7,9},{8,10},{9,11},{10,... | collective-permute-start | bytes 393224 | tf_op jit(solution)/shard_map/ppermute | solution.py:375
  12.4 7.1 %collective-permute-start.2 = (bf16[128,512]{1,0:T(8,128)(2,1)S(1)}, bf16[128,512]{1,0:T(8,128)(2,1)S(1)}, u32[]{:S(2)}, u32[]{:S(2)}) collective-permute-start(bf16[128,512]{1,0:T(8,128)(2,1)S(1)} %get-tuple-element.37), channel_id=1, source_target_pairs={{0,63},{1,0},{2,1},{3,2},{4,3},{5,4},{6,5},{7,6},{8,7},{9,8},{10,9... | collective-permute-start | bytes 393224 | tf_op jit(solution)/shard_map/ppermute | solution.py:375
  13.4 6.2 %collective-permute-start.3 = (bf16[128,512]{1,0:T(8,128)(2,1)S(1)}, bf16[128,512]{1,0:T(8,128)(2,1)S(1)}, u32[]{:S(2)}, u32[]{:S(2)}) collective-permute-start(bf16[128,512]{1,0:T(8,128)(2,1)S(1)} %get-tuple-element.38), channel_id=1, source_target_pairs={{0,1},{1,2},{2,3},{3,4},{4,5},{5,6},{6,7},{7,8},{8,9},{9,10},{10,1... | collective-permute-start | bytes 393224 | tf_op jit(solution)/shard_map/ppermute | solution.py:375
  14.2 16.5 %copy-start.1 = (bf16[1,4,512,128]{3,2,1,0:T(8,128)(2,1)S(1)}, bf16[1,4,512,128]{3,2,1,0:T(8,128)(2,1)}, u32[]{:S(2)}) copy-start(bf16[1,4,512,128]{3,2,1,0:T(8,128)(2,1)} %param.23) | copy-start | bytes 1572868
  14.2 16.5 %copy-start.2 = (bf16[256,256]{1,0:T(8,128)(2,1)S(1)}, bf16[256,256]{1,0:T(8,128)(2,1)}, u32[]{:S(2)}) copy-start(bf16[256,256]{1,0:T(8,128)(2,1)} %w2_ref.1) | copy-start | bytes 393220
  14.2 16.5 %copy-start.3 = (bf16[128,256]{1,0:T(8,128)(2,1)S(1)}, bf16[128,256]{1,0:T(8,128)(2,1)}, u32[]{:S(2)}) copy-start(bf16[128,256]{1,0:T(8,128)(2,1)} %w1_ref.1) | copy-start | bytes 196612
  14.2 16.5 %copy-start.4 = (bf16[256,128]{1,0:T(8,128)(2,1)S(1)}, bf16[256,128]{1,0:T(8,128)(2,1)}, u32[]{:S(2)}) copy-start(bf16[256,128]{1,0:T(8,128)(2,1)} %w3_ref.1) | copy-start | bytes 196612
  21.6 7.0 %collective-permute-start.4 = (bf16[2,512,128]{2,1,0:T(8,128)(2,1)S(1)}, bf16[2,512,128]{2,1,0:T(8,128)(2,1)S(1)}, u32[]{:S(2)}, u32[]{:S(2)}) collective-permute-start(bf16[2,512,128]{2,1,0:T(8,128)(2,1)S(1)} %get-tuple-element.41), channel_id=1, source_target_pairs={{0,63},{1,0},{2,1},{3,2},{4,3},{5,4},{6,5},{7,6},{8,7},{9,8},{10,9... | collective-permute-start | bytes 786440 | tf_op jit(solution)/shard_map/ppermute | solution.py:375
  27.4 3.3 %collective-permute-start.5 = (bf16[2,512,128]{2,1,0:T(8,128)(2,1)S(1)}, bf16[2,512,128]{2,1,0:T(8,128)(2,1)S(1)}, u32[]{:S(2)}, u32[]{:S(2)}) collective-permute-start(bf16[2,512,128]{2,1,0:T(8,128)(2,1)S(1)} %get-tuple-element.42), channel_id=1, source_target_pairs={{0,1},{1,2},{2,3},{3,4},{4,5},{5,6},{6,7},{7,8},{8,9},{9,10},{10,1... | collective-permute-start | bytes 786440 | tf_op jit(solution)/shard_map/ppermute | solution.py:375
  36.9 23.1 %all-to-all-start = ((bf16[32,40,128]{2,1,0:T(8,128)(2,1)}), bf16[32,40,128]{2,1,0:T(8,128)(2,1)S(1)}, u32[]{:S(2)}, u32[]{:S(2)}) async-start(bf16[32,40,128]{2,1,0:T(8,128)(2,1)} %bitcast.9), calls=%async_computation | async-start | bytes 655360 | tf_op jit(solution)/shard_map/all_to_all | solution.py:473
  47.6 16.3 %collective-permute-start.6 = (bf16[2,512,128]{2,1,0:T(8,128)(2,1)S(1)}, bf16[2,512,128]{2,1,0:T(8,128)(2,1)S(1)}, u32[]{:S(2)}, u32[]{:S(2)}) collective-permute-start(bf16[2,512,128]{2,1,0:T(8,128)(2,1)S(1)} %get-tuple-element.46), channel_id=1, source_target_pairs={{0,1},{1,2},{2,3},{3,4},{4,5},{5,6},{6,7},{7,8},{8,9},{9,10},{10,1... | collective-permute-start | bytes 786440 | tf_op jit(solution)/shard_map/ppermute | solution.py:375
  49.4 14.6 %collective-permute-start.7 = (bf16[2,512,128]{2,1,0:T(8,128)(2,1)S(1)}, bf16[2,512,128]{2,1,0:T(8,128)(2,1)S(1)}, u32[]{:S(2)}, u32[]{:S(2)}) collective-permute-start(bf16[2,512,128]{2,1,0:T(8,128)(2,1)S(1)} %get-tuple-element.47), channel_id=1, source_target_pairs={{0,63},{1,0},{2,1},{3,2},{4,3},{5,4},{6,5},{7,6},{8,7},{9,8},{10,9... | collective-permute-start | bytes 786440 | tf_op jit(solution)/shard_map/ppermute | solution.py:375
  60.6 12.2 %all-to-all-start.1 = ((bf16[8,40,128]{2,1,0:T(8,128)(2,1)}), bf16[8,40,128]{2,1,0:T(8,128)(2,1)S(1)}, u32[]{:S(2)}, u32[]{:S(2)}) async-start(bf16[8,40,128]{2,1,0:T(8,128)(2,1)} %part_sum.1), calls=%async_computation.1 | async-start | bytes 163840 | tf_op jit(solution)/shard_map/all_to_all | solution.py:493
  67.3 11.9 %collective-permute-start.8 = (bf16[128,512]{1,0:T(8,128)(2,1)S(1)}, bf16[128,512]{1,0:T(8,128)(2,1)S(1)}, u32[]{:S(2)}, u32[]{:S(2)}) collective-permute-start(bf16[128,512]{1,0:T(8,128)(2,1)S(1)} %get-tuple-element.48), channel_id=1, source_target_pairs={{0,2},{1,3},{2,4},{3,5},{4,6},{5,7},{6,8},{7,9},{8,10},{9,11},{10,... | collective-permute-start | bytes 393224 | tf_op jit(solution)/shard_map/ppermute | solution.py:375
  67.4 11.8 %collective-permute-start.9 = (bf16[128,512]{1,0:T(8,128)(2,1)S(1)}, bf16[128,512]{1,0:T(8,128)(2,1)S(1)}, u32[]{:S(2)}, u32[]{:S(2)}) collective-permute-start(bf16[128,512]{1,0:T(8,128)(2,1)S(1)} %get-tuple-element.49), channel_id=1, source_target_pairs={{0,1},{1,2},{2,3},{3,4},{4,5},{5,6},{6,7},{7,8},{8,9},{9,10},{10,1... | collective-permute-start | bytes 393224 | tf_op jit(solution)/shard_map/ppermute | solution.py:375
  67.5 11.7 %collective-permute-start.10 = (bf16[128,512]{1,0:T(8,128)(2,1)S(1)}, bf16[128,512]{1,0:T(8,128)(2,1)S(1)}, u32[]{:S(2)}, u32[]{:S(2)}) collective-permute-start(bf16[128,512]{1,0:T(8,128)(2,1)S(1)} %get-tuple-element.51), channel_id=1, source_target_pairs={{0,63},{1,0},{2,1},{3,2},{4,3},{5,4},{6,5},{7,6},{8,7},{9,8},{10,9... | collective-permute-start | bytes 393224 | tf_op jit(solution)/shard_map/ppermute | solution.py:375
  68.0 11.2 %collective-permute-start.11 = (bf16[128,512]{1,0:T(8,128)(2,1)S(1)}, bf16[128,512]{1,0:T(8,128)(2,1)S(1)}, u32[]{:S(2)}, u32[]{:S(2)}) collective-permute-start(bf16[128,512]{1,0:T(8,128)(2,1)S(1)} %get-tuple-element.52), channel_id=1, source_target_pairs={{0,62},{1,63},{2,0},{3,1},{4,2},{5,3},{6,4},{7,5},{8,6},{9,7},{10,... | collective-permute-start | bytes 393224 | tf_op jit(solution)/shard_map/ppermute | solution.py:375
  73.6 15.2 %all-to-all-start.2 = ((bf16[32,40,128]{2,1,0:T(8,128)(2,1)}), bf16[32,40,128]{2,1,0:T(8,128)(2,1)S(1)}, u32[]{:S(2)}, u32[]{:S(2)}) async-start(bf16[32,40,128]{2,1,0:T(8,128)(2,1)} %whole_sum.1), calls=%async_computation.2 | async-start | bytes 655360 | tf_op jit(solution)/shard_map/all_to_all | solution.py:515

commit v7 on v6

--- a/solution.py
+++ b/solution.py
@@ -19,7 +19,7 @@
 PREPARE_COST = 10**9
 PART_COST = 0
 ADJOINT_COST = 10**11
-SCATTER_COST = 10**11
+SCATTER_COST = 0
 CHOOSE_COST = 2 * 10**9
 
 VMEM = pl.BlockSpec(memory_space=pltpu.VMEM)

time: 90.1 us -> 92.4 us (1.026)
  waiting for transfers between devices: 26.2 us -> 27.6 us
  starting transfers between devices: 43.1 us -> 44.1 us
    all_to_all x1, waiting for transfers between devices: 7.13 us -> 1.73 us  [body(): lax.all_to_all(whole_sum, groups, 0, 0).reshape(group * PART_ROWS, ch)]
    all_to_all x1, waiting for transfers between devices: 0.01 us -> 3.89 us  [body(): parts = lax.all_to_all(part_sum, 'z', 0, 0)]
    ppermute x12, waiting for transfers between devices: 8.56 us -> 11.4 us  [shifted(): lax.ppermute(block, SPACE, [(i, (i + by) % count) for i in range(count)])]
    ppermute x12, starting transfers between devices: 23.5 us -> 24.8 us  [shifted(): lax.ppermute(block, SPACE, [(i, (i + by) % count) for i in range(count)])]
  transfers between devices with their start and end apart: 15 -> 15, of which waited for: 6 -> 10; matrix products, arithmetic and copies ran while one was open for 0% -> 0% of each run, Pallas kernels for 8% -> 7%
where the time goes in v7:
time: 92.4 us; the launch traced here: 91.9 us
  starting transfers between devices  44.1 us (48%)
  waiting for transfers between devices  27.6 us (30%)
  Pallas kernels  18.2 us (20%)
  local copies, waits for them, and re-layouts  1.1 us (1%)
    ppermute x12, starting transfers between devices, shifted(): lax.ppermute(block, SPACE, [(i, (i + by) % count) for i in range(count)])  24.8 us
    ppermute x12, waiting for transfers between devices, shifted(): lax.ppermute(block, SPACE, [(i, (i + by) % count) for i in range(count)])  11.4 us
    all_to_all x1, starting transfers between devices, body(): parts = lax.all_to_all(grads.reshape(group, PART_ROWS, ch), groups, 0, 0)  10.7 us
    all_to_all x1, waiting for transfers between devices, body(): parts = lax.all_to_all(grads.reshape(group, PART_ROWS, ch), groups, 0, 0)  10.6 us
    pallas_call x1, Pallas kernels, body(): call(mlp_kernel, [shape((band_rows, lon, ch), BF16), shape((band_rows, lo...  6.16 us
    all_to_all x1, starting transfers between devices, body(): lax.all_to_all(whole_sum, groups, 0, 0).reshape(group * PART_ROWS, ch)  5.29 us
    all_to_all x1, waiting for transfers between devices, body(): parts = lax.all_to_all(part_sum, 'z', 0, 0)  3.89 us
    all_to_all x1, starting transfers between devices, body(): parts = lax.all_to_all(part_sum, 'z', 0, 0)  3.36 us
  transfers between devices with their start and end apart: 15, of which 10 were waited for; matrix products, arithmetic and copies ran while one was open for 0% of the time, Pallas kernels for 7%

profile of v7, /device:TPU:1, one launch (start us, length us, event | category | flops | bytes accessed | tf_op | source)
XLA Modules:
  0.0 91.9 jit_solution(5526840731301753034)
XLA Ops:
  0.6 0.0 copy-start.8
  0.6 0.7 copy-done.8
  1.3 0.0 copy-start
  1.3 0.6 choose.1
  2.0 0.0 copy-start.6
  2.0 0.0 copy-start.7
  2.0 0.0 copy-start.9
  2.0 0.0 copy-start.10
  2.0 0.0 copy-start.11
  2.0 0.3 copy-done
  2.4 0.0 copy-done.5
  2.4 1.3 %pack.1 = (bf16[128,512]{1,0:T(8,128)(2,1)S(1)}, bf16[128,512]{1,0:T(8,128)(2,1)S(1)}, bf16[128,512]{1,0:T(8,128)(2,1)S(1)}, bf16[128,512]{1,0:T(8,128)(2,1)S(1)}, bf16[128,512]{1,0:T(8,128)(2,1)S(1)}) custom-call(bf16[4,512,128]{2,1,0:T(8,128)(2,1)S(1)} %bitcast.14, bf16[640,1536]{1,0:T(8,128)(2,1)S(1)} %get-tuple-element.34.select_ref, s32[1,5]{1,0:T(1,128)S(1)} %copy-done.5), custom_call_target="tpu_custom_call" | custom-call | bytes 1310720 | tf_op jit(solution)/shard_map/pack/pallas_call | solution.py:415
  3.7 8.7 %collective-permute-start = (bf16[128,512]{1,0:T(8,128)(2,1)S(1)}, bf16[128,512]{1,0:T(8,128)(2,1)S(1)}, u32[]{:S(2)}, u32[]{:S(2)}) collective-permute-start(bf16[128,512]{1,0:T(8,128)(2,1)S(1)} %get-tuple-element.35), channel_id=1, source_target_pairs={{0,62},{1,63},{2,0},{3,1},{4,2},{5,3},{6,4},{7,5},{8,6},{9,7},{10,... | collective-permute-start | bytes 393224 | tf_op jit(solution)/shard_map/ppermute | solution.py:375
  12.4 0.0 collective-permute-start.1
  12.4 1.0 %collective-permute-start.2 = (bf16[128,512]{1,0:T(8,128)(2,1)S(1)}, bf16[128,512]{1,0:T(8,128)(2,1)S(1)}, u32[]{:S(2)}, u32[]{:S(2)}) collective-permute-start(bf16[128,512]{1,0:T(8,128)(2,1)S(1)} %get-tuple-element.37), channel_id=1, source_target_pairs={{0,63},{1,0},{2,1},{3,2},{4,3},{5,4},{6,5},{7,6},{8,7},{9,8},{10,9... | collective-permute-start | bytes 393224 | tf_op jit(solution)/shard_map/ppermute | solution.py:375
  13.4 0.8 collective-permute-start.3
  14.1 0.0 copy-done.6
  14.1 0.0 copy-done.7
  14.1 0.0 copy-done.9
  14.2 0.0 copy-done.10
  14.2 0.0 copy-done.11
  14.2 0.0 copy-start.1
  14.2 0.0 copy-start.2
  14.2 0.0 copy-start.3
  14.2 0.0 copy-start.4
  14.2 0.3 collective-permute-done.refs_0_
  14.6 5.0 %collective-permute-done.1.refs_1_ = bf16[128,512]{1,0:T(8,128)(2,1)S(1)} collective-permute-done((bf16[128,512]{1,0:T(8,128)(2,1)S(1)}, bf16[128,512]{1,0:T(8,128)(2,1)S(1)}, u32[]{:S(2)}, u32[]{:S(2)}) %collective-permute-start.1) | collective-permute-done | bytes 131104 | tf_op jit(solution)/shard_map/ppermute | solution.py:375
  19.5 0.0 collective-permute-done.2.refs_2_
  19.5 0.0 collective-permute-done.3.refs_3_
  19.5 2.0 %interp.1 = (f32[4,512,128]{2,1,0:T(8,128)S(1)}, bf16[2,512,128]{2,1,0:T(8,128)(2,1)S(1)}, bf16[2,512,128]{2,1,0:T(8,128)(2,1)S(1)}) custom-call(bf16[128,512]{1,0:T(8,128)(2,1)S(1)} %collective-permute-done.refs_0_, bf16[128,512]{1,0:T(8,128)(2,1)S(1)} %collective-permute-done.1.refs_1_, bf16[128,512]{1,0:T(8,128)(2,1)S(1)} %collective-permute-done.2.refs_2_, ...), custom_call_target="tpu_custom_call" | custom-call | bytes 3145728 | tf_op jit(solution)/shard_map/interp/pallas_call | solution.py:440
  21.6 5.8 %collective-permute-start.4 = (bf16[2,512,128]{2,1,0:T(8,128)(2,1)S(1)}, bf16[2,512,128]{2,1,0:T(8,128)(2,1)S(1)}, u32[]{:S(2)}, u32[]{:S(2)}) collective-permute-start(bf16[2,512,128]{2,1,0:T(8,128)(2,1)S(1)} %get-tuple-element.41), channel_id=1, source_target_pairs={{0,63},{1,0},{2,1},{3,2},{4,3},{5,4},{6,5},{7,6},{8,7},{9,8},{10,9... | collective-permute-start | bytes 786440 | tf_op jit(solution)/shard_map/ppermute | solution.py:375
  27.4 0.0 collective-permute-start.5
  27.4 0.1 pad_add_fusion.place_ref
  27.5 1.1 %collective-permute-done.4.after_ref = bf16[2,512,128]{2,1,0:T(8,128)(2,1)S(1)} collective-permute-done((bf16[2,512,128]{2,1,0:T(8,128)(2,1)S(1)}, bf16[2,512,128]{2,1,0:T(8,128)(2,1)S(1)}, u32[]{:S(2)}, u32[]{:S(2)}) %collective-permute-start.4) | collective-permute-done | bytes 262176 | tf_op jit(solution)/shard_map/ppermute | solution.py:375
  28.5 2.2 %collective-permute-done.5.before_ref = bf16[2,512,128]{2,1,0:T(8,128)(2,1)S(1)} collective-permute-done((bf16[2,512,128]{2,1,0:T(8,128)(2,1)S(1)}, bf16[2,512,128]{2,1,0:T(8,128)(2,1)S(1)}, u32[]{:S(2)}, u32[]{:S(2)}) %collective-permute-start.5) | collective-permute-done | bytes 262176 | tf_op jit(solution)/shard_map/ppermute | solution.py:375
  30.7 0.0 copy-done.1
  30.7 0.0 copy-done.2
  30.7 0.0 copy-done.3
  30.7 0.0 copy-done.4
  30.7 6.2 %smooth_mlp.1 = (bf16[4,512,128]{2,1,0:T(8,128)(2,1)}, f32[4,512,128]{2,1,0:T(8,128)S(1)}, bf16[1280,128]{1,0:T(8,128)(2,1)}) custom-call(f32[4,512,128]{2,1,0:T(8,128)S(1)} %get-tuple-element.40.dep_ref, bf16[2,512,128]{2,1,0:T(8,128)(2,1)S(1)} %collective-permute-done.4.after_ref, bf16[2,512,128]{2,1,0:T(8,128)(2,1)S(1)} %collective-permute-done.5.before_ref, ...), custom_call_target="tpu_custom_call" | custom-call | bytes 3801088 | tf_op jit(solution)/shard_map/smooth_mlp/pallas_call | solution.py:452
  36.9 10.7 %all-to-all-start = ((bf16[32,40,128]{2,1,0:T(8,128)(2,1)}), bf16[32,40,128]{2,1,0:T(8,128)(2,1)S(1)}, u32[]{:S(2)}, u32[]{:S(2)}) async-start(bf16[32,40,128]{2,1,0:T(8,128)(2,1)} %bitcast.9), calls=%async_computation | async-start | bytes 655360 | tf_op jit(solution)/shard_map/all_to_all | solution.py:473
  47.6 0.1 edges.1
  47.6 1.7 %collective-permute-start.6 = (bf16[2,512,128]{2,1,0:T(8,128)(2,1)S(1)}, bf16[2,512,128]{2,1,0:T(8,128)(2,1)S(1)}, u32[]{:S(2)}, u32[]{:S(2)}) collective-permute-start(bf16[2,512,128]{2,1,0:T(8,128)(2,1)S(1)} %get-tuple-element.46), channel_id=1, source_target_pairs={{0,1},{1,2},{2,3},{3,4},{4,5},{5,6},{6,7},{7,8},{8,9},{9,10},{10,1... | collective-permute-start | bytes 786440 | tf_op jit(solution)/shard_map/ppermute | solution.py:375
  49.4 0.0 collective-permute-start.7
  49.4 10.6 %all-to-all-done.parts_ref = bf16[32,40,128]{2,1,0:T(8,128)(2,1)S(1)} async-done(((bf16[32,40,128]{2,1,0:T(8,128)(2,1)}), bf16[32,40,128]{2,1,0:T(8,128)(2,1)S(1)}, u32[]{:S(2)}, u32[]{:S(2)}) %all-to-all-start) | async-done | bytes 327712 | tf_op jit(solution)/shard_map/all_to_all | solution.py:473
  59.9 0.7 part_sum.1
  60.6 3.4 %all-to-all-start.1 = ((bf16[8,40,128]{2,1,0:T(8,128)(2,1)}), bf16[8,40,128]{2,1,0:T(8,128)(2,1)S(1)}, u32[]{:S(2)}, u32[]{:S(2)}) async-start(bf16[8,40,128]{2,1,0:T(8,128)(2,1)} %part_sum.1), calls=%async_computation.1 | async-start | bytes 163840 | tf_op jit(solution)/shard_map/all_to_all | solution.py:493
  64.0 0.0 collective-permute-done.6.before_ref
  64.0 0.0 collective-permute-done.7.after_ref
  64.0 3.3 %adjoint.1 = (bf16[128,512]{1,0:T(8,128)(2,1)S(1)}, bf16[128,512]{1,0:T(8,128)(2,1)S(1)}, bf16[128,512]{1,0:T(8,128)(2,1)S(1)}, bf16[128,512]{1,0:T(8,128)(2,1)S(1)}, bf16[128,512]{1,0:T(8,128)(2,1)S(1)}) custom-call(f32[4,512,128]{2,1,0:T(8,128)S(1)} %get-tuple-element.45.scaled_ref, bf16[2,512,128]{2,1,0:T(8,128)(2,1)S(1)} %collective-permute-done.6.before_ref, ...), custom_call_target="tpu_custom_call" | custom-call | flops 99999997952 | bytes 1310720 | tf_op jit(solution)/shard_map/adjoint/pallas_call | solution.py:474
  67.3 3.9 %all-to-all-done.1.parts_ref = bf16[8,40,128]{2,1,0:T(8,128)(2,1)S(1)} async-done(((bf16[8,40,128]{2,1,0:T(8,128)(2,1)}), bf16[8,40,128]{2,1,0:T(8,128)(2,1)S(1)}, u32[]{:S(2)}, u32[]{:S(2)}) %all-to-all-start.1) | async-done | bytes 81952 | tf_op jit(solution)/shard_map/all_to_all | solution.py:493
  71.2 0.8 whole_sum.1
  72.0 5.3 %all-to-all-start.2 = ((bf16[32,40,128]{2,1,0:T(8,128)(2,1)}), bf16[32,40,128]{2,1,0:T(8,128)(2,1)S(1)}, u32[]{:S(2)}, u32[]{:S(2)}) async-start(bf16[32,40,128]{2,1,0:T(8,128)(2,1)} %whole_sum.1), calls=%async_computation.2 | async-start | bytes 655360 | tf_op jit(solution)/shard_map/all_to_all | solution.py:515
  77.3 1.5 %collective-permute-start.8 = (bf16[128,512]{1,0:T(8,128)(2,1)S(1)}, bf16[128,512]{1,0:T(8,128)(2,1)S(1)}, u32[]{:S(2)}, u32[]{:S(2)}) collective-permute-start(bf16[128,512]{1,0:T(8,128)(2,1)S(1)} %get-tuple-element.48), channel_id=1, source_target_pairs={{0,2},{1,3},{2,4},{3,5},{4,6},{5,7},{6,8},{7,9},{8,10},{9,11},{10,... | collective-permute-start | bytes 393224 | tf_op jit(solution)/shard_map/ppermute | solution.py:375
  78.7 1.7 %collective-permute-start.9 = (bf16[128,512]{1,0:T(8,128)(2,1)S(1)}, bf16[128,512]{1,0:T(8,128)(2,1)S(1)}, u32[]{:S(2)}, u32[]{:S(2)}) collective-permute-start(bf16[128,512]{1,0:T(8,128)(2,1)S(1)} %get-tuple-element.49), channel_id=1, source_target_pairs={{0,1},{1,2},{2,3},{3,4},{4,5},{5,6},{6,7},{7,8},{8,9},{9,10},{10,1... | collective-permute-start | bytes 393224 | tf_op jit(solution)/shard_map/ppermute | solution.py:375
  80.4 0.0 collective-permute-start.10
  80.4 3.6 %collective-permute-start.11 = (bf16[128,512]{1,0:T(8,128)(2,1)S(1)}, bf16[128,512]{1,0:T(8,128)(2,1)S(1)}, u32[]{:S(2)}, u32[]{:S(2)}) collective-permute-start(bf16[128,512]{1,0:T(8,128)(2,1)S(1)} %get-tuple-element.52), channel_id=1, source_target_pairs={{0,62},{1,63},{2,0},{3,1},{4,2},{5,3},{6,4},{7,5},{8,6},{9,7},{10,... | collective-permute-start | bytes 393224 | tf_op jit(solution)/shard_map/ppermute | solution.py:375
  84.1 1.8 %collective-permute-done.8.refs_0_ = bf16[128,512]{1,0:T(8,128)(2,1)S(1)} collective-permute-done((bf16[128,512]{1,0:T(8,128)(2,1)S(1)}, bf16[128,512]{1,0:T(8,128)(2,1)S(1)}, u32[]{:S(2)}, u32[]{:S(2)}) %collective-permute-start.8) | collective-permute-done | bytes 131104 | tf_op jit(solution)/shard_map/ppermute | solution.py:375
  85.8 0.0 collective-permute-done.9.refs_1_
  85.8 0.5 collective-permute-done.10.refs_3_
  86.3 0.6 collective-permute-done.11.refs_4_
  86.9 2.5 %scatter.1 = (f32[4,512,128]{2,1,0:T(8,128)}, f32[8,128]{1,0:T(8,128)S(1)}) custom-call(s32[8,128]{1,0:T(8,128)S(1)} %get-tuple-element.44.cells_ref, s32[1,5]{1,0:T(1,128)S(1)} %copy-done.5, bf16[128,512]{1,0:T(8,128)(2,1)S(1)} %collective-permute-done.8.refs_0_, bf16[128,512]{1,0:T(8,128)(2,1)S(1)} %collective-permute-done.9.refs_1_, ...), custom_call_target="tpu_custom_call" | custom-call | bytes 2105344 | tf_op jit(solution)/shard_map/scatter/pallas_call | solution.py:498
  89.4 1.7 %all-to-all-done.2 = bf16[32,40,128]{2,1,0:T(8,128)(2,1)S(1)} async-done(((bf16[32,40,128]{2,1,0:T(8,128)(2,1)}), bf16[32,40,128]{2,1,0:T(8,128)(2,1)S(1)}, u32[]{:S(2)}, u32[]{:S(2)}) %all-to-all-start.2) | async-done | bytes 327712 | tf_op jit(solution)/shard_map/all_to_all | solution.py:515
  91.1 0.8 unpack.1
  (2 shorter events, 0.0 us)
Async XLA Ops:
  0.6 0.7 copy-start.8
  1.3 1.0 %copy-start = (bf16[1,4,512,128]{3,2,1,0:T(8,128)(2,1)S(1)}, bf16[1,4,512,128]{3,2,1,0:T(8,128)(2,1)}, u32[]{:S(2)}) copy-start(bf16[1,4,512,128]{3,2,1,0:T(8,128)(2,1)} %param.12) | copy-start | bytes 1572868
  1.3 1.0 %copy-start.5 = (s32[1,5]{1,0:T(1,128)S(1)}, s32[1,5]{1,0:T(1,128)}, u32[]{:S(2)}) copy-start(s32[1,5]{1,0:T(1,128)} %count_ref.3) | copy-start | bytes 64
  2.0 12.2 %copy-start.6 = (s32[4,4,512]{2,1,0:T(4,128)S(1)}, s32[4,4,512]{2,1,0:T(4,128)}, u32[]{:S(2)}) copy-start(s32[4,4,512]{2,1,0:T(4,128)} %slot_ref.1) | copy-start | bytes 98308
  2.0 12.2 %copy-start.7 = (f32[4,4,512]{2,1,0:T(4,128)S(1)}, f32[4,4,512]{2,1,0:T(4,128)}, u32[]{:S(2)}) copy-start(f32[4,4,512]{2,1,0:T(4,128)} %weight_ref.1) | copy-start | bytes 98308
  2.0 12.1 %copy-start.9 = (f32[256]{0:T(256)S(1)}, f32[256]{0:T(256)}, u32[]{:S(2)}) copy-start(f32[256]{0:T(256)} %param.19) | copy-start | bytes 3076
  2.0 12.1 %copy-start.10 = (f32[256]{0:T(256)S(1)}, f32[256]{0:T(256)}, u32[]{:S(2)}) copy-start(f32[256]{0:T(256)} %param.21) | copy-start | bytes 3076
  2.0 12.1 %copy-start.11 = (f32[128]{0:T(128)S(1)}, f32[128]{0:T(128)}, u32[]{:S(2)}) copy-start(f32[128]{0:T(128)} %param.17) | copy-start | bytes 1540
  3.7 10.8 %collective-permute-start = (bf16[128,512]{1,0:T(8,128)(2,1)S(1)}, bf16[128,512]{1,0:T(8,128)(2,1)S(1)}, u32[]{:S(2)}, u32[]{:S(2)}) collective-permute-start(bf16[128,512]{1,0:T(8,128)(2,1)S(1)} %get-tuple-element.35), channel_id=1, source_target_pairs={{0,62},{1,63},{2,0},{3,1},{4,2},{5,3},{6,4},{7,5},{8,6},{9,7},{10,... | collective-permute-start | bytes 393224 | tf_op jit(solution)/shard_map/ppermute | solution.py:375
  12.4 7.1 %collective-permute-start.1 = (bf16[128,512]{1,0:T(8,128)(2,1)S(1)}, bf16[128,512]{1,0:T(8,128)(2,1)S(1)}, u32[]{:S(2)}, u32[]{:S(2)}) collective-permute-start(bf16[128,512]{1,0:T(8,128)(2,1)S(1)} %get-tuple-element.36), channel_id=1, source_target_pairs={{0,2},{1,3},{2,4},{3,5},{4,6},{5,7},{6,8},{7,9},{8,10},{9,11},{10,... | collective-permute-start | bytes 393224 | tf_op jit(solution)/shard_map/ppermute | solution.py:375
  12.4 7.1 %collective-permute-start.2 = (bf16[128,512]{1,0:T(8,128)(2,1)S(1)}, bf16[128,512]{1,0:T(8,128)(2,1)S(1)}, u32[]{:S(2)}, u32[]{:S(2)}) collective-permute-start(bf16[128,512]{1,0:T(8,128)(2,1)S(1)} %get-tuple-element.37), channel_id=1, source_target_pairs={{0,63},{1,0},{2,1},{3,2},{4,3},{5,4},{6,5},{7,6},{8,7},{9,8},{10,9... | collective-permute-start | bytes 393224 | tf_op jit(solution)/shard_map/ppermute | solution.py:375
  13.4 6.2 %collective-permute-start.3 = (bf16[128,512]{1,0:T(8,128)(2,1)S(1)}, bf16[128,512]{1,0:T(8,128)(2,1)S(1)}, u32[]{:S(2)}, u32[]{:S(2)}) collective-permute-start(bf16[128,512]{1,0:T(8,128)(2,1)S(1)} %get-tuple-element.38), channel_id=1, source_target_pairs={{0,1},{1,2},{2,3},{3,4},{4,5},{5,6},{6,7},{7,8},{8,9},{9,10},{10,1... | collective-permute-start | bytes 393224 | tf_op jit(solution)/shard_map/ppermute | solution.py:375
  14.2 16.5 %copy-start.1 = (bf16[1,4,512,128]{3,2,1,0:T(8,128)(2,1)S(1)}, bf16[1,4,512,128]{3,2,1,0:T(8,128)(2,1)}, u32[]{:S(2)}) copy-start(bf16[1,4,512,128]{3,2,1,0:T(8,128)(2,1)} %param.23) | copy-start | bytes 1572868
  14.2 16.5 %copy-start.2 = (bf16[256,256]{1,0:T(8,128)(2,1)S(1)}, bf16[256,256]{1,0:T(8,128)(2,1)}, u32[]{:S(2)}) copy-start(bf16[256,256]{1,0:T(8,128)(2,1)} %w2_ref.1) | copy-start | bytes 393220
  14.2 16.5 %copy-start.3 = (bf16[128,256]{1,0:T(8,128)(2,1)S(1)}, bf16[128,256]{1,0:T(8,128)(2,1)}, u32[]{:S(2)}) copy-start(bf16[128,256]{1,0:T(8,128)(2,1)} %w1_ref.1) | copy-start | bytes 196612
  14.2 16.5 %copy-start.4 = (bf16[256,128]{1,0:T(8,128)(2,1)S(1)}, bf16[256,128]{1,0:T(8,128)(2,1)}, u32[]{:S(2)}) copy-start(bf16[256,128]{1,0:T(8,128)(2,1)} %w3_ref.1) | copy-start | bytes 196612
  21.6 7.0 %collective-permute-start.4 = (bf16[2,512,128]{2,1,0:T(8,128)(2,1)S(1)}, bf16[2,512,128]{2,1,0:T(8,128)(2,1)S(1)}, u32[]{:S(2)}, u32[]{:S(2)}) collective-permute-start(bf16[2,512,128]{2,1,0:T(8,128)(2,1)S(1)} %get-tuple-element.41), channel_id=1, source_target_pairs={{0,63},{1,0},{2,1},{3,2},{4,3},{5,4},{6,5},{7,6},{8,7},{9,8},{10,9... | collective-permute-start | bytes 786440 | tf_op jit(solution)/shard_map/ppermute | solution.py:375
  27.4 3.3 %collective-permute-start.5 = (bf16[2,512,128]{2,1,0:T(8,128)(2,1)S(1)}, bf16[2,512,128]{2,1,0:T(8,128)(2,1)S(1)}, u32[]{:S(2)}, u32[]{:S(2)}) collective-permute-start(bf16[2,512,128]{2,1,0:T(8,128)(2,1)S(1)} %get-tuple-element.42), channel_id=1, source_target_pairs={{0,1},{1,2},{2,3},{3,4},{4,5},{5,6},{6,7},{7,8},{8,9},{9,10},{10,1... | collective-permute-start | bytes 786440 | tf_op jit(solution)/shard_map/ppermute | solution.py:375
  36.9 23.1 %all-to-all-start = ((bf16[32,40,128]{2,1,0:T(8,128)(2,1)}), bf16[32,40,128]{2,1,0:T(8,128)(2,1)S(1)}, u32[]{:S(2)}, u32[]{:S(2)}) async-start(bf16[32,40,128]{2,1,0:T(8,128)(2,1)} %bitcast.9), calls=%async_computation | async-start | bytes 655360 | tf_op jit(solution)/shard_map/all_to_all | solution.py:473
  47.6 16.3 %collective-permute-start.6 = (bf16[2,512,128]{2,1,0:T(8,128)(2,1)S(1)}, bf16[2,512,128]{2,1,0:T(8,128)(2,1)S(1)}, u32[]{:S(2)}, u32[]{:S(2)}) collective-permute-start(bf16[2,512,128]{2,1,0:T(8,128)(2,1)S(1)} %get-tuple-element.46), channel_id=1, source_target_pairs={{0,1},{1,2},{2,3},{3,4},{4,5},{5,6},{6,7},{7,8},{8,9},{9,10},{10,1... | collective-permute-start | bytes 786440 | tf_op jit(solution)/shard_map/ppermute | solution.py:375
  49.4 14.6 %collective-permute-start.7 = (bf16[2,512,128]{2,1,0:T(8,128)(2,1)S(1)}, bf16[2,512,128]{2,1,0:T(8,128)(2,1)S(1)}, u32[]{:S(2)}, u32[]{:S(2)}) collective-permute-start(bf16[2,512,128]{2,1,0:T(8,128)(2,1)S(1)} %get-tuple-element.47), channel_id=1, source_target_pairs={{0,63},{1,0},{2,1},{3,2},{4,3},{5,4},{6,5},{7,6},{8,7},{9,8},{10,9... | collective-permute-start | bytes 786440 | tf_op jit(solution)/shard_map/ppermute | solution.py:375
  60.6 10.6 %all-to-all-start.1 = ((bf16[8,40,128]{2,1,0:T(8,128)(2,1)}), bf16[8,40,128]{2,1,0:T(8,128)(2,1)S(1)}, u32[]{:S(2)}, u32[]{:S(2)}) async-start(bf16[8,40,128]{2,1,0:T(8,128)(2,1)} %part_sum.1), calls=%async_computation.1 | async-start | bytes 163840 | tf_op jit(solution)/shard_map/all_to_all | solution.py:493
  72.0 19.2 %all-to-all-start.2 = ((bf16[32,40,128]{2,1,0:T(8,128)(2,1)}), bf16[32,40,128]{2,1,0:T(8,128)(2,1)S(1)}, u32[]{:S(2)}, u32[]{:S(2)}) async-start(bf16[32,40,128]{2,1,0:T(8,128)(2,1)} %whole_sum.1), calls=%async_computation.2 | async-start | bytes 655360 | tf_op jit(solution)/shard_map/all_to_all | solution.py:515
  77.3 8.6 %collective-permute-start.8 = (bf16[128,512]{1,0:T(8,128)(2,1)S(1)}, bf16[128,512]{1,0:T(8,128)(2,1)S(1)}, u32[]{:S(2)}, u32[]{:S(2)}) collective-permute-start(bf16[128,512]{1,0:T(8,128)(2,1)S(1)} %get-tuple-element.48), channel_id=1, source_target_pairs={{0,2},{1,3},{2,4},{3,5},{4,6},{5,7},{6,8},{7,9},{8,10},{9,11},{10,... | collective-permute-start | bytes 393224 | tf_op jit(solution)/shard_map/ppermute | solution.py:375
  78.7 7.1 %collective-permute-start.9 = (bf16[128,512]{1,0:T(8,128)(2,1)S(1)}, bf16[128,512]{1,0:T(8,128)(2,1)S(1)}, u32[]{:S(2)}, u32[]{:S(2)}) collective-permute-start(bf16[128,512]{1,0:T(8,128)(2,1)S(1)} %get-tuple-element.49), channel_id=1, source_target_pairs={{0,1},{1,2},{2,3},{3,4},{4,5},{5,6},{6,7},{7,8},{8,9},{9,10},{10,1... | collective-permute-start | bytes 393224 | tf_op jit(solution)/shard_map/ppermute | solution.py:375
  80.4 5.9 %collective-permute-start.10 = (bf16[128,512]{1,0:T(8,128)(2,1)S(1)}, bf16[128,512]{1,0:T(8,128)(2,1)S(1)}, u32[]{:S(2)}, u32[]{:S(2)}) collective-permute-start(bf16[128,512]{1,0:T(8,128)(2,1)S(1)} %get-tuple-element.51), channel_id=1, source_target_pairs={{0,63},{1,0},{2,1},{3,2},{4,3},{5,4},{6,5},{7,6},{8,7},{9,8},{10,9... | collective-permute-start | bytes 393224 | tf_op jit(solution)/shard_map/ppermute | solution.py:375
  80.4 6.5 %collective-permute-start.11 = (bf16[128,512]{1,0:T(8,128)(2,1)S(1)}, bf16[128,512]{1,0:T(8,128)(2,1)S(1)}, u32[]{:S(2)}, u32[]{:S(2)}) collective-permute-start(bf16[128,512]{1,0:T(8,128)(2,1)S(1)} %get-tuple-element.52), channel_id=1, source_target_pairs={{0,62},{1,63},{2,0},{3,1},{4,2},{5,3},{6,4},{7,5},{8,6},{9,7},{10,... | collective-permute-start | bytes 393224 | tf_op jit(solution)/shard_map/ppermute | solution.py:375

commit v8 on v5

--- a/solution.py
+++ b/solution.py
@@ -272,8 +272,8 @@
 def adjoint_kernel(
     offsets,
     scaled_ref,
+    after_ref,
     before_ref,
-    after_ref,
     place_ref,
     table_ref,
     *refs,
@@ -321,12 +321,12 @@
         outs[offset][...] = slot_grads[offset * quads : (offset + 1) * quads]
 
 
-def scatter_kernel(offsets, cells_ref, count_ref, *refs):
-    blocks = refs[:offsets]
+def scatter_kernel(offsets, order, cells_ref, count_ref, *refs):
+    blocks = dict(zip(order, refs[:offsets]))
     out_ref, done_ref, table, hit = refs[offsets:]
     done_ref[...] = jnp.zeros_like(done_ref)
     band_rows, lon, ch = out_ref.shape
-    quads = blocks[0].shape[0]
+    quads = refs[0].shape[0]
     box_at = lax.broadcasted_iota(jnp.int32, ((band_rows - 1) * lon, quads), 0)
     for offset in range(offsets):
         table[offset * quads : (offset + 1) * quads] = jnp.where(
@@ -482,7 +482,7 @@
         ],
         flops=ADJOINT_COST,
         name="adjoint",
-    )(scaled, before, after, place, table)
+    )(scaled, after, before, place, table)
     (part_sum,) = call(
         functools.partial(sum_kernel, depth),
         [shape((depth, PART_ROWS, ch), BF16)],
@@ -496,7 +496,7 @@
         for e in range(offsets)
     ]
     field_grad, done = call(
-        functools.partial(scatter_kernel, offsets),
+        functools.partial(scatter_kernel, offsets, order),
         [shape((band_rows, lon, ch), F32), shape((8, ch), F32)],
         [VMEM] * (offsets + 2),
         [
@@ -505,7 +505,7 @@
         ],
         flops=SCATTER_COST,
         name="scatter",
-    )(cells, send_count, *back)
+    )(cells, send_count, *(back[e] for e in order))
     (whole_sum,) = call(
         functools.partial(sum_kernel, group),
         [shape((group, PART_ROWS, ch), BF16)],

time: 90.4 us -> 90.1 us (level)
    all_to_all x1, starting transfers between devices: 9.69 us -> 5.13 us  [body(): parts = lax.all_to_all(grads.reshape(group, PART_ROWS, ch), groups, 0, 0)]
    all_to_all x1, starting transfers between devices: 3.36 us -> 5.55 us  [body(): parts = lax.all_to_all(part_sum, 'z', 0, 0)]
    all_to_all x1, starting transfers between devices: 5.29 us -> 7.23 us  [body(): lax.all_to_all(whole_sum, groups, 0, 0).reshape(group * PART_ROWS, ch)]
where the time goes in v8:
time: 90.1 us; the launch traced here: 89.7 us
  starting transfers between devices  46.2 us (51%)
  waiting for transfers between devices  23.2 us (26%)
  Pallas kernels  18.3 us (20%)
  local copies, waits for them, and re-layouts  1.1 us (1%)
    ppermute x12, starting transfers between devices, shifted(): lax.ppermute(block, SPACE, [(i, (i + by) % count) for i in range(count)])  28.3 us
    ppermute x12, waiting for transfers between devices, shifted(): lax.ppermute(block, SPACE, [(i, (i + by) % count) for i in range(count)])  8.56 us
    all_to_all x1, starting transfers between devices, body(): lax.all_to_all(whole_sum, groups, 0, 0).reshape(group * PART_ROWS, ch)  7.23 us
    all_to_all x1, waiting for transfers between devices, body(): lax.all_to_all(whole_sum, groups, 0, 0).reshape(group * PART_ROWS, ch)  7.12 us
    all_to_all x1, waiting for transfers between devices, body(): parts = lax.all_to_all(grads.reshape(group, PART_ROWS, ch), groups, 0, 0)  6.18 us
    pallas_call x1, Pallas kernels, body(): call(mlp_kernel, [shape((band_rows, lon, ch), BF16), shape((band_rows, lo...  6.18 us
    all_to_all x1, starting transfers between devices, body(): parts = lax.all_to_all(part_sum, 'z', 0, 0)  5.55 us
    all_to_all x1, starting transfers between devices, body(): parts = lax.all_to_all(grads.reshape(group, PART_ROWS, ch), groups, 0, 0)  5.13 us
  transfers between devices with their start and end apart: 15, of which 7 were waited for; matrix products, arithmetic and copies ran while one was open for 0% of the time, Pallas kernels for 7%

profile of v8, /device:TPU:1, one launch (start us, length us, event | category | flops | bytes accessed | tf_op | source)
XLA Modules:
  0.0 89.7 jit_solution(10947085170900645259)
XLA Ops:
  0.6 0.0 copy-start.8
  0.6 0.7 copy-done.8
  1.3 0.0 copy-start
  1.3 0.0 copy-start.5
  1.3 0.6 choose.1
  2.0 0.0 copy-start.6
  2.0 0.0 copy-start.7
  2.0 0.0 copy-start.9
  2.0 0.0 copy-start.10
  2.0 0.0 copy-start.11
  2.0 0.3 copy-done
  2.4 0.0 copy-done.5
  2.4 1.3 %pack.1 = (bf16[128,512]{1,0:T(8,128)(2,1)S(1)}, bf16[128,512]{1,0:T(8,128)(2,1)S(1)}, bf16[128,512]{1,0:T(8,128)(2,1)S(1)}, bf16[128,512]{1,0:T(8,128)(2,1)S(1)}, bf16[128,512]{1,0:T(8,128)(2,1)S(1)}) custom-call(bf16[4,512,128]{2,1,0:T(8,128)(2,1)S(1)} %bitcast.14, bf16[640,1536]{1,0:T(8,128)(2,1)S(1)} %get-tuple-element.34.select_ref, s32[1,5]{1,0:T(1,128)S(1)} %copy-done.5), custom_call_target="tpu_custom_call" | custom-call | bytes 1310720 | tf_op jit(solution)/shard_map/pack/pallas_call | solution.py:414
  3.7 8.7 %collective-permute-start = (bf16[128,512]{1,0:T(8,128)(2,1)S(1)}, bf16[128,512]{1,0:T(8,128)(2,1)S(1)}, u32[]{:S(2)}, u32[]{:S(2)}) collective-permute-start(bf16[128,512]{1,0:T(8,128)(2,1)S(1)} %get-tuple-element.35), channel_id=1, source_target_pairs={{0,62},{1,63},{2,0},{3,1},{4,2},{5,3},{6,4},{7,5},{8,6},{9,7},{10,... | collective-permute-start | bytes 393224 | tf_op jit(solution)/shard_map/ppermute | solution.py:374
  12.4 0.0 collective-permute-start.1
  12.4 1.0 %collective-permute-start.2 = (bf16[128,512]{1,0:T(8,128)(2,1)S(1)}, bf16[128,512]{1,0:T(8,128)(2,1)S(1)}, u32[]{:S(2)}, u32[]{:S(2)}) collective-permute-start(bf16[128,512]{1,0:T(8,128)(2,1)S(1)} %get-tuple-element.37), channel_id=1, source_target_pairs={{0,63},{1,0},{2,1},{3,2},{4,3},{5,4},{6,5},{7,6},{8,7},{9,8},{10,9... | collective-permute-start | bytes 393224 | tf_op jit(solution)/shard_map/ppermute | solution.py:374
  13.4 0.8 collective-permute-start.3
  14.1 0.0 copy-done.6
  14.1 0.0 copy-done.7
  14.1 0.0 copy-done.9
  14.2 0.0 copy-done.10
  14.2 0.0 copy-done.11
  14.2 0.0 copy-start.1
  14.2 0.0 copy-start.2
  14.2 0.0 copy-start.3
  14.2 0.0 copy-start.4
  14.2 0.3 collective-permute-done.refs_0_
  14.6 5.0 %collective-permute-done.1.refs_1_ = bf16[128,512]{1,0:T(8,128)(2,1)S(1)} collective-permute-done((bf16[128,512]{1,0:T(8,128)(2,1)S(1)}, bf16[128,512]{1,0:T(8,128)(2,1)S(1)}, u32[]{:S(2)}, u32[]{:S(2)}) %collective-permute-start.1) | collective-permute-done | bytes 131104 | tf_op jit(solution)/shard_map/ppermute | solution.py:374
  19.5 0.0 collective-permute-done.2.refs_2_
  19.5 0.0 collective-permute-done.3.refs_3_
  19.5 2.0 %interp.1 = (f32[4,512,128]{2,1,0:T(8,128)S(1)}, bf16[2,512,128]{2,1,0:T(8,128)(2,1)S(1)}, bf16[2,512,128]{2,1,0:T(8,128)(2,1)S(1)}) custom-call(bf16[128,512]{1,0:T(8,128)(2,1)S(1)} %collective-permute-done.refs_0_, bf16[128,512]{1,0:T(8,128)(2,1)S(1)} %collective-permute-done.1.refs_1_, bf16[128,512]{1,0:T(8,128)(2,1)S(1)} %collective-permute-done.2.refs_2_, ...), custom_call_target="tpu_custom_call" | custom-call | bytes 3145728 | tf_op jit(solution)/shard_map/interp/pallas_call | solution.py:439
  21.6 5.8 %collective-permute-start.4 = (bf16[2,512,128]{2,1,0:T(8,128)(2,1)S(1)}, bf16[2,512,128]{2,1,0:T(8,128)(2,1)S(1)}, u32[]{:S(2)}, u32[]{:S(2)}) collective-permute-start(bf16[2,512,128]{2,1,0:T(8,128)(2,1)S(1)} %get-tuple-element.41), channel_id=1, source_target_pairs={{0,63},{1,0},{2,1},{3,2},{4,3},{5,4},{6,5},{7,6},{8,7},{9,8},{10,9... | collective-permute-start | bytes 786440 | tf_op jit(solution)/shard_map/ppermute | solution.py:374
  27.4 0.0 collective-permute-start.5
  27.4 0.1 pad_add_fusion.place_ref
  27.5 1.1 %collective-permute-done.4.after_ref = bf16[2,512,128]{2,1,0:T(8,128)(2,1)S(1)} collective-permute-done((bf16[2,512,128]{2,1,0:T(8,128)(2,1)S(1)}, bf16[2,512,128]{2,1,0:T(8,128)(2,1)S(1)}, u32[]{:S(2)}, u32[]{:S(2)}) %collective-permute-start.4) | collective-permute-done | bytes 262176 | tf_op jit(solution)/shard_map/ppermute | solution.py:374
  28.6 2.2 %collective-permute-done.5.before_ref = bf16[2,512,128]{2,1,0:T(8,128)(2,1)S(1)} collective-permute-done((bf16[2,512,128]{2,1,0:T(8,128)(2,1)S(1)}, bf16[2,512,128]{2,1,0:T(8,128)(2,1)S(1)}, u32[]{:S(2)}, u32[]{:S(2)}) %collective-permute-start.5) | collective-permute-done | bytes 262176 | tf_op jit(solution)/shard_map/ppermute | solution.py:374
  30.7 0.0 copy-done.1
  30.7 0.0 copy-done.2
  30.7 0.0 copy-done.3
  30.7 0.0 copy-done.4
  30.7 6.2 %smooth_mlp.1 = (bf16[4,512,128]{2,1,0:T(8,128)(2,1)}, f32[4,512,128]{2,1,0:T(8,128)S(1)}, bf16[2,512,128]{2,1,0:T(8,128)(2,1)}, bf16[2,512,128]{2,1,0:T(8,128)(2,1)}, bf16[1280,128]{1,0:T(8,128)(2,1)}) custom-call(f32[4,512,128]{2,1,0:T(8,128)S(1)} %get-tuple-element.40.dep_ref, bf16[2,512,128]{2,1,0:T(8,128)(2,1)S(1)} %collective-permute-done.4.after_ref, ...), custom_call_target="tpu_custom_call" | custom-call | bytes 4849664 | tf_op jit(solution)/shard_map/smooth_mlp/pallas_call | solution.py:451
  36.9 6.1 %collective-permute-start.6 = (bf16[2,512,128]{2,1,0:T(8,128)(2,1)}, bf16[2,512,128]{2,1,0:T(8,128)(2,1)S(1)}, u32[]{:S(2)}, u32[]{:S(2)}) collective-permute-start(bf16[2,512,128]{2,1,0:T(8,128)(2,1)} %get-tuple-element.46), channel_id=1, source_target_pairs={{0,63},{1,0},{2,1},{3,2},{4,3},{5,4},{6,5},{7,6},{8,7},{9,8},{10,9... | collective-permute-start | bytes 786440 | tf_op jit(solution)/shard_map/ppermute | solution.py:374
  43.0 0.0 collective-permute-start.7
  43.0 5.1 %all-to-all-start = ((bf16[32,40,128]{2,1,0:T(8,128)(2,1)}), bf16[32,40,128]{2,1,0:T(8,128)(2,1)S(1)}, u32[]{:S(2)}, u32[]{:S(2)}) async-start(bf16[32,40,128]{2,1,0:T(8,128)(2,1)} %bitcast.9), calls=%async_computation | async-start | bytes 655360 | tf_op jit(solution)/shard_map/all_to_all | solution.py:473
  48.1 0.0 collective-permute-done.6.after_ref
  48.1 0.0 collective-permute-done.7.before_ref
  48.1 3.3 %adjoint.1 = (bf16[128,512]{1,0:T(8,128)(2,1)S(1)}, bf16[128,512]{1,0:T(8,128)(2,1)S(1)}, bf16[128,512]{1,0:T(8,128)(2,1)S(1)}, bf16[128,512]{1,0:T(8,128)(2,1)S(1)}, bf16[128,512]{1,0:T(8,128)(2,1)S(1)}) custom-call(f32[4,512,128]{2,1,0:T(8,128)S(1)} %get-tuple-element.45.scaled_ref, bf16[2,512,128]{2,1,0:T(8,128)(2,1)S(1)} %collective-permute-done.6.after_ref, ...), custom_call_target="tpu_custom_call" | custom-call | flops 99999997952 | bytes 1310720 | tf_op jit(solution)/shard_map/adjoint/pallas_call | solution.py:474
  51.5 6.2 %all-to-all-done.parts_ref = bf16[32,40,128]{2,1,0:T(8,128)(2,1)S(1)} async-done(((bf16[32,40,128]{2,1,0:T(8,128)(2,1)}), bf16[32,40,128]{2,1,0:T(8,128)(2,1)S(1)}, u32[]{:S(2)}, u32[]{:S(2)}) %all-to-all-start) | async-done | bytes 327712 | tf_op jit(solution)/shard_map/all_to_all | solution.py:473
  57.7 0.7 part_sum.1
  58.4 5.6 %all-to-all-start.1 = ((bf16[8,40,128]{2,1,0:T(8,128)(2,1)}), bf16[8,40,128]{2,1,0:T(8,128)(2,1)S(1)}, u32[]{:S(2)}, u32[]{:S(2)}) async-start(bf16[8,40,128]{2,1,0:T(8,128)(2,1)} %part_sum.1), calls=%async_computation.1 | async-start | bytes 163840 | tf_op jit(solution)/shard_map/all_to_all | solution.py:493
  63.9 0.5 collective-permute-start.8
  64.4 4.3 %collective-permute-start.9 = (bf16[128,512]{1,0:T(8,128)(2,1)S(1)}, bf16[128,512]{1,0:T(8,128)(2,1)S(1)}, u32[]{:S(2)}, u32[]{:S(2)}) collective-permute-start(bf16[128,512]{1,0:T(8,128)(2,1)S(1)} %get-tuple-element.49), channel_id=1, source_target_pairs={{0,62},{1,63},{2,0},{3,1},{4,2},{5,3},{6,4},{7,5},{8,6},{9,7},{10,... | collective-permute-start | bytes 393224 | tf_op jit(solution)/shard_map/ppermute | solution.py:374
  68.7 0.0 collective-permute-start.10
  68.7 1.1 %collective-permute-start.11 = (bf16[128,512]{1,0:T(8,128)(2,1)S(1)}, bf16[128,512]{1,0:T(8,128)(2,1)S(1)}, u32[]{:S(2)}, u32[]{:S(2)}) collective-permute-start(bf16[128,512]{1,0:T(8,128)(2,1)S(1)} %get-tuple-element.51), channel_id=1, source_target_pairs={{0,63},{1,0},{2,1},{3,2},{4,3},{5,4},{6,5},{7,6},{8,7},{9,8},{10,9... | collective-permute-start | bytes 393224 | tf_op jit(solution)/shard_map/ppermute | solution.py:374
  69.8 1.4 %all-to-all-done.1.parts_ref = bf16[8,40,128]{2,1,0:T(8,128)(2,1)S(1)} async-done(((bf16[8,40,128]{2,1,0:T(8,128)(2,1)}), bf16[8,40,128]{2,1,0:T(8,128)(2,1)S(1)}, u32[]{:S(2)}, u32[]{:S(2)}) %all-to-all-start.1) | async-done | bytes 81952 | tf_op jit(solution)/shard_map/all_to_all | solution.py:493
  71.2 0.8 whole_sum.1
  72.0 7.2 %all-to-all-start.2 = ((bf16[32,40,128]{2,1,0:T(8,128)(2,1)}), bf16[32,40,128]{2,1,0:T(8,128)(2,1)S(1)}, u32[]{:S(2)}, u32[]{:S(2)}) async-start(bf16[32,40,128]{2,1,0:T(8,128)(2,1)} %whole_sum.1), calls=%async_computation.2 | async-start | bytes 655360 | tf_op jit(solution)/shard_map/all_to_all | solution.py:515
  79.2 0.0 collective-permute-done.8.refs_0_
  79.2 0.0 collective-permute-done.9.refs_1_
  79.2 0.0 collective-permute-done.10.refs_2_
  79.2 0.0 collective-permute-done.11.refs_3_
  79.2 2.5 %scatter.1 = (f32[4,512,128]{2,1,0:T(8,128)}, f32[8,128]{1,0:T(8,128)S(1)}) custom-call(s32[8,128]{1,0:T(8,128)S(1)} %get-tuple-element.44.cells_ref, s32[1,5]{1,0:T(1,128)S(1)} %copy-done.5, bf16[128,512]{1,0:T(8,128)(2,1)S(1)} %collective-permute-done.8.refs_0_, bf16[128,512]{1,0:T(8,128)(2,1)S(1)} %collective-permute-done.9.refs_1_, ...), custom_call_target="tpu_custom_call" | custom-call | flops 99999997952 | bytes 2105344 | tf_op jit(solution)/shard_map/scatter/pallas_call | solution.py:498
  81.7 7.1 %all-to-all-done.2 = bf16[32,40,128]{2,1,0:T(8,128)(2,1)S(1)} async-done(((bf16[32,40,128]{2,1,0:T(8,128)(2,1)}), bf16[32,40,128]{2,1,0:T(8,128)(2,1)S(1)}, u32[]{:S(2)}, u32[]{:S(2)}) %all-to-all-start.2) | async-done | bytes 327712 | tf_op jit(solution)/shard_map/all_to_all | solution.py:515
  88.9 0.8 unpack.1
  (1 shorter events, 0.0 us)
Async XLA Ops:
  0.6 0.7 copy-start.8
  1.3 1.0 %copy-start = (bf16[1,4,512,128]{3,2,1,0:T(8,128)(2,1)S(1)}, bf16[1,4,512,128]{3,2,1,0:T(8,128)(2,1)}, u32[]{:S(2)}) copy-start(bf16[1,4,512,128]{3,2,1,0:T(8,128)(2,1)} %param.12) | copy-start | bytes 1572868
  1.3 1.0 %copy-start.5 = (s32[1,5]{1,0:T(1,128)S(1)}, s32[1,5]{1,0:T(1,128)}, u32[]{:S(2)}) copy-start(s32[1,5]{1,0:T(1,128)} %count_ref.3) | copy-start | bytes 64
  2.0 12.2 %copy-start.6 = (s32[4,4,512]{2,1,0:T(4,128)S(1)}, s32[4,4,512]{2,1,0:T(4,128)}, u32[]{:S(2)}) copy-start(s32[4,4,512]{2,1,0:T(4,128)} %slot_ref.1) | copy-start | bytes 98308
  2.0 12.2 %copy-start.7 = (f32[4,4,512]{2,1,0:T(4,128)S(1)}, f32[4,4,512]{2,1,0:T(4,128)}, u32[]{:S(2)}) copy-start(f32[4,4,512]{2,1,0:T(4,128)} %weight_ref.1) | copy-start | bytes 98308
  2.0 12.1 %copy-start.9 = (f32[256]{0:T(256)S(1)}, f32[256]{0:T(256)}, u32[]{:S(2)}) copy-start(f32[256]{0:T(256)} %param.19) | copy-start | bytes 3076
  2.0 12.1 %copy-start.10 = (f32[256]{0:T(256)S(1)}, f32[256]{0:T(256)}, u32[]{:S(2)}) copy-start(f32[256]{0:T(256)} %param.21) | copy-start | bytes 3076
  2.0 12.1 %copy-start.11 = (f32[128]{0:T(128)S(1)}, f32[128]{0:T(128)}, u32[]{:S(2)}) copy-start(f32[128]{0:T(128)} %param.17) | copy-start | bytes 1540
  3.7 10.8 %collective-permute-start = (bf16[128,512]{1,0:T(8,128)(2,1)S(1)}, bf16[128,512]{1,0:T(8,128)(2,1)S(1)}, u32[]{:S(2)}, u32[]{:S(2)}) collective-permute-start(bf16[128,512]{1,0:T(8,128)(2,1)S(1)} %get-tuple-element.35), channel_id=1, source_target_pairs={{0,62},{1,63},{2,0},{3,1},{4,2},{5,3},{6,4},{7,5},{8,6},{9,7},{10,... | collective-permute-start | bytes 393224 | tf_op jit(solution)/shard_map/ppermute | solution.py:374
  12.4 7.1 %collective-permute-start.1 = (bf16[128,512]{1,0:T(8,128)(2,1)S(1)}, bf16[128,512]{1,0:T(8,128)(2,1)S(1)}, u32[]{:S(2)}, u32[]{:S(2)}) collective-permute-start(bf16[128,512]{1,0:T(8,128)(2,1)S(1)} %get-tuple-element.36), channel_id=1, source_target_pairs={{0,2},{1,3},{2,4},{3,5},{4,6},{5,7},{6,8},{7,9},{8,10},{9,11},{10,... | collective-permute-start | bytes 393224 | tf_op jit(solution)/shard_map/ppermute | solution.py:374
  12.4 7.1 %collective-permute-start.2 = (bf16[128,512]{1,0:T(8,128)(2,1)S(1)}, bf16[128,512]{1,0:T(8,128)(2,1)S(1)}, u32[]{:S(2)}, u32[]{:S(2)}) collective-permute-start(bf16[128,512]{1,0:T(8,128)(2,1)S(1)} %get-tuple-element.37), channel_id=1, source_target_pairs={{0,63},{1,0},{2,1},{3,2},{4,3},{5,4},{6,5},{7,6},{8,7},{9,8},{10,9... | collective-permute-start | bytes 393224 | tf_op jit(solution)/shard_map/ppermute | solution.py:374
  13.4 6.2 %collective-permute-start.3 = (bf16[128,512]{1,0:T(8,128)(2,1)S(1)}, bf16[128,512]{1,0:T(8,128)(2,1)S(1)}, u32[]{:S(2)}, u32[]{:S(2)}) collective-permute-start(bf16[128,512]{1,0:T(8,128)(2,1)S(1)} %get-tuple-element.38), channel_id=1, source_target_pairs={{0,1},{1,2},{2,3},{3,4},{4,5},{5,6},{6,7},{7,8},{8,9},{9,10},{10,1... | collective-permute-start | bytes 393224 | tf_op jit(solution)/shard_map/ppermute | solution.py:374
  14.2 16.5 %copy-start.1 = (bf16[1,4,512,128]{3,2,1,0:T(8,128)(2,1)S(1)}, bf16[1,4,512,128]{3,2,1,0:T(8,128)(2,1)}, u32[]{:S(2)}) copy-start(bf16[1,4,512,128]{3,2,1,0:T(8,128)(2,1)} %param.23) | copy-start | bytes 1572868
  14.2 16.5 %copy-start.2 = (bf16[256,256]{1,0:T(8,128)(2,1)S(1)}, bf16[256,256]{1,0:T(8,128)(2,1)}, u32[]{:S(2)}) copy-start(bf16[256,256]{1,0:T(8,128)(2,1)} %w2_ref.1) | copy-start | bytes 393220
  14.2 16.5 %copy-start.3 = (bf16[128,256]{1,0:T(8,128)(2,1)S(1)}, bf16[128,256]{1,0:T(8,128)(2,1)}, u32[]{:S(2)}) copy-start(bf16[128,256]{1,0:T(8,128)(2,1)} %w1_ref.1) | copy-start | bytes 196612
  14.2 16.5 %copy-start.4 = (bf16[256,128]{1,0:T(8,128)(2,1)S(1)}, bf16[256,128]{1,0:T(8,128)(2,1)}, u32[]{:S(2)}) copy-start(bf16[256,128]{1,0:T(8,128)(2,1)} %w3_ref.1) | copy-start | bytes 196612
  21.6 7.0 %collective-permute-start.4 = (bf16[2,512,128]{2,1,0:T(8,128)(2,1)S(1)}, bf16[2,512,128]{2,1,0:T(8,128)(2,1)S(1)}, u32[]{:S(2)}, u32[]{:S(2)}) collective-permute-start(bf16[2,512,128]{2,1,0:T(8,128)(2,1)S(1)} %get-tuple-element.41), channel_id=1, source_target_pairs={{0,63},{1,0},{2,1},{3,2},{4,3},{5,4},{6,5},{7,6},{8,7},{9,8},{10,9... | collective-permute-start | bytes 786440 | tf_op jit(solution)/shard_map/ppermute | solution.py:374
  27.4 3.3 %collective-permute-start.5 = (bf16[2,512,128]{2,1,0:T(8,128)(2,1)S(1)}, bf16[2,512,128]{2,1,0:T(8,128)(2,1)S(1)}, u32[]{:S(2)}, u32[]{:S(2)}) collective-permute-start(bf16[2,512,128]{2,1,0:T(8,128)(2,1)S(1)} %get-tuple-element.42), channel_id=1, source_target_pairs={{0,1},{1,2},{2,3},{3,4},{4,5},{5,6},{6,7},{7,8},{8,9},{9,10},{10,1... | collective-permute-start | bytes 786440 | tf_op jit(solution)/shard_map/ppermute | solution.py:374
  36.9 11.2 %collective-permute-start.6 = (bf16[2,512,128]{2,1,0:T(8,128)(2,1)}, bf16[2,512,128]{2,1,0:T(8,128)(2,1)S(1)}, u32[]{:S(2)}, u32[]{:S(2)}) collective-permute-start(bf16[2,512,128]{2,1,0:T(8,128)(2,1)} %get-tuple-element.46), channel_id=1, source_target_pairs={{0,63},{1,0},{2,1},{3,2},{4,3},{5,4},{6,5},{7,6},{8,7},{9,8},{10,9... | collective-permute-start | bytes 786440 | tf_op jit(solution)/shard_map/ppermute | solution.py:374
  43.0 5.2 %collective-permute-start.7 = (bf16[2,512,128]{2,1,0:T(8,128)(2,1)}, bf16[2,512,128]{2,1,0:T(8,128)(2,1)S(1)}, u32[]{:S(2)}, u32[]{:S(2)}) collective-permute-start(bf16[2,512,128]{2,1,0:T(8,128)(2,1)} %get-tuple-element.47), channel_id=1, source_target_pairs={{0,1},{1,2},{2,3},{3,4},{4,5},{5,6},{6,7},{7,8},{8,9},{9,10},{10,1... | collective-permute-start | bytes 786440 | tf_op jit(solution)/shard_map/ppermute | solution.py:374
  43.0 14.7 %all-to-all-start = ((bf16[32,40,128]{2,1,0:T(8,128)(2,1)}), bf16[32,40,128]{2,1,0:T(8,128)(2,1)S(1)}, u32[]{:S(2)}, u32[]{:S(2)}) async-start(bf16[32,40,128]{2,1,0:T(8,128)(2,1)} %bitcast.9), calls=%async_computation | async-start | bytes 655360 | tf_op jit(solution)/shard_map/all_to_all | solution.py:473
  58.4 12.9 %all-to-all-start.1 = ((bf16[8,40,128]{2,1,0:T(8,128)(2,1)}), bf16[8,40,128]{2,1,0:T(8,128)(2,1)S(1)}, u32[]{:S(2)}, u32[]{:S(2)}) async-start(bf16[8,40,128]{2,1,0:T(8,128)(2,1)} %part_sum.1), calls=%async_computation.1 | async-start | bytes 163840 | tf_op jit(solution)/shard_map/all_to_all | solution.py:493
  63.9 15.3 %collective-permute-start.8 = (bf16[128,512]{1,0:T(8,128)(2,1)S(1)}, bf16[128,512]{1,0:T(8,128)(2,1)S(1)}, u32[]{:S(2)}, u32[]{:S(2)}) collective-permute-start(bf16[128,512]{1,0:T(8,128)(2,1)S(1)} %get-tuple-element.48), channel_id=1, source_target_pairs={{0,2},{1,3},{2,4},{3,5},{4,6},{5,7},{6,8},{7,9},{8,10},{9,11},{10,... | collective-permute-start | bytes 393224 | tf_op jit(solution)/shard_map/ppermute | solution.py:374
  64.4 14.8 %collective-permute-start.9 = (bf16[128,512]{1,0:T(8,128)(2,1)S(1)}, bf16[128,512]{1,0:T(8,128)(2,1)S(1)}, u32[]{:S(2)}, u32[]{:S(2)}) collective-permute-start(bf16[128,512]{1,0:T(8,128)(2,1)S(1)} %get-tuple-element.49), channel_id=1, source_target_pairs={{0,62},{1,63},{2,0},{3,1},{4,2},{5,3},{6,4},{7,5},{8,6},{9,7},{10,... | collective-permute-start | bytes 393224 | tf_op jit(solution)/shard_map/ppermute | solution.py:374
  68.7 10.5 %collective-permute-start.10 = (bf16[128,512]{1,0:T(8,128)(2,1)S(1)}, bf16[128,512]{1,0:T(8,128)(2,1)S(1)}, u32[]{:S(2)}, u32[]{:S(2)}) collective-permute-start(bf16[128,512]{1,0:T(8,128)(2,1)S(1)} %get-tuple-element.50), channel_id=1, source_target_pairs={{0,1},{1,2},{2,3},{3,4},{4,5},{5,6},{6,7},{7,8},{8,9},{9,10},{10,1... | collective-permute-start | bytes 393224 | tf_op jit(solution)/shard_map/ppermute | solution.py:374
  68.7 10.5 %collective-permute-start.11 = (bf16[128,512]{1,0:T(8,128)(2,1)S(1)}, bf16[128,512]{1,0:T(8,128)(2,1)S(1)}, u32[]{:S(2)}, u32[]{:S(2)}) collective-permute-start(bf16[128,512]{1,0:T(8,128)(2,1)S(1)} %get-tuple-element.51), channel_id=1, source_target_pairs={{0,63},{1,0},{2,1},{3,2},{4,3},{5,4},{6,5},{7,6},{8,7},{9,8},{10,9... | collective-permute-start | bytes 393224 | tf_op jit(solution)/shard_map/ppermute | solution.py:374
  72.0 16.9 %all-to-all-start.2 = ((bf16[32,40,128]{2,1,0:T(8,128)(2,1)}), bf16[32,40,128]{2,1,0:T(8,128)(2,1)S(1)}, u32[]{:S(2)}, u32[]{:S(2)}) async-start(bf16[32,40,128]{2,1,0:T(8,128)(2,1)} %whole_sum.1), calls=%async_computation.2 | async-start | bytes 655360 | tf_op jit(solution)/shard_map/all_to_all | solution.py:515

commit v9 on v8

--- a/solution.py
+++ b/solution.py
@@ -496,7 +496,7 @@
         for e in range(offsets)
     ]
     field_grad, done = call(
-        functools.partial(scatter_kernel, offsets, order),
+        functools.partial(scatter_kernel, offsets, range(offsets)),
         [shape((band_rows, lon, ch), F32), shape((8, ch), F32)],
         [VMEM] * (offsets + 2),
         [
@@ -505,7 +505,7 @@
         ],
         flops=SCATTER_COST,
         name="scatter",
-    )(cells, send_count, *(back[e] for e in order))
+    )(cells, send_count, *back)
     (whole_sum,) = call(
         functools.partial(sum_kernel, group),
         [shape((group, PART_ROWS, ch), BF16)],

time: 90.1 us -> 88.3 us (0.980)
  starting transfers between devices: 46.2 us -> 44.3 us
    all_to_all x1, starting transfers between devices: 7.23 us -> 5.37 us  [body(): lax.all_to_all(whole_sum, groups, 0, 0).reshape(group * PART_ROWS, ch)]
where the time goes in v9:
time: 88.3 us; the launch traced here: 87.8 us
  starting transfers between devices  44.3 us (50%)
  waiting for transfers between devices  23.3 us (26%)
  Pallas kernels  18.2 us (21%)
  local copies, waits for them, and re-layouts  1.1 us (1%)
    ppermute x12, starting transfers between devices, shifted(): lax.ppermute(block, SPACE, [(i, (i + by) % count) for i in range(count)])  28.2 us
    ppermute x12, waiting for transfers between devices, shifted(): lax.ppermute(block, SPACE, [(i, (i + by) % count) for i in range(count)])  8.56 us
    all_to_all x1, waiting for transfers between devices, body(): lax.all_to_all(whole_sum, groups, 0, 0).reshape(group * PART_ROWS, ch)  7.12 us
    all_to_all x1, waiting for transfers between devices, body(): parts = lax.all_to_all(grads.reshape(group, PART_ROWS, ch), groups, 0, 0)  6.18 us
    pallas_call x1, Pallas kernels, body(): call(mlp_kernel, [shape((band_rows, lon, ch), BF16), shape((band_rows, lo...  6.18 us
    all_to_all x1, starting transfers between devices, body(): parts = lax.all_to_all(part_sum, 'z', 0, 0)  5.55 us
    all_to_all x1, starting transfers between devices, body(): lax.all_to_all(whole_sum, groups, 0, 0).reshape(group * PART_ROWS, ch)  5.37 us
    all_to_all x1, starting transfers between devices, body(): parts = lax.all_to_all(grads.reshape(group, PART_ROWS, ch), groups, 0, 0)  5.13 us
  transfers between devices with their start and end apart: 15, of which 7 were waited for; matrix products, arithmetic and copies ran while one was open for 0% of the time, Pallas kernels for 7%

profile of v9, /device:TPU:1, one launch (start us, length us, event | category | flops | bytes accessed | tf_op | source)
XLA Modules:
  0.0 87.8 jit_solution(17993339488462297018)
XLA Ops:
  0.6 0.0 copy-start.8
  0.6 0.7 copy-done.8
  1.3 0.0 copy-start
  1.3 0.0 copy-start.5
  1.3 0.6 choose.1
  2.0 0.0 copy-start.6
  2.0 0.0 copy-start.7
  2.0 0.0 copy-start.9
  2.0 0.0 copy-start.10
  2.0 0.0 copy-start.11
  2.0 0.3 copy-done
  2.4 0.0 copy-done.5
  2.4 1.3 %pack.1 = (bf16[128,512]{1,0:T(8,128)(2,1)S(1)}, bf16[128,512]{1,0:T(8,128)(2,1)S(1)}, bf16[128,512]{1,0:T(8,128)(2,1)S(1)}, bf16[128,512]{1,0:T(8,128)(2,1)S(1)}, bf16[128,512]{1,0:T(8,128)(2,1)S(1)}) custom-call(bf16[4,512,128]{2,1,0:T(8,128)(2,1)S(1)} %bitcast.14, bf16[640,1536]{1,0:T(8,128)(2,1)S(1)} %get-tuple-element.34.select_ref, s32[1,5]{1,0:T(1,128)S(1)} %copy-done.5), custom_call_target="tpu_custom_call" | custom-call | bytes 1310720 | tf_op jit(solution)/shard_map/pack/pallas_call | solution.py:414
  3.7 8.7 %collective-permute-start = (bf16[128,512]{1,0:T(8,128)(2,1)S(1)}, bf16[128,512]{1,0:T(8,128)(2,1)S(1)}, u32[]{:S(2)}, u32[]{:S(2)}) collective-permute-start(bf16[128,512]{1,0:T(8,128)(2,1)S(1)} %get-tuple-element.35), channel_id=1, source_target_pairs={{0,62},{1,63},{2,0},{3,1},{4,2},{5,3},{6,4},{7,5},{8,6},{9,7},{10,... | collective-permute-start | bytes 393224 | tf_op jit(solution)/shard_map/ppermute | solution.py:374
  12.4 0.0 collective-permute-start.1
  12.4 1.0 %collective-permute-start.2 = (bf16[128,512]{1,0:T(8,128)(2,1)S(1)}, bf16[128,512]{1,0:T(8,128)(2,1)S(1)}, u32[]{:S(2)}, u32[]{:S(2)}) collective-permute-start(bf16[128,512]{1,0:T(8,128)(2,1)S(1)} %get-tuple-element.37), channel_id=1, source_target_pairs={{0,63},{1,0},{2,1},{3,2},{4,3},{5,4},{6,5},{7,6},{8,7},{9,8},{10,9... | collective-permute-start | bytes 393224 | tf_op jit(solution)/shard_map/ppermute | solution.py:374
  13.4 0.8 collective-permute-start.3
  14.1 0.0 copy-done.6
  14.1 0.0 copy-done.7
  14.1 0.0 copy-done.9
  14.2 0.0 copy-done.10
  14.2 0.0 copy-done.11
  14.2 0.0 copy-start.1
  14.2 0.0 copy-start.2
  14.2 0.0 copy-start.3
  14.2 0.0 copy-start.4
  14.2 0.3 collective-permute-done.refs_0_
  14.6 5.0 %collective-permute-done.1.refs_1_ = bf16[128,512]{1,0:T(8,128)(2,1)S(1)} collective-permute-done((bf16[128,512]{1,0:T(8,128)(2,1)S(1)}, bf16[128,512]{1,0:T(8,128)(2,1)S(1)}, u32[]{:S(2)}, u32[]{:S(2)}) %collective-permute-start.1) | collective-permute-done | bytes 131104 | tf_op jit(solution)/shard_map/ppermute | solution.py:374
  19.5 0.0 collective-permute-done.2.refs_2_
  19.5 0.0 collective-permute-done.3.refs_3_
  19.5 2.0 %interp.1 = (f32[4,512,128]{2,1,0:T(8,128)S(1)}, bf16[2,512,128]{2,1,0:T(8,128)(2,1)S(1)}, bf16[2,512,128]{2,1,0:T(8,128)(2,1)S(1)}) custom-call(bf16[128,512]{1,0:T(8,128)(2,1)S(1)} %collective-permute-done.refs_0_, bf16[128,512]{1,0:T(8,128)(2,1)S(1)} %collective-permute-done.1.refs_1_, bf16[128,512]{1,0:T(8,128)(2,1)S(1)} %collective-permute-done.2.refs_2_, ...), custom_call_target="tpu_custom_call" | custom-call | bytes 3145728 | tf_op jit(solution)/shard_map/interp/pallas_call | solution.py:439
  21.6 5.8 %collective-permute-start.4 = (bf16[2,512,128]{2,1,0:T(8,128)(2,1)S(1)}, bf16[2,512,128]{2,1,0:T(8,128)(2,1)S(1)}, u32[]{:S(2)}, u32[]{:S(2)}) collective-permute-start(bf16[2,512,128]{2,1,0:T(8,128)(2,1)S(1)} %get-tuple-element.41), channel_id=1, source_target_pairs={{0,63},{1,0},{2,1},{3,2},{4,3},{5,4},{6,5},{7,6},{8,7},{9,8},{10,9... | collective-permute-start | bytes 786440 | tf_op jit(solution)/shard_map/ppermute | solution.py:374
  27.4 0.0 collective-permute-start.5
  27.4 0.1 pad_add_fusion.place_ref
  27.5 1.1 %collective-permute-done.4.after_ref = bf16[2,512,128]{2,1,0:T(8,128)(2,1)S(1)} collective-permute-done((bf16[2,512,128]{2,1,0:T(8,128)(2,1)S(1)}, bf16[2,512,128]{2,1,0:T(8,128)(2,1)S(1)}, u32[]{:S(2)}, u32[]{:S(2)}) %collective-permute-start.4) | collective-permute-done | bytes 262176 | tf_op jit(solution)/shard_map/ppermute | solution.py:374
  28.6 2.2 %collective-permute-done.5.before_ref = bf16[2,512,128]{2,1,0:T(8,128)(2,1)S(1)} collective-permute-done((bf16[2,512,128]{2,1,0:T(8,128)(2,1)S(1)}, bf16[2,512,128]{2,1,0:T(8,128)(2,1)S(1)}, u32[]{:S(2)}, u32[]{:S(2)}) %collective-permute-start.5) | collective-permute-done | bytes 262176 | tf_op jit(solution)/shard_map/ppermute | solution.py:374
  30.7 0.0 copy-done.1
  30.7 0.0 copy-done.2
  30.7 0.0 copy-done.3
  30.7 0.0 copy-done.4
  30.7 6.2 %smooth_mlp.1 = (bf16[4,512,128]{2,1,0:T(8,128)(2,1)}, f32[4,512,128]{2,1,0:T(8,128)S(1)}, bf16[2,512,128]{2,1,0:T(8,128)(2,1)}, bf16[2,512,128]{2,1,0:T(8,128)(2,1)}, bf16[1280,128]{1,0:T(8,128)(2,1)}) custom-call(f32[4,512,128]{2,1,0:T(8,128)S(1)} %get-tuple-element.40.dep_ref, bf16[2,512,128]{2,1,0:T(8,128)(2,1)S(1)} %collective-permute-done.4.after_ref, ...), custom_call_target="tpu_custom_call" | custom-call | bytes 4849664 | tf_op jit(solution)/shard_map/smooth_mlp/pallas_call | solution.py:451
  36.9 6.1 %collective-permute-start.6 = (bf16[2,512,128]{2,1,0:T(8,128)(2,1)}, bf16[2,512,128]{2,1,0:T(8,128)(2,1)S(1)}, u32[]{:S(2)}, u32[]{:S(2)}) collective-permute-start(bf16[2,512,128]{2,1,0:T(8,128)(2,1)} %get-tuple-element.46), channel_id=1, source_target_pairs={{0,63},{1,0},{2,1},{3,2},{4,3},{5,4},{6,5},{7,6},{8,7},{9,8},{10,9... | collective-permute-start | bytes 786440 | tf_op jit(solution)/shard_map/ppermute | solution.py:374
  43.0 0.0 collective-permute-start.7
  43.0 5.1 %all-to-all-start = ((bf16[32,40,128]{2,1,0:T(8,128)(2,1)}), bf16[32,40,128]{2,1,0:T(8,128)(2,1)S(1)}, u32[]{:S(2)}, u32[]{:S(2)}) async-start(bf16[32,40,128]{2,1,0:T(8,128)(2,1)} %bitcast.9), calls=%async_computation | async-start | bytes 655360 | tf_op jit(solution)/shard_map/all_to_all | solution.py:473
  48.1 0.0 collective-permute-done.6.after_ref
  48.1 0.0 collective-permute-done.7.before_ref
  48.1 3.3 %adjoint.1 = (bf16[128,512]{1,0:T(8,128)(2,1)S(1)}, bf16[128,512]{1,0:T(8,128)(2,1)S(1)}, bf16[128,512]{1,0:T(8,128)(2,1)S(1)}, bf16[128,512]{1,0:T(8,128)(2,1)S(1)}, bf16[128,512]{1,0:T(8,128)(2,1)S(1)}) custom-call(f32[4,512,128]{2,1,0:T(8,128)S(1)} %get-tuple-element.45.scaled_ref, bf16[2,512,128]{2,1,0:T(8,128)(2,1)S(1)} %collective-permute-done.6.after_ref, ...), custom_call_target="tpu_custom_call" | custom-call | flops 99999997952 | bytes 1310720 | tf_op jit(solution)/shard_map/adjoint/pallas_call | solution.py:474
  51.5 6.2 %all-to-all-done.parts_ref = bf16[32,40,128]{2,1,0:T(8,128)(2,1)S(1)} async-done(((bf16[32,40,128]{2,1,0:T(8,128)(2,1)}), bf16[32,40,128]{2,1,0:T(8,128)(2,1)S(1)}, u32[]{:S(2)}, u32[]{:S(2)}) %all-to-all-start) | async-done | bytes 327712 | tf_op jit(solution)/shard_map/all_to_all | solution.py:473
  57.7 0.7 part_sum.1
  58.4 5.6 %all-to-all-start.1 = ((bf16[8,40,128]{2,1,0:T(8,128)(2,1)}), bf16[8,40,128]{2,1,0:T(8,128)(2,1)S(1)}, u32[]{:S(2)}, u32[]{:S(2)}) async-start(bf16[8,40,128]{2,1,0:T(8,128)(2,1)} %part_sum.1), calls=%async_computation.1 | async-start | bytes 163840 | tf_op jit(solution)/shard_map/all_to_all | solution.py:493
  63.9 0.5 collective-permute-start.8
  64.4 0.9 %collective-permute-start.9 = (bf16[128,512]{1,0:T(8,128)(2,1)S(1)}, bf16[128,512]{1,0:T(8,128)(2,1)S(1)}, u32[]{:S(2)}, u32[]{:S(2)}) collective-permute-start(bf16[128,512]{1,0:T(8,128)(2,1)S(1)} %get-tuple-element.49), channel_id=1, source_target_pairs={{0,1},{1,2},{2,3},{3,4},{4,5},{5,6},{6,7},{7,8},{8,9},{9,10},{10,1... | collective-permute-start | bytes 393224 | tf_op jit(solution)/shard_map/ppermute | solution.py:374
  65.3 0.0 collective-permute-start.10
  65.3 4.4 %collective-permute-start.11 = (bf16[128,512]{1,0:T(8,128)(2,1)S(1)}, bf16[128,512]{1,0:T(8,128)(2,1)S(1)}, u32[]{:S(2)}, u32[]{:S(2)}) collective-permute-start(bf16[128,512]{1,0:T(8,128)(2,1)S(1)} %get-tuple-element.52), channel_id=1, source_target_pairs={{0,62},{1,63},{2,0},{3,1},{4,2},{5,3},{6,4},{7,5},{8,6},{9,7},{10,... | collective-permute-start | bytes 393224 | tf_op jit(solution)/shard_map/ppermute | solution.py:374
  69.8 1.4 %all-to-all-done.1.parts_ref = bf16[8,40,128]{2,1,0:T(8,128)(2,1)S(1)} async-done(((bf16[8,40,128]{2,1,0:T(8,128)(2,1)}), bf16[8,40,128]{2,1,0:T(8,128)(2,1)S(1)}, u32[]{:S(2)}, u32[]{:S(2)}) %all-to-all-start.1) | async-done | bytes 81952 | tf_op jit(solution)/shard_map/all_to_all | solution.py:493
  71.2 0.8 whole_sum.1
  72.0 5.4 %all-to-all-start.2 = ((bf16[32,40,128]{2,1,0:T(8,128)(2,1)}), bf16[32,40,128]{2,1,0:T(8,128)(2,1)S(1)}, u32[]{:S(2)}, u32[]{:S(2)}) async-start(bf16[32,40,128]{2,1,0:T(8,128)(2,1)} %whole_sum.1), calls=%async_computation.2 | async-start | bytes 655360 | tf_op jit(solution)/shard_map/all_to_all | solution.py:515
  77.3 0.0 collective-permute-done.8.refs_0_
  77.4 0.0 collective-permute-done.9.refs_1_
  77.4 0.0 collective-permute-done.10.refs_3_
  77.4 0.0 collective-permute-done.11.refs_4_
  77.4 2.5 %scatter.1 = (f32[4,512,128]{2,1,0:T(8,128)}, f32[8,128]{1,0:T(8,128)S(1)}) custom-call(s32[8,128]{1,0:T(8,128)S(1)} %get-tuple-element.44.cells_ref, s32[1,5]{1,0:T(1,128)S(1)} %copy-done.5, bf16[128,512]{1,0:T(8,128)(2,1)S(1)} %collective-permute-done.8.refs_0_, bf16[128,512]{1,0:T(8,128)(2,1)S(1)} %collective-permute-done.9.refs_1_, ...), custom_call_target="tpu_custom_call" | custom-call | flops 99999997952 | bytes 2105344 | tf_op jit(solution)/shard_map/scatter/pallas_call | solution.py:498
  79.9 7.1 %all-to-all-done.2 = bf16[32,40,128]{2,1,0:T(8,128)(2,1)S(1)} async-done(((bf16[32,40,128]{2,1,0:T(8,128)(2,1)}), bf16[32,40,128]{2,1,0:T(8,128)(2,1)S(1)}, u32[]{:S(2)}, u32[]{:S(2)}) %all-to-all-start.2) | async-done | bytes 327712 | tf_op jit(solution)/shard_map/all_to_all | solution.py:515
  87.0 0.8 unpack.1
  (1 shorter events, 0.0 us)
Async XLA Ops:
  0.6 0.7 copy-start.8
  1.3 1.0 %copy-start = (bf16[1,4,512,128]{3,2,1,0:T(8,128)(2,1)S(1)}, bf16[1,4,512,128]{3,2,1,0:T(8,128)(2,1)}, u32[]{:S(2)}) copy-start(bf16[1,4,512,128]{3,2,1,0:T(8,128)(2,1)} %param.12) | copy-start | bytes 1572868
  1.3 1.0 %copy-start.5 = (s32[1,5]{1,0:T(1,128)S(1)}, s32[1,5]{1,0:T(1,128)}, u32[]{:S(2)}) copy-start(s32[1,5]{1,0:T(1,128)} %count_ref.3) | copy-start | bytes 64
  2.0 12.2 %copy-start.6 = (s32[4,4,512]{2,1,0:T(4,128)S(1)}, s32[4,4,512]{2,1,0:T(4,128)}, u32[]{:S(2)}) copy-start(s32[4,4,512]{2,1,0:T(4,128)} %slot_ref.1) | copy-start | bytes 98308
  2.0 12.2 %copy-start.7 = (f32[4,4,512]{2,1,0:T(4,128)S(1)}, f32[4,4,512]{2,1,0:T(4,128)}, u32[]{:S(2)}) copy-start(f32[4,4,512]{2,1,0:T(4,128)} %weight_ref.1) | copy-start | bytes 98308
  2.0 12.1 %copy-start.9 = (f32[256]{0:T(256)S(1)}, f32[256]{0:T(256)}, u32[]{:S(2)}) copy-start(f32[256]{0:T(256)} %param.19) | copy-start | bytes 3076
  2.0 12.1 %copy-start.10 = (f32[256]{0:T(256)S(1)}, f32[256]{0:T(256)}, u32[]{:S(2)}) copy-start(f32[256]{0:T(256)} %param.21) | copy-start | bytes 3076
  2.0 12.1 %copy-start.11 = (f32[128]{0:T(128)S(1)}, f32[128]{0:T(128)}, u32[]{:S(2)}) copy-start(f32[128]{0:T(128)} %param.17) | copy-start | bytes 1540
  3.7 10.8 %collective-permute-start = (bf16[128,512]{1,0:T(8,128)(2,1)S(1)}, bf16[128,512]{1,0:T(8,128)(2,1)S(1)}, u32[]{:S(2)}, u32[]{:S(2)}) collective-permute-start(bf16[128,512]{1,0:T(8,128)(2,1)S(1)} %get-tuple-element.35), channel_id=1, source_target_pairs={{0,62},{1,63},{2,0},{3,1},{4,2},{5,3},{6,4},{7,5},{8,6},{9,7},{10,... | collective-permute-start | bytes 393224 | tf_op jit(solution)/shard_map/ppermute | solution.py:374
  12.4 7.1 %collective-permute-start.1 = (bf16[128,512]{1,0:T(8,128)(2,1)S(1)}, bf16[128,512]{1,0:T(8,128)(2,1)S(1)}, u32[]{:S(2)}, u32[]{:S(2)}) collective-permute-start(bf16[128,512]{1,0:T(8,128)(2,1)S(1)} %get-tuple-element.36), channel_id=1, source_target_pairs={{0,2},{1,3},{2,4},{3,5},{4,6},{5,7},{6,8},{7,9},{8,10},{9,11},{10,... | collective-permute-start | bytes 393224 | tf_op jit(solution)/shard_map/ppermute | solution.py:374
  12.4 7.1 %collective-permute-start.2 = (bf16[128,512]{1,0:T(8,128)(2,1)S(1)}, bf16[128,512]{1,0:T(8,128)(2,1)S(1)}, u32[]{:S(2)}, u32[]{:S(2)}) collective-permute-start(bf16[128,512]{1,0:T(8,128)(2,1)S(1)} %get-tuple-element.37), channel_id=1, source_target_pairs={{0,63},{1,0},{2,1},{3,2},{4,3},{5,4},{6,5},{7,6},{8,7},{9,8},{10,9... | collective-permute-start | bytes 393224 | tf_op jit(solution)/shard_map/ppermute | solution.py:374
  13.4 6.2 %collective-permute-start.3 = (bf16[128,512]{1,0:T(8,128)(2,1)S(1)}, bf16[128,512]{1,0:T(8,128)(2,1)S(1)}, u32[]{:S(2)}, u32[]{:S(2)}) collective-permute-start(bf16[128,512]{1,0:T(8,128)(2,1)S(1)} %get-tuple-element.38), channel_id=1, source_target_pairs={{0,1},{1,2},{2,3},{3,4},{4,5},{5,6},{6,7},{7,8},{8,9},{9,10},{10,1... | collective-permute-start | bytes 393224 | tf_op jit(solution)/shard_map/ppermute | solution.py:374
  14.2 16.5 %copy-start.1 = (bf16[1,4,512,128]{3,2,1,0:T(8,128)(2,1)S(1)}, bf16[1,4,512,128]{3,2,1,0:T(8,128)(2,1)}, u32[]{:S(2)}) copy-start(bf16[1,4,512,128]{3,2,1,0:T(8,128)(2,1)} %param.23) | copy-start | bytes 1572868
  14.2 16.5 %copy-start.2 = (bf16[256,256]{1,0:T(8,128)(2,1)S(1)}, bf16[256,256]{1,0:T(8,128)(2,1)}, u32[]{:S(2)}) copy-start(bf16[256,256]{1,0:T(8,128)(2,1)} %w2_ref.1) | copy-start | bytes 393220
  14.2 16.5 %copy-start.3 = (bf16[128,256]{1,0:T(8,128)(2,1)S(1)}, bf16[128,256]{1,0:T(8,128)(2,1)}, u32[]{:S(2)}) copy-start(bf16[128,256]{1,0:T(8,128)(2,1)} %w1_ref.1) | copy-start | bytes 196612
  14.2 16.5 %copy-start.4 = (bf16[256,128]{1,0:T(8,128)(2,1)S(1)}, bf16[256,128]{1,0:T(8,128)(2,1)}, u32[]{:S(2)}) copy-start(bf16[256,128]{1,0:T(8,128)(2,1)} %w3_ref.1) | copy-start | bytes 196612
  21.6 7.0 %collective-permute-start.4 = (bf16[2,512,128]{2,1,0:T(8,128)(2,1)S(1)}, bf16[2,512,128]{2,1,0:T(8,128)(2,1)S(1)}, u32[]{:S(2)}, u32[]{:S(2)}) collective-permute-start(bf16[2,512,128]{2,1,0:T(8,128)(2,1)S(1)} %get-tuple-element.41), channel_id=1, source_target_pairs={{0,63},{1,0},{2,1},{3,2},{4,3},{5,4},{6,5},{7,6},{8,7},{9,8},{10,9... | collective-permute-start | bytes 786440 | tf_op jit(solution)/shard_map/ppermute | solution.py:374
  27.4 3.3 %collective-permute-start.5 = (bf16[2,512,128]{2,1,0:T(8,128)(2,1)S(1)}, bf16[2,512,128]{2,1,0:T(8,128)(2,1)S(1)}, u32[]{:S(2)}, u32[]{:S(2)}) collective-permute-start(bf16[2,512,128]{2,1,0:T(8,128)(2,1)S(1)} %get-tuple-element.42), channel_id=1, source_target_pairs={{0,1},{1,2},{2,3},{3,4},{4,5},{5,6},{6,7},{7,8},{8,9},{9,10},{10,1... | collective-permute-start | bytes 786440 | tf_op jit(solution)/shard_map/ppermute | solution.py:374
  36.9 11.2 %collective-permute-start.6 = (bf16[2,512,128]{2,1,0:T(8,128)(2,1)}, bf16[2,512,128]{2,1,0:T(8,128)(2,1)S(1)}, u32[]{:S(2)}, u32[]{:S(2)}) collective-permute-start(bf16[2,512,128]{2,1,0:T(8,128)(2,1)} %get-tuple-element.46), channel_id=1, source_target_pairs={{0,63},{1,0},{2,1},{3,2},{4,3},{5,4},{6,5},{7,6},{8,7},{9,8},{10,9... | collective-permute-start | bytes 786440 | tf_op jit(solution)/shard_map/ppermute | solution.py:374
  43.0 5.2 %collective-permute-start.7 = (bf16[2,512,128]{2,1,0:T(8,128)(2,1)}, bf16[2,512,128]{2,1,0:T(8,128)(2,1)S(1)}, u32[]{:S(2)}, u32[]{:S(2)}) collective-permute-start(bf16[2,512,128]{2,1,0:T(8,128)(2,1)} %get-tuple-element.47), channel_id=1, source_target_pairs={{0,1},{1,2},{2,3},{3,4},{4,5},{5,6},{6,7},{7,8},{8,9},{9,10},{10,1... | collective-permute-start | bytes 786440 | tf_op jit(solution)/shard_map/ppermute | solution.py:374
  43.0 14.7 %all-to-all-start = ((bf16[32,40,128]{2,1,0:T(8,128)(2,1)}), bf16[32,40,128]{2,1,0:T(8,128)(2,1)S(1)}, u32[]{:S(2)}, u32[]{:S(2)}) async-start(bf16[32,40,128]{2,1,0:T(8,128)(2,1)} %bitcast.9), calls=%async_computation | async-start | bytes 655360 | tf_op jit(solution)/shard_map/all_to_all | solution.py:473
  58.4 12.9 %all-to-all-start.1 = ((bf16[8,40,128]{2,1,0:T(8,128)(2,1)}), bf16[8,40,128]{2,1,0:T(8,128)(2,1)S(1)}, u32[]{:S(2)}, u32[]{:S(2)}) async-start(bf16[8,40,128]{2,1,0:T(8,128)(2,1)} %part_sum.1), calls=%async_computation.1 | async-start | bytes 163840 | tf_op jit(solution)/shard_map/all_to_all | solution.py:493
  63.9 13.4 %collective-permute-start.8 = (bf16[128,512]{1,0:T(8,128)(2,1)S(1)}, bf16[128,512]{1,0:T(8,128)(2,1)S(1)}, u32[]{:S(2)}, u32[]{:S(2)}) collective-permute-start(bf16[128,512]{1,0:T(8,128)(2,1)S(1)} %get-tuple-element.48), channel_id=1, source_target_pairs={{0,2},{1,3},{2,4},{3,5},{4,6},{5,7},{6,8},{7,9},{8,10},{9,11},{10,... | collective-permute-start | bytes 393224 | tf_op jit(solution)/shard_map/ppermute | solution.py:374
  64.4 12.9 %collective-permute-start.9 = (bf16[128,512]{1,0:T(8,128)(2,1)S(1)}, bf16[128,512]{1,0:T(8,128)(2,1)S(1)}, u32[]{:S(2)}, u32[]{:S(2)}) collective-permute-start(bf16[128,512]{1,0:T(8,128)(2,1)S(1)} %get-tuple-element.49), channel_id=1, source_target_pairs={{0,1},{1,2},{2,3},{3,4},{4,5},{5,6},{6,7},{7,8},{8,9},{9,10},{10,1... | collective-permute-start | bytes 393224 | tf_op jit(solution)/shard_map/ppermute | solution.py:374
  65.3 12.0 %collective-permute-start.10 = (bf16[128,512]{1,0:T(8,128)(2,1)S(1)}, bf16[128,512]{1,0:T(8,128)(2,1)S(1)}, u32[]{:S(2)}, u32[]{:S(2)}) collective-permute-start(bf16[128,512]{1,0:T(8,128)(2,1)S(1)} %get-tuple-element.51), channel_id=1, source_target_pairs={{0,63},{1,0},{2,1},{3,2},{4,3},{5,4},{6,5},{7,6},{8,7},{9,8},{10,9... | collective-permute-start | bytes 393224 | tf_op jit(solution)/shard_map/ppermute | solution.py:374
  65.3 12.1 %collective-permute-start.11 = (bf16[128,512]{1,0:T(8,128)(2,1)S(1)}, bf16[128,512]{1,0:T(8,128)(2,1)S(1)}, u32[]{:S(2)}, u32[]{:S(2)}) collective-permute-start(bf16[128,512]{1,0:T(8,128)(2,1)S(1)} %get-tuple-element.52), channel_id=1, source_target_pairs={{0,62},{1,63},{2,0},{3,1},{4,2},{5,3},{6,4},{7,5},{8,6},{9,7},{10,... | collective-permute-start | bytes 393224 | tf_op jit(solution)/shard_map/ppermute | solution.py:374
  72.0 15.0 %all-to-all-start.2 = ((bf16[32,40,128]{2,1,0:T(8,128)(2,1)}), bf16[32,40,128]{2,1,0:T(8,128)(2,1)S(1)}, u32[]{:S(2)}, u32[]{:S(2)}) async-start(bf16[32,40,128]{2,1,0:T(8,128)(2,1)} %whole_sum.1), calls=%async_computation.2 | async-start | bytes 655360 | tf_op jit(solution)/shard_map/all_to_all | solution.py:515

commit v10 on v9

--- a/solution.py
+++ b/solution.py
@@ -422,7 +422,7 @@
         packed[e] if e == reach else shifted(packed[e], e - reach, bands)
         for e in range(offsets)
     ]
-    order = sorted(range(offsets), key=lambda e: -abs(e - reach))
+    order = sorted(range(offsets), key=lambda e: (-abs(e - reach), -e))
     (table,) = call(
         prepare_kernel,
         [shape((TABLE_AT + 16, lon), F32)],

time: 88.3 us -> 90.7 us (1.027)
  starting transfers between devices: 44.3 us -> 45.8 us
    all_to_all x1, starting transfers between devices: 5.55 us -> 7.28 us  [body(): parts = lax.all_to_all(part_sum, 'z', 0, 0)]
where the time goes in v10:
time: 90.7 us; the launch traced here: 90.2 us
  starting transfers between devices  45.8 us (50%)
  waiting for transfers between devices  24.1 us (27%)
  Pallas kernels  18.3 us (20%)
  local copies, waits for them, and re-layouts  1.1 us (1%)
    ppermute x12, starting transfers between devices, shifted(): lax.ppermute(block, SPACE, [(i, (i + by) % count) for i in range(count)])  28 us
    ppermute x12, waiting for transfers between devices, shifted(): lax.ppermute(block, SPACE, [(i, (i + by) % count) for i in range(count)])  9.37 us
    all_to_all x1, starting transfers between devices, body(): parts = lax.all_to_all(part_sum, 'z', 0, 0)  7.28 us
    all_to_all x1, waiting for transfers between devices, body(): lax.all_to_all(whole_sum, groups, 0, 0).reshape(group * PART_ROWS, ch)  7.12 us
    all_to_all x1, waiting for transfers between devices, body(): parts = lax.all_to_all(grads.reshape(group, PART_ROWS, ch), groups, 0, 0)  6.18 us
    pallas_call x1, Pallas kernels, body(): call(mlp_kernel, [shape((band_rows, lon, ch), BF16), shape((band_rows, lo...  6.18 us
    all_to_all x1, starting transfers between devices, body(): lax.all_to_all(whole_sum, groups, 0, 0).reshape(group * PART_ROWS, ch)  5.37 us
    all_to_all x1, starting transfers between devices, body(): parts = lax.all_to_all(grads.reshape(group, PART_ROWS, ch), groups, 0, 0)  5.13 us
  transfers between devices with their start and end apart: 15, of which 7 were waited for; matrix products, arithmetic and copies ran while one was open for 0% of the time, Pallas kernels for 7%

profile of v10, /device:TPU:1, one launch (start us, length us, event | category | flops | bytes accessed | tf_op | source)
XLA Modules:
  0.0 90.2 jit_solution(2331649980548641757)
XLA Ops:
  0.6 0.0 copy-start.8
  0.6 0.7 copy-done.8
  1.3 0.0 copy-start
  1.3 0.0 copy-start.5
  1.3 0.6 choose.1
  2.0 0.0 copy-start.6
  2.0 0.0 copy-start.7
  2.0 0.0 copy-start.9
  2.0 0.0 copy-start.10
  2.0 0.0 copy-start.11
  2.0 0.3 copy-done
  2.4 0.0 copy-done.5
  2.4 1.3 %pack.1 = (bf16[128,512]{1,0:T(8,128)(2,1)S(1)}, bf16[128,512]{1,0:T(8,128)(2,1)S(1)}, bf16[128,512]{1,0:T(8,128)(2,1)S(1)}, bf16[128,512]{1,0:T(8,128)(2,1)S(1)}, bf16[128,512]{1,0:T(8,128)(2,1)S(1)}) custom-call(bf16[4,512,128]{2,1,0:T(8,128)(2,1)S(1)} %bitcast.14, bf16[640,1536]{1,0:T(8,128)(2,1)S(1)} %get-tuple-element.34.select_ref, s32[1,5]{1,0:T(1,128)S(1)} %copy-done.5), custom_call_target="tpu_custom_call" | custom-call | bytes 1310720 | tf_op jit(solution)/shard_map/pack/pallas_call | solution.py:414
  3.7 2.1 %collective-permute-start = (bf16[128,512]{1,0:T(8,128)(2,1)S(1)}, bf16[128,512]{1,0:T(8,128)(2,1)S(1)}, u32[]{:S(2)}, u32[]{:S(2)}) collective-permute-start(bf16[128,512]{1,0:T(8,128)(2,1)S(1)} %get-tuple-element.35), channel_id=1, source_target_pairs={{0,2},{1,3},{2,4},{3,5},{4,6},{5,7},{6,8},{7,9},{8,10},{9,11},{10,... | collective-permute-start | bytes 393224 | tf_op jit(solution)/shard_map/ppermute | solution.py:374
  5.8 6.6 %collective-permute-start.1 = (bf16[128,512]{1,0:T(8,128)(2,1)S(1)}, bf16[128,512]{1,0:T(8,128)(2,1)S(1)}, u32[]{:S(2)}, u32[]{:S(2)}) collective-permute-start(bf16[128,512]{1,0:T(8,128)(2,1)S(1)} %get-tuple-element.36), channel_id=1, source_target_pairs={{0,62},{1,63},{2,0},{3,1},{4,2},{5,3},{6,4},{7,5},{8,6},{9,7},{10,... | collective-permute-start | bytes 393224 | tf_op jit(solution)/shard_map/ppermute | solution.py:374
  12.5 0.0 collective-permute-start.2
  12.5 1.0 %collective-permute-start.3 = (bf16[128,512]{1,0:T(8,128)(2,1)S(1)}, bf16[128,512]{1,0:T(8,128)(2,1)S(1)}, u32[]{:S(2)}, u32[]{:S(2)}) collective-permute-start(bf16[128,512]{1,0:T(8,128)(2,1)S(1)} %get-tuple-element.38), channel_id=1, source_target_pairs={{0,63},{1,0},{2,1},{3,2},{4,3},{5,4},{6,5},{7,6},{8,7},{9,8},{10,9... | collective-permute-start | bytes 393224 | tf_op jit(solution)/shard_map/ppermute | solution.py:374
  13.4 0.0 copy-done.6
  13.4 0.0 copy-done.7
  13.4 0.0 copy-done.9
  13.4 0.0 copy-done.10
  13.5 0.0 copy-done.11
  13.5 0.0 copy-start.1
  13.5 0.0 copy-start.2
  13.5 0.0 copy-start.3
  13.5 0.0 copy-start.4
  13.5 2.1 %collective-permute-done.refs_0_ = bf16[128,512]{1,0:T(8,128)(2,1)S(1)} collective-permute-done((bf16[128,512]{1,0:T(8,128)(2,1)S(1)}, bf16[128,512]{1,0:T(8,128)(2,1)S(1)}, u32[]{:S(2)}, u32[]{:S(2)}) %collective-permute-start) | collective-permute-done | bytes 131104 | tf_op jit(solution)/shard_map/ppermute | solution.py:374
  15.6 0.0 collective-permute-done.1.refs_1_
  15.6 0.0 collective-permute-done.2.refs_2_
  15.6 1.3 %collective-permute-done.3.refs_3_ = bf16[128,512]{1,0:T(8,128)(2,1)S(1)} collective-permute-done((bf16[128,512]{1,0:T(8,128)(2,1)S(1)}, bf16[128,512]{1,0:T(8,128)(2,1)S(1)}, u32[]{:S(2)}, u32[]{:S(2)}) %collective-permute-start.3) | collective-permute-done | bytes 131104 | tf_op jit(solution)/shard_map/ppermute | solution.py:374
  16.9 2.0 %interp.1 = (f32[4,512,128]{2,1,0:T(8,128)S(1)}, bf16[2,512,128]{2,1,0:T(8,128)(2,1)S(1)}, bf16[2,512,128]{2,1,0:T(8,128)(2,1)S(1)}) custom-call(bf16[128,512]{1,0:T(8,128)(2,1)S(1)} %collective-permute-done.refs_0_, bf16[128,512]{1,0:T(8,128)(2,1)S(1)} %collective-permute-done.1.refs_1_, bf16[128,512]{1,0:T(8,128)(2,1)S(1)} %collective-permute-done.2.refs_2_, ...), custom_call_target="tpu_custom_call" | custom-call | bytes 3145728 | tf_op jit(solution)/shard_map/interp/pallas_call | solution.py:439
  18.9 4.3 %collective-permute-start.4 = (bf16[2,512,128]{2,1,0:T(8,128)(2,1)S(1)}, bf16[2,512,128]{2,1,0:T(8,128)(2,1)S(1)}, u32[]{:S(2)}, u32[]{:S(2)}) collective-permute-start(bf16[2,512,128]{2,1,0:T(8,128)(2,1)S(1)} %get-tuple-element.41), channel_id=1, source_target_pairs={{0,63},{1,0},{2,1},{3,2},{4,3},{5,4},{6,5},{7,6},{8,7},{9,8},{10,9... | collective-permute-start | bytes 786440 | tf_op jit(solution)/shard_map/ppermute | solution.py:374
  23.3 0.0 collective-permute-start.5
  23.3 0.1 pad_add_fusion.place_ref
  23.3 1.4 %collective-permute-done.4.after_ref = bf16[2,512,128]{2,1,0:T(8,128)(2,1)S(1)} collective-permute-done((bf16[2,512,128]{2,1,0:T(8,128)(2,1)S(1)}, bf16[2,512,128]{2,1,0:T(8,128)(2,1)S(1)}, u32[]{:S(2)}, u32[]{:S(2)}) %collective-permute-start.4) | collective-permute-done | bytes 262176 | tf_op jit(solution)/shard_map/ppermute | solution.py:374
  24.8 4.6 %collective-permute-done.5.before_ref = bf16[2,512,128]{2,1,0:T(8,128)(2,1)S(1)} collective-permute-done((bf16[2,512,128]{2,1,0:T(8,128)(2,1)S(1)}, bf16[2,512,128]{2,1,0:T(8,128)(2,1)S(1)}, u32[]{:S(2)}, u32[]{:S(2)}) %collective-permute-start.5) | collective-permute-done | bytes 262176 | tf_op jit(solution)/shard_map/ppermute | solution.py:374
  29.4 0.0 copy-done.1
  29.4 0.0 copy-done.2
  29.4 0.0 copy-done.3
  29.4 0.0 copy-done.4
  29.4 6.2 %smooth_mlp.1 = (bf16[4,512,128]{2,1,0:T(8,128)(2,1)}, f32[4,512,128]{2,1,0:T(8,128)S(1)}, bf16[2,512,128]{2,1,0:T(8,128)(2,1)}, bf16[2,512,128]{2,1,0:T(8,128)(2,1)}, bf16[1280,128]{1,0:T(8,128)(2,1)}) custom-call(f32[4,512,128]{2,1,0:T(8,128)S(1)} %get-tuple-element.40.dep_ref, bf16[2,512,128]{2,1,0:T(8,128)(2,1)S(1)} %collective-permute-done.4.after_ref, ...), custom_call_target="tpu_custom_call" | custom-call | bytes 4849664 | tf_op jit(solution)/shard_map/smooth_mlp/pallas_call | solution.py:451
  35.6 8.1 %collective-permute-start.6 = (bf16[2,512,128]{2,1,0:T(8,128)(2,1)}, bf16[2,512,128]{2,1,0:T(8,128)(2,1)S(1)}, u32[]{:S(2)}, u32[]{:S(2)}) collective-permute-start(bf16[2,512,128]{2,1,0:T(8,128)(2,1)} %get-tuple-element.46), channel_id=1, source_target_pairs={{0,63},{1,0},{2,1},{3,2},{4,3},{5,4},{6,5},{7,6},{8,7},{9,8},{10,9... | collective-permute-start | bytes 786440 | tf_op jit(solution)/shard_map/ppermute | solution.py:374
  43.6 0.0 collective-permute-start.7
  43.6 5.1 %all-to-all-start = ((bf16[32,40,128]{2,1,0:T(8,128)(2,1)}), bf16[32,40,128]{2,1,0:T(8,128)(2,1)S(1)}, u32[]{:S(2)}, u32[]{:S(2)}) async-start(bf16[32,40,128]{2,1,0:T(8,128)(2,1)} %bitcast.9), calls=%async_computation | async-start | bytes 655360 | tf_op jit(solution)/shard_map/all_to_all | solution.py:473
  48.8 0.0 collective-permute-done.6.after_ref
  48.8 0.0 collective-permute-done.7.before_ref
  48.8 3.3 %adjoint.1 = (bf16[128,512]{1,0:T(8,128)(2,1)S(1)}, bf16[128,512]{1,0:T(8,128)(2,1)S(1)}, bf16[128,512]{1,0:T(8,128)(2,1)S(1)}, bf16[128,512]{1,0:T(8,128)(2,1)S(1)}, bf16[128,512]{1,0:T(8,128)(2,1)S(1)}) custom-call(f32[4,512,128]{2,1,0:T(8,128)S(1)} %get-tuple-element.45.scaled_ref, bf16[2,512,128]{2,1,0:T(8,128)(2,1)S(1)} %collective-permute-done.6.after_ref, ...), custom_call_target="tpu_custom_call" | custom-call | flops 99999997952 | bytes 1310720 | tf_op jit(solution)/shard_map/adjoint/pallas_call | solution.py:474
  52.1 6.2 %all-to-all-done.parts_ref = bf16[32,40,128]{2,1,0:T(8,128)(2,1)S(1)} async-done(((bf16[32,40,128]{2,1,0:T(8,128)(2,1)}), bf16[32,40,128]{2,1,0:T(8,128)(2,1)S(1)}, u32[]{:S(2)}, u32[]{:S(2)}) %all-to-all-start) | async-done | bytes 327712 | tf_op jit(solution)/shard_map/all_to_all | solution.py:473
  58.3 0.7 part_sum.1
  59.0 7.3 %all-to-all-start.1 = ((bf16[8,40,128]{2,1,0:T(8,128)(2,1)}), bf16[8,40,128]{2,1,0:T(8,128)(2,1)S(1)}, u32[]{:S(2)}, u32[]{:S(2)}) async-start(bf16[8,40,128]{2,1,0:T(8,128)(2,1)} %part_sum.1), calls=%async_computation.1 | async-start | bytes 163840 | tf_op jit(solution)/shard_map/all_to_all | solution.py:493
  66.3 0.5 collective-permute-start.8
  66.8 0.9 collective-permute-start.9
  67.7 0.0 collective-permute-start.10
  67.7 4.4 %collective-permute-start.11 = (bf16[128,512]{1,0:T(8,128)(2,1)S(1)}, bf16[128,512]{1,0:T(8,128)(2,1)S(1)}, u32[]{:S(2)}, u32[]{:S(2)}) collective-permute-start(bf16[128,512]{1,0:T(8,128)(2,1)S(1)} %get-tuple-element.52), channel_id=1, source_target_pairs={{0,62},{1,63},{2,0},{3,1},{4,2},{5,3},{6,4},{7,5},{8,6},{9,7},{10,... | collective-permute-start | bytes 393224 | tf_op jit(solution)/shard_map/ppermute | solution.py:374
  72.2 1.4 %all-to-all-done.1.parts_ref = bf16[8,40,128]{2,1,0:T(8,128)(2,1)S(1)} async-done(((bf16[8,40,128]{2,1,0:T(8,128)(2,1)}), bf16[8,40,128]{2,1,0:T(8,128)(2,1)S(1)}, u32[]{:S(2)}, u32[]{:S(2)}) %all-to-all-start.1) | async-done | bytes 81952 | tf_op jit(solution)/shard_map/all_to_all | solution.py:493
  73.6 0.8 whole_sum.1
  74.4 5.4 %all-to-all-start.2 = ((bf16[32,40,128]{2,1,0:T(8,128)(2,1)}), bf16[32,40,128]{2,1,0:T(8,128)(2,1)S(1)}, u32[]{:S(2)}, u32[]{:S(2)}) async-start(bf16[32,40,128]{2,1,0:T(8,128)(2,1)} %whole_sum.1), calls=%async_computation.2 | async-start | bytes 655360 | tf_op jit(solution)/shard_map/all_to_all | solution.py:515
  79.7 0.0 collective-permute-done.8.refs_0_
  79.8 0.0 collective-permute-done.9.refs_1_
  79.8 0.0 collective-permute-done.10.refs_3_
  79.8 0.0 collective-permute-done.11.refs_4_
  79.8 2.5 %scatter.1 = (f32[4,512,128]{2,1,0:T(8,128)}, f32[8,128]{1,0:T(8,128)S(1)}) custom-call(s32[8,128]{1,0:T(8,128)S(1)} %get-tuple-element.44.cells_ref, s32[1,5]{1,0:T(1,128)S(1)} %copy-done.5, bf16[128,512]{1,0:T(8,128)(2,1)S(1)} %collective-permute-done.8.refs_0_, bf16[128,512]{1,0:T(8,128)(2,1)S(1)} %collective-permute-done.9.refs_1_, ...), custom_call_target="tpu_custom_call" | custom-call | flops 99999997952 | bytes 2105344 | tf_op jit(solution)/shard_map/scatter/pallas_call | solution.py:498
  82.3 7.1 %all-to-all-done.2 = bf16[32,40,128]{2,1,0:T(8,128)(2,1)S(1)} async-done(((bf16[32,40,128]{2,1,0:T(8,128)(2,1)}), bf16[32,40,128]{2,1,0:T(8,128)(2,1)S(1)}, u32[]{:S(2)}, u32[]{:S(2)}) %all-to-all-start.2) | async-done | bytes 327712 | tf_op jit(solution)/shard_map/all_to_all | solution.py:515
  89.4 0.8 unpack.1
  (1 shorter events, 0.0 us)
Async XLA Ops:
  0.6 0.7 copy-start.8
  1.3 1.0 %copy-start = (bf16[1,4,512,128]{3,2,1,0:T(8,128)(2,1)S(1)}, bf16[1,4,512,128]{3,2,1,0:T(8,128)(2,1)}, u32[]{:S(2)}) copy-start(bf16[1,4,512,128]{3,2,1,0:T(8,128)(2,1)} %param.12) | copy-start | bytes 1572868
  1.3 1.0 %copy-start.5 = (s32[1,5]{1,0:T(1,128)S(1)}, s32[1,5]{1,0:T(1,128)}, u32[]{:S(2)}) copy-start(s32[1,5]{1,0:T(1,128)} %count_ref.3) | copy-start | bytes 64
  2.0 11.5 %copy-start.6 = (s32[4,4,512]{2,1,0:T(4,128)S(1)}, s32[4,4,512]{2,1,0:T(4,128)}, u32[]{:S(2)}) copy-start(s32[4,4,512]{2,1,0:T(4,128)} %slot_ref.1) | copy-start | bytes 98308
  2.0 11.5 %copy-start.7 = (f32[4,4,512]{2,1,0:T(4,128)S(1)}, f32[4,4,512]{2,1,0:T(4,128)}, u32[]{:S(2)}) copy-start(f32[4,4,512]{2,1,0:T(4,128)} %weight_ref.1) | copy-start | bytes 98308
  2.0 11.4 %copy-start.9 = (f32[256]{0:T(256)S(1)}, f32[256]{0:T(256)}, u32[]{:S(2)}) copy-start(f32[256]{0:T(256)} %param.19) | copy-start | bytes 3076
  2.0 11.4 %copy-start.10 = (f32[256]{0:T(256)S(1)}, f32[256]{0:T(256)}, u32[]{:S(2)}) copy-start(f32[256]{0:T(256)} %param.21) | copy-start | bytes 3076
  2.0 11.4 %copy-start.11 = (f32[128]{0:T(128)S(1)}, f32[128]{0:T(128)}, u32[]{:S(2)}) copy-start(f32[128]{0:T(128)} %param.17) | copy-start | bytes 1540
  3.7 11.9 %collective-permute-start = (bf16[128,512]{1,0:T(8,128)(2,1)S(1)}, bf16[128,512]{1,0:T(8,128)(2,1)S(1)}, u32[]{:S(2)}, u32[]{:S(2)}) collective-permute-start(bf16[128,512]{1,0:T(8,128)(2,1)S(1)} %get-tuple-element.35), channel_id=1, source_target_pairs={{0,2},{1,3},{2,4},{3,5},{4,6},{5,7},{6,8},{7,9},{8,10},{9,11},{10,... | collective-permute-start | bytes 393224 | tf_op jit(solution)/shard_map/ppermute | solution.py:374
  5.8 9.8 %collective-permute-start.1 = (bf16[128,512]{1,0:T(8,128)(2,1)S(1)}, bf16[128,512]{1,0:T(8,128)(2,1)S(1)}, u32[]{:S(2)}, u32[]{:S(2)}) collective-permute-start(bf16[128,512]{1,0:T(8,128)(2,1)S(1)} %get-tuple-element.36), channel_id=1, source_target_pairs={{0,62},{1,63},{2,0},{3,1},{4,2},{5,3},{6,4},{7,5},{8,6},{9,7},{10,... | collective-permute-start | bytes 393224 | tf_op jit(solution)/shard_map/ppermute | solution.py:374
  12.5 3.1 %collective-permute-start.2 = (bf16[128,512]{1,0:T(8,128)(2,1)S(1)}, bf16[128,512]{1,0:T(8,128)(2,1)S(1)}, u32[]{:S(2)}, u32[]{:S(2)}) collective-permute-start(bf16[128,512]{1,0:T(8,128)(2,1)S(1)} %get-tuple-element.37), channel_id=1, source_target_pairs={{0,1},{1,2},{2,3},{3,4},{4,5},{5,6},{6,7},{7,8},{8,9},{9,10},{10,1... | collective-permute-start | bytes 393224 | tf_op jit(solution)/shard_map/ppermute | solution.py:374
  12.5 4.4 %collective-permute-start.3 = (bf16[128,512]{1,0:T(8,128)(2,1)S(1)}, bf16[128,512]{1,0:T(8,128)(2,1)S(1)}, u32[]{:S(2)}, u32[]{:S(2)}) collective-permute-start(bf16[128,512]{1,0:T(8,128)(2,1)S(1)} %get-tuple-element.38), channel_id=1, source_target_pairs={{0,63},{1,0},{2,1},{3,2},{4,3},{5,4},{6,5},{7,6},{8,7},{9,8},{10,9... | collective-permute-start | bytes 393224 | tf_op jit(solution)/shard_map/ppermute | solution.py:374
  13.5 15.9 %copy-start.1 = (bf16[1,4,512,128]{3,2,1,0:T(8,128)(2,1)S(1)}, bf16[1,4,512,128]{3,2,1,0:T(8,128)(2,1)}, u32[]{:S(2)}) copy-start(bf16[1,4,512,128]{3,2,1,0:T(8,128)(2,1)} %param.23) | copy-start | bytes 1572868
  13.5 15.9 %copy-start.2 = (bf16[256,256]{1,0:T(8,128)(2,1)S(1)}, bf16[256,256]{1,0:T(8,128)(2,1)}, u32[]{:S(2)}) copy-start(bf16[256,256]{1,0:T(8,128)(2,1)} %w2_ref.1) | copy-start | bytes 393220
  13.5 15.9 %copy-start.3 = (bf16[128,256]{1,0:T(8,128)(2,1)S(1)}, bf16[128,256]{1,0:T(8,128)(2,1)}, u32[]{:S(2)}) copy-start(bf16[128,256]{1,0:T(8,128)(2,1)} %w1_ref.1) | copy-start | bytes 196612
  13.5 15.9 %copy-start.4 = (bf16[256,128]{1,0:T(8,128)(2,1)S(1)}, bf16[256,128]{1,0:T(8,128)(2,1)}, u32[]{:S(2)}) copy-start(bf16[256,128]{1,0:T(8,128)(2,1)} %w3_ref.1) | copy-start | bytes 196612
  18.9 5.9 %collective-permute-start.4 = (bf16[2,512,128]{2,1,0:T(8,128)(2,1)S(1)}, bf16[2,512,128]{2,1,0:T(8,128)(2,1)S(1)}, u32[]{:S(2)}, u32[]{:S(2)}) collective-permute-start(bf16[2,512,128]{2,1,0:T(8,128)(2,1)S(1)} %get-tuple-element.41), channel_id=1, source_target_pairs={{0,63},{1,0},{2,1},{3,2},{4,3},{5,4},{6,5},{7,6},{8,7},{9,8},{10,9... | collective-permute-start | bytes 786440 | tf_op jit(solution)/shard_map/ppermute | solution.py:374
  23.3 6.1 %collective-permute-start.5 = (bf16[2,512,128]{2,1,0:T(8,128)(2,1)S(1)}, bf16[2,512,128]{2,1,0:T(8,128)(2,1)S(1)}, u32[]{:S(2)}, u32[]{:S(2)}) collective-permute-start(bf16[2,512,128]{2,1,0:T(8,128)(2,1)S(1)} %get-tuple-element.42), channel_id=1, source_target_pairs={{0,1},{1,2},{2,3},{3,4},{4,5},{5,6},{6,7},{7,8},{8,9},{9,10},{10,1... | collective-permute-start | bytes 786440 | tf_op jit(solution)/shard_map/ppermute | solution.py:374
  35.6 13.2 %collective-permute-start.6 = (bf16[2,512,128]{2,1,0:T(8,128)(2,1)}, bf16[2,512,128]{2,1,0:T(8,128)(2,1)S(1)}, u32[]{:S(2)}, u32[]{:S(2)}) collective-permute-start(bf16[2,512,128]{2,1,0:T(8,128)(2,1)} %get-tuple-element.46), channel_id=1, source_target_pairs={{0,63},{1,0},{2,1},{3,2},{4,3},{5,4},{6,5},{7,6},{8,7},{9,8},{10,9... | collective-permute-start | bytes 786440 | tf_op jit(solution)/shard_map/ppermute | solution.py:374
  43.6 5.2 %collective-permute-start.7 = (bf16[2,512,128]{2,1,0:T(8,128)(2,1)}, bf16[2,512,128]{2,1,0:T(8,128)(2,1)S(1)}, u32[]{:S(2)}, u32[]{:S(2)}) collective-permute-start(bf16[2,512,128]{2,1,0:T(8,128)(2,1)} %get-tuple-element.47), channel_id=1, source_target_pairs={{0,1},{1,2},{2,3},{3,4},{4,5},{5,6},{6,7},{7,8},{8,9},{9,10},{10,1... | collective-permute-start | bytes 786440 | tf_op jit(solution)/shard_map/ppermute | solution.py:374
  43.6 14.7 %all-to-all-start = ((bf16[32,40,128]{2,1,0:T(8,128)(2,1)}), bf16[32,40,128]{2,1,0:T(8,128)(2,1)S(1)}, u32[]{:S(2)}, u32[]{:S(2)}) async-start(bf16[32,40,128]{2,1,0:T(8,128)(2,1)} %bitcast.9), calls=%async_computation | async-start | bytes 655360 | tf_op jit(solution)/shard_map/all_to_all | solution.py:473
  59.0 14.6 %all-to-all-start.1 = ((bf16[8,40,128]{2,1,0:T(8,128)(2,1)}), bf16[8,40,128]{2,1,0:T(8,128)(2,1)S(1)}, u32[]{:S(2)}, u32[]{:S(2)}) async-start(bf16[8,40,128]{2,1,0:T(8,128)(2,1)} %part_sum.1), calls=%async_computation.1 | async-start | bytes 163840 | tf_op jit(solution)/shard_map/all_to_all | solution.py:493
  66.3 13.4 %collective-permute-start.8 = (bf16[128,512]{1,0:T(8,128)(2,1)S(1)}, bf16[128,512]{1,0:T(8,128)(2,1)S(1)}, u32[]{:S(2)}, u32[]{:S(2)}) collective-permute-start(bf16[128,512]{1,0:T(8,128)(2,1)S(1)} %get-tuple-element.48), channel_id=1, source_target_pairs={{0,2},{1,3},{2,4},{3,5},{4,6},{5,7},{6,8},{7,9},{8,10},{9,11},{10,... | collective-permute-start | bytes 393224 | tf_op jit(solution)/shard_map/ppermute | solution.py:374
  66.8 12.9 %collective-permute-start.9 = (bf16[128,512]{1,0:T(8,128)(2,1)S(1)}, bf16[128,512]{1,0:T(8,128)(2,1)S(1)}, u32[]{:S(2)}, u32[]{:S(2)}) collective-permute-start(bf16[128,512]{1,0:T(8,128)(2,1)S(1)} %get-tuple-element.49), channel_id=1, source_target_pairs={{0,1},{1,2},{2,3},{3,4},{4,5},{5,6},{6,7},{7,8},{8,9},{9,10},{10,1... | collective-permute-start | bytes 393224 | tf_op jit(solution)/shard_map/ppermute | solution.py:374
  67.7 12.0 %collective-permute-start.10 = (bf16[128,512]{1,0:T(8,128)(2,1)S(1)}, bf16[128,512]{1,0:T(8,128)(2,1)S(1)}, u32[]{:S(2)}, u32[]{:S(2)}) collective-permute-start(bf16[128,512]{1,0:T(8,128)(2,1)S(1)} %get-tuple-element.51), channel_id=1, source_target_pairs={{0,63},{1,0},{2,1},{3,2},{4,3},{5,4},{6,5},{7,6},{8,7},{9,8},{10,9... | collective-permute-start | bytes 393224 | tf_op jit(solution)/shard_map/ppermute | solution.py:374
  67.7 12.1 %collective-permute-start.11 = (bf16[128,512]{1,0:T(8,128)(2,1)S(1)}, bf16[128,512]{1,0:T(8,128)(2,1)S(1)}, u32[]{:S(2)}, u32[]{:S(2)}) collective-permute-start(bf16[128,512]{1,0:T(8,128)(2,1)S(1)} %get-tuple-element.52), channel_id=1, source_target_pairs={{0,62},{1,63},{2,0},{3,1},{4,2},{5,3},{6,4},{7,5},{8,6},{9,7},{10,... | collective-permute-start | bytes 393224 | tf_op jit(solution)/shard_map/ppermute | solution.py:374
  74.4 15.0 %all-to-all-start.2 = ((bf16[32,40,128]{2,1,0:T(8,128)(2,1)}), bf16[32,40,128]{2,1,0:T(8,128)(2,1)S(1)}, u32[]{:S(2)}, u32[]{:S(2)}) async-start(bf16[32,40,128]{2,1,0:T(8,128)(2,1)} %whole_sum.1), calls=%async_computation.2 | async-start | bytes 655360 | tf_op jit(solution)/shard_map/all_to_all | solution.py:515

commit v11 on v10

--- a/solution.py
+++ b/solution.py
@@ -422,7 +422,7 @@
         packed[e] if e == reach else shifted(packed[e], e - reach, bands)
         for e in range(offsets)
     ]
-    order = sorted(range(offsets), key=lambda e: (-abs(e - reach), -e))
+    order = sorted(range(offsets), key=lambda e: (-abs(e - reach), abs(e - reach) * (e - reach) * (2 * abs(e - reach) - 3)))
     (table,) = call(
         prepare_kernel,
         [shape((TABLE_AT + 16, lon), F32)],

time: 90.7 us -> 88.9 us (0.980)
  starting transfers between devices: 45.8 us -> 43.2 us
    all_to_all x1, starting transfers between devices: 7.28 us -> 5.56 us  [body(): parts = lax.all_to_all(part_sum, 'z', 0, 0)]
where the time goes in v11:
time: 88.9 us; the launch traced here: 88.4 us
  starting transfers between devices  43.2 us (49%)
  waiting for transfers between devices  24.9 us (28%)
  Pallas kernels  18.3 us (21%)
  local copies, waits for them, and re-layouts  1.1 us (1%)
    ppermute x12, starting transfers between devices, shifted(): lax.ppermute(block, SPACE, [(i, (i + by) % count) for i in range(count)])  27.2 us
    ppermute x12, waiting for transfers between devices, shifted(): lax.ppermute(block, SPACE, [(i, (i + by) % count) for i in range(count)])  10.2 us
    all_to_all x1, waiting for transfers between devices, body(): lax.all_to_all(whole_sum, groups, 0, 0).reshape(group * PART_ROWS, ch)  7.11 us
    all_to_all x1, waiting for transfers between devices, body(): parts = lax.all_to_all(grads.reshape(group, PART_ROWS, ch), groups, 0, 0)  6.18 us
    pallas_call x1, Pallas kernels, body(): call(mlp_kernel, [shape((band_rows, lon, ch), BF16), shape((band_rows, lo...  6.18 us
    all_to_all x1, starting transfers between devices, body(): parts = lax.all_to_all(part_sum, 'z', 0, 0)  5.56 us
    all_to_all x1, starting transfers between devices, body(): lax.all_to_all(whole_sum, groups, 0, 0).reshape(group * PART_ROWS, ch)  5.37 us
    all_to_all x1, starting transfers between devices, body(): parts = lax.all_to_all(grads.reshape(group, PART_ROWS, ch), groups, 0, 0)  5.13 us
  transfers between devices with their start and end apart: 15, of which 7 were waited for; matrix products, arithmetic and copies ran while one was open for 0% of the time, Pallas kernels for 7%

profile of v11, /device:TPU:1, one launch (start us, length us, event | category | flops | bytes accessed | tf_op | source)
XLA Modules:
  0.0 88.4 jit_solution(17438417151651516022)
XLA Ops:
  0.6 0.0 copy-start.8
  0.6 0.7 copy-done.8
  1.3 0.0 copy-start
  1.3 0.0 copy-start.5
  1.3 0.6 choose.1
  2.0 0.0 copy-start.6
  2.0 0.0 copy-start.7
  2.0 0.0 copy-start.9
  2.0 0.0 copy-start.10
  2.0 0.0 copy-start.11
  2.0 0.3 copy-done
  2.4 0.0 copy-done.5
  2.4 1.3 %pack.1 = (bf16[128,512]{1,0:T(8,128)(2,1)S(1)}, bf16[128,512]{1,0:T(8,128)(2,1)S(1)}, bf16[128,512]{1,0:T(8,128)(2,1)S(1)}, bf16[128,512]{1,0:T(8,128)(2,1)S(1)}, bf16[128,512]{1,0:T(8,128)(2,1)S(1)}) custom-call(bf16[4,512,128]{2,1,0:T(8,128)(2,1)S(1)} %bitcast.14, bf16[640,1536]{1,0:T(8,128)(2,1)S(1)} %get-tuple-element.34.select_ref, s32[1,5]{1,0:T(1,128)S(1)} %copy-done.5), custom_call_target="tpu_custom_call" | custom-call | bytes 1310720 | tf_op jit(solution)/shard_map/pack/pallas_call | solution.py:414
  3.7 8.7 %collective-permute-start = (bf16[128,512]{1,0:T(8,128)(2,1)S(1)}, bf16[128,512]{1,0:T(8,128)(2,1)S(1)}, u32[]{:S(2)}, u32[]{:S(2)}) collective-permute-start(bf16[128,512]{1,0:T(8,128)(2,1)S(1)} %get-tuple-element.35), channel_id=1, source_target_pairs={{0,62},{1,63},{2,0},{3,1},{4,2},{5,3},{6,4},{7,5},{8,6},{9,7},{10,... | collective-permute-start | bytes 393224 | tf_op jit(solution)/shard_map/ppermute | solution.py:374
  12.4 0.0 collective-permute-start.1
  12.4 0.0 collective-permute-start.2
  12.4 1.0 %collective-permute-start.3 = (bf16[128,512]{1,0:T(8,128)(2,1)S(1)}, bf16[128,512]{1,0:T(8,128)(2,1)S(1)}, u32[]{:S(2)}, u32[]{:S(2)}) collective-permute-start(bf16[128,512]{1,0:T(8,128)(2,1)S(1)} %get-tuple-element.38), channel_id=1, source_target_pairs={{0,63},{1,0},{2,1},{3,2},{4,3},{5,4},{6,5},{7,6},{8,7},{9,8},{10,9... | collective-permute-start | bytes 393224 | tf_op jit(solution)/shard_map/ppermute | solution.py:374
  13.4 0.0 copy-done.6
  13.4 0.0 copy-done.7
  13.4 0.0 copy-done.9
  13.4 0.0 copy-done.10
  13.4 0.0 copy-done.11
  13.4 0.0 copy-start.1
  13.4 0.0 copy-start.2
  13.4 0.0 copy-start.3
  13.4 0.0 copy-start.4
  13.4 1.1 %collective-permute-done.refs_0_ = bf16[128,512]{1,0:T(8,128)(2,1)S(1)} collective-permute-done((bf16[128,512]{1,0:T(8,128)(2,1)S(1)}, bf16[128,512]{1,0:T(8,128)(2,1)S(1)}, u32[]{:S(2)}, u32[]{:S(2)}) %collective-permute-start) | collective-permute-done | bytes 131104 | tf_op jit(solution)/shard_map/ppermute | solution.py:374
  14.6 5.0 %collective-permute-done.1.refs_1_ = bf16[128,512]{1,0:T(8,128)(2,1)S(1)} collective-permute-done((bf16[128,512]{1,0:T(8,128)(2,1)S(1)}, bf16[128,512]{1,0:T(8,128)(2,1)S(1)}, u32[]{:S(2)}, u32[]{:S(2)}) %collective-permute-start.1) | collective-permute-done | bytes 131104 | tf_op jit(solution)/shard_map/ppermute | solution.py:374
  19.5 0.0 collective-permute-done.2.refs_2_
  19.5 0.0 collective-permute-done.3.refs_3_
  19.5 2.0 %interp.1 = (f32[4,512,128]{2,1,0:T(8,128)S(1)}, bf16[2,512,128]{2,1,0:T(8,128)(2,1)S(1)}, bf16[2,512,128]{2,1,0:T(8,128)(2,1)S(1)}) custom-call(bf16[128,512]{1,0:T(8,128)(2,1)S(1)} %collective-permute-done.refs_0_, bf16[128,512]{1,0:T(8,128)(2,1)S(1)} %collective-permute-done.1.refs_1_, bf16[128,512]{1,0:T(8,128)(2,1)S(1)} %collective-permute-done.2.refs_2_, ...), custom_call_target="tpu_custom_call" | custom-call | bytes 3145728 | tf_op jit(solution)/shard_map/interp/pallas_call | solution.py:439
  21.6 3.6 %collective-permute-start.4 = (bf16[2,512,128]{2,1,0:T(8,128)(2,1)S(1)}, bf16[2,512,128]{2,1,0:T(8,128)(2,1)S(1)}, u32[]{:S(2)}, u32[]{:S(2)}) collective-permute-start(bf16[2,512,128]{2,1,0:T(8,128)(2,1)S(1)} %get-tuple-element.41), channel_id=1, source_target_pairs={{0,63},{1,0},{2,1},{3,2},{4,3},{5,4},{6,5},{7,6},{8,7},{9,8},{10,9... | collective-permute-start | bytes 786440 | tf_op jit(solution)/shard_map/ppermute | solution.py:374
  25.1 0.0 collective-permute-start.5
  25.1 0.1 pad_add_fusion.place_ref
  25.2 2.2 %collective-permute-done.4.after_ref = bf16[2,512,128]{2,1,0:T(8,128)(2,1)S(1)} collective-permute-done((bf16[2,512,128]{2,1,0:T(8,128)(2,1)S(1)}, bf16[2,512,128]{2,1,0:T(8,128)(2,1)S(1)}, u32[]{:S(2)}, u32[]{:S(2)}) %collective-permute-start.4) | collective-permute-done | bytes 262176 | tf_op jit(solution)/shard_map/ppermute | solution.py:374
  27.4 1.9 %collective-permute-done.5.before_ref = bf16[2,512,128]{2,1,0:T(8,128)(2,1)S(1)} collective-permute-done((bf16[2,512,128]{2,1,0:T(8,128)(2,1)S(1)}, bf16[2,512,128]{2,1,0:T(8,128)(2,1)S(1)}, u32[]{:S(2)}, u32[]{:S(2)}) %collective-permute-start.5) | collective-permute-done | bytes 262176 | tf_op jit(solution)/shard_map/ppermute | solution.py:374
  29.3 0.0 copy-done.1
  29.3 0.0 copy-done.2
  29.3 0.0 copy-done.3
  29.3 0.0 copy-done.4
  29.3 6.2 %smooth_mlp.1 = (bf16[4,512,128]{2,1,0:T(8,128)(2,1)}, f32[4,512,128]{2,1,0:T(8,128)S(1)}, bf16[2,512,128]{2,1,0:T(8,128)(2,1)}, bf16[2,512,128]{2,1,0:T(8,128)(2,1)}, bf16[1280,128]{1,0:T(8,128)(2,1)}) custom-call(f32[4,512,128]{2,1,0:T(8,128)S(1)} %get-tuple-element.40.dep_ref, bf16[2,512,128]{2,1,0:T(8,128)(2,1)S(1)} %collective-permute-done.4.after_ref, ...), custom_call_target="tpu_custom_call" | custom-call | bytes 4849664 | tf_op jit(solution)/shard_map/smooth_mlp/pallas_call | solution.py:451
  35.5 8.1 %collective-permute-start.6 = (bf16[2,512,128]{2,1,0:T(8,128)(2,1)}, bf16[2,512,128]{2,1,0:T(8,128)(2,1)S(1)}, u32[]{:S(2)}, u32[]{:S(2)}) collective-permute-start(bf16[2,512,128]{2,1,0:T(8,128)(2,1)} %get-tuple-element.46), channel_id=1, source_target_pairs={{0,63},{1,0},{2,1},{3,2},{4,3},{5,4},{6,5},{7,6},{8,7},{9,8},{10,9... | collective-permute-start | bytes 786440 | tf_op jit(solution)/shard_map/ppermute | solution.py:374
  43.6 0.0 collective-permute-start.7
  43.6 5.1 %all-to-all-start = ((bf16[32,40,128]{2,1,0:T(8,128)(2,1)}), bf16[32,40,128]{2,1,0:T(8,128)(2,1)S(1)}, u32[]{:S(2)}, u32[]{:S(2)}) async-start(bf16[32,40,128]{2,1,0:T(8,128)(2,1)} %bitcast.9), calls=%async_computation | async-start | bytes 655360 | tf_op jit(solution)/shard_map/all_to_all | solution.py:473
  48.7 0.0 collective-permute-done.6.after_ref
  48.7 0.0 collective-permute-done.7.before_ref
  48.7 3.3 %adjoint.1 = (bf16[128,512]{1,0:T(8,128)(2,1)S(1)}, bf16[128,512]{1,0:T(8,128)(2,1)S(1)}, bf16[128,512]{1,0:T(8,128)(2,1)S(1)}, bf16[128,512]{1,0:T(8,128)(2,1)S(1)}, bf16[128,512]{1,0:T(8,128)(2,1)S(1)}) custom-call(f32[4,512,128]{2,1,0:T(8,128)S(1)} %get-tuple-element.45.scaled_ref, bf16[2,512,128]{2,1,0:T(8,128)(2,1)S(1)} %collective-permute-done.6.after_ref, ...), custom_call_target="tpu_custom_call" | custom-call | flops 99999997952 | bytes 1310720 | tf_op jit(solution)/shard_map/adjoint/pallas_call | solution.py:474
  52.1 6.2 %all-to-all-done.parts_ref = bf16[32,40,128]{2,1,0:T(8,128)(2,1)S(1)} async-done(((bf16[32,40,128]{2,1,0:T(8,128)(2,1)}), bf16[32,40,128]{2,1,0:T(8,128)(2,1)S(1)}, u32[]{:S(2)}, u32[]{:S(2)}) %all-to-all-start) | async-done | bytes 327712 | tf_op jit(solution)/shard_map/all_to_all | solution.py:473
  58.3 0.7 part_sum.1
  59.0 5.6 %all-to-all-start.1 = ((bf16[8,40,128]{2,1,0:T(8,128)(2,1)}), bf16[8,40,128]{2,1,0:T(8,128)(2,1)S(1)}, u32[]{:S(2)}, u32[]{:S(2)}) async-start(bf16[8,40,128]{2,1,0:T(8,128)(2,1)} %part_sum.1), calls=%async_computation.1 | async-start | bytes 163840 | tf_op jit(solution)/shard_map/all_to_all | solution.py:493
  64.5 0.5 collective-permute-start.8
  65.1 0.9 %collective-permute-start.9 = (bf16[128,512]{1,0:T(8,128)(2,1)S(1)}, bf16[128,512]{1,0:T(8,128)(2,1)S(1)}, u32[]{:S(2)}, u32[]{:S(2)}) collective-permute-start(bf16[128,512]{1,0:T(8,128)(2,1)S(1)} %get-tuple-element.49), channel_id=1, source_target_pairs={{0,1},{1,2},{2,3},{3,4},{4,5},{5,6},{6,7},{7,8},{8,9},{9,10},{10,1... | collective-permute-start | bytes 393224 | tf_op jit(solution)/shard_map/ppermute | solution.py:374
  65.9 0.0 collective-permute-start.10
  65.9 4.4 %collective-permute-start.11 = (bf16[128,512]{1,0:T(8,128)(2,1)S(1)}, bf16[128,512]{1,0:T(8,128)(2,1)S(1)}, u32[]{:S(2)}, u32[]{:S(2)}) collective-permute-start(bf16[128,512]{1,0:T(8,128)(2,1)S(1)} %get-tuple-element.52), channel_id=1, source_target_pairs={{0,62},{1,63},{2,0},{3,1},{4,2},{5,3},{6,4},{7,5},{8,6},{9,7},{10,... | collective-permute-start | bytes 393224 | tf_op jit(solution)/shard_map/ppermute | solution.py:374
  70.4 1.4 %all-to-all-done.1.parts_ref = bf16[8,40,128]{2,1,0:T(8,128)(2,1)S(1)} async-done(((bf16[8,40,128]{2,1,0:T(8,128)(2,1)}), bf16[8,40,128]{2,1,0:T(8,128)(2,1)S(1)}, u32[]{:S(2)}, u32[]{:S(2)}) %all-to-all-start.1) | async-done | bytes 81952 | tf_op jit(solution)/shard_map/all_to_all | solution.py:493
  71.8 0.8 whole_sum.1
  72.6 5.4 %all-to-all-start.2 = ((bf16[32,40,128]{2,1,0:T(8,128)(2,1)}), bf16[32,40,128]{2,1,0:T(8,128)(2,1)S(1)}, u32[]{:S(2)}, u32[]{:S(2)}) async-start(bf16[32,40,128]{2,1,0:T(8,128)(2,1)} %whole_sum.1), calls=%async_computation.2 | async-start | bytes 655360 | tf_op jit(solution)/shard_map/all_to_all | solution.py:515
  78.0 0.0 collective-permute-done.8.refs_0_
  78.0 0.0 collective-permute-done.9.refs_1_
  78.0 0.0 collective-permute-done.10.refs_3_
  78.0 0.0 collective-permute-done.11.refs_4_
  78.0 2.5 %scatter.1 = (f32[4,512,128]{2,1,0:T(8,128)}, f32[8,128]{1,0:T(8,128)S(1)}) custom-call(s32[8,128]{1,0:T(8,128)S(1)} %get-tuple-element.44.cells_ref, s32[1,5]{1,0:T(1,128)S(1)} %copy-done.5, bf16[128,512]{1,0:T(8,128)(2,1)S(1)} %collective-permute-done.8.refs_0_, bf16[128,512]{1,0:T(8,128)(2,1)S(1)} %collective-permute-done.9.refs_1_, ...), custom_call_target="tpu_custom_call" | custom-call | flops 99999997952 | bytes 2105344 | tf_op jit(solution)/shard_map/scatter/pallas_call | solution.py:498
  80.5 7.1 %all-to-all-done.2 = bf16[32,40,128]{2,1,0:T(8,128)(2,1)S(1)} async-done(((bf16[32,40,128]{2,1,0:T(8,128)(2,1)}), bf16[32,40,128]{2,1,0:T(8,128)(2,1)S(1)}, u32[]{:S(2)}, u32[]{:S(2)}) %all-to-all-start.2) | async-done | bytes 327712 | tf_op jit(solution)/shard_map/all_to_all | solution.py:515
  87.6 0.8 unpack.1
  (1 shorter events, 0.0 us)
Async XLA Ops:
  0.6 0.7 copy-start.8
  1.3 1.0 %copy-start = (bf16[1,4,512,128]{3,2,1,0:T(8,128)(2,1)S(1)}, bf16[1,4,512,128]{3,2,1,0:T(8,128)(2,1)}, u32[]{:S(2)}) copy-start(bf16[1,4,512,128]{3,2,1,0:T(8,128)(2,1)} %param.12) | copy-start | bytes 1572868
  1.3 1.0 %copy-start.5 = (s32[1,5]{1,0:T(1,128)S(1)}, s32[1,5]{1,0:T(1,128)}, u32[]{:S(2)}) copy-start(s32[1,5]{1,0:T(1,128)} %count_ref.3) | copy-start | bytes 64
  2.0 11.4 %copy-start.6 = (s32[4,4,512]{2,1,0:T(4,128)S(1)}, s32[4,4,512]{2,1,0:T(4,128)}, u32[]{:S(2)}) copy-start(s32[4,4,512]{2,1,0:T(4,128)} %slot_ref.1) | copy-start | bytes 98308
  2.0 11.4 %copy-start.7 = (f32[4,4,512]{2,1,0:T(4,128)S(1)}, f32[4,4,512]{2,1,0:T(4,128)}, u32[]{:S(2)}) copy-start(f32[4,4,512]{2,1,0:T(4,128)} %weight_ref.1) | copy-start | bytes 98308
  2.0 11.4 %copy-start.9 = (f32[256]{0:T(256)S(1)}, f32[256]{0:T(256)}, u32[]{:S(2)}) copy-start(f32[256]{0:T(256)} %param.19) | copy-start | bytes 3076
  2.0 11.4 %copy-start.10 = (f32[256]{0:T(256)S(1)}, f32[256]{0:T(256)}, u32[]{:S(2)}) copy-start(f32[256]{0:T(256)} %param.21) | copy-start | bytes 3076
  2.0 11.3 %copy-start.11 = (f32[128]{0:T(128)S(1)}, f32[128]{0:T(128)}, u32[]{:S(2)}) copy-start(f32[128]{0:T(128)} %param.17) | copy-start | bytes 1540
  3.7 10.8 %collective-permute-start = (bf16[128,512]{1,0:T(8,128)(2,1)S(1)}, bf16[128,512]{1,0:T(8,128)(2,1)S(1)}, u32[]{:S(2)}, u32[]{:S(2)}) collective-permute-start(bf16[128,512]{1,0:T(8,128)(2,1)S(1)} %get-tuple-element.35), channel_id=1, source_target_pairs={{0,62},{1,63},{2,0},{3,1},{4,2},{5,3},{6,4},{7,5},{8,6},{9,7},{10,... | collective-permute-start | bytes 393224 | tf_op jit(solution)/shard_map/ppermute | solution.py:374
  12.4 7.1 %collective-permute-start.1 = (bf16[128,512]{1,0:T(8,128)(2,1)S(1)}, bf16[128,512]{1,0:T(8,128)(2,1)S(1)}, u32[]{:S(2)}, u32[]{:S(2)}) collective-permute-start(bf16[128,512]{1,0:T(8,128)(2,1)S(1)} %get-tuple-element.36), channel_id=1, source_target_pairs={{0,2},{1,3},{2,4},{3,5},{4,6},{5,7},{6,8},{7,9},{8,10},{9,11},{10,... | collective-permute-start | bytes 393224 | tf_op jit(solution)/shard_map/ppermute | solution.py:374
  12.4 7.1 %collective-permute-start.2 = (bf16[128,512]{1,0:T(8,128)(2,1)S(1)}, bf16[128,512]{1,0:T(8,128)(2,1)S(1)}, u32[]{:S(2)}, u32[]{:S(2)}) collective-permute-start(bf16[128,512]{1,0:T(8,128)(2,1)S(1)} %get-tuple-element.37), channel_id=1, source_target_pairs={{0,1},{1,2},{2,3},{3,4},{4,5},{5,6},{6,7},{7,8},{8,9},{9,10},{10,1... | collective-permute-start | bytes 393224 | tf_op jit(solution)/shard_map/ppermute | solution.py:374
  12.4 7.1 %collective-permute-start.3 = (bf16[128,512]{1,0:T(8,128)(2,1)S(1)}, bf16[128,512]{1,0:T(8,128)(2,1)S(1)}, u32[]{:S(2)}, u32[]{:S(2)}) collective-permute-start(bf16[128,512]{1,0:T(8,128)(2,1)S(1)} %get-tuple-element.38), channel_id=1, source_target_pairs={{0,63},{1,0},{2,1},{3,2},{4,3},{5,4},{6,5},{7,6},{8,7},{9,8},{10,9... | collective-permute-start | bytes 393224 | tf_op jit(solution)/shard_map/ppermute | solution.py:374
  13.4 15.9 %copy-start.1 = (bf16[1,4,512,128]{3,2,1,0:T(8,128)(2,1)S(1)}, bf16[1,4,512,128]{3,2,1,0:T(8,128)(2,1)}, u32[]{:S(2)}) copy-start(bf16[1,4,512,128]{3,2,1,0:T(8,128)(2,1)} %param.23) | copy-start | bytes 1572868
  13.4 15.9 %copy-start.2 = (bf16[256,256]{1,0:T(8,128)(2,1)S(1)}, bf16[256,256]{1,0:T(8,128)(2,1)}, u32[]{:S(2)}) copy-start(bf16[256,256]{1,0:T(8,128)(2,1)} %w2_ref.1) | copy-start | bytes 393220
  13.4 15.9 %copy-start.3 = (bf16[128,256]{1,0:T(8,128)(2,1)S(1)}, bf16[128,256]{1,0:T(8,128)(2,1)}, u32[]{:S(2)}) copy-start(bf16[128,256]{1,0:T(8,128)(2,1)} %w1_ref.1) | copy-start | bytes 196612
  13.4 15.9 %copy-start.4 = (bf16[256,128]{1,0:T(8,128)(2,1)S(1)}, bf16[256,128]{1,0:T(8,128)(2,1)}, u32[]{:S(2)}) copy-start(bf16[256,128]{1,0:T(8,128)(2,1)} %w3_ref.1) | copy-start | bytes 196612
  21.6 5.9 %collective-permute-start.4 = (bf16[2,512,128]{2,1,0:T(8,128)(2,1)S(1)}, bf16[2,512,128]{2,1,0:T(8,128)(2,1)S(1)}, u32[]{:S(2)}, u32[]{:S(2)}) collective-permute-start(bf16[2,512,128]{2,1,0:T(8,128)(2,1)S(1)} %get-tuple-element.41), channel_id=1, source_target_pairs={{0,63},{1,0},{2,1},{3,2},{4,3},{5,4},{6,5},{7,6},{8,7},{9,8},{10,9... | collective-permute-start | bytes 786440 | tf_op jit(solution)/shard_map/ppermute | solution.py:374
  25.1 4.2 %collective-permute-start.5 = (bf16[2,512,128]{2,1,0:T(8,128)(2,1)S(1)}, bf16[2,512,128]{2,1,0:T(8,128)(2,1)S(1)}, u32[]{:S(2)}, u32[]{:S(2)}) collective-permute-start(bf16[2,512,128]{2,1,0:T(8,128)(2,1)S(1)} %get-tuple-element.42), channel_id=1, source_target_pairs={{0,1},{1,2},{2,3},{3,4},{4,5},{5,6},{6,7},{7,8},{8,9},{9,10},{10,1... | collective-permute-start | bytes 786440 | tf_op jit(solution)/shard_map/ppermute | solution.py:374
  35.5 13.2 %collective-permute-start.6 = (bf16[2,512,128]{2,1,0:T(8,128)(2,1)}, bf16[2,512,128]{2,1,0:T(8,128)(2,1)S(1)}, u32[]{:S(2)}, u32[]{:S(2)}) collective-permute-start(bf16[2,512,128]{2,1,0:T(8,128)(2,1)} %get-tuple-element.46), channel_id=1, source_target_pairs={{0,63},{1,0},{2,1},{3,2},{4,3},{5,4},{6,5},{7,6},{8,7},{9,8},{10,9... | collective-permute-start | bytes 786440 | tf_op jit(solution)/shard_map/ppermute | solution.py:374
  43.6 5.2 %collective-permute-start.7 = (bf16[2,512,128]{2,1,0:T(8,128)(2,1)}, bf16[2,512,128]{2,1,0:T(8,128)(2,1)S(1)}, u32[]{:S(2)}, u32[]{:S(2)}) collective-permute-start(bf16[2,512,128]{2,1,0:T(8,128)(2,1)} %get-tuple-element.47), channel_id=1, source_target_pairs={{0,1},{1,2},{2,3},{3,4},{4,5},{5,6},{6,7},{7,8},{8,9},{9,10},{10,1... | collective-permute-start | bytes 786440 | tf_op jit(solution)/shard_map/ppermute | solution.py:374
  43.6 14.7 %all-to-all-start = ((bf16[32,40,128]{2,1,0:T(8,128)(2,1)}), bf16[32,40,128]{2,1,0:T(8,128)(2,1)S(1)}, u32[]{:S(2)}, u32[]{:S(2)}) async-start(bf16[32,40,128]{2,1,0:T(8,128)(2,1)} %bitcast.9), calls=%async_computation | async-start | bytes 655360 | tf_op jit(solution)/shard_map/all_to_all | solution.py:473
  59.0 12.9 %all-to-all-start.1 = ((bf16[8,40,128]{2,1,0:T(8,128)(2,1)}), bf16[8,40,128]{2,1,0:T(8,128)(2,1)S(1)}, u32[]{:S(2)}, u32[]{:S(2)}) async-start(bf16[8,40,128]{2,1,0:T(8,128)(2,1)} %part_sum.1), calls=%async_computation.1 | async-start | bytes 163840 | tf_op jit(solution)/shard_map/all_to_all | solution.py:493
  64.5 13.4 %collective-permute-start.8 = (bf16[128,512]{1,0:T(8,128)(2,1)S(1)}, bf16[128,512]{1,0:T(8,128)(2,1)S(1)}, u32[]{:S(2)}, u32[]{:S(2)}) collective-permute-start(bf16[128,512]{1,0:T(8,128)(2,1)S(1)} %get-tuple-element.48), channel_id=1, source_target_pairs={{0,2},{1,3},{2,4},{3,5},{4,6},{5,7},{6,8},{7,9},{8,10},{9,11},{10,... | collective-permute-start | bytes 393224 | tf_op jit(solution)/shard_map/ppermute | solution.py:374
  65.1 12.9 %collective-permute-start.9 = (bf16[128,512]{1,0:T(8,128)(2,1)S(1)}, bf16[128,512]{1,0:T(8,128)(2,1)S(1)}, u32[]{:S(2)}, u32[]{:S(2)}) collective-permute-start(bf16[128,512]{1,0:T(8,128)(2,1)S(1)} %get-tuple-element.49), channel_id=1, source_target_pairs={{0,1},{1,2},{2,3},{3,4},{4,5},{5,6},{6,7},{7,8},{8,9},{9,10},{10,1... | collective-permute-start | bytes 393224 | tf_op jit(solution)/shard_map/ppermute | solution.py:374
  65.9 12.0 %collective-permute-start.10 = (bf16[128,512]{1,0:T(8,128)(2,1)S(1)}, bf16[128,512]{1,0:T(8,128)(2,1)S(1)}, u32[]{:S(2)}, u32[]{:S(2)}) collective-permute-start(bf16[128,512]{1,0:T(8,128)(2,1)S(1)} %get-tuple-element.51), channel_id=1, source_target_pairs={{0,63},{1,0},{2,1},{3,2},{4,3},{5,4},{6,5},{7,6},{8,7},{9,8},{10,9... | collective-permute-start | bytes 393224 | tf_op jit(solution)/shard_map/ppermute | solution.py:374
  65.9 12.1 %collective-permute-start.11 = (bf16[128,512]{1,0:T(8,128)(2,1)S(1)}, bf16[128,512]{1,0:T(8,128)(2,1)S(1)}, u32[]{:S(2)}, u32[]{:S(2)}) collective-permute-start(bf16[128,512]{1,0:T(8,128)(2,1)S(1)} %get-tuple-element.52), channel_id=1, source_target_pairs={{0,62},{1,63},{2,0},{3,1},{4,2},{5,3},{6,4},{7,5},{8,6},{9,7},{10,... | collective-permute-start | bytes 393224 | tf_op jit(solution)/shard_map/ppermute | solution.py:374
  72.6 15.0 %all-to-all-start.2 = ((bf16[32,40,128]{2,1,0:T(8,128)(2,1)}), bf16[32,40,128]{2,1,0:T(8,128)(2,1)S(1)}, u32[]{:S(2)}, u32[]{:S(2)}) async-start(bf16[32,40,128]{2,1,0:T(8,128)(2,1)} %whole_sum.1), calls=%async_computation.2 | async-start | bytes 655360 | tf_op jit(solution)/shard_map/all_to_all | solution.py:515
